TPU v7x, 32 devices: a whole 2x2x4 slice. The times are simulated.
32 devices in a mesh: dp: 4 (over y, x), wide: 8 (over z, core).
Axes of the slice: x: 2, y: 2, z: 4, core: 2. Of those that a mesh axis runs over, the one named last changes fastest.
Arguments:
- images: bfloat16 [2048, 49, 192], P(('dp', 'wide')), may hold values from -18 to 18
- dom_label: int32 [2048], P(('dp', 'wide')), may hold values from 0 to 7, as said below
- class_label: int32 [2048], P(('dp', 'wide')), may hold values from 0 to 999
- expand_weight: float32 [1152, 1536], P('wide'), may hold values from -0.3125 to 0.3125
- expand_first: float32 [1152, 1536], P('wide'), may hold values from -0.0006629126 to 0.0006629126
- expand_second: float32 [1152, 1536], P('wide'), may hold values from 6.1035155e-09 to 2.4414062e-08
- expand_state: float32 [2, 8, 1152, 4], P(None, None, 'wide'), may hold values from -1 to 1, as said below
- project_weight: float32 [320, 9216], P('wide'), may hold values from -0.125 to 0.125
- project_first: float32 [320, 9216], P('wide'), may hold values from -0.0006629126 to 0.0006629126
- project_second: float32 [320, 9216], P('wide'), may hold values from 6.103516e-08 to 2.4414064e-07
- project_state: float32 [2, 8, 320, 4], P(None, None, 'wide'), may hold values from -1 to 1, as said below
- head_weight: float32 [1280, 2560], P('wide'), may hold values from -0.25 to 0.25
- head_first: float32 [1280, 2560], P('wide'), may hold values from -0.0006629126 to 0.0006629126
- head_second: float32 [1280, 2560], P('wide'), may hold values from 6.103516e-08 to 2.4414064e-07
- head_state: float32 [2, 8, 1280, 4], P(None, None, 'wide'), may hold values from -1 to 1, as said below
- depth_weight: float32 [8, 9, 1152], P(None, None, 'wide'), may hold values from -1.5 to 1.5
- depth_first: float32 [8, 9, 1152], P(None, None, 'wide'), may hold values from -0.0006629126 to 0.0006629126
- depth_second: float32 [8, 9, 1152], P(None, None, 'wide'), may hold values from 6.103516e-08 to 2.4414064e-07
- classifier_weight: float32 [1280, 1000], P('wide'), may hold values from -0.3125 to 0.3125
- classifier_first: float32 [1280, 1000], P('wide'), may hold values from -0.00041926274 to 0.00041926274
- classifier_second: float32 [1280, 1000], P('wide'), may hold values from 2.4414062e-08 to 9.765625e-08
- excite_weight: float32 [2, 1152, 48], replicated, may hold values from -0.4 to 0.4
- excite_first: float32 [2, 1152, 48], replicated, may hold values from -0.0006629126 to 0.0006629126
- excite_second: float32 [2, 1152, 48], replicated, may hold values from 6.103516e-08 to 2.4414064e-07
- router_weight: float32 [512, 8], replicated, may hold values from -1.25 to 1.25
- router_first: float32 [512, 8], replicated, may hold values from -0.0006629126 to 0.0006629126
- router_second: float32 [512, 8], replicated, may hold values from 6.103516e-08 to 2.4414064e-07
- gains_weight: float32 [5400], replicated, may hold values from 0.5 to 1.5
- gains_first: float32 [5400], replicated, may hold values from -0.0013258252 to 0.0013258252
- gains_second: float32 [5400], replicated, may hold values from 2.4414064e-07 to 9.765625e-07
Outputs:
- loss: float32 [], replicated
- expand_moment: float32 [1152, 1536], P('wide')
- expand_rotated: float32 [1152, 1536], P('wide')
- expand_basis: float32 [2, 8, 1152, 4], P(None, None, 'wide')
- expand_master: float32 [1152, 1536], P('wide')
- project_moment: float32 [320, 9216], P('wide')
- project_rotated: float32 [320, 9216], P('wide')
- project_basis: float32 [2, 8, 320, 4], P(None, None, 'wide')
- project_master: float32 [320, 9216], P('wide')
- head_moment: float32 [1280, 2560], P('wide')
- head_rotated: float32 [1280, 2560], P('wide')
- head_basis: float32 [2, 8, 1280, 4], P(None, None, 'wide')
- head_master: float32 [1280, 2560], P('wide')
- depth_moment: float32 [8, 9, 1152], P(None, None, 'wide')
- depth_squares: float32 [8, 9, 1152], P(None, None, 'wide')
- depth_master: float32 [8, 9, 1152], P(None, None, 'wide')
- classifier_moment: float32 [1280, 1000], P('wide')
- classifier_squares: float32 [1280, 1000], P('wide')
- classifier_master: float32 [1280, 1000], P('wide')
- excite_moment: float32 [2, 1152, 48], replicated
- excite_squares: float32 [2, 1152, 48], replicated
- excite_master: float32 [2, 1152, 48], replicated
- router_moment: float32 [512, 8], replicated
- router_squares: float32 [512, 8], replicated
- router_master: float32 [512, 8], replicated
- gains_moment: float32 [5400], replicated
- gains_squares: float32 [5400], replicated
- gains_master: float32 [5400], replicated
Inputs may be any that keep to these rules, and one draw needn't show every extreme that they name: `dom_label`: nondecreasing along the images, so that the images come grouped by dominant expert; every expert is some image's, some far more often than others. `expand_state`: first half: per expert and block of 4 output channels a positive diagonal matrix of trace one; second half: an orthogonal matrix per block. `project_state`: as expand_state. `head_state`: as expand_state.
All inputs are finite; a program needn't handle non-finite values.
Results may differ from a plain program's by a relative error of at most 0.02.
Values may be sent and summed in bfloat16 or wider, within the bound.
A program may use at most 576 MiB of HBM per device.

v0:
```python
import jax
import jax.numpy as jnp
from jax import lax
from jax.sharding import PartitionSpec as P

SIDE = 7
PIX = 49
KSIZE = 3
EXPERTS = 8
BLK = 4
STEP = 10
C_IN = 192
C_MID = 1152
C_SE = 48
C_OUT = 320
C_HEAD = 1280
CLASSES = 1000


HIGH = lax.Precision.HIGHEST
beta_one = 0.9
beta_two = 0.95
eps_adam = 1e-08
eps_norm = 1e-05
decay = 0.01
rate_matrix = 0.08
rate_gains = 0.5
boost = 1.0
balance_weight = 4.0
stat_gain = 15000.0


def silu(value):
    return value * jax.nn.sigmoid(value)


def silu_slope(value):
    sig = jax.nn.sigmoid(value)
    return sig * (1.0 + value * (1.0 - sig))


def depthwise(act, kern):
    grid = act.reshape(act.shape[0], SIDE, SIDE, act.shape[-1])
    margin = KSIZE // 2
    padded = jnp.pad(grid, ((0, 0), (margin, margin), (margin, margin), (0, 0)))
    total = jnp.zeros_like(grid)
    for tap in range(KSIZE * KSIZE):
        row_at = tap // KSIZE
        col_at = tap % KSIZE
        total = (
            total
            + padded[:, row_at : row_at + SIDE, col_at : col_at + SIDE, :]
            * kern[:, tap][:, None, None, :]
        )
    return total.reshape(act.shape)


def excite_branch(hidden, kern_depth, excite_w, bias_se, bias_ex):
    act = silu(depthwise(silu(hidden), kern_depth))
    pooled = jnp.mean(act, axis=1)
    squeeze = silu(jnp.dot(pooled, excite_w[0], precision=HIGH) + bias_se)
    gate = jax.nn.sigmoid(jnp.dot(squeeze, excite_w[1].T, precision=HIGH) + bias_ex)
    return act * gate[:, None, :]


def split_gains(gains):
    widths = [C_SE, C_MID, C_OUT, C_OUT, C_HEAD, C_HEAD, CLASSES]
    pieces = []
    start = 0
    for width in widths:
        pieces.append(gains[start : start + width])
        start = start + width
    return pieces


def mixed(route, flat):
    cube = flat.reshape(flat.shape[0], EXPERTS, -1)
    return jnp.einsum("ne,dec->ncd", route, cube, preferred_element_type=jnp.float32)


def convolve(act, kern):
    return jnp.einsum("npc,ncd->npd", act, kern, preferred_element_type=jnp.float32)


def kern_grad(act, grad_out):
    return jnp.einsum("npc,npd->ncd", act, grad_out, preferred_element_type=jnp.float32)


def input_grad(grad_out, kern):
    return jnp.einsum("npd,ncd->npc", grad_out, kern, preferred_element_type=jnp.float32)


def route_grad(kern_g, flat):
    cube = flat.reshape(flat.shape[0], EXPERTS, -1)
    return jnp.einsum("ncd,dec->ne", kern_g, cube, preferred_element_type=jnp.float32)


def expert_grad(route, kern_g):
    cube = jnp.einsum("ne,ncd->dec", route, kern_g, preferred_element_type=jnp.float32)
    return cube.reshape(cube.shape[0], -1)


def balance_grad(means, every):
    return balance_weight * 2.0 * (means - jnp.mean(means)) / (EXPERTS * every)


def orthonormal(matrix):
    columns = []
    for index in range(BLK):
        column = matrix[..., index]
        for previous in columns:
            column = column - jnp.sum(previous * column, axis=-1, keepdims=True) * previous
        column = column * lax.rsqrt(jnp.sum(column * column, axis=-1, keepdims=True))
        columns.append(column)
    return jnp.stack(columns, axis=-1)


def to_cube(flat):
    return flat.reshape(flat.shape[0], EXPERTS, -1).transpose(1, 2, 0)


def to_flat(cube):
    return cube.transpose(2, 0, 1).reshape(cube.shape[2], -1)


def soap_cube(weight, grad, first, second, state, every):
    blocks = weight.shape[2] // BLK
    gained = stat_gain * every / grad.shape[1]
    corr_one = 1.0 - beta_one**STEP
    corr_two = 1.0 - beta_two**STEP
    stats = state[0].reshape(EXPERTS, blocks, BLK, BLK)
    basis = state[1].reshape(EXPERTS, blocks, BLK, BLK)
    cut = grad.reshape(EXPERTS, grad.shape[1], blocks, BLK)
    turned = jnp.einsum("eibj,ebjl->eibl", cut, basis, precision=HIGH)
    first_new = beta_one * first + (1.0 - beta_one) * grad
    second_new = beta_two * second + (1.0 - beta_two) * (turned * turned).reshape(grad.shape)
    moment = jnp.einsum("eibj,ebjl->eibl", first_new.reshape(cut.shape), basis, precision=HIGH)
    ratio = moment / corr_one / (jnp.sqrt(second_new.reshape(cut.shape) / corr_two) + eps_adam)
    back = jnp.einsum("eibl,ebjl->eibj", ratio, basis, precision=HIGH).reshape(grad.shape)
    weight_new = weight - rate_matrix * (back + decay * weight)
    summed = beta_two * stats + (1.0 - beta_two) * gained * jnp.einsum(
        "eibj,eibl->ebjl", cut, cut, precision=HIGH
    )
    trace = jnp.sum(jnp.diagonal(summed, axis1=-2, axis2=-1), axis=-1)
    stats_new = summed / trace[..., None, None]
    basis_new = orthonormal(jnp.einsum("ebjl,eblm->ebjm", stats_new, basis, precision=HIGH))
    state_new = jnp.stack([stats_new.reshape(state[0].shape), basis_new.reshape(state[1].shape)])
    return (first_new, second_new, state_new, weight_new)


def soap(weight, grad, first, second, state, every):
    first_new, second_new, state_new, weight_new = soap_cube(
        to_cube(weight), to_cube(grad), to_cube(first), to_cube(second), state, every
    )
    return (to_flat(first_new), to_flat(second_new), state_new, to_flat(weight_new))


def adam(weight, grad, first, second, rate):
    corr_one = 1.0 - beta_one**STEP
    corr_two = 1.0 - beta_two**STEP
    first_new = beta_one * first + (1.0 - beta_one) * grad
    second_new = beta_two * second + (1.0 - beta_two) * grad * grad
    weight_new = weight - rate * (
        first_new / corr_one / (jnp.sqrt(second_new / corr_two) + eps_adam) + decay * weight
    )
    return (first_new, second_new, weight_new)


def local(
    images,
    dom_label,
    class_label,
    expand_weight,
    expand_first,
    expand_second,
    expand_state,
    project_weight,
    project_first,
    project_second,
    project_state,
    head_weight,
    head_first,
    head_second,
    head_state,
    depth_weight,
    depth_first,
    depth_second,
    classifier_weight,
    classifier_first,
    classifier_second,
    excite_weight,
    excite_first,
    excite_second,
    router_weight,
    router_first,
    router_second,
    gains_weight,
    gains_first,
    gains_second,
):
    low_type = jnp.bfloat16
    every = images.shape[0] * lax.axis_size("dp") * lax.axis_size("wide")
    count = every * PIX
    bias_se, bias_ex, gain_one, shift_one, gain_two, shift_two, bias_cls = split_gains(gains_weight)
    hot = (dom_label[:, None] == jnp.arange(EXPERTS)[None, :]).astype(jnp.float32)
    class_hot = (class_label[:, None] == jnp.arange(CLASSES)[None, :]).astype(jnp.float32)
    expand_low, depth_low, project_low, head_low, class_low = (
        lax.all_gather(expand_weight.astype(low_type), "wide", axis=0, tiled=True),
        lax.all_gather(depth_weight.astype(low_type), "wide", axis=2, tiled=True),
        lax.all_gather(project_weight.astype(low_type), "wide", axis=0, tiled=True),
        lax.all_gather(head_weight.astype(low_type), "wide", axis=0, tiled=True),
        lax.all_gather(classifier_weight.astype(low_type), "wide", axis=0, tiled=True),
    )
    pooled_one = jnp.mean(images.astype(jnp.float32), axis=1)
    route_one = jax.nn.sigmoid(
        jnp.dot(pooled_one, router_weight[:C_IN], precision=HIGH) + boost * hot
    )
    route_one_low = route_one.astype(low_type)
    kern_expand = mixed(route_one_low, expand_low).astype(low_type)
    hidden = convolve(images, kern_expand)
    kern_depth = jnp.einsum(
        "ne,ekc->nkc", route_one_low, depth_low, preferred_element_type=jnp.float32
    )
    scaled_full, branch_pull = jax.vjp(
        excite_branch, hidden, kern_depth, excite_weight, bias_se, bias_ex
    )
    scaled = scaled_full.astype(low_type)
    kern_project = mixed(route_one_low, project_low).astype(low_type)
    before = convolve(scaled, kern_project)
    sums_one = lax.psum(
        (
            jnp.sum(before, axis=(0, 1)),
            jnp.sum(before * before, axis=(0, 1)),
            jnp.sum(route_one, axis=0),
        ),
        ("dp", "wide"),
    )
    center_one = sums_one[0] / count
    inv_one = lax.rsqrt(sums_one[1] / count - center_one * center_one + eps_norm)
    hat_one = (before - center_one) * inv_one
    normed = (hat_one * gain_one + shift_one).astype(low_type)
    pooled_two = jnp.mean(normed.astype(jnp.float32), axis=1)
    route_two = jax.nn.sigmoid(
        jnp.dot(pooled_two, router_weight[C_IN:], precision=HIGH) + boost * hot
    )
    route_two_low = route_two.astype(low_type)
    kern_head = mixed(route_two_low, head_low).astype(low_type)
    widened = convolve(normed, kern_head)
    sums_two = lax.psum(
        (
            jnp.sum(widened, axis=(0, 1)),
            jnp.sum(widened * widened, axis=(0, 1)),
            jnp.sum(route_two, axis=0),
        ),
        ("dp", "wide"),
    )
    center_two = sums_two[0] / count
    inv_two = lax.rsqrt(sums_two[1] / count - center_two * center_two + eps_norm)
    hat_two = (widened - center_two) * inv_two
    lifted = hat_two * gain_two + shift_two
    feats = jnp.mean(silu(lifted), axis=1).astype(low_type)
    logits = jnp.dot(feats, class_low, preferred_element_type=jnp.float32) + bias_cls
    top = jnp.max(logits, axis=1, keepdims=True)
    powers = jnp.exp(logits - top)
    totals = jnp.sum(powers, axis=1, keepdims=True)
    cross_part = jnp.sum(top[:, 0] + jnp.log(totals[:, 0]) - jnp.sum(logits * class_hot, axis=1))
    means_one = sums_one[2] / every
    means_two = sums_two[2] / every
    grad_logits = ((powers / totals - class_hot) / every).astype(low_type)
    grad_class = jnp.dot(feats.T, grad_logits, preferred_element_type=jnp.float32)
    grad_bias_cls = jnp.sum(grad_logits.astype(jnp.float32), axis=0)
    grad_feats = jnp.dot(grad_logits, class_low.T, preferred_element_type=jnp.float32)
    grad_lifted = grad_feats[:, None, :] / PIX * silu_slope(lifted)
    back_two = lax.psum(
        (jnp.sum(grad_lifted, axis=(0, 1)), jnp.sum(grad_lifted * hat_two, axis=(0, 1))),
        ("dp", "wide"),
    )
    grad_widened = (
        inv_two * gain_two * (grad_lifted - back_two[0] / count - hat_two * back_two[1] / count)
    ).astype(low_type)
    kern_head_grad = kern_grad(normed, grad_widened).astype(low_type)
    grad_head = expert_grad(route_two_low, kern_head_grad)
    grad_route_two = route_grad(kern_head_grad, head_low) + balance_grad(means_two, every)
    grad_logit_two = grad_route_two * route_two * (1.0 - route_two)
    grad_router_two = jnp.dot(pooled_two.T, grad_logit_two, precision=HIGH)
    grad_normed = (
        input_grad(grad_widened, kern_head)
        + jnp.dot(grad_logit_two, router_weight[C_IN:].T, precision=HIGH)[:, None, :] / PIX
    )
    back_one = lax.psum(
        (jnp.sum(grad_normed, axis=(0, 1)), jnp.sum(grad_normed * hat_one, axis=(0, 1))),
        ("dp", "wide"),
    )
    grad_before = (
        inv_one * gain_one * (grad_normed - back_one[0] / count - hat_one * back_one[1] / count)
    ).astype(low_type)
    kern_project_grad = kern_grad(scaled, grad_before).astype(low_type)
    grad_scaled = input_grad(grad_before, kern_project)
    grad_hidden, kern_depth_grad, grad_excite, grad_bias_se, grad_bias_ex = branch_pull(grad_scaled)
    kern_expand_grad = kern_grad(images, grad_hidden.astype(low_type)).astype(low_type)
    grad_expand = expert_grad(route_one_low, kern_expand_grad)
    grad_project = expert_grad(route_one_low, kern_project_grad)
    grad_depth = jnp.sum(route_one_low[:, :, None, None] * kern_depth_grad[:, None, :, :], axis=0)
    depth_term = jnp.sum(kern_depth_grad[:, None, :, :] * depth_low[None, :, :, :], axis=(2, 3))
    grad_route_one = (
        route_grad(kern_expand_grad, expand_low)
        + route_grad(kern_project_grad, project_low)
        + depth_term
        + balance_grad(means_one, every)
    )
    grad_logit_one = grad_route_one * route_one * (1.0 - route_one)
    grad_router_one = jnp.dot(pooled_one.T, grad_logit_one, precision=HIGH)
    small = lax.psum(
        (
            grad_excite,
            jnp.concatenate([grad_router_one, grad_router_two], axis=0),
            jnp.concatenate([grad_bias_se, grad_bias_ex, grad_bias_cls]),
            cross_part,
        ),
        ("dp", "wide"),
    )
    full = (grad_expand, grad_depth, grad_project, grad_head, grad_class)
    shares = (
        lax.psum_scatter(
            full[0].astype(jnp.bfloat16), "wide", scatter_dimension=0, tiled=True
        ).astype(jnp.float32),
        lax.psum_scatter(
            full[1].astype(jnp.bfloat16), "wide", scatter_dimension=2, tiled=True
        ).astype(jnp.float32),
        lax.psum_scatter(
            full[2].astype(jnp.bfloat16), "wide", scatter_dimension=0, tiled=True
        ).astype(jnp.float32),
        lax.psum_scatter(
            full[3].astype(jnp.bfloat16), "wide", scatter_dimension=0, tiled=True
        ).astype(jnp.float32),
        lax.psum_scatter(
            full[4].astype(jnp.bfloat16), "wide", scatter_dimension=0, tiled=True
        ).astype(jnp.float32),
    )
    reduced = (
        lax.psum(shares[0].astype(jnp.bfloat16), "dp").astype(jnp.float32),
        lax.psum(shares[1].astype(jnp.bfloat16), "dp").astype(jnp.float32),
        lax.psum(shares[2].astype(jnp.bfloat16), "dp").astype(jnp.float32),
        lax.psum(shares[3].astype(jnp.bfloat16), "dp").astype(jnp.float32),
        lax.psum(shares[4].astype(jnp.bfloat16), "dp").astype(jnp.float32),
    )
    loss = small[3] / every + balance_weight * (
        jnp.mean((means_one - jnp.mean(means_one)) ** 2)
        + jnp.mean((means_two - jnp.mean(means_two)) ** 2)
    )
    bias_grads = small[2]
    grad_gains = jnp.concatenate(
        [
            bias_grads[: C_SE + C_MID],
            back_one[1],
            back_one[0],
            back_two[1],
            back_two[0],
            bias_grads[C_SE + C_MID :],
        ]
    )
    expand_out = soap(expand_weight, reduced[0], expand_first, expand_second, expand_state, every)
    project_out = soap(
        project_weight, reduced[2], project_first, project_second, project_state, every
    )
    head_out = soap(head_weight, reduced[3], head_first, head_second, head_state, every)
    depth_out = adam(depth_weight, reduced[1], depth_first, depth_second, rate_matrix)
    class_out = adam(
        classifier_weight, reduced[4], classifier_first, classifier_second, rate_matrix
    )
    excite_out = adam(excite_weight, small[0], excite_first, excite_second, rate_matrix)
    router_out = adam(router_weight, small[1], router_first, router_second, rate_matrix)
    gains_out = adam(gains_weight, grad_gains, gains_first, gains_second, rate_gains)
    return (
        loss,
        expand_out[0],
        expand_out[1],
        expand_out[2],
        expand_out[3],
        project_out[0],
        project_out[1],
        project_out[2],
        project_out[3],
        head_out[0],
        head_out[1],
        head_out[2],
        head_out[3],
        depth_out[0],
        depth_out[1],
        depth_out[2],
        class_out[0],
        class_out[1],
        class_out[2],
        excite_out[0],
        excite_out[1],
        excite_out[2],
        router_out[0],
        router_out[1],
        router_out[2],
        gains_out[0],
        gains_out[1],
        gains_out[2],
    )


def solution(mesh):
    return jax.shard_map(
        local,
        mesh=mesh,
        in_specs=(
            P(("dp", "wide"), None, None),
            P(("dp", "wide")),
            P(("dp", "wide")),
            P("wide", None),
            P("wide", None),
            P("wide", None),
            P(None, None, "wide", None),
            P("wide", None),
            P("wide", None),
            P("wide", None),
            P(None, None, "wide", None),
            P("wide", None),
            P("wide", None),
            P("wide", None),
            P(None, None, "wide", None),
            P(None, None, "wide"),
            P(None, None, "wide"),
            P(None, None, "wide"),
            P("wide", None),
            P("wide", None),
            P("wide", None),
            P(),
            P(),
            P(),
            P(),
            P(),
            P(),
            P(),
            P(),
            P(),
        ),
        out_specs=(
            P(),
            P("wide", None),
            P("wide", None),
            P(None, None, "wide", None),
            P("wide", None),
            P("wide", None),
            P("wide", None),
            P(None, None, "wide", None),
            P("wide", None),
            P("wide", None),
            P("wide", None),
            P(None, None, "wide", None),
            P("wide", None),
            P(None, None, "wide"),
            P(None, None, "wide"),
            P(None, None, "wide"),
            P("wide", None),
            P("wide", None),
            P("wide", None),
            P(),
            P(),
            P(),
            P(),
            P(),
            P(),
            P(),
            P(),
            P(),
        ),
        check_vma=False,
    )
```

profile of v0, /device:TPU:0, one launch (start us, length us, event | category | flops | bytes accessed | tf_op | source)
XLA Modules:
  0.0 1737.0 jit_solution(14774766642019492613)
XLA Ops:
  21.8 45.1 %all_gather.16 = bf16[8,9,1152]{1,0,2:T(8,128)(2,1)S(1)} all-gather(bf16[8,9,144]{1,0,2:T(8,128)(2,1)S(1)} %copy.680), channel_id=1, replica_groups=mesh['dp'=4,'wide'=8] {'wide'}, dimensions={2}, use_global_device_ids=true | all-gather | bytes 186624 | tf_op jit(solution)/shard_map/all_gather | solution.py:209
  91.4 42.3 %fusion.33 = (f32[64,49,1152]{2,1,0:T(8,128)}, f32[64,49,1152]{2,1,0:T(8,128)}) fusion(bf16[64,49,192]{2,0,1:T(8,128)(2,1)} %param.30, bf16[64,1152,192]{1,0,2:T(8,128)(2,1)} %convolution_convert_fusion.4), kind=kOutput, calls=%fused_computation.70 | convolution fusion | flops 1401716736 | bytes 58417152 | tf_op jit(solution)/shard_map/npc,ncd->npd/dot_general | solution.py:82
  133.9 14.5 copy.679
  148.5 41.4 %multiply_reduce_fusion.15 = (f32[64,1152]{1,0:T(8,128)S(1)}, f32[64,7,7,1152]{3,0,2,1:T(8,128)}) fusion(f32[64,1152]{1,0:T(8,128)S(1)} %copy-done.25, f32[64,1152]{1,0:T(8,128)S(1)} %copy-done.27, f32[64,1152]{1,0:T(8,128)S(1)} %copy-done.29, f32[64,1152]{1,0:T(8,128)S(1)} %copy-done.31, f32[64,7,7,1152]{3,0,2,1:T(8,128)} %bitcast.500, ...), kind=kLoop, calls=%fused_computation.85 | loop fusion | flops 79405056 | bytes 31850496 | tf_op jit(solution)/shard_map/jvp()/reduce_sum | solution.py:60
  198.7 20.9 %convolution_convert_fusion.3 = bf16[64,320,1152]{2,0,1:T(8,128)(2,1)} fusion(bf16[320,8,1152]{2,1,0:T(8,128)(2,1)} %bitcast.510, bf16[64,8]{0,1:T(8,128)(2,1)S(1)} %copy-done.67), kind=kOutput, calls=%fused_computation.6 | convolution fusion | flops 401080320 | bytes 53085184 | tf_op jit(solution)/shard_map/ne,dec->ncd/dot_general | solution.py:78
  219.7 45.1 %fusion.230 = (f32[320]{0:T(512)S(1)}, f32[320]{0:T(512)S(1)}, f32[64,49,320]{2,1,0:T(8,128)}) fusion(bf16[64,320,1152]{2,0,1:T(8,128)(2,1)} %convolution_convert_fusion.3, f32[64,1152]{1,0:T(8,128)S(1)} %fusion.57, f32[64,49,1152]{2,0,1:T(8,128)} %bitcast.502), kind=kOutput, calls=%fused_computation.415 | convolution fusion | flops 2336796160 | bytes 65948160 | tf_op jit(solution)/shard_map/npc,ncd->npd/dot_general | solution.py:82
  264.8 40.2 %all-reduce.25 = (f32[320]{0:T(512)S(1)}, f32[320]{0:T(512)S(1)}) all-reduce(f32[320]{0:T(512)S(1)} %get-tuple-element.211, f32[320]{0:T(512)S(1)} %get-tuple-element.210), channel_id=1, replica_groups=mesh['dp'=4,'wide'=8] {'dp','wide'}, use_global_device_ids=true, to_apply=%region_5.6 | all-reduce | flops 640 | bytes 5120 | tf_op jit(solution)/shard_map/psum | solution.py:230
  320.1 23.0 %convolution_convert_fusion.2 = bf16[64,1280,320]{1,0,2:T(8,128)(2,1)} fusion(bf16[1280,8,320]{0,2,1:T(8,128)(2,1)} %bitcast.507, f32[64,8]{0,1:T(8,128)S(1)} %get-tuple-element.364), kind=kOutput, calls=%fused_computation.5 | convolution fusion | flops 445645312 | bytes 58984448 | tf_op jit(solution)/shard_map/ne,dec->ncd/dot_general | solution.py:78
  343.1 60.5 %fusion.229 = (f32[1280]{0:T(1024)S(1)}, f32[1280]{0:T(1024)S(1)}, f32[64,49,1280]{2,1,0:T(8,128)}) fusion(bf16[64,49,320]{2,1,0:T(8,128)(2,1)S(1)} %get-tuple-element.295, bf16[64,1280,320]{1,0,2:T(8,128)(2,1)} %convolution_convert_fusion.2), kind=kOutput, calls=%fused_computation.414 | convolution fusion | flops 2581050880 | bytes 70502400 | tf_op jit(solution)/shard_map/npc,ncd->npd/dot_general | solution.py:82
  403.6 40.9 %all-reduce.24 = (f32[1280]{0:T(1024)S(1)}, f32[1280]{0:T(1024)S(1)}) all-reduce(f32[1280]{0:T(1024)S(1)} %get-tuple-element.207, f32[1280]{0:T(1024)S(1)} %get-tuple-element.206), channel_id=1, replica_groups=mesh['dp'=4,'wide'=8] {'dp','wide'}, use_global_device_ids=true, to_apply=%region_10.11 | all-reduce | flops 2560 | bytes 20480 | tf_op jit(solution)/shard_map/psum | solution.py:249
  474.1 39.6 %all-reduce.23 = (f32[8]{0:T(128)S(1)}, f32[1280]{0:T(1024)S(1)}, f32[1280]{0:T(1024)S(1)}) all-reduce(f32[8]{0:T(128)S(1)} %get-tuple-element.363, f32[1280]{0:T(1024)S(1)} %get-tuple-element.205, f32[1280]{0:T(1024)S(1)} %get-tuple-element.204), channel_id=1, replica_groups=mesh['dp'=4,'wide'=8] {'dp','wide'}, use_global_device_ids=true, to_apply=%region_22.23 | all-reduce | flops 2568 | bytes 20544 | tf_op jit(solution)/shard_map/psum | solution.py:249
  515.6 29.6 %convolution_convert_fusion.1 = bf16[64,320,1280]{2,1,0:T(8,128)(2,1)} fusion(bf16[64,49,320]{2,1,0:T(8,128)(2,1)S(1)} %get-tuple-element.295, f32[64,49,1280]{2,1,0:T(8,128)} %get-tuple-element.360, f32[1280]{0:T(1024)S(1)} %get-tuple-element.238, f32[1280]{0:T(1024)S(1)} %broadcast_multiply_fusion.14, f32[1280]{0:T(1024)S(1)} %get-tuple-element.343, ...), kind=kOutput, calls=%fused_computation.4 | convolution fusion | flops 2667479040 | bytes 70855680 | tf_op jit(solution)/shard_map/npc,npd->ncd/dot_general | solution.py:86
  545.3 68.9 %fusion.122 = f32[64,8]{0,1:T(8,128)S(1)} fusion(f32[64,8]{0,1:T(8,128)S(1)} %get-tuple-element.364, bf16[1280,8,320]{0,2,1:T(8,128)(2,1)} %bitcast.508, bf16[64,320,1280]{2,1,0:T(8,128)(2,1)} %convolution_convert_fusion.1, f32[8]{0:T(128)S(1)} %get-tuple-element.353), kind=kOutput, calls=%fused_computation.199 | convolution fusion | flops 419432448 | bytes 58986528 | tf_op jit(solution)/shard_map/ncd,dec->ne/dot_general | solution.py:95
  614.5 43.1 %add_reduce_fusion = (f32[320]{0:T(512)S(1)}, f32[320]{0:T(512)S(1)}, f32[64,49,320]{2,1,0:T(8,128)}) fusion(f32[64,320]{1,0:T(8,128)S(1)} %convolution_multiply_fusion.9, f32[320]{0:T(512)S(1)} %get-tuple-element.348, f32[64,49,320]{2,1,0:T(8,128)} %get-tuple-element.359, f32[320]{0:T(512)S(1)} %get-tuple-element.351, ...), kind=kOutput, calls=%fused_computation.106 | convolution fusion | flops 2647285248 | bytes 76963840 | tf_op jit(solution)/shard_map/npd,ncd->npc/dot_general | solution.py:90
  657.6 40.8 %all-reduce.22 = (f32[8]{0:T(128)}, f32[320]{0:T(512)S(1)}, f32[320]{0:T(512)S(1)}) all-reduce(f32[8]{0:T(128)S(1)} %copy-done.94, f32[320]{0:T(512)S(1)} %get-tuple-element.209, f32[320]{0:T(512)S(1)} %get-tuple-element.208), channel_id=1, replica_groups=mesh['dp'=4,'wide'=8] {'dp','wide'}, use_global_device_ids=true, to_apply=%region_18.19 | all-reduce | flops 648 | bytes 5184 | tf_op jit(solution)/shard_map/psum | solution.py:230
  704.8 49.7 %multiply_reduce_fusion.6 = (f32[64,1152]{1,0:T(8,128)}, f32[64,49,1152]{2,1,0:T(8,128)}) fusion(f32[64,49,1152]{2,0,1:T(8,128)} %bitcast.503, bf16[64,49,320]{2,1,0:T(8,128)(2,1)S(1)} %multiply_convert_fusion.2, bf16[64,320,1152]{2,0,1:T(8,128)(2,1)} %convolution_convert_fusion.3), kind=kOutput, calls=%fused_computation.67 | convolution fusion | flops 2333712384 | bytes 78389248 | tf_op jit(solution)/shard_map/npd,ncd->npc/dot_general | solution.py:90
  757.1 24.6 %multiply_reduce_fusion.5 = (f32[64,1152]{1,0:T(8,128)}, f32[64,49,1152]{2,1,0:T(8,128)}) fusion(f32[64,49,1152]{2,1,0:T(8,128)} %get-tuple-element.358, f32[64,49,1152]{2,0,1:T(8,128)} %bitcast.504, f32[64,1152]{1,0:T(8,128)S(1)} %convolution_multiply_fusion.2, f32[64,49,1152]{2,1,0:T(8,128)} %get-tuple-element.367, f32[64,1152]{1,0:T(8,128)S(1)} %copy-done.11), kind=kLoop, calls=%fused_computation.66 | loop fusion | flops 61341696 | bytes 58687488 | tf_op jit(solution)/shard_map/transpose(jvp())/reduce_sum | solution.py:52
  781.7 13.6 copy.694
  795.4 82.0 %multiply_reduce_fusion.14 = (f32[64,1152]{1,0:T(8,128)}, f32[64,1152]{1,0:T(8,128)}, f32[64,1152]{1,0:T(8,128)}, f32[64,1152]{1,0:T(8,128)}, f32[64,1152]{1,0:T...) fusion(f32[64,7,7,1152]{3,0,2,1:T(8,128)} %bitcast.506, ...), kind=kLoop, calls=%fused_computation.84 | loop fusion | flops 89726976 | bytes 163971072 | tf_op jit(solution)/shard_map/transpose(jvp())/reduce_sum | solution.py:52
  877.4 24.3 %pad_add_fusion = f32[64,9,9,1152]{3,0,2,1:T(8,128)} fusion(f32[64,7,7,1152]{3,0,2,1:T(8,128)} %get-tuple-element.300, f32[64,7,7,1152]{3,0,2,1:T(8,128)} %get-tuple-element.299, f32[64,7,7,1152]{3,0,2,1:T(8,128)} %get-tuple-element.298), kind=kLoop, calls=%fused_computation.41 | loop fusion | flops 11943936 | bytes 67239936 | tf_op jit(solution)/shard_map/transpose(jvp())/add_any | solution.py:52
  901.7 33.5 %pad_add_fusion.1 = f32[64,7,7,1152]{3,0,2,1:T(8,128)} fusion(f32[64,7,7,1152]{3,0,2,1:T(8,128)} %get-tuple-element.306, f32[64,7,7,1152]{3,0,2,1:T(8,128)} %get-tuple-element.305, f32[64,7,7,1152]{3,0,2,1:T(8,128)} %get-tuple-element.304, f32[64,7,7,1152]{3,0,2,1:T(8,128)} %get-tuple-element.303, f32[64,7,7,1152]{3,0,2,1:T(8,128)} %get-tuple-element.302, ...), kind=kLoop, calls=%fused_computation.71 | loop fusion | flops 21676032 | bytes 115605504 | tf_op jit(solution)/shard_map/transpose(jvp())/add_any | solution.py:52
  935.1 24.6 %convert_bitcast_fusion = bf16[64,192,1152]{2,1,0:T(8,128)(2,1)} fusion(f32[64,49,1152]{2,0,1:T(8,128)} %bitcast.517, f32[64,49,1152]{2,1,0:T(8,128)} %get-tuple-element.358, bf16[64,49,192]{2,0,1:T(8,128)(2,1)S(1)} %copy-done.43), kind=kOutput, calls=%fused_computation.33 | convolution fusion | flops 1437548544 | bytes 58417152 | tf_op jit(solution)/shard_map/npc,npd->ncd/dot_general | solution.py:86
  959.7 37.9 %fusion.45 = bf16[1152,8,192]{0,1,2:T(8,128)(2,1)} fusion(bf16[64,192,1152]{2,1,0:T(8,128)(2,1)} %convert_bitcast_fusion, bf16[64,8]{0,1:T(8,128)(2,1)S(1)} %copy-done.68), kind=kOutput, calls=%fused_computation.109 | convolution fusion | flops 228261888 | bytes 31851520 | tf_op jit(solution)/shard_map/ne,ncd->dec/dot_general | solution.py:99
  1004.0 62.6 %convert_bitcast_fusion.1 = bf16[1280,8,320]{0,1,2:T(8,128)(2,1)S(1)} fusion(bf16[64,320,1280]{2,1,0:T(8,128)(2,1)} %convolution_convert_fusion.1, f32[64,8]{0,1:T(8,128)S(1)} %copy-done.73), kind=kOutput, calls=%fused_computation.96 | convolution fusion | flops 422707712 | bytes 58984448 | tf_op jit(solution)/shard_map/ne,ncd->dec/dot_general | solution.py:99
  1082.8 23.5 %convolution_convert_fusion = bf16[64,1152,320]{1,2,0:T(8,128)(2,1)} fusion(bf16[64,49,320]{2,1,0:T(8,128)(2,1)S(1)} %copy-done.21, f32[64,1152]{1,0:T(8,128)S(1)} %copy-done.12, f32[64,49,1152]{2,0,1:T(8,128)} %bitcast.505), kind=kOutput, calls=%fused_computation.3 | convolution fusion | flops 2357379072 | bytes 63938560 | tf_op jit(solution)/shard_map/npc,npd->ncd/dot_general | solution.py:86
  1106.4 44.1 %fusion.37 = bf16[1152,320,8]{0,2,1:T(8,128)(2,1)} fusion(bf16[64,1152,320]{1,2,0:T(8,128)(2,1)} %convolution_convert_fusion, bf16[64,8]{0,1:T(8,128)(2,1)S(1)} %copy-done.68), kind=kOutput, calls=%fused_computation.97 | convolution fusion | flops 380436480 | bytes 53085184 | tf_op jit(solution)/shard_map/ne,ncd->dec/dot_general | solution.py:99
  1220.0 43.9 %fusion.90 = f32[64,8]{0,1:T(8,128)} fusion(bf16[1152,8,192]{0,2,1:T(8,128)(2,1)S(1)} %bitcast.515, bf16[64,192,1152]{2,1,0:T(8,128)(2,1)} %convert_bitcast_fusion), kind=kOutput, calls=%fused_computation.183 | convolution fusion | flops 226492416 | bytes 31852544 | tf_op jit(solution)/shard_map/ncd,dec->ne/dot_general | solution.py:95
  1293.2 44.0 %fusion.133 = f32[64,8]{0,1:T(8,128)S(1)} fusion(f32[64,8]{0,1:T(8,128)S(1)} %copy-done.89, f32[64,8]{0,1:T(8,128)S(1)} %copy.793, f32[64,8]{0,1:T(8,128)S(1)} %copy-done.97, bf16[320,8,1152]{2,1,0:T(8,128)(2,1)} %bitcast.511, bf16[64,1152,320]{1,2,0:T(8,128)(2,1)} %convolution_convert_fusion, f32[8]{0:T(128)S(1)} %get-tuple-element.355), kind=kOutput, calls=%fused_computation.202 | convolution fusion | flops 377490432 | bytes 53092384 | tf_op jit(solution)/shard_map/ncd,dec->ne/dot_general | solution.py:95
  1341.5 40.6 %all-reduce.21 = (f32[]{:T(128)}, f32[512,8]{0,1:T(8,128)S(1)}, f32[2200]{0:T(1024)S(1)}) all-reduce(f32[]{:T(128)} %subtract_reduce_fusion, f32[512,8]{0,1:T(8,128)S(1)} %pad_maximum_fusion, f32[2200]{0:T(1024)S(1)} %concatenate.22), channel_id=1, replica_groups=mesh['dp'=4,'wide'=8] {'dp','wide'}, use_global_device_ids=true, to_apply=%region_16.17 | all-reduce | flops 6297 | bytes 50376 | tf_op jit(solution)/shard_map/psum | solution.py:313
  1393.2 31.9 %reduce-scatter.20.cloned.1.call-done = bf16[144,72]{1,0:T(8,128)(2,1)} async-done(((bf16[1152,72]{1,0:T(8,128)(2,1)}), bf16[144,72]{1,0:T(8,128)(2,1)}) %reduce-scatter.20.cloned.1.call-update) | async-done | bytes 20752
  1426.7 17.3 psum.147
  1444.7 71.7 %all-reduce.32.cloned.1.call-done = (bf16[144,1536]{0,1:T(8,128)(2,1)}, bf16[40,9216]{1,0:T(8,128)(2,1)}, bf16[160,2560]{0,1:T(8,128)(2,1)}, bf16[160,1000]{1,0:T(8,128)(2,1)}) async-done(((bf16[144,1536]{0,1:T(8,128)(2,1)}, bf16[40,9216]{1,0:T(8,128)(2,1)}, bf16[160,2560]{0,1:T(8,128)(2,1)}, bf16[160,1000]{1,0:T(8,128)(2,1)}), (bf16[144,1536]{0,1:T(8,128)(2,1)}, bf16[40,9216]{1,0:T(8,128)(2,1)}, ...) | async-done | bytes 2318864 | tf_op jit(solution)/shard_map/psum | solution.py:341
  (483 shorter events, 451.1 us)
Async XLA Ops:
  7.2 61.8 %copy-start.59 = (f32[512,8]{0,1:T(8,128)S(1)}, f32[512,8]{0,1:T(8,128)}, u32[]{:S(2)}) copy-start(f32[512,8]{0,1:T(8,128)} %param.54) | copy-start | bytes 49156
  7.2 66.2 %all-gather.5.cloned.1.call-start = ((), (), s32[]{:S(2)}) async-start(), calls=%async_computation.5 | async-start | bytes 3981312 | tf_op jit(solution)/shard_map/all_gather | solution.py:208
  9.3 182.9 %all-gather.7.cloned.1.call-start = ((), (), s32[]{:S(2)}) async-start(), calls=%async_computation.6 | async-start | bytes 6635520 | tf_op jit(solution)/shard_map/all_gather | solution.py:210
  11.7 299.0 %all-gather.9.cloned.1.call-start = ((), (), s32[]{:S(2)}) async-start(), calls=%async_computation.7 | async-start | bytes 7372800 | tf_op jit(solution)/shard_map/all_gather | solution.py:211
  14.1 440.6 %all-gather.11.cloned.1.call-start = ((), (), s32[]{:S(2)}) async-start(), calls=%async_computation.8 | async-start | bytes 2949120 | tf_op jit(solution)/shard_map/all_gather | solution.py:212
  16.1 1272.3 %reduce-scatter.16.cloned.1.call-start = ((), (), s32[]{:S(2)}) async-start(), calls=%async_computation.12 | async-start | bytes 3981312
  219.7 85.4 %copy-start.61 = (f32[5400]{0:T(1024)S(1)}, f32[5400]{0:T(1024)}, u32[]{:S(2)}) copy-start(f32[5400]{0:T(1024)} %param.57) | copy-start | bytes 64804
  219.7 90.6 %copy-start.91 = (s32[64]{0:T(128)S(1)}, s32[64]{0:T(128)}, u32[]{:S(2)}) copy-start(s32[64]{0:T(128)} %param.31) | copy-start | bytes 772
  310.6 234.6 %copy-start.72 = (f32[64,8]{0,1:T(8,128)}, f32[64,8]{0,1:T(8,128)S(1)}, u32[]{:S(2)}) copy-start(f32[64,8]{0,1:T(8,128)S(1)} %get-tuple-element.364) | copy-start | bytes 6148
  454.7 90.5 %copy-start.15 = (f32[64,1280]{1,0:T(8,128)}, f32[64,1280]{1,0:T(8,128)S(1)}, u32[]{:S(2)}) copy-start(f32[64,1280]{1,0:T(8,128)S(1)} %multiply_reduce_fusion.3) | copy-start | bytes 983044
  458.1 87.2 %copy-start.87 = (f32[64]{0:T(128)}, f32[64]{0:T(128)S(1)}, u32[]{:S(2)}) copy-start(f32[64]{0:T(128)S(1)} %get-tuple-element.214) | copy-start | bytes 772
  513.8 100.7 %copy-start.80 = (f32[1280]{0:T(1024)}, f32[1280]{0:T(1024)S(1)}, u32[]{:S(2)}) copy-start(f32[1280]{0:T(1024)S(1)} %get-tuple-element.238) | copy-start | bytes 15364
  614.5 84.5 %copy-start.79 = (f32[320]{0:T(512)S(1)}, f32[320]{0:T(512)}, u32[]{:S(2)}) copy-start(f32[320]{0:T(512)} %get-tuple-element.340) | copy-start | bytes 3844
  1003.9 286.7 %reduce-scatter.18.cloned.1.call-start = ((), (), s32[]{:S(2)}) async-start(), calls=%async_computation.13 | async-start | bytes 7372800
  1080.3 212.6 %reduce-scatter.14.cloned.1.call-start = ((), (), s32[]{:S(2)}) async-start(), calls=%async_computation.10 | async-start | bytes 2949120 | tf_op jit(solution)/shard_map/reduce_scatter | solution.py:336
  1082.7 210.2 %reduce-scatter.12.cloned.1.call-start = ((), (), s32[]{:S(2)}) async-start(), calls=%async_computation.9 | async-start | bytes 6635520 | tf_op jit(solution)/shard_map/reduce_scatter | solution.py:330
  1157.2 233.7 %all-reduce.30.cloned.1.call-start = ((), (), s32[]{:S(2)}) async-start(), calls=%async_computation.11 | async-start | bytes 884736 | tf_op jit(solution)/shard_map/psum | solution.py:313
  1196.9 355.5 %copy-start.63 = (s32[4]{0:T(128)}, s32[4]{0:T(128)S(1)}, u32[]{:S(2)}) copy-start(s32[4]{0:T(128)S(1)} %or_bitcast_fusion) | copy-start | bytes 52
  1264.0 161.1 %reduce-scatter.20.cloned.1.call-start = ((), (), s32[]{:S(2)}) async-start(), calls=%async_computation.14 | async-start | bytes 331776
  1286.4 230.0 %all-reduce.32.cloned.1.call-start = ((), (), s32[]{:S(2)}) async-start(), calls=%async_computation.15 | async-start | bytes 6324224 | tf_op jit(solution)/shard_map/psum | solution.py:341
  1293.1 91.0 %copy-start.70 = (f32[1280]{0:T(1024)S(1)}, f32[1280]{0:T(1024)}, u32[]{:S(2)}) copy-start(f32[1280]{0:T(1024)} %copy-done.69) | copy-start | bytes 15364
  1293.1 91.0 %copy-start.78 = (f32[320]{0:T(512)S(1)}, f32[320]{0:T(512)}, u32[]{:S(2)}) copy-start(f32[320]{0:T(512)} %copy-done.77) | copy-start | bytes 3844
  1293.1 91.0 %copy-start.81 = (f32[1280]{0:T(1024)S(1)}, f32[1280]{0:T(1024)}, u32[]{:S(2)}) copy-start(f32[1280]{0:T(1024)} %copy-done.80) | copy-start | bytes 15364
  1293.1 91.0 %copy-start.83 = (f32[320]{0:T(512)S(1)}, f32[320]{0:T(512)}, u32[]{:S(2)}) copy-start(f32[320]{0:T(512)} %copy-done.82) | copy-start | bytes 3844
  1293.1 91.1 %copy-start.60 = (f32[512,8]{0,1:T(8,128)S(1)}, f32[512,8]{0,1:T(8,128)}, u32[]{:S(2)}) copy-start(f32[512,8]{0,1:T(8,128)} %param.54) | copy-start | bytes 49156
  1293.1 92.4 %copy-start.62 = (f32[5400]{0:T(1024)S(1)}, f32[5400]{0:T(1024)}, u32[]{:S(2)}) copy-start(f32[5400]{0:T(1024)} %param.57) | copy-start | bytes 64804
  1293.1 97.7 %copy-start.19 = (f32[2,1152,48]{1,2,0:T(8,128)S(1)}, f32[2,1152,48]{1,2,0:T(8,128)}, u32[]{:S(2)}) copy-start(f32[2,1152,48]{1,2,0:T(8,128)} %param.51) | copy-start | bytes 1327108
  1293.1 97.7 %copy-start.54 = (f32[2,1152,48]{1,2,0:T(8,128)S(1)}, f32[2,1152,48]{1,2,0:T(8,128)}, u32[]{:S(2)}) copy-start(f32[2,1152,48]{1,2,0:T(8,128)} %param.53) | copy-start | bytes 1327108
  1293.2 150.8 %copy-start.55 = (f32[8,9,144]{2,0,1:T(8,128)S(1)}, f32[8,9,144]{2,0,1:T(8,128)}, u32[]{:S(2)}) copy-start(f32[8,9,144]{2,0,1:T(8,128)} %param.45) | copy-start | bytes 124420
  1293.2 150.8 %copy-start.64 = (f32[8,9,144]{2,0,1:T(8,128)S(1)}, f32[8,9,144]{2,0,1:T(8,128)}, u32[]{:S(2)}) copy-start(f32[8,9,144]{2,0,1:T(8,128)} %param.47) | copy-start | bytes 124420
  1293.2 150.8 %copy-start.65 = (f32[8,9,144]{2,0,1:T(8,128)S(1)}, f32[8,9,144]{2,0,1:T(8,128)}, u32[]{:S(2)}) copy-start(f32[8,9,144]{2,0,1:T(8,128)} %param.46) | copy-start | bytes 124420
  1293.2 223.2 %copy-start.5 = (f32[144,1536]{0,1:T(8,128)S(1)}, f32[144,1536]{0,1:T(8,128)}, u32[]{:S(2)}) copy-start(f32[144,1536]{0,1:T(8,128)} %copy.688) | copy-start | bytes 2654212
  (78 other events, 1943.6 us)
Sparse Core Ops, SparseCore 0:
  10.3 63.1 all-gather.4
  75.7 60.4 all-gather.6
  138.3 65.5 all-gather.8
  206.0 32.4 all-gather.10
  1004.0 44.5 reduce-scatter.15
  1080.5 73.0 reduce-scatter.17
  1156.0 35.8 reduce-scatter.13
  1194.3 65.1 reduce-scatter.11
  1265.4 125.4 all-reduce.29
  1393.6 31.4 reduce-scatter.19
  1429.7 86.6 all-reduce.31
where the time goes:
time: 1750 us; the launch traced here: 1740 us
  matrix products  757 us (43%)
  other arithmetic  328 us (19%)
  blocking collectives  265 us (15%)
  local copies, waits for them, and re-layouts  258 us (15%)
  waiting for transfers between devices  109 us (6%)
  between operations  20.1 us (1%)
    dot_general x3, matrix products, route_grad(): jnp.einsum('ncd,dec->ne', kern_g, cube, preferred_element_type=jnp.float32)  157 us
    dot_general x3, matrix products, convolve(): jnp.einsum('npc,ncd->npd', act, kern, preferred_element_type=jnp.float32)  148 us
    dot_general x3, matrix products, expert_grad(): jnp.einsum('ne,ncd->dec', route, kern_g, preferred_element_type=jnp.float32)  145 us
    reduce_sum x2, other arithmetic, depthwise(): padded[:, row_at:row_at + SIDE, col_at:col_at + SIDE, :]  107 us
    dot_general x2, matrix products, input_grad(): jnp.einsum('npd,ncd->npc', grad_out, kern, preferred_element_type=jnp.flo...  92.8 us
    psum x2, blocking collectives, local(): lax.psum((jnp.sum(before, axis=(0, 1)), jnp.sum(before * before, axis=(0,...  81 us
    psum x2, blocking collectives, local(): lax.psum((jnp.sum(widened, axis=(0, 1)), jnp.sum(widened * widened, axis=...  80.5 us
    dot_general x3, matrix products, kern_grad(): jnp.einsum('npc,npd->ncd', act, grad_out, preferred_element_type=jnp.floa...  77.8 us
  transfers between devices with their start and end apart: 11, of which 4 were waited for; matrix products, arithmetic and copies ran while one was open for 38% of the time, Pallas kernels for 0%

commit v1 on v0

--- a/solution.py
+++ b/solution.py
@@ -1,6 +1,10 @@
+import functools
+
 import jax
 import jax.numpy as jnp
 from jax import lax
+from jax.experimental import pallas as pl
+from jax.experimental.pallas import tpu as pltpu
 from jax.sharding import PartitionSpec as P
 
 SIDE = 7
@@ -40,27 +44,119 @@
 
 
 def depthwise(act, kern):
-    grid = act.reshape(act.shape[0], SIDE, SIDE, act.shape[-1])
-    margin = KSIZE // 2
-    padded = jnp.pad(grid, ((0, 0), (margin, margin), (margin, margin), (0, 0)))
+    grid = act.reshape((SIDE, SIDE) + act.shape[1:])
+    padded = jnp.pad(grid, ((1, 1), (1, 1), (0, 0), (0, 0)))
     total = jnp.zeros_like(grid)
     for tap in range(KSIZE * KSIZE):
         row_at = tap // KSIZE
         col_at = tap % KSIZE
-        total = (
-            total
-            + padded[:, row_at : row_at + SIDE, col_at : col_at + SIDE, :]
-            * kern[:, tap][:, None, None, :]
+        total = total + padded[row_at : row_at + SIDE, col_at : col_at + SIDE] * kern[tap]
+    return total.reshape(act.shape)
+
+
+def depthwise_kern_grad(act, grad_out):
+    grid = act.reshape((SIDE, SIDE) + act.shape[1:])
+    padded = jnp.pad(grid, ((1, 1), (1, 1), (0, 0), (0, 0)))
+    grad = grad_out.reshape((SIDE, SIDE) + act.shape[1:])
+    taps = []
+    for tap in range(KSIZE * KSIZE):
+        row_at = tap // KSIZE
+        col_at = tap % KSIZE
+        window = padded[row_at : row_at + SIDE, col_at : col_at + SIDE]
+        taps.append(jnp.sum(window * grad, axis=(0, 1)))
+    return jnp.stack(taps)
+
+
+MESH = pl.DeviceIdType.MESH
+
+
+def sum_kernel(n_wide, n_dp, x_ref, o_ref, wide_slots, dp_slots, part, s_wide, r_wide, s_dp, r_dp):
+    me_wide = lax.axis_index("wide")
+    me_dp = lax.axis_index("dp")
+    barrier = pltpu.get_barrier_semaphore()
+    for k in range(1, n_wide):
+        pl.semaphore_signal(
+            barrier, inc=1, device_id={"wide": lax.rem(me_wide + k, n_wide)}, device_id_type=MESH
         )
-    return total.reshape(act.shape)
-
-
-def excite_branch(hidden, kern_depth, excite_w, bias_se, bias_ex):
-    act = silu(depthwise(silu(hidden), kern_depth))
-    pooled = jnp.mean(act, axis=1)
-    squeeze = silu(jnp.dot(pooled, excite_w[0], precision=HIGH) + bias_se)
-    gate = jax.nn.sigmoid(jnp.dot(squeeze, excite_w[1].T, precision=HIGH) + bias_ex)
-    return act * gate[:, None, :]
+    for k in range(1, n_dp):
+        pl.semaphore_signal(
+            barrier, inc=1, device_id={"dp": lax.rem(me_dp + k, n_dp)}, device_id_type=MESH
+        )
+    pl.semaphore_wait(barrier, n_wide + n_dp - 2)
+
+    def exchange(src, slots, me, axis, size, send, recv):
+        copies = []
+        for k in range(1, size):
+            copy = pltpu.make_async_remote_copy(
+                src_ref=src,
+                dst_ref=slots.at[me],
+                send_sem=send.at[k],
+                recv_sem=recv.at[k],
+                device_id={axis: lax.rem(me + k, size)},
+                device_id_type=MESH,
+            )
+            copy.start()
+            copies.append(copy)
+        slots[me] = src[...]
+        for copy in copies:
+            copy.wait()
+        total = slots[0]
+        for k in range(1, size):
+            total = total + slots[k]
+        return total
+
+    part[...] = exchange(x_ref, wide_slots, me_wide, "wide", n_wide, s_wide, r_wide)
+    o_ref[...] = exchange(part, dp_slots, me_dp, "dp", n_dp, s_dp, r_dp)
+
+
+def sum_all(parts, ident):
+    shapes = [part.shape for part in parts]
+    sizes = [part.size for part in parts]
+    flat = jnp.concatenate([part.reshape(-1) for part in parts])
+    rows = -(-flat.size // 1024) * 8
+    flat = jnp.pad(flat, (0, rows * 128 - flat.size)).reshape(rows, 128)
+    n_wide = lax.axis_size("wide")
+    n_dp = lax.axis_size("dp")
+    out = pl.pallas_call(
+        functools.partial(sum_kernel, n_wide, n_dp),
+        out_shape=jax.ShapeDtypeStruct((rows, 128), jnp.float32),
+        in_specs=[pl.BlockSpec(memory_space=pltpu.VMEM)],
+        out_specs=pl.BlockSpec(memory_space=pltpu.VMEM),
+        scratch_shapes=[
+            pltpu.VMEM((n_wide, rows, 128), jnp.float32),
+            pltpu.VMEM((n_dp, rows, 128), jnp.float32),
+            pltpu.VMEM((rows, 128), jnp.float32),
+            pltpu.SemaphoreType.DMA((n_wide,)),
+            pltpu.SemaphoreType.DMA((n_wide,)),
+            pltpu.SemaphoreType.DMA((n_dp,)),
+            pltpu.SemaphoreType.DMA((n_dp,)),
+        ],
+        compiler_params=pltpu.CompilerParams(collective_id=ident, has_side_effects=True),
+    )(flat)
+    out = out.reshape(-1)
+    found = []
+    start = 0
+    for shape, size in zip(shapes, sizes):
+        found.append(out[start : start + size].reshape(shape))
+        start = start + size
+    return found
+
+
+def rows_nt(left, right):
+    return lax.dot_general(
+        left, right, (((1,), (1,)), ((), ())), preferred_element_type=jnp.float32
+    )
+
+
+def rows_tn(left, right):
+    return lax.dot_general(
+        left, right, (((0,), (0,)), ((), ())), preferred_element_type=jnp.float32
+    )
+
+
+def scaled_by(route, act):
+    cube = act[:, :, None, :] * route[None, :, :, None]
+    return cube.reshape(act.shape[0] * act.shape[1], -1)
 
 
 def split_gains(gains):
@@ -71,33 +167,6 @@
         pieces.append(gains[start : start + width])
         start = start + width
     return pieces
-
-
-def mixed(route, flat):
-    cube = flat.reshape(flat.shape[0], EXPERTS, -1)
-    return jnp.einsum("ne,dec->ncd", route, cube, preferred_element_type=jnp.float32)
-
-
-def convolve(act, kern):
-    return jnp.einsum("npc,ncd->npd", act, kern, preferred_element_type=jnp.float32)
-
-
-def kern_grad(act, grad_out):
-    return jnp.einsum("npc,npd->ncd", act, grad_out, preferred_element_type=jnp.float32)
-
-
-def input_grad(grad_out, kern):
-    return jnp.einsum("npd,ncd->npc", grad_out, kern, preferred_element_type=jnp.float32)
-
-
-def route_grad(kern_g, flat):
-    cube = flat.reshape(flat.shape[0], EXPERTS, -1)
-    return jnp.einsum("ncd,dec->ne", kern_g, cube, preferred_element_type=jnp.float32)
-
-
-def expert_grad(route, kern_g):
-    cube = jnp.einsum("ne,ncd->dec", route, kern_g, preferred_element_type=jnp.float32)
-    return cube.reshape(cube.shape[0], -1)
 
 
 def balance_grad(means, every):
@@ -199,66 +268,79 @@
     gains_second,
 ):
     low_type = jnp.bfloat16
+    count_images = images.shape[0]
     every = images.shape[0] * lax.axis_size("dp") * lax.axis_size("wide")
     count = every * PIX
+    rows = PIX * count_images
     bias_se, bias_ex, gain_one, shift_one, gain_two, shift_two, bias_cls = split_gains(gains_weight)
     hot = (dom_label[:, None] == jnp.arange(EXPERTS)[None, :]).astype(jnp.float32)
     class_hot = (class_label[:, None] == jnp.arange(CLASSES)[None, :]).astype(jnp.float32)
-    expand_low, depth_low, project_low, head_low, class_low = (
-        lax.all_gather(expand_weight.astype(low_type), "wide", axis=0, tiled=True),
-        lax.all_gather(depth_weight.astype(low_type), "wide", axis=2, tiled=True),
-        lax.all_gather(project_weight.astype(low_type), "wide", axis=0, tiled=True),
-        lax.all_gather(head_weight.astype(low_type), "wide", axis=0, tiled=True),
-        lax.all_gather(classifier_weight.astype(low_type), "wide", axis=0, tiled=True),
-    )
-    pooled_one = jnp.mean(images.astype(jnp.float32), axis=1)
+    img = images.transpose(1, 0, 2)
+    expand_low = lax.all_gather(expand_weight.astype(low_type), "wide", axis=0, tiled=True)
+    project_low = lax.all_gather(project_weight.astype(low_type), "wide", axis=0, tiled=True)
+    head_low = lax.all_gather(head_weight.astype(low_type), "wide", axis=0, tiled=True)
+    class_low = lax.all_gather(classifier_weight.astype(low_type), "wide", axis=0, tiled=True)
+    depth_own = depth_weight.astype(low_type).transpose(2, 0, 1).reshape(depth_weight.shape[2], -1)
+    depth_low = lax.all_gather(depth_own, "wide", axis=0, tiled=True)
+    depth_low = depth_low.reshape(C_MID, EXPERTS, KSIZE * KSIZE).transpose(1, 2, 0)
+    project_cube = project_low.reshape(C_OUT, EXPERTS, C_MID).transpose(1, 0, 2)
+    project_cube = project_cube.reshape(EXPERTS * C_OUT, C_MID)
+
+    pooled_one = jnp.mean(img.astype(jnp.float32), axis=0)
     route_one = jax.nn.sigmoid(
         jnp.dot(pooled_one, router_weight[:C_IN], precision=HIGH) + boost * hot
     )
-    route_one_low = route_one.astype(low_type)
-    kern_expand = mixed(route_one_low, expand_low).astype(low_type)
-    hidden = convolve(images, kern_expand)
+    r_one = route_one.astype(low_type)
+    img_routed = scaled_by(r_one, img)
+    hidden = rows_nt(img_routed, expand_low).reshape(PIX, count_images, C_MID)
     kern_depth = jnp.einsum(
-        "ne,ekc->nkc", route_one_low, depth_low, preferred_element_type=jnp.float32
-    )
-    scaled_full, branch_pull = jax.vjp(
-        excite_branch, hidden, kern_depth, excite_weight, bias_se, bias_ex
-    )
-    scaled = scaled_full.astype(low_type)
-    kern_project = mixed(route_one_low, project_low).astype(low_type)
-    before = convolve(scaled, kern_project)
-    sums_one = lax.psum(
+        "ne,ekc->knc", r_one, depth_low, preferred_element_type=jnp.float32
+    )
+    start = silu(hidden)
+    turned = depthwise(start, kern_depth)
+    act = silu(turned)
+    pooled_act = jnp.mean(act, axis=0)
+    squeeze_in = jnp.dot(pooled_act, excite_weight[0], precision=HIGH) + bias_se
+    squeeze = silu(squeeze_in)
+    gate = jax.nn.sigmoid(jnp.dot(squeeze, excite_weight[1].T, precision=HIGH) + bias_ex)
+    scaled = (act * gate).astype(low_type)
+    scaled_rows = scaled.reshape(rows, C_MID)
+    each = rows_nt(scaled_rows, project_cube).astype(low_type)
+    each = each.reshape(PIX, count_images, EXPERTS, C_OUT)
+    r_one_wide = r_one.astype(jnp.float32)[None, :, :, None]
+    before = jnp.sum(each.astype(jnp.float32) * r_one_wide, axis=2)
+    sums_one = sum_all(
         (
             jnp.sum(before, axis=(0, 1)),
             jnp.sum(before * before, axis=(0, 1)),
             jnp.sum(route_one, axis=0),
         ),
-        ("dp", "wide"),
+        1,
     )
     center_one = sums_one[0] / count
     inv_one = lax.rsqrt(sums_one[1] / count - center_one * center_one + eps_norm)
     hat_one = (before - center_one) * inv_one
     normed = (hat_one * gain_one + shift_one).astype(low_type)
-    pooled_two = jnp.mean(normed.astype(jnp.float32), axis=1)
+    pooled_two = jnp.mean(normed.astype(jnp.float32), axis=0)
     route_two = jax.nn.sigmoid(
         jnp.dot(pooled_two, router_weight[C_IN:], precision=HIGH) + boost * hot
     )
-    route_two_low = route_two.astype(low_type)
-    kern_head = mixed(route_two_low, head_low).astype(low_type)
-    widened = convolve(normed, kern_head)
-    sums_two = lax.psum(
+    r_two = route_two.astype(low_type)
+    normed_routed = scaled_by(r_two, normed)
+    widened = rows_nt(normed_routed, head_low).reshape(PIX, count_images, C_HEAD)
+    sums_two = sum_all(
         (
             jnp.sum(widened, axis=(0, 1)),
             jnp.sum(widened * widened, axis=(0, 1)),
             jnp.sum(route_two, axis=0),
         ),
-        ("dp", "wide"),
+        2,
     )
     center_two = sums_two[0] / count
     inv_two = lax.rsqrt(sums_two[1] / count - center_two * center_two + eps_norm)
     hat_two = (widened - center_two) * inv_two
     lifted = hat_two * gain_two + shift_two
-    feats = jnp.mean(silu(lifted), axis=1).astype(low_type)
+    feats = jnp.mean(silu(lifted), axis=0).astype(low_type)
     logits = jnp.dot(feats, class_low, preferred_element_type=jnp.float32) + bias_cls
     top = jnp.max(logits, axis=1, keepdims=True)
     powers = jnp.exp(logits - top)
@@ -266,50 +348,75 @@
     cross_part = jnp.sum(top[:, 0] + jnp.log(totals[:, 0]) - jnp.sum(logits * class_hot, axis=1))
     means_one = sums_one[2] / every
     means_two = sums_two[2] / every
+
     grad_logits = ((powers / totals - class_hot) / every).astype(low_type)
-    grad_class = jnp.dot(feats.T, grad_logits, preferred_element_type=jnp.float32)
+    grad_class = rows_tn(feats, grad_logits)
     grad_bias_cls = jnp.sum(grad_logits.astype(jnp.float32), axis=0)
-    grad_feats = jnp.dot(grad_logits, class_low.T, preferred_element_type=jnp.float32)
-    grad_lifted = grad_feats[:, None, :] / PIX * silu_slope(lifted)
-    back_two = lax.psum(
-        (jnp.sum(grad_lifted, axis=(0, 1)), jnp.sum(grad_lifted * hat_two, axis=(0, 1))),
-        ("dp", "wide"),
+    grad_feats = rows_nt(grad_logits, class_low)
+    grad_lifted = grad_feats / PIX * silu_slope(lifted)
+    back_two = sum_all(
+        (jnp.sum(grad_lifted, axis=(0, 1)), jnp.sum(grad_lifted * hat_two, axis=(0, 1))), 3
     )
     grad_widened = (
         inv_two * gain_two * (grad_lifted - back_two[0] / count - hat_two * back_two[1] / count)
     ).astype(low_type)
-    kern_head_grad = kern_grad(normed, grad_widened).astype(low_type)
-    grad_head = expert_grad(route_two_low, kern_head_grad)
-    grad_route_two = route_grad(kern_head_grad, head_low) + balance_grad(means_two, every)
+    grad_widened_rows = grad_widened.reshape(rows, C_HEAD)
+    grad_head = rows_tn(grad_widened_rows, normed_routed)
+    turned_two = jnp.dot(grad_widened_rows, head_low, preferred_element_type=jnp.float32)
+    turned_two = turned_two.reshape(PIX, count_images, EXPERTS, C_OUT)
+    grad_route_two = jnp.sum(
+        turned_two * normed.astype(jnp.float32)[:, :, None, :], axis=(0, 3)
+    ) + balance_grad(means_two, every)
     grad_logit_two = grad_route_two * route_two * (1.0 - route_two)
     grad_router_two = jnp.dot(pooled_two.T, grad_logit_two, precision=HIGH)
     grad_normed = (
-        input_grad(grad_widened, kern_head)
-        + jnp.dot(grad_logit_two, router_weight[C_IN:].T, precision=HIGH)[:, None, :] / PIX
-    )
-    back_one = lax.psum(
-        (jnp.sum(grad_normed, axis=(0, 1)), jnp.sum(grad_normed * hat_one, axis=(0, 1))),
-        ("dp", "wide"),
+        jnp.sum(turned_two * r_two.astype(jnp.float32)[None, :, :, None], axis=2)
+        + jnp.dot(grad_logit_two, router_weight[C_IN:].T, precision=HIGH) / PIX
+    )
+    back_one = sum_all(
+        (jnp.sum(grad_normed, axis=(0, 1)), jnp.sum(grad_normed * hat_one, axis=(0, 1))), 4
     )
     grad_before = (
         inv_one * gain_one * (grad_normed - back_one[0] / count - hat_one * back_one[1] / count)
     ).astype(low_type)
-    kern_project_grad = kern_grad(scaled, grad_before).astype(low_type)
-    grad_scaled = input_grad(grad_before, kern_project)
-    grad_hidden, kern_depth_grad, grad_excite, grad_bias_se, grad_bias_ex = branch_pull(grad_scaled)
-    kern_expand_grad = kern_grad(images, grad_hidden.astype(low_type)).astype(low_type)
-    grad_expand = expert_grad(route_one_low, kern_expand_grad)
-    grad_project = expert_grad(route_one_low, kern_project_grad)
-    grad_depth = jnp.sum(route_one_low[:, :, None, None] * kern_depth_grad[:, None, :, :], axis=0)
-    depth_term = jnp.sum(kern_depth_grad[:, None, :, :] * depth_low[None, :, :, :], axis=(2, 3))
-    grad_route_one = (
-        route_grad(kern_expand_grad, expand_low)
-        + route_grad(kern_project_grad, project_low)
-        + depth_term
-        + balance_grad(means_one, every)
-    )
+
+    before_routed = scaled_by(r_one, grad_before)
+    grad_project = rows_tn(before_routed, scaled_rows).reshape(EXPERTS, C_OUT, C_MID)
+    grad_project = grad_project.transpose(1, 0, 2).reshape(C_OUT, EXPERTS * C_MID)
+    route_project = jnp.sum(
+        each.astype(jnp.float32) * grad_before.astype(jnp.float32)[:, :, None, :], axis=(0, 3)
+    )
+    grad_scaled = jnp.dot(before_routed, project_cube, preferred_element_type=jnp.float32)
+    grad_scaled = grad_scaled.reshape(PIX, count_images, C_MID)
+    grad_gate = jnp.sum(grad_scaled * act, axis=0)
+    grad_gate = grad_gate * gate * (1.0 - gate)
+    grad_squeeze = jnp.dot(grad_gate, excite_weight[1], precision=HIGH) * silu_slope(squeeze_in)
+    grad_excite = jnp.stack(
+        [
+            jnp.dot(pooled_act.T, grad_squeeze, precision=HIGH),
+            jnp.dot(grad_gate.T, squeeze, precision=HIGH),
+        ]
+    )
+    grad_pooled = jnp.dot(grad_squeeze, excite_weight[0].T, precision=HIGH)
+    grad_turned = (grad_scaled * gate + grad_pooled / PIX) * silu_slope(turned)
+    kern_depth_grad = depthwise_kern_grad(start, grad_turned)
+    grad_start = depthwise(grad_turned, kern_depth[::-1])
+    grad_hidden = (grad_start * silu_slope(hidden)).astype(low_type).reshape(rows, C_MID)
+    grad_expand = rows_tn(grad_hidden, img_routed)
+    turned_one = jnp.dot(grad_hidden, expand_low, preferred_element_type=jnp.float32)
+    turned_one = turned_one.reshape(PIX, count_images, EXPERTS, C_IN)
+    route_expand = jnp.sum(turned_one * img.astype(jnp.float32)[:, :, None, :], axis=(0, 3))
+    grad_depth = jnp.einsum(
+        "ne,knc->ekc", r_one.astype(jnp.float32), kern_depth_grad, precision=HIGH
+    )
+    depth_term = jnp.einsum(
+        "knc,ekc->ne", kern_depth_grad, depth_low.astype(jnp.float32), precision=HIGH
+    )
+    grad_route_one = route_expand + route_project + depth_term + balance_grad(means_one, every)
     grad_logit_one = grad_route_one * route_one * (1.0 - route_one)
     grad_router_one = jnp.dot(pooled_one.T, grad_logit_one, precision=HIGH)
+    grad_bias_se = jnp.sum(grad_squeeze, axis=0)
+    grad_bias_ex = jnp.sum(grad_gate, axis=0)
     small = lax.psum(
         (
             grad_excite,
@@ -325,7 +432,7 @@
             full[0].astype(jnp.bfloat16), "wide", scatter_dimension=0, tiled=True
         ).astype(jnp.float32),
         lax.psum_scatter(
-            full[1].astype(jnp.bfloat16), "wide", scatter_dimension=2, tiled=True
+            full[1].transpose(2, 0, 1).astype(jnp.bfloat16).reshape(C_MID, -1), "wide", scatter_dimension=0, tiled=True
         ).astype(jnp.float32),
         lax.psum_scatter(
             full[2].astype(jnp.bfloat16), "wide", scatter_dimension=0, tiled=True
@@ -344,6 +451,7 @@
         lax.psum(shares[3].astype(jnp.bfloat16), "dp").astype(jnp.float32),
         lax.psum(shares[4].astype(jnp.bfloat16), "dp").astype(jnp.float32),
     )
+    depth_reduced = reduced[1].reshape(-1, EXPERTS, KSIZE * KSIZE).transpose(1, 2, 0)
     loss = small[3] / every + balance_weight * (
         jnp.mean((means_one - jnp.mean(means_one)) ** 2)
         + jnp.mean((means_two - jnp.mean(means_two)) ** 2)
@@ -364,7 +472,7 @@
         project_weight, reduced[2], project_first, project_second, project_state, every
     )
     head_out = soap(head_weight, reduced[3], head_first, head_second, head_state, every)
-    depth_out = adam(depth_weight, reduced[1], depth_first, depth_second, rate_matrix)
+    depth_out = adam(depth_weight, depth_reduced, depth_first, depth_second, rate_matrix)
     class_out = adam(
         classifier_weight, reduced[4], classifier_first, classifier_second, rate_matrix
     )

time: 1750 us -> 1410 us (0.81)
  matrix products: 757 us -> 320 us
  blocking collectives: 265 us -> 74.2 us
  local copies, waits for them, and re-layouts: 258 us -> 422 us
  Pallas kernels: 0 us -> 44.5 us
  waiting for transfers between devices: 109 us -> 153 us
  other arithmetic: 328 us -> 365 us
    dot_general x27 -> x21, matrix products: 689 us -> 262 us  [the longest x4 85.7 us: rows_nt(): lax.dot_general(left, right, (((1,), (1,)), ((), ())), preferred_element_...]
    mul x2 -> x15, local copies, waits for them, and re-layouts: 16 us -> 237 us  [the longest x12 184 us: scaled_by(): cube = act[:, :, None, :] * route[None, :, :, None]]
    psum x4 -> x0, blocking collectives: 162 us -> none  [the longest x2 81 us: local(): lax.psum((jnp.sum(before, axis=(0, 1)), jnp.sum(before * before, axis=(0,...]
    add_any x4 -> x0, other arithmetic: 63.8 us -> none  [the longest x2 57.7 us: depthwise(): padded[:, row_at:row_at + SIDE, col_at:col_at + SIDE, :]]
    psum x1, waiting for transfers between devices: 3.86 us -> 64.8 us  [local(): lax.psum((grad_excite, jnp.concatenate([grad_router_one, grad_router_two]...]
    reduce_sum x8 -> x12, other arithmetic: 170 us -> 218 us  [the longest x2 94.2 us: depthwise_kern_grad(): taps.append(jnp.sum(window * grad, axis=(0, 1)))]
    pallas_call x0 -> x4, Pallas kernels: none -> 44.5 us  [sum_all(): pl.pallas_call(functools.partial(sum_kernel, n_wide, n_dp), out_shape=jax...]
    unnamed x226 -> x229, local copies, waits for them, and re-layouts: 72.2 us -> 31 us
  transfers between devices with their start and end apart: 11 -> 11, of which waited for: 4 -> 3; matrix products, arithmetic and copies ran while one was open for 38% -> 49% of each run, Pallas kernels for 0% -> 2%
where the time goes in v1:
time: 1410 us; the launch traced here: 1400 us
  local copies, waits for them, and re-layouts  422 us (30%)
  other arithmetic  365 us (26%)
  matrix products  320 us (23%)
  waiting for transfers between devices  153 us (11%)
  blocking collectives  74.2 us (5%)
  Pallas kernels  44.5 us (3%)
  between operations  20.3 us (1%)
    mul x12, local copies, waits for them, and re-layouts, scaled_by(): cube = act[:, :, None, :] * route[None, :, :, None]  184 us
    reduce_sum x2, other arithmetic, depthwise_kern_grad(): taps.append(jnp.sum(window * grad, axis=(0, 1)))  94.2 us
    dot_general x4, matrix products, rows_nt(): lax.dot_general(left, right, (((1,), (1,)), ((), ())), preferred_element_...  85.7 us
    dot_general x4, matrix products, rows_tn(): lax.dot_general(left, right, (((0,), (0,)), ((), ())), preferred_element_...  73.6 us
    psum x1, waiting for transfers between devices, local(): lax.psum((grad_excite, jnp.concatenate([grad_router_one, grad_router_two]...  64.8 us
    psum x1, waiting for transfers between devices, local(): lax.psum(shares[0].astype(jnp.bfloat16), 'dp').astype(jnp.float32)  56 us
    mul x2, local copies, waits for them, and re-layouts, local(): before = jnp.sum(each.astype(jnp.float32) * r_one_wide, axis=2)  51.6 us
    reduce_sum x1, other arithmetic, local(): before = jnp.sum(each.astype(jnp.float32) * r_one_wide, axis=2)  51.2 us
  transfers between devices with their start and end apart: 11, of which 3 were waited for; matrix products, arithmetic and copies ran while one was open for 49% of the time, Pallas kernels for 2%

profile of v1, /device:TPU:0, one launch (start us, length us, event | category | flops | bytes accessed | tf_op | source)
XLA Modules:
  0.0 1399.3 jit_solution(12246506024700281367)
XLA Ops:
  19.0 12.9 mul.1509
  31.9 38.8 %mul.1511 = f32[3136,2560]{1,0:T(8,128)} reshape(f32[49,64,8,320]{3,2,1,0:T(8,128)} %mul.1509) | data formatting | bytes 64225280 | tf_op jit(solution)/shard_map/mul | solution.py:311
  70.8 17.0 %all_gather.16 = bf16[1152,72]{1,0:T(8,128)(2,1)S(1)} all-gather(bf16[144,72]{1,0:T(8,128)(2,1)S(1)} %copy.608), channel_id=1, replica_groups=mesh['dp'=4,'wide'=8] {'wide'}, dimensions={0}, use_global_device_ids=true | all-gather | bytes 186624 | tf_op jit(solution)/shard_map/all_gather | solution.py:284
  95.8 20.3 %mul.1471 = bf16[49,64,1536]{2,1,0:T(8,128)(2,1)} reshape(bf16[49,64,8,192]{3,2,1,0:T(8,128)(2,1)} %mul.1470) | data formatting | bytes 19267584 | tf_op jit(solution)/shard_map/mul | solution.py:158
  122.4 20.5 %mul.1585 = bf16[3136,1536]{1,0:T(8,128)(2,1)} reshape(bf16[49,64,8,192]{3,2,1,0:T(8,128)(2,1)} %broadcast_multiply_fusion.2) | data formatting | bytes 19267584 | tf_op jit(solution)/shard_map/mul | solution.py:158
  142.9 23.0 %fusion.26 = (f32[49,64,1152]{2,1,0:T(8,128)}, f32[49,64,1152]{2,1,0:T(8,128)}) fusion(bf16[1152,1536]{1,0:T(8,128)(2,1)} %all-gather.5.cloned.1.call-done, bf16[49,64,1536]{2,1,0:T(8,128)(2,1)} %mul.1471, bf16[64,1536]{1,0:T(8,128)(2,1)S(1)} %mul.1473), kind=kOutput, calls=%fused_computation.79 | convolution fusion | flops 11117395968 | bytes 42270720 | tf_op jit(solution)/shard_map/dot_general | solution.py:146
  166.0 41.3 %multiply_reduce_fusion.19 = (f32[64,1152]{1,0:T(8,128)S(1)}, f32[7,7,64,1152]{3,2,1,0:T(8,128)}) fusion(f32[64,1152]{1,0:T(8,128)S(1)} %get-tuple-element.296, f32[64,1152]{1,0:T(8,128)S(1)} %get-tuple-element.297, f32[64,1152]{1,0:T(8,128)S(1)} %get-tuple-element.298, f32[64,1152]{1,0:T(8,128)S(1)} %get-tuple-element.299, f32[7,7,64,1152]{3,2,1,0:T(8,128)} %bitcast.615, ...), kind=kLoop, calls=%fused_computation.76 | loop fusion | flops 79405056 | bytes 31850496 | tf_op jit(solution)/shard_map/reduce_sum | solution.py:302
  228.9 32.4 %multiply_reduce_fusion.4 = (f32[2560]{0:T(1024)S(1)}, f32[3136,2560]{1,0:T(8,128)}) fusion(f32[3136,2560]{1,0:T(8,128)} %mul.1511, bf16[3136,1152]{1,0:T(8,128)(2,1)} %bitcast.626, bf16[2560,1152]{1,0:T(8,128)(2,1)} %bitcast.633), kind=kOutput, calls=%fused_computation.23 | convolution fusion | flops 18528991232 | bytes 77359104 | tf_op jit(solution)/shard_map/dot_general | solution.py:146
  261.3 39.1 %reshape.557 = f32[49,64,8,320]{3,2,1,0:T(8,128)} reshape(f32[3136,2560]{1,0:T(8,128)} %get-tuple-element.349) | data formatting | bytes 64225280 | tf_op jit(solution)/shard_map/convert_element_type | solution.py:311
  300.4 51.2 %multiply_reduce_fusion.3 = f32[49,64,320]{2,1,0:T(8,128)} fusion(f32[49,64,8,320]{3,2,1,0:T(8,128)} %reshape.557, f32[64,8]{1,0:T(8,128)S(1)} %copy-done.64), kind=kLoop, calls=%fused_computation.22 | loop fusion | flops 15052800 | bytes 36128768 | tf_op jit(solution)/shard_map/reduce_sum | solution.py:311
  355.2 11.7 shard_map.501
  383.2 29.0 %mul.1520 = bf16[49,64,2560]{2,1,0:T(8,128)(2,1)} reshape(bf16[49,64,8,320]{3,2,1,0:T(8,128)(2,1)} %mul.1519) | data formatting | bytes 32112640 | tf_op jit(solution)/shard_map/mul | solution.py:158
  413.7 27.6 %fusion.174 = (f32[1280]{0:T(1024)S(1)}, f32[1280]{0:T(1024)S(1)}, f32[49,64,1280]{2,1,0:T(8,128)}) fusion(bf16[1280,2560]{1,0:T(8,128)(2,1)} %all-gather.9.cloned.1.call-done, bf16[49,64,2560]{2,1,0:T(8,128)(2,1)} %mul.1520, bf16[64,2560]{1,0:T(8,128)(2,1)S(1)} %mul.1522), kind=kOutput, calls=%fused_computation.429 | convolution fusion | flops 20572155904 | bytes 39004160 | tf_op jit(solution)/shard_map/dot_general | solution.py:146
  509.1 12.1 multiply_convert_fusion
  521.2 40.9 %multiply_reduce_fusion.1 = (f32[64,8]{0,1:T(8,128)S(1)}, f32[49,64,320]{2,1,0:T(8,128)S(1)}) fusion(f32[49,64,320]{2,1,0:T(8,128)} %get-tuple-element.286, f32[64,8]{0,1:T(8,128)S(1)} %get-tuple-element.284, bf16[8,320,1280,1]{2,1,0,3:T(8,128)(2,1)} %bitcast.630, bf16[49,64,1280]{2,1,0:T(8,128)(2,1)S(1)} %multiply_convert_fusion), kind=kOutput, calls=%fused_computation.20 | convolution fusion | flops 20583198720 | bytes 22614016 | tf_op jit(solution)/shard_map/dot_general | solution.py:365
  594.4 41.7 %copy.616 = bf16[49,64,8,320]{1,2,3,0:T(8,128)(2,1)} copy(bf16[49,64,8,320]{3,2,1,0:T(8,128)(2,1)} %broadcast_multiply_fusion.1) | data formatting | bytes 32112640 | tf_op jit(solution)/shard_map/mul | solution.py:158
  636.1 32.7 %multiply_reduce_fusion.18 = (f32[64,1152]{1,0:T(8,128)S(1)}, f32[49,64,1152]{2,1,0:T(8,128)}) fusion(f32[7,7,64,1152]{3,2,1,0:T(8,128)} %get-tuple-element.289, bf16[49,64,8,320]{1,2,3,0:T(8,128)(2,1)} %copy.616, bf16[320,8,1152]{2,1,0:T(8,128)(2,1)} %bitcast.621), kind=kOutput, calls=%fused_computation.74 | convolution fusion | flops 18518482944 | bytes 51150848 | tf_op jit(solution)/shard_map/dot_general | solution.py:389
  670.4 21.7 %multiply_reduce_fusion.13 = (f32[64,1152]{1,0:T(8,128)}, f32[49,64,1152]{2,1,0:T(8,128)}) fusion(f32[49,64,1152]{2,1,0:T(8,128)} %get-tuple-element.347, f32[7,7,64,1152]{3,2,1,0:T(8,128)} %get-tuple-element.289, f32[64,1152]{1,0:T(8,128)S(1)} %convolution_multiply_fusion.2, f32[49,64,1152]{2,1,0:T(8,128)} %get-tuple-element.355, f32[64,1152]{1,0:T(8,128)S(1)} %copy-done.11), kind=kLoop, calls=%fused_computation.69 | loop fusion | flops 57729024 | bytes 58687488 | tf_op jit(solution)/shard_map/reduce_sum | solution.py:66
  692.2 72.5 %multiply_reduce_fusion.9 = (f32[64,1152]{1,0:T(8,128)}, f32[64,1152]{1,0:T(8,128)}, f32[64,1152]{1,0:T(8,128)}, f32[64,1152]{1,0:T(8,128)}, f32[64,1152]{1,0:T(...) fusion(f32[7,7,64,1152]{3,2,1,0:T(8,128)} %bitcast.617, ...), kind=kLoop, calls=%fused_computation.65 | loop fusion | flops 118628352 | bytes 48365568 | tf_op jit(solution)/shard_map/reduce_sum | solution.py:66
  779.3 15.7 %convolution_convert_fusion.2 = bf16[1152,1536]{1,0:T(8,128)(2,1)} fusion(bf16[3136,1152]{1,0:T(8,128)(2,1)S(1)} %bitcast.628, bf16[3136,1536]{1,0:T(8,128)(2,1)} %mul.1585), kind=kOutput, calls=%fused_computation.88 | convolution fusion | flops 11099897856 | bytes 20398080 | tf_op jit(solution)/shard_map/dot_general | solution.py:152
  795.0 29.1 %mul.1656 = bf16[3136,2560]{1,0:T(8,128)(2,1)} reshape(bf16[49,64,8,320]{3,2,1,0:T(8,128)(2,1)} %broadcast_multiply_fusion.1) | data formatting | bytes 32112640 | tf_op jit(solution)/shard_map/mul | solution.py:158
  824.1 21.9 %copy.644 = bf16[2560,3136]{1,0:T(8,128)(2,1)} copy(bf16[2560,3136]{0,1:T(8,128)(2,1)} %bitcast.614) | data formatting | bytes 32112640 | tf_op jit(solution)/shard_map/dot_general | solution.py:152
  846.0 26.9 %fusion.35 = bf16[8,40,8,1152]{3,2,1,0:T(8,128)(2,1)S(1)} fusion(bf16[8,320,3136]{2,1,0:T(8,128)(2,1)} %bitcast.623, bf16[3136,1152,1]{1,0,2:T(8,128)(2,1)} %bitcast.627), kind=kOutput, calls=%fused_computation.94 | convolution fusion | flops 18499829760 | bytes 29179904 | tf_op jit(solution)/shard_map/dot_general | solution.py:152
  886.9 29.1 %mul.1729 = bf16[3136,2560]{1,0:T(8,128)(2,1)} reshape(bf16[49,64,8,320]{3,2,1,0:T(8,128)(2,1)} %broadcast_multiply_fusion) | data formatting | bytes 32112640 | tf_op jit(solution)/shard_map/mul | solution.py:158
  916.0 28.6 %convolution_convert_fusion.1 = bf16[1280,2560]{1,0:T(8,128)(2,1)} fusion(bf16[3136,1280]{1,0:T(8,128)(2,1)} %bitcast.624, bf16[3136,2560]{1,0:T(8,128)(2,1)} %mul.1729), kind=kOutput, calls=%fused_computation.80 | convolution fusion | flops 20555366400 | bytes 30638080 | tf_op jit(solution)/shard_map/dot_general | solution.py:152
  985.5 22.0 %multiply_reduce_fusion.5 = f32[64,8]{0,1:T(8,128)} fusion(bf16[8,192,1152,1]{2,1,0,3:T(8,128)(2,1)} %bitcast.639, f32[49,64,192]{2,1,0:T(8,128)} %bitcast_convert_fusion, bf16[49,64,1152]{2,1,0:T(8,128)(2,1)} %copy-done.13), kind=kOutput, calls=%fused_computation.24 | convolution fusion | flops 11107762176 | bytes 13174784 | tf_op jit(solution)/shard_map/dot_general | solution.py:406
  1009.6 16.1 %multiply_reduce_fusion = f32[64,8]{1,0:T(8,128)} fusion(f32[49,64,8,320]{3,2,1,0:T(8,128)} %reshape.557, f32[49,64,320]{2,1,0:T(8,128)} %get-tuple-element.280), kind=kLoop, calls=%fused_computation.19 | loop fusion | flops 16055808 | bytes 36128768 | tf_op jit(solution)/shard_map/reduce_sum | solution.py:386
  1036.9 39.4 %all-reduce.6 = (f32[]{:T(128)}, f32[512,8]{0,1:T(8,128)S(1)}, f32[2200]{0:T(1024)S(1)}) all-reduce(f32[]{:T(128)} %subtract_reduce_fusion, f32[512,8]{0,1:T(8,128)S(1)} %pad_maximum_fusion.1, f32[2200]{0:T(1024)S(1)} %concatenate.38), channel_id=1, replica_groups=mesh['dp'=4,'wide'=8] {'dp','wide'}, use_global_device_ids=true, to_apply=%region_16.17 | all-reduce | flops 6297 | bytes 50376 | tf_op jit(solution)/shard_map/psum | solution.py:420
  1081.9 64.8 %all-reduce.11.cloned.1.call-done = f32[2,1152,48]{1,2,0:T(8,128)} async-done(((f32[2,1152,48]{1,2,0:T(8,128)}), f32[2,1152,48]{1,2,0:T(8,128)}) %all-reduce.11.cloned.1.call-update) | async-done | bytes 442384 | tf_op jit(solution)/shard_map/psum | solution.py:420
  1149.3 31.6 %reduce-scatter.16.cloned.1.call-done = bf16[144,72]{1,0:T(8,128)(2,1)} async-done(((bf16[1152,72]{1,0:T(8,128)(2,1)}), bf16[144,72]{1,0:T(8,128)(2,1)}) %reduce-scatter.16.cloned.1.call-update) | async-done | bytes 20752
  1181.8 17.8 %psum.67 = bf16[8,9,144]{2,0,1:T(8,128)(2,1)S(1)} all-reduce(bf16[8,9,144]{2,0,1:T(8,128)(2,1)S(1)} %bitcast.665), channel_id=1, replica_groups=mesh['dp'=4,'wide'=8] {'dp'}, use_global_device_ids=true, to_apply=%region_77.78 | all-reduce | flops 10368 | bytes 41472 | tf_op jit(solution)/shard_map/psum | solution.py:449
  1201.2 56.0 %all-reduce.13.cloned.1.call-done = (bf16[144,1536]{1,0:T(8,128)(2,1)}, bf16[40,9216]{1,0:T(8,128)(2,1)}, bf16[160,2560]{1,0:T(8,128)(2,1)}, bf16[160,1000]{1,0:T(8,128)(2,1)}) async-done(((bf16[144,1536]{1,0:T(8,128)(2,1)}, bf16[40,9216]{1,0:T(8,128)(2,1)}, bf16[160,2560]{1,0:T(8,128)(2,1)}, bf16[160,1000]{1,0:T(8,128)(2,1)}), (bf16[144,1536]{1,0:T(8,128)(2,1)}, bf16[40,9216]{1,0:T(8,128)(2,1)}, ...) | async-done | bytes 2318864 | tf_op jit(solution)/shard_map/psum | solution.py:448
  (509 shorter events, 393.7 us)
Async XLA Ops:
  7.3 135.7 %all-gather.5.cloned.1.call-start = ((), (), s32[]{:S(2)}) async-start(), calls=%async_computation.5 | async-start | bytes 3981312 | tf_op jit(solution)/shard_map/all_gather | solution.py:279
  9.4 209.6 %all-gather.7.cloned.1.call-start = ((), (), s32[]{:S(2)}) async-start(), calls=%async_computation.6 | async-start | bytes 6635520 | tf_op jit(solution)/shard_map/all_gather | solution.py:280
  11.8 401.9 %all-gather.9.cloned.1.call-start = ((), (), s32[]{:S(2)}) async-start(), calls=%async_computation.7 | async-start | bytes 7372800 | tf_op jit(solution)/shard_map/all_gather | solution.py:281
  14.3 448.9 %all-gather.11.cloned.1.call-start = ((), (), s32[]{:S(2)}) async-start(), calls=%async_computation.8 | async-start | bytes 2949120 | tf_op jit(solution)/shard_map/all_gather | solution.py:282
  15.2 1010.5 %reduce-scatter.14.cloned.1.call-start = ((), (), s32[]{:S(2)}) async-start(), calls=%async_computation.12 | async-start | bytes 2949120 | tf_op jit(solution)/shard_map/reduce_scatter | solution.py:443
  18.3 69.8 %copy-start.85 = (bf16[64,8]{0,1:T(8,128)(2,1)}, bf16[64,8]{0,1:T(8,128)(2,1)S(1)}, u32[]{:S(2)}) copy-start(bf16[64,8]{0,1:T(8,128)(2,1)S(1)} %get-tuple-element.343) | copy-start | bytes 3076
  18.5 103.6 %copy-start.65 = (bf16[64,8]{1,0:T(8,128)(2,1)}, bf16[64,8]{1,0:T(8,128)(2,1)S(1)}, u32[]{:S(2)}) copy-start(bf16[64,8]{1,0:T(8,128)(2,1)S(1)} %copy.606) | copy-start | bytes 3076
  90.3 75.6 %copy-start.29 = (f32[64,1152]{1,0:T(8,128)}, f32[64,1152]{1,0:T(8,128)S(1)}, u32[]{:S(2)}) copy-start(f32[64,1152]{1,0:T(8,128)S(1)} %get-tuple-element.295) | copy-start | bytes 884740
  90.3 75.6 %copy-start.31 = (f32[64,1152]{1,0:T(8,128)}, f32[64,1152]{1,0:T(8,128)S(1)}, u32[]{:S(2)}) copy-start(f32[64,1152]{1,0:T(8,128)S(1)} %get-tuple-element.296) | copy-start | bytes 884740
  90.3 75.6 %copy-start.33 = (f32[64,1152]{1,0:T(8,128)}, f32[64,1152]{1,0:T(8,128)S(1)}, u32[]{:S(2)}) copy-start(f32[64,1152]{1,0:T(8,128)S(1)} %get-tuple-element.297) | copy-start | bytes 884740
  90.3 75.6 %copy-start.35 = (f32[64,1152]{1,0:T(8,128)}, f32[64,1152]{1,0:T(8,128)S(1)}, u32[]{:S(2)}) copy-start(f32[64,1152]{1,0:T(8,128)S(1)} %get-tuple-element.298) | copy-start | bytes 884740
  90.3 75.6 %copy-start.37 = (f32[64,1152]{1,0:T(8,128)}, f32[64,1152]{1,0:T(8,128)S(1)}, u32[]{:S(2)}) copy-start(f32[64,1152]{1,0:T(8,128)S(1)} %get-tuple-element.299) | copy-start | bytes 884740
  90.4 75.6 %copy-start.39 = (f32[64,1152]{1,0:T(8,128)}, f32[64,1152]{1,0:T(8,128)S(1)}, u32[]{:S(2)}) copy-start(f32[64,1152]{1,0:T(8,128)S(1)} %get-tuple-element.300) | copy-start | bytes 884740
  166.0 41.3 %copy-start.23 = (f32[2,1152,48]{1,2,0:T(8,128)S(1)}, f32[2,1152,48]{1,2,0:T(8,128)}, u32[]{:S(2)}) copy-start(f32[2,1152,48]{1,2,0:T(8,128)} %param.51) | copy-start | bytes 1327108
  166.0 41.3 %slice-start.2 = ((f32[5400]{0:T(1024)}), f32[48]{0:T(128)S(1)}, s32[]{:S(2)}) async-start(f32[5400]{0:T(1024)} %param.57), calls=%async_computation.18 | async-start | bytes 1024 | tf_op jit(solution)/shard_map/slice | solution.py:167
  300.4 54.2 %copy-start.98 = (f32[8]{0:T(128)S(1)}, f32[8]{0:T(128)}, u32[]{:S(2)}) copy-start(f32[8]{0:T(128)} %get-tuple-element.344) | copy-start | bytes 100
  300.4 66.5 %copy-start.79 = (f32[5400]{0:T(1024)S(1)}, f32[5400]{0:T(1024)}, u32[]{:S(2)}) copy-start(f32[5400]{0:T(1024)} %param.57) | copy-start | bytes 64804
  412.6 149.7 %copy-start.87 = (f32[64,8]{0,1:T(8,128)}, f32[64,8]{0,1:T(8,128)S(1)}, u32[]{:S(2)}) copy-start(f32[64,8]{0,1:T(8,128)S(1)} %get-tuple-element.350) | copy-start | bytes 6148
  509.1 53.1 %copy-start.94 = (f32[8]{0:T(128)}, f32[8]{0:T(128)S(1)}, u32[]{:S(2)}) copy-start(f32[8]{0:T(128)S(1)} %get-tuple-element.333) | copy-start | bytes 100
  509.1 53.5 %slice-start = ((s8[4816896]{0:T(1024)(128)(4,1)}), s8[4194304]{0:T(1024)(128)(4,1)S(1)}, s32[]{:S(2)}) async-start(s8[4816896]{0:T(1024)(128)(4,1)} %bitcast.612), calls=%async_computation.16 | async-start | bytes 8388608
  521.2 41.0 %copy-start.6 = (bf16[49,64,1280]{2,1,0:T(8,128)(2,1)}, bf16[49,64,1280]{2,1,0:T(8,128)(2,1)S(1)}, u32[]{:S(2)}) copy-start(bf16[49,64,1280]{2,1,0:T(8,128)(2,1)S(1)} %multiply_convert_fusion) | copy-start | bytes 24084484
  521.2 41.4 %slice-start.1 = ((s8[4816896]{0:T(1024)(128)(4,1)}), s8[622592]{0:T(1024)(128)(4,1)S(1)}, s32[]{:S(2)}) async-start(s8[4816896]{0:T(1024)(128)(4,1)} %bitcast.612), calls=%async_computation.17 | async-start | bytes 1245184
  764.8 261.0 %reduce-scatter.8.cloned.1.call-start = ((), (), s32[]{:S(2)}) async-start(), calls=%async_computation.9 | async-start | bytes 3981312 | tf_op jit(solution)/shard_map/reduce_scatter | solution.py:431
  795.0 230.8 %reduce-scatter.10.cloned.1.call-start = ((), (), s32[]{:S(2)}) async-start(), calls=%async_computation.10 | async-start | bytes 6635520 | tf_op jit(solution)/shard_map/reduce_scatter | solution.py:437
  876.4 149.3 %reduce-scatter.12.cloned.1.call-start = ((), (), s32[]{:S(2)}) async-start(), calls=%async_computation.11 | async-start | bytes 7372800 | tf_op jit(solution)/shard_map/reduce_scatter | solution.py:440
  944.7 201.9 %all-reduce.11.cloned.1.call-start = ((), (), s32[]{:S(2)}) async-start(), calls=%async_computation.13 | async-start | bytes 884736 | tf_op jit(solution)/shard_map/psum | solution.py:420
  1007.5 173.4 %reduce-scatter.16.cloned.1.call-start = ((), (), s32[]{:S(2)}) async-start(), calls=%async_computation.14 | async-start | bytes 331776
  1009.6 247.7 %all-reduce.13.cloned.1.call-start = ((), (), s32[]{:S(2)}) async-start(), calls=%async_computation.15 | async-start | bytes 4653056 | tf_op jit(solution)/shard_map/psum | solution.py:448
  1009.6 69.5 %copy-start.75 = (f32[512,8]{0,1:T(8,128)S(1)}, f32[512,8]{0,1:T(8,128)}, u32[]{:S(2)}) copy-start(f32[512,8]{0,1:T(8,128)} %param.54) | copy-start | bytes 49156
  1025.7 235.6 %copy-start.20 = (f32[8,36,4,4]{3,2,1,0:T(4,128)S(1)}, f32[8,36,4,4]{3,2,1,0:T(4,128)}, u32[]{:S(2)}) copy-start(f32[8,36,4,4]{3,2,1,0:T(4,128)} %copy.642) | copy-start | bytes 55300
  1027.4 172.2 %copy-start.62 = (f32[8,9,144]{2,0,1:T(8,128)S(1)}, f32[8,9,144]{2,0,1:T(8,128)}, u32[]{:S(2)}) copy-start(f32[8,9,144]{2,0,1:T(8,128)} %param.45) | copy-start | bytes 124420
  1027.4 172.2 %copy-start.82 = (f32[8,9,144]{2,0,1:T(8,128)S(1)}, f32[8,9,144]{2,0,1:T(8,128)}, u32[]{:S(2)}) copy-start(f32[8,9,144]{2,0,1:T(8,128)} %param.47) | copy-start | bytes 124420
  (81 other events, 1093.4 us)
Sparse Core Ops, SparseCore 0:
  10.3 44.2 all-gather.4
  56.8 62.6 all-gather.6
  121.7 65.5 all-gather.8
  189.4 32.4 all-gather.10
  764.9 36.6 reduce-scatter.13
  803.7 42.9 reduce-scatter.7
  876.5 65.3 reduce-scatter.9
  944.8 71.5 reduce-scatter.11
  1022.3 124.2 all-reduce.10
  1149.4 31.4 reduce-scatter.15
  1184.4 72.7 all-reduce.12

commit v2 on v1

v2 whole, which is shorter than its diff:
```python
import functools

import jax
import jax.numpy as jnp
from jax import lax
from jax.experimental import pallas as pl
from jax.experimental.pallas import tpu as pltpu
from jax.sharding import PartitionSpec as P

SIDE = 7
PIX = 49
KSIZE = 3
EXPERTS = 8
BLK = 4
STEP = 10
C_IN = 192
C_MID = 1152
C_SE = 48
C_OUT = 320
C_HEAD = 1280
CLASSES = 1000


HIGH = lax.Precision.HIGHEST
beta_one = 0.9
beta_two = 0.95
eps_adam = 1e-08
eps_norm = 1e-05
decay = 0.01
rate_matrix = 0.08
rate_gains = 0.5
boost = 1.0
balance_weight = 4.0
stat_gain = 15000.0


def split_gains(gains):
    widths = [C_SE, C_MID, C_OUT, C_OUT, C_HEAD, C_HEAD, CLASSES]
    pieces = []
    start = 0
    for width in widths:
        pieces.append(gains[start : start + width])
        start = start + width
    return pieces


MESH = pl.DeviceIdType.MESH


def sum_kernel(n_wide, n_dp, x_ref, o_ref, wide_slots, dp_slots, part, s_wide, r_wide, s_dp, r_dp):
    me_wide = lax.axis_index("wide")
    me_dp = lax.axis_index("dp")
    barrier = pltpu.get_barrier_semaphore()
    for k in range(1, n_wide):
        pl.semaphore_signal(
            barrier, inc=1, device_id={"wide": lax.rem(me_wide + k, n_wide)}, device_id_type=MESH
        )
    for k in range(1, n_dp):
        pl.semaphore_signal(
            barrier, inc=1, device_id={"dp": lax.rem(me_dp + k, n_dp)}, device_id_type=MESH
        )
    pl.semaphore_wait(barrier, n_wide + n_dp - 2)

    def exchange(src, slots, me, axis, size, send, recv):
        copies = []
        for k in range(1, size):
            copy = pltpu.make_async_remote_copy(
                src_ref=src,
                dst_ref=slots.at[me],
                send_sem=send.at[k],
                recv_sem=recv.at[k],
                device_id={axis: lax.rem(me + k, size)},
                device_id_type=MESH,
            )
            copy.start()
            copies.append(copy)
        slots[me] = src[...]
        for copy in copies:
            copy.wait()
        total = slots[0]
        for k in range(1, size):
            total = total + slots[k]
        return total

    part[...] = exchange(x_ref, wide_slots, me_wide, "wide", n_wide, s_wide, r_wide)
    o_ref[...] = exchange(part, dp_slots, me_dp, "dp", n_dp, s_dp, r_dp)


def sum_all(parts, ident):
    shapes = [part.shape for part in parts]
    sizes = [part.size for part in parts]
    flat = jnp.concatenate([part.reshape(-1) for part in parts])
    rows = -(-flat.size // 1024) * 8
    flat = jnp.pad(flat, (0, rows * 128 - flat.size)).reshape(rows, 128)
    n_wide = lax.axis_size("wide")
    n_dp = lax.axis_size("dp")
    out = pl.pallas_call(
        functools.partial(sum_kernel, n_wide, n_dp),
        out_shape=jax.ShapeDtypeStruct((rows, 128), jnp.float32),
        in_specs=[pl.BlockSpec(memory_space=pltpu.VMEM)],
        out_specs=pl.BlockSpec(memory_space=pltpu.VMEM),
        scratch_shapes=[
            pltpu.VMEM((n_wide, rows, 128), jnp.float32),
            pltpu.VMEM((n_dp, rows, 128), jnp.float32),
            pltpu.VMEM((rows, 128), jnp.float32),
            pltpu.SemaphoreType.DMA((n_wide,)),
            pltpu.SemaphoreType.DMA((n_wide,)),
            pltpu.SemaphoreType.DMA((n_dp,)),
            pltpu.SemaphoreType.DMA((n_dp,)),
        ],
        compiler_params=pltpu.CompilerParams(collective_id=ident, has_side_effects=True),
    )(flat)
    out = out.reshape(-1)
    found = []
    start = 0
    for shape, size in zip(shapes, sizes):
        found.append(out[start : start + size].reshape(shape))
        start = start + size
    return found


def balance_grad(means, every):
    return balance_weight * 2.0 * (means - jnp.mean(means)) / (EXPERTS * every)


GROUP = 16
PAIRS = EXPERTS // 2
ROWS = PIX * GROUP
LOW = jnp.bfloat16
FULL = jnp.float32
VMEM_CAP = 60 * 1024 * 1024


def sig(value):
    return 0.5 + 0.5 * jnp.tanh(0.5 * value)


def dot_nn(left, right, precision=None):
    return lax.dot_general(
        left, right, (((1,), (0,)), ((), ())), precision=precision, preferred_element_type=FULL
    )


def dot_nt(left, right, precision=None):
    return lax.dot_general(
        left, right, (((1,), (1,)), ((), ())), precision=precision, preferred_element_type=FULL
    )


def dot_tn(left, right, precision=None):
    return lax.dot_general(
        left, right, (((0,), (0,)), ((), ())), precision=precision, preferred_element_type=FULL
    )


def images_block(width):
    return pl.BlockSpec((PIX, GROUP, width), lambda i: (0, i, 0))


def group_block(width):
    return pl.BlockSpec((GROUP, width), lambda i: (i, 0))


def pair_block(width):
    return pl.BlockSpec((PAIRS, GROUP, width), lambda i: (0, i, 0))


def whole(*shape):
    return pl.BlockSpec(shape, lambda i: (0,) * len(shape), pipeline_mode=pl.Buffered(1))


def total_block(*shape):
    return pl.BlockSpec(shape, lambda i: (0,) * len(shape))


def device_kernel(kernel, name, grid, in_specs, outs, out_specs, scratch, flops, moved):
    return pl.pallas_call(
        kernel,
        name=name,
        grid=(grid,),
        in_specs=in_specs,
        out_shape=[jax.ShapeDtypeStruct(shape, dtype) for shape, dtype in outs],
        out_specs=out_specs,
        scratch_shapes=scratch,
        compiler_params=pltpu.CompilerParams(
            vmem_limit_bytes=VMEM_CAP, dimension_semantics=("arbitrary",)
        ),
        cost_estimate=pl.CostEstimate(flops=flops, bytes_accessed=moved, transcendentals=0),
    )


def pair_scale(route, pair, width):
    lane = lax.broadcasted_iota(jnp.int32, (route.shape[0], 2 * width), 1)
    return jnp.where(
        lane < width, route[:, 2 * pair : 2 * pair + 1], route[:, 2 * pair + 1 : 2 * pair + 2]
    )


def pair_columns(sums, width):
    count = sums[0].shape[0]
    lane = lax.broadcasted_iota(jnp.int32, (count, 2 * width), 1)
    place = lax.broadcasted_iota(jnp.int32, (count, EXPERTS), 1)
    found = jnp.zeros((count, EXPERTS), FULL)
    for pair in range(PAIRS):
        first = jnp.sum(jnp.where(lane < width, sums[pair], 0.0), axis=1, keepdims=True)
        second = jnp.sum(jnp.where(lane < width, 0.0, sums[pair]), axis=1, keepdims=True)
        found = found + jnp.where(place == 2 * pair, first, 0.0)
        found = found + jnp.where(place == 2 * pair + 1, second, 0.0)
    return found


def taps_of(pixel):
    row, col = pixel // SIDE, pixel % SIDE
    found = []
    for tap in range(KSIZE * KSIZE):
        at_row, at_col = row + tap // KSIZE - 1, col + tap % KSIZE - 1
        if 0 <= at_row < SIDE and 0 <= at_col < SIDE:
            found.append((tap, at_row * SIDE + at_col))
    return found


def expand_kernel(
    img_ref, hot_ref, router_ref, expand_ref, depth_ref, excite_ref, bias_se_ref, bias_ex_ref,
    hidden_ref, turned_ref, scaled_ref, route_ref, pair_in_ref, pair_out_ref, gate_ref,
    squeeze_ref, pooled_one_ref, pooled_act_ref, route_sum_ref,
    routed, hidden_full, act_full, kern,
):
    pooled = img_ref[0].astype(FULL)
    for pixel in range(1, PIX):
        pooled = pooled + img_ref[pixel].astype(FULL)
    pooled = pooled[:, :C_IN] * (1.0 / PIX)
    pooled_one_ref[...] = pooled
    route = sig(dot_nt(pooled, router_ref[...], HIGH) + hot_ref[...])
    route_ref[...] = route

    @pl.when(pl.program_id(0) == 0)
    def _():
        route_sum_ref[...] = jnp.zeros_like(route_sum_ref)

    route_sum_ref[...] += jnp.sum(route, axis=0, keepdims=True)
    low = route.astype(LOW).astype(FULL)
    for pair in range(PAIRS):
        scale = pair_scale(low, pair, C_IN).astype(LOW)
        pair_in_ref[pair] = scale
        pair_out_ref[pair] = pair_scale(low, pair, C_OUT).astype(LOW)
        place = slice(2 * pair * C_IN, 2 * (pair + 1) * C_IN)
        for pixel in range(PIX):
            routed[pixel, :, place] = img_ref[pixel] * scale
    columns = [low[:, expert : expert + 1] for expert in range(EXPERTS)]
    for tap in range(KSIZE * KSIZE):
        total = columns[0] * depth_ref[tap, 0:1, :]
        for expert in range(1, EXPERTS):
            total = total + columns[expert] * depth_ref[tap, expert : expert + 1, :]
        kern[tap] = total
    product = dot_nt(routed[...].reshape(ROWS, EXPERTS * C_IN), expand_ref[...])
    hidden_full[...] = product.reshape(PIX, GROUP, C_MID)

    def chunk(index, carry):
        lanes = pl.ds(pl.multiple_of(index * 128, 128), 128)
        taps = [kern[tap, :, lanes] for tap in range(KSIZE * KSIZE)]
        start = [None] * PIX

        def fill(row):
            for pixel in range(row * SIDE, row * SIDE + SIDE):
                value = hidden_full[pixel, :, lanes]
                hidden_ref[pixel, :, lanes] = value.astype(LOW)
                start[pixel] = value * sig(value)

        fill(0)
        pooled_act = jnp.zeros((GROUP, 128), FULL)
        for row in range(SIDE):
            if row + 1 < SIDE:
                fill(row + 1)
            for pixel in range(row * SIDE, row * SIDE + SIDE):
                total = None
                for tap, source in taps_of(pixel):
                    term = start[source] * taps[tap]
                    total = term if total is None else total + term
                turned_ref[pixel, :, lanes] = total.astype(LOW)
                act = total * sig(total)
                pooled_act = pooled_act + act
                act_full[pixel, :, lanes] = act
        pooled_act_ref[:, lanes] = pooled_act * (1.0 / PIX)
        return carry

    lax.fori_loop(0, C_MID // 128, chunk, 0)
    squeeze = dot_nt(pooled_act_ref[...], excite_ref[0], HIGH) + bias_se_ref[...]
    squeeze_ref[...] = squeeze
    gate = sig(dot_nn(squeeze * sig(squeeze), excite_ref[1], HIGH) + bias_ex_ref[...])
    gate_ref[...] = gate

    def finish(pixel, carry):
        scaled_ref[pixel] = (act_full[pixel] * gate).astype(LOW)
        return carry

    lax.fori_loop(0, PIX, finish, 0)


def expand_forward(img_two, hot, router, expand_low, depth_full, excite, bias_se, bias_ex):
    images = img_two.shape[1]
    return device_kernel(
        expand_kernel,
        "expand_forward",
        images // GROUP,
        [
            images_block(2 * C_IN), group_block(EXPERTS), whole(EXPERTS, C_IN),
            whole(C_MID, EXPERTS * C_IN), whole(KSIZE * KSIZE, EXPERTS, C_MID),
            whole(2, C_SE, C_MID), whole(1, C_SE), whole(1, C_MID),
        ],
        [
            ((PIX, images, C_MID), LOW), ((PIX, images, C_MID), LOW), ((PIX, images, C_MID), LOW),
            ((images, EXPERTS), FULL), ((PAIRS, images, 2 * C_IN), LOW),
            ((PAIRS, images, 2 * C_OUT), LOW), ((images, C_MID), FULL), ((images, C_SE), FULL),
            ((images, C_IN), FULL), ((images, C_MID), FULL), ((1, EXPERTS), FULL),
        ],
        [
            images_block(C_MID), images_block(C_MID), images_block(C_MID), group_block(EXPERTS),
            pair_block(2 * C_IN), pair_block(2 * C_OUT), group_block(C_MID), group_block(C_SE),
            group_block(C_IN), group_block(C_MID), total_block(1, EXPERTS),
        ],
        [
            pltpu.VMEM((PIX, GROUP, EXPERTS * C_IN), LOW), pltpu.VMEM((PIX, GROUP, C_MID), FULL),
            pltpu.VMEM((PIX, GROUP, C_MID), FULL), pltpu.VMEM((KSIZE * KSIZE, GROUP, C_MID), FULL),
        ],
        2 * PIX * images * EXPERTS * C_IN * C_MID,
        PIX * images * 4 * C_MID * 2,
    )(img_two, hot, router, expand_low, depth_full, excite, bias_se, bias_ex)


def stack_experts(source, stacked, sem):
    copies = [
        pltpu.make_async_copy(
            source.at[:, expert * C_MID : (expert + 1) * C_MID],
            stacked.at[expert * C_OUT : (expert + 1) * C_OUT],
            sem.at[expert],
        )
        for expert in range(EXPERTS)
    ]
    for copy in copies:
        copy.start()
    for copy in copies:
        copy.wait()


def project_kernel(
    scaled_ref, source, pair_ref, each_ref, before_ref, sums_ref, product, weight_ref, sem
):
    half = 2 * 2 * C_OUT
    flat = scaled_ref[...].reshape(ROWS, C_MID)

    @pl.when(pl.program_id(0) == 0)
    def _():
        stack_experts(source, weight_ref, sem)
        sums_ref[...] = jnp.zeros_like(sums_ref)

    for part in range(2):
        product[part] = dot_nt(flat, weight_ref[part * half : (part + 1) * half]).reshape(
            PIX, GROUP, half
        )
    scales = [pair_ref[pair].astype(FULL) for pair in range(PAIRS)]

    def mix(pixel, carry):
        plain, square = carry
        total = jnp.zeros((GROUP, 2 * C_OUT), FULL)
        for pair in range(PAIRS):
            part, place = pair // 2, pair % 2 * 2 * C_OUT
            value = product[part, pixel, :, place : place + 2 * C_OUT]
            each_ref[pixel, :, pair * 2 * C_OUT : (pair + 1) * 2 * C_OUT] = value.astype(LOW)
            total = total + value * scales[pair]
        before = (total + pltpu.roll(total, C_OUT, 1))[:, :C_OUT]
        before_ref[pixel] = before
        return plain + before, square + before * before

    zero = jnp.zeros((GROUP, C_OUT), FULL)
    plain, square = lax.fori_loop(0, PIX, mix, (zero, zero))
    sums_ref[0:1] += jnp.sum(plain, axis=0, keepdims=True)
    sums_ref[1:2] += jnp.sum(square, axis=0, keepdims=True)


def project_forward(scaled, project_low, pair_out):
    images = scaled.shape[1]
    wide = EXPERTS * C_OUT
    return device_kernel(
        project_kernel,
        "project_forward",
        images // GROUP,
        [images_block(C_MID), pl.BlockSpec(memory_space=pl.ANY), pair_block(2 * C_OUT)],
        [((PIX, images, wide), LOW), ((PIX, images, C_OUT), FULL), ((2, C_OUT), FULL)],
        [images_block(wide), images_block(C_OUT), total_block(2, C_OUT)],
        [
            pltpu.VMEM((2, PIX, GROUP, wide // 2), FULL), pltpu.VMEM((wide, C_MID), LOW),
            pltpu.SemaphoreType.DMA((EXPERTS,)),
        ],
        2 * PIX * images * wide * C_MID,
        PIX * images * (wide + C_MID) * 2,
    )(scaled, project_low, pair_out)


def head_kernel(
    before_ref, norm_ref, hot_ref, router_ref, weight_ref,
    widened_ref, twice_ref, route_ref, pair_ref, pooled_ref, sums_ref, route_sum_ref,
    routed, padded,
):
    @pl.when(pl.program_id(0) == 0)
    def _():
        sums_ref[...] = jnp.zeros_like(sums_ref)
        route_sum_ref[...] = jnp.zeros_like(route_sum_ref)
        padded[...] = jnp.zeros_like(padded)

    gain, shift = norm_ref[0:1], norm_ref[1:2]
    pooled = jnp.zeros((GROUP, C_OUT), FULL)
    for pixel in range(PIX):
        normed = (before_ref[pixel] * gain + shift).astype(LOW).astype(FULL)
        pooled = pooled + normed
        padded[:, :C_OUT] = normed
        value = padded[...]
        twice_ref[pixel] = (value + pltpu.roll(value, C_OUT, 1)).astype(LOW)
    pooled = pooled * (1.0 / PIX)
    pooled_ref[...] = pooled
    route = sig(dot_nt(pooled, router_ref[...], HIGH) + hot_ref[...])
    route_ref[...] = route
    route_sum_ref[...] += jnp.sum(route, axis=0, keepdims=True)
    low = route.astype(LOW).astype(FULL)
    for pair in range(PAIRS):
        scale = pair_scale(low, pair, C_OUT).astype(LOW)
        pair_ref[pair] = scale
        place = slice(2 * pair * C_OUT, 2 * (pair + 1) * C_OUT)
        for pixel in range(PIX):
            routed[pixel, :, place] = twice_ref[pixel] * scale
    product = dot_nt(routed[...].reshape(ROWS, EXPERTS * C_OUT), weight_ref[...])
    widened_ref[...] = product.reshape(PIX, GROUP, C_HEAD).astype(LOW)
    sums_ref[0:1] += jnp.sum(product, axis=0, keepdims=True)
    sums_ref[1:2] += jnp.sum(product * product, axis=0, keepdims=True)


def head_forward(before, norm, hot, router, head_low):
    images = before.shape[1]
    wide = EXPERTS * C_OUT
    return device_kernel(
        head_kernel,
        "head_forward",
        images // GROUP,
        [
            images_block(C_OUT), whole(2, C_OUT), group_block(EXPERTS), whole(EXPERTS, C_OUT),
            whole(C_HEAD, wide),
        ],
        [
            ((PIX, images, C_HEAD), LOW), ((PIX, images, 2 * C_OUT), LOW),
            ((images, EXPERTS), FULL), ((PAIRS, images, 2 * C_OUT), LOW), ((images, C_OUT), FULL),
            ((2, C_HEAD), FULL), ((1, EXPERTS), FULL),
        ],
        [
            images_block(C_HEAD), images_block(2 * C_OUT), group_block(EXPERTS),
            pair_block(2 * C_OUT), group_block(C_OUT), total_block(2, C_HEAD),
            total_block(1, EXPERTS),
        ],
        [pltpu.VMEM((PIX, GROUP, wide), LOW), pltpu.VMEM((GROUP, 2 * C_OUT), FULL)],
        2 * PIX * images * wide * C_HEAD,
        PIX * images * (C_HEAD + C_OUT) * 2,
    )(before, norm, hot, router, head_low)


def loss_kernel(
    widened_ref, norm_ref, label_ref, class_ref, bias_ref,
    feats_ref, logits_ref, grad_feats_ref, sums_ref, cross_ref, bias_grad_ref,
    silu_sum, slope_sum, cross_sum,
):
    step = pl.program_id(0)
    rows = pl.ds(pl.multiple_of(step * GROUP, GROUP), GROUP)
    gain, shift, inv, offset = (norm_ref[k : k + 1] for k in range(4))

    def pixel_sums(pixel, carry):
        total, slope, moved = carry
        value = widened_ref[pixel].astype(FULL)
        lifted = value * gain + shift
        part = sig(lifted)
        grown = lifted * part
        bent = part + grown * (1.0 - part)
        return total + grown, slope + bent, moved + bent * (value * inv + offset)

    zero = jnp.zeros((GROUP, C_HEAD), FULL)
    total, slope, moved = lax.fori_loop(0, PIX, pixel_sums, (zero, zero, zero))
    silu_sum[rows] = total
    slope_sum[rows] = slope
    cross_sum[rows] = moved

    @pl.when(step == pl.num_programs(0) - 1)
    def _():
        feats = (silu_sum[...] * (1.0 / PIX)).astype(LOW)
        feats_ref[...] = feats
        logits = dot_nn(feats, class_ref[...]) + bias_ref[...]
        lane = lax.broadcasted_iota(jnp.int32, logits.shape, 1)
        picked = lane == label_ref[...]
        top = jnp.max(logits, axis=1, keepdims=True)
        powers = jnp.exp(logits - top)
        totals = jnp.sum(powers, axis=1, keepdims=True)
        cross = top + jnp.log(totals) - jnp.sum(
            jnp.where(picked, logits, 0.0), axis=1, keepdims=True
        )
        cross_ref[...] = jnp.sum(cross, axis=0, keepdims=True)
        grad = (powers / totals - jnp.where(picked, 1.0, 0.0)) * norm_ref[4:5, 0:1]
        grad = grad.astype(LOW)
        logits_ref[...] = grad
        bias_grad_ref[...] = jnp.sum(grad.astype(FULL), axis=0, keepdims=True)
        grad_feats = dot_nt(grad, class_ref[...]) * (1.0 / PIX)
        grad_feats_ref[...] = grad_feats
        sums_ref[0:1] = jnp.sum(grad_feats * slope_sum[...], axis=0, keepdims=True)
        sums_ref[1:2] = jnp.sum(grad_feats * cross_sum[...], axis=0, keepdims=True)


def loss_part(widened, norm, label, class_low, bias):
    images = widened.shape[1]
    return device_kernel(
        loss_kernel,
        "loss_part",
        images // GROUP,
        [
            images_block(C_HEAD), whole(8, C_HEAD), whole(images, 1), whole(C_HEAD, CLASSES),
            whole(1, CLASSES),
        ],
        [
            ((images, C_HEAD), LOW), ((images, CLASSES), LOW), ((images, C_HEAD), FULL),
            ((2, C_HEAD), FULL), ((1, 1), FULL), ((1, CLASSES), FULL),
        ],
        [
            total_block(images, C_HEAD), total_block(images, CLASSES), total_block(images, C_HEAD),
            total_block(2, C_HEAD), total_block(1, 1), total_block(1, CLASSES),
        ],
        [pltpu.VMEM((images, C_HEAD), FULL)] * 3,
        4 * images * C_HEAD * CLASSES,
        PIX * images * C_HEAD * 2,
    )(widened, norm, label, class_low, bias)


def head_back_kernel(
    widened_ref, grad_feats_ref, coef_ref, weight_ref, pair_ref, twice_ref, before_ref, norm_ref,
    route_ref, balance_ref, router_ref,
    grad_wide_ref, grad_normed_ref, logit_ref, sums_ref,
    product, mixed,
):
    half = 2 * 2 * C_OUT

    @pl.when(pl.program_id(0) == 0)
    def _():
        sums_ref[...] = jnp.zeros_like(sums_ref)

    gain, shift, by_value, constant = (coef_ref[k : k + 1] for k in range(4))
    grad_feats = grad_feats_ref[...]

    def widen(pixel, carry):
        value = widened_ref[pixel].astype(FULL)
        lifted = value * gain + shift
        part = sig(lifted)
        bent = part + lifted * part * (1.0 - part)
        grad = grad_feats * bent * gain + value * by_value + constant
        grad_wide_ref[pixel] = grad.astype(LOW)
        return carry

    lax.fori_loop(0, PIX, widen, 0)
    flat = grad_wide_ref[...].reshape(ROWS, C_HEAD)
    route_sums = []
    for part in range(2):
        product[part] = dot_nn(flat, weight_ref[:, part * half : (part + 1) * half]).reshape(
            PIX, GROUP, half
        )
    scales = [pair_ref[pair].astype(FULL) for pair in range(PAIRS)]

    def mix(pixel, carry):
        twice = twice_ref[pixel].astype(FULL)
        total = jnp.zeros((GROUP, 2 * C_OUT), FULL)
        found = []
        for pair in range(PAIRS):
            part, place = pair // 2, pair % 2 * 2 * C_OUT
            value = product[part, pixel, :, place : place + 2 * C_OUT]
            total = total + value * scales[pair]
            found.append(carry[pair] + value * twice)
        mixed[pixel] = (total + pltpu.roll(total, C_OUT, 1))[:, :C_OUT]
        return tuple(found)

    zero = jnp.zeros((GROUP, 2 * C_OUT), FULL)
    route_sums = lax.fori_loop(0, PIX, mix, (zero,) * PAIRS)
    route = route_ref[...]
    grad_route = pair_columns(route_sums, C_OUT) + balance_ref[...]
    logit = grad_route * route * (1.0 - route)
    logit_ref[...] = logit
    added = dot_nn(logit, router_ref[...], HIGH) * (1.0 / PIX)

    def close(pixel, carry):
        plain, cross = carry
        grad = mixed[pixel] + added
        grad_normed_ref[pixel] = grad
        hat = before_ref[pixel] * norm_ref[0:1] + norm_ref[1:2]
        return plain + grad, cross + grad * hat

    zero = jnp.zeros((GROUP, C_OUT), FULL)
    plain, cross = lax.fori_loop(0, PIX, close, (zero, zero))
    sums_ref[0:1] += jnp.sum(plain, axis=0, keepdims=True)
    sums_ref[1:2] += jnp.sum(cross, axis=0, keepdims=True)


def head_back(
    widened, grad_feats, coef, head_low, pair_two, twice, before, norm, route, balance, router_t
):
    images = widened.shape[1]
    wide = EXPERTS * C_OUT
    return device_kernel(
        head_back_kernel,
        "head_back",
        images // GROUP,
        [
            images_block(C_HEAD), group_block(C_HEAD), whole(4, C_HEAD), whole(C_HEAD, wide),
            pair_block(2 * C_OUT), images_block(2 * C_OUT), images_block(C_OUT), whole(2, C_OUT),
            group_block(EXPERTS), whole(1, EXPERTS), whole(EXPERTS, C_OUT),
        ],
        [
            ((PIX, images, C_HEAD), LOW), ((PIX, images, C_OUT), FULL), ((images, EXPERTS), FULL),
            ((2, C_OUT), FULL),
        ],
        [
            images_block(C_HEAD), images_block(C_OUT), group_block(EXPERTS), total_block(2, C_OUT),
        ],
        [pltpu.VMEM((2, PIX, GROUP, wide // 2), FULL), pltpu.VMEM((PIX, GROUP, C_OUT), FULL)],
        2 * PIX * images * wide * C_HEAD,
        PIX * images * (2 * C_HEAD + C_OUT) * 2,
    )(widened, grad_feats, coef, head_low, pair_two, twice, before, norm, route, balance, router_t)


def kern_grad_kernel(grad_ref, twice_ref, pair_ref, out_ref, turned, routed):
    images = twice_ref.shape[1]

    @pl.when(pl.program_id(0) == 0)
    def _():
        turned[...] = grad_ref[...].reshape(turned.shape[1], turned.shape[0]).T

    scale = pair_ref[0]
    for pixel in range(PIX):
        routed[pixel * images : (pixel + 1) * images] = twice_ref[pixel] * scale
    out_ref[...] = dot_nn(turned[...], routed[...]).astype(LOW)


def kern_grad(grad, twice, pair_scales, name):
    images, out_width, width = grad.shape[1], grad.shape[2], twice.shape[2]
    rows = PIX * images
    return device_kernel(
        kern_grad_kernel,
        name,
        PAIRS,
        [
            whole(PIX, images, out_width), whole(PIX, images, width),
            pl.BlockSpec((1, images, width), lambda i: (i, 0, 0)),
        ],
        [((out_width, PAIRS * width), LOW)],
        [pl.BlockSpec((out_width, width), lambda i: (0, i))],
        [pltpu.VMEM((out_width, rows), LOW), pltpu.VMEM((rows, width), LOW)],
        2 * rows * out_width * PAIRS * width,
        rows * out_width * 2,
    )(grad, twice, pair_scales)[0]


def project_grad_kernel(grad_ref, scaled_ref, scale_ref, out_ref, turned, routed):
    rows = turned.shape[1]

    @pl.when(pl.program_id(0) == 0)
    def _():
        turned[...] = grad_ref[...].reshape(rows, C_OUT).T

    for side in range(2):
        routed[side * C_OUT : (side + 1) * C_OUT] = turned[...] * scale_ref[0, side : side + 1]
    product = dot_nn(routed[...], scaled_ref[...].reshape(rows, C_MID)).astype(LOW)
    for side in range(2):
        out_ref[:, side * C_MID : (side + 1) * C_MID] = product[side * C_OUT : (side + 1) * C_OUT]


def project_grad(grad, scaled, scale):
    images = grad.shape[1]
    rows = PIX * images
    return device_kernel(
        project_grad_kernel,
        "project_grad",
        PAIRS,
        [
            whole(PIX, images, C_OUT), whole(PIX, images, C_MID),
            pl.BlockSpec((1, 2, rows), lambda i: (i, 0, 0)),
        ],
        [((C_OUT, EXPERTS * C_MID), LOW)],
        [pl.BlockSpec((C_OUT, 2 * C_MID), lambda i: (0, i))],
        [pltpu.VMEM((C_OUT, rows), LOW), pltpu.VMEM((2 * C_OUT, rows), LOW)],
        2 * rows * EXPERTS * C_OUT * C_MID,
        rows * (C_OUT + C_MID) * 2,
    )(grad, scaled, scale)[0]


def project_back_kernel(
    grad_ref, before_ref, coef_ref, pair_ref, each_ref, source,
    grad_before_ref, grad_scaled_ref, route_ref,
    routed, padded, weight_ref, sem,
):
    @pl.when(pl.program_id(0) == 0)
    def _():
        stack_experts(source, weight_ref, sem)
        padded[...] = jnp.zeros_like(padded)

    gain, by_value, constant = (coef_ref[k : k + 1] for k in range(3))
    scales = [pair_ref[pair] for pair in range(PAIRS)]

    def turn(pixel, carry):
        grad = grad_ref[pixel] * gain + before_ref[pixel] * by_value + constant
        grad = grad.astype(LOW)
        grad_before_ref[pixel] = grad
        padded[:, :C_OUT] = grad.astype(FULL)
        value = padded[...]
        value = value + pltpu.roll(value, C_OUT, 1)
        low = value.astype(LOW)
        found = []
        for pair in range(PAIRS):
            place = slice(2 * pair * C_OUT, 2 * (pair + 1) * C_OUT)
            routed[pixel, :, place] = low * scales[pair]
            found.append(carry[pair] + each_ref[pixel, :, place].astype(FULL) * value)
        return tuple(found)

    zero = jnp.zeros((GROUP, 2 * C_OUT), FULL)
    route_sums = lax.fori_loop(0, PIX, turn, (zero,) * PAIRS)
    route_ref[...] = pair_columns(route_sums, C_OUT)
    product = dot_nn(routed[...].reshape(ROWS, EXPERTS * C_OUT), weight_ref[...])
    grad_scaled_ref[...] = product.reshape(PIX, GROUP, C_MID).astype(LOW)


def project_back(grad_normed, before, coef, pair_out, each, project_low):
    images = before.shape[1]
    wide = EXPERTS * C_OUT
    return device_kernel(
        project_back_kernel,
        "project_back",
        images // GROUP,
        [
            images_block(C_OUT), images_block(C_OUT), whole(3, C_OUT), pair_block(2 * C_OUT),
            images_block(wide), pl.BlockSpec(memory_space=pl.ANY),
        ],
        [
            ((PIX, images, C_OUT), LOW), ((PIX, images, C_MID), LOW), ((images, EXPERTS), FULL),
        ],
        [images_block(C_OUT), images_block(C_MID), group_block(EXPERTS)],
        [
            pltpu.VMEM((PIX, GROUP, wide), LOW), pltpu.VMEM((GROUP, 2 * C_OUT), FULL),
            pltpu.VMEM((wide, C_MID), LOW), pltpu.SemaphoreType.DMA((EXPERTS,)),
        ],
        2 * PIX * images * wide * C_MID,
        PIX * images * (C_MID + wide) * 2,
    )(grad_normed, before, coef, pair_out, each, project_low)


def expand_back_kernel(
    grad_scaled_ref, turned_ref, hidden_ref, img_ref, gate_ref, squeeze_ref, excite_ref, depth_ref,
    route_ref, route_part_ref, balance_ref, weight_ref,
    grad_hidden_ref, logit_ref, grad_gate_ref, grad_squeeze_ref, grad_depth_ref,
    kern, start, grad_turned, grad_kern, pooled, product,
):
    @pl.when(pl.program_id(0) == 0)
    def _():
        grad_depth_ref[...] = jnp.zeros_like(grad_depth_ref)

    route = route_ref[...]
    low = route.astype(LOW).astype(FULL)
    columns = [low[:, expert : expert + 1] for expert in range(EXPERTS)]
    for tap in range(KSIZE * KSIZE):
        total = columns[0] * depth_ref[tap, 0:1, :]
        for expert in range(1, EXPERTS):
            total = total + columns[expert] * depth_ref[tap, expert : expert + 1, :]
        kern[tap] = total

    def gate_sum(pixel, carry):
        value = turned_ref[pixel].astype(FULL)
        return carry + grad_scaled_ref[pixel].astype(FULL) * (value * sig(value))

    gate = gate_ref[...]
    grad_gate = lax.fori_loop(0, PIX, gate_sum, jnp.zeros((GROUP, C_MID), FULL))
    grad_gate = grad_gate * gate * (1.0 - gate)
    grad_gate_ref[...] = grad_gate
    squeeze = squeeze_ref[...]
    part = sig(squeeze)
    grad_squeeze = dot_nt(grad_gate, excite_ref[1], HIGH) * (part + squeeze * part * (1.0 - part))
    grad_squeeze_ref[...] = grad_squeeze
    pooled[...] = dot_nn(grad_squeeze, excite_ref[0], HIGH) * (1.0 / PIX)

    def chunk(index, carry):
        lanes = pl.ds(pl.multiple_of(index * 128, 128), 128)
        gate_part = gate_ref[:, lanes]
        pooled_part = pooled[:, lanes]
        for pixel in range(PIX):
            value = turned_ref[pixel, :, lanes].astype(FULL)
            part = sig(value)
            grad = grad_scaled_ref[pixel, :, lanes].astype(FULL) * gate_part + pooled_part
            grad_turned[pixel] = grad * (part + value * part * (1.0 - part))
            value = hidden_ref[pixel, :, lanes].astype(FULL)
            start[pixel] = value * sig(value)
        taps = [kern[tap, :, lanes] for tap in range(KSIZE * KSIZE)]
        sums = [None] * (KSIZE * KSIZE)
        for pixel in range(PIX):
            total = None
            here = grad_turned[pixel]
            for tap, source in taps_of(pixel):
                term = start[source] * here
                sums[tap] = term if sums[tap] is None else sums[tap] + term
                term = grad_turned[source] * taps[KSIZE * KSIZE - 1 - tap]
                total = term if total is None else total + term
            value = hidden_ref[pixel, :, lanes].astype(FULL)
            part = sig(value)
            grad = total * (part + value * part * (1.0 - part))
            grad_hidden_ref[pixel, :, lanes] = grad.astype(LOW)
        for tap in range(KSIZE * KSIZE):
            grad_kern[tap, :, lanes] = sums[tap]
        return carry

    lax.fori_loop(0, C_MID // 128, chunk, 0)
    depth_term = jnp.zeros((GROUP, EXPERTS), FULL)
    for tap in range(KSIZE * KSIZE):
        value = grad_kern[tap]
        grad_depth_ref[tap] += dot_tn(low, value, HIGH)
        depth_term = depth_term + dot_nt(value, depth_ref[tap], HIGH)
    product[...] = dot_nn(grad_hidden_ref[...].reshape(ROWS, C_MID), weight_ref[...]).reshape(
        PIX, GROUP, EXPERTS * C_IN
    )

    def route_part(pixel, carry):
        value = img_ref[pixel].astype(FULL)
        return tuple(
            carry[pair] + product[pixel, :, 2 * pair * C_IN : 2 * (pair + 1) * C_IN] * value
            for pair in range(PAIRS)
        )

    zero = jnp.zeros((GROUP, 2 * C_IN), FULL)
    route_sums = lax.fori_loop(0, PIX, route_part, (zero,) * PAIRS)
    grad_route = (
        pair_columns(route_sums, C_IN) + route_part_ref[...] + depth_term + balance_ref[...]
    )
    logit_ref[...] = grad_route * route * (1.0 - route)


def expand_back(
    grad_scaled, turned, hidden, img_two, gate, squeeze, excite, depth_full, route, route_part,
    balance, expand_low,
):
    images = hidden.shape[1]
    taps = KSIZE * KSIZE
    return device_kernel(
        expand_back_kernel,
        "expand_back",
        images // GROUP,
        [
            images_block(C_MID), images_block(C_MID), images_block(C_MID), images_block(2 * C_IN),
            group_block(C_MID), group_block(C_SE), whole(2, C_SE, C_MID),
            whole(taps, EXPERTS, C_MID), group_block(EXPERTS), group_block(EXPERTS),
            whole(1, EXPERTS), whole(C_MID, EXPERTS * C_IN),
        ],
        [
            ((PIX, images, C_MID), LOW), ((images, EXPERTS), FULL), ((images, C_MID), FULL),
            ((images, C_SE), FULL), ((taps, EXPERTS, C_MID), FULL),
        ],
        [
            images_block(C_MID), group_block(EXPERTS), group_block(C_MID), group_block(C_SE),
            total_block(taps, EXPERTS, C_MID),
        ],
        [
            pltpu.VMEM((taps, GROUP, C_MID), FULL), pltpu.VMEM((PIX, GROUP, 128), FULL),
            pltpu.VMEM((PIX, GROUP, 128), FULL), pltpu.VMEM((taps, GROUP, C_MID), FULL),
            pltpu.VMEM((GROUP, C_MID), FULL), pltpu.VMEM((PIX, GROUP, EXPERTS * C_IN), FULL),
        ],
        2 * PIX * images * EXPERTS * C_IN * C_MID,
        PIX * images * 4 * C_MID * 2,
    )(
        grad_scaled, turned, hidden, img_two, gate, squeeze, excite, depth_full, route, route_part,
        balance, expand_low,
    )


def soap_kernel(
    gained, weight_ref, grad_ref, first_ref, second_ref, state_ref,
    first_out, second_out, state_out, weight_out, raised,
):
    step = pl.program_id(0)
    height, width = weight_ref.shape
    half = width // 2
    upper = -(-half // 128) * 128
    lower = half // 128 * 128
    corr_one = 1.0 - beta_one**STEP
    corr_two = 1.0 - beta_two**STEP

    def iota(shape, axis):
        return lax.broadcasted_iota(jnp.int32, shape, axis)

    pick = (iota((height, BLK), 0) % BLK == iota((height, BLK), 1)).astype(FULL)
    pick_t = (iota((BLK, height), 1) % BLK == iota((BLK, height), 0)).astype(FULL)
    same = iota((height, height), 0) // BLK == iota((height, height), 1) // BLK
    ones = same.astype(FULL)

    def spread_out(rows):
        return jnp.where(same, dot_nn(pick, rows, HIGH), 0.0)

    def by_half(product, value):
        first = product(0, value[:, :upper])
        second = product(1, value[:, lower:])
        if upper == lower:
            return jnp.concatenate([first, second], axis=1)
        lane = iota((height, upper - lower), 1)
        middle = jnp.where(lane < half - lower, first[:, lower:], second[:, : upper - lower])
        return jnp.concatenate([first[:, :lower], middle, second[:, upper - lower :]], axis=1)

    old = [state_ref[1, 2 * step + side] for side in range(2)]
    turns = [spread_out(rows) for rows in old]
    grad = grad_ref[...].astype(FULL)
    turned = by_half(lambda side, value: dot_nn(turns[side], value, HIGH), grad)
    first_new = beta_one * first_ref[...] + (1.0 - beta_one) * grad
    second_new = beta_two * second_ref[...] + (1.0 - beta_two) * (turned * turned)
    first_out[...] = first_new
    second_out[...] = second_new
    moment = by_half(lambda side, value: dot_nn(turns[side], value, HIGH), first_new)
    ratio = moment / corr_one / (jnp.sqrt(second_new / corr_two) + eps_adam)
    back = by_half(lambda side, value: dot_tn(turns[side], value, HIGH), ratio)
    weight = weight_ref[...]
    weight_out[...] = weight - rate_matrix * (back + decay * weight)

    for side in range(2):
        if side == 0:
            piece = grad[:, :upper]
            piece = jnp.where(iota(piece.shape, 1) < half, piece, 0.0)
        else:
            piece = grad[:, lower:]
            piece = jnp.where(iota(piece.shape, 1) >= half - lower, piece, 0.0)
        gram = jnp.where(same, dot_nt(piece, piece, HIGH), 0.0)
        summed = beta_two * state_ref[0, 2 * step + side]
        summed = summed + (1.0 - beta_two) * gained * dot_nn(pick_t, gram, HIGH)
        diagonal = jnp.sum(summed * pick_t, axis=0, keepdims=True)
        trace = dot_nn(diagonal, ones, HIGH)
        stats = summed / trace
        state_out[0, 2 * step + side] = stats
        lifted = dot_nn(old[side], spread_out(stats), HIGH)
        for column in range(BLK):
            raised[column, pl.ds(2 * step + side, 1), :] = lifted[column : column + 1]

    @pl.when(step == pl.num_programs(0) - 1)
    def _():
        columns = []
        for index in range(BLK):
            column = raised[index]
            for previous in columns:
                column = column - dot_nn(previous * column, ones, HIGH) * previous
            column = column * lax.rsqrt(dot_nn(column * column, ones, HIGH))
            columns.append(column)
            for expert in range(EXPERTS):
                state_out[1, expert, index : index + 1, :] = column[expert : expert + 1]


def soap(weight, grad, first, second, state, every):
    height, total = weight.shape
    width = total // PAIRS
    turned_state = state.transpose(0, 1, 3, 2)
    gained = stat_gain * every / (total // EXPERTS)
    column = pl.BlockSpec((height, width), lambda i: (0, i))
    sheet = jax.ShapeDtypeStruct(weight.shape, FULL)
    first_new, second_new, state_new, weight_new = device_kernel(
        functools.partial(soap_kernel, gained),
        "soap",
        PAIRS,
        [column, column, column, column, whole(2, EXPERTS, BLK, height)],
        [(weight.shape, FULL), (weight.shape, FULL), (turned_state.shape, FULL),
         (weight.shape, FULL)],
        [column, column, total_block(2, EXPERTS, BLK, height), column],
        [pltpu.VMEM((BLK, EXPERTS, height), FULL)],
        2 * height * height * total,
        weight.size * 26,
    )(weight, grad, first, second, turned_state)
    return (first_new, second_new, state_new.transpose(0, 1, 3, 2), weight_new)


def adam(weight, grad, first, second, rate):
    corr_one = 1.0 - beta_one**STEP
    corr_two = 1.0 - beta_two**STEP
    first_new = beta_one * first + (1.0 - beta_one) * grad
    second_new = beta_two * second + (1.0 - beta_two) * grad * grad
    weight_new = weight - rate * (
        first_new / corr_one / (jnp.sqrt(second_new / corr_two) + eps_adam) + decay * weight
    )
    return (first_new, second_new, weight_new)


def local(
    images,
    dom_label,
    class_label,
    expand_weight,
    expand_first,
    expand_second,
    expand_state,
    project_weight,
    project_first,
    project_second,
    project_state,
    head_weight,
    head_first,
    head_second,
    head_state,
    depth_weight,
    depth_first,
    depth_second,
    classifier_weight,
    classifier_first,
    classifier_second,
    excite_weight,
    excite_first,
    excite_second,
    router_weight,
    router_first,
    router_second,
    gains_weight,
    gains_first,
    gains_second,
):
    low_type = jnp.bfloat16
    images_here = images.shape[0]
    every = images.shape[0] * lax.axis_size("dp") * lax.axis_size("wide")
    count = every * PIX
    bias_se, bias_ex, gain_one, shift_one, gain_two, shift_two, bias_cls = split_gains(gains_weight)
    hot = boost * (dom_label[:, None] == jnp.arange(EXPERTS)[None, :]).astype(jnp.float32)
    img = images.transpose(1, 0, 2)
    img_two = jnp.concatenate([img, img], axis=2)
    expand_low = lax.all_gather(expand_weight.astype(low_type), "wide", axis=0, tiled=True)
    project_low = lax.all_gather(project_weight.astype(low_type), "wide", axis=0, tiled=True)
    head_low = lax.all_gather(head_weight.astype(low_type), "wide", axis=0, tiled=True)
    class_low = lax.all_gather(classifier_weight.astype(low_type), "wide", axis=0, tiled=True)
    depth_own = depth_weight.astype(low_type).transpose(2, 0, 1).reshape(depth_weight.shape[2], -1)
    depth_low = lax.all_gather(depth_own, "wide", axis=0, tiled=True)
    depth_full = depth_low.reshape(C_MID, EXPERTS, KSIZE * KSIZE).transpose(2, 1, 0).astype(FULL)
    excite = excite_weight.transpose(0, 2, 1)
    router = router_weight.T
    router_one, router_two = router[:, :C_IN], router[:, C_IN:]

    (
        hidden, turned, scaled, route_one, pair_in, pair_one, gate, squeeze, pooled_one,
        pooled_act, route_one_sum,
    ) = expand_forward(
        img_two, hot, router_one, expand_low, depth_full, excite, bias_se[None], bias_ex[None]
    )
    each, before, sums_one = project_forward(scaled, project_low, pair_one)
    sums_one, route_one_sum = sum_all((sums_one, route_one_sum), 1)
    center_one = sums_one[0] / count
    inv_one = lax.rsqrt(sums_one[1] / count - center_one * center_one + eps_norm)
    scale_one = inv_one * gain_one
    norm_one = jnp.stack([scale_one, shift_one - center_one * scale_one])
    widened, twice, route_two, pair_two, pooled_two, sums_two, route_two_sum = head_forward(
        before, norm_one, hot, router_two, head_low
    )
    sums_two, route_two_sum = sum_all((sums_two, route_two_sum), 2)
    center_two = sums_two[0] / count
    inv_two = lax.rsqrt(sums_two[1] / count - center_two * center_two + eps_norm)
    scale_two = inv_two * gain_two
    norm_two = jnp.stack(
        [scale_two, shift_two - center_two * scale_two, inv_two, -center_two * inv_two]
        + [jnp.full_like(inv_two, 1.0 / every)] * 4
    )
    feats, grad_logits, grad_feats, back_two, cross_part, grad_bias_cls = loss_part(
        widened, norm_two, class_label[:, None], class_low, bias_cls[None]
    )
    grad_class = dot_tn(feats, grad_logits)
    back_two, cross_total, grad_bias_cls = sum_all((back_two, cross_part, grad_bias_cls), 3)
    means_one = route_one_sum[0] / every
    means_two = route_two_sum[0] / every
    by_value = -scale_two * inv_two * back_two[1] / count
    coef_two = jnp.stack(
        [
            scale_two, shift_two - center_two * scale_two, by_value,
            -scale_two * back_two[0] / count - center_two * by_value,
        ]
    )
    hat_one = jnp.stack([inv_one, -center_one * inv_one])
    grad_widened, grad_normed, grad_logit_two, back_one = head_back(
        widened, grad_feats, coef_two, head_low, pair_two, twice, before, hat_one, route_two,
        balance_grad(means_two, every)[None], router_two,
    )
    grad_head = kern_grad(grad_widened, twice, pair_two, "head_grad")
    grad_head, grad_class, back_one = lax.optimization_barrier((grad_head, grad_class, back_one))
    grad_router_two = dot_tn(pooled_two, grad_logit_two, HIGH)
    (back_one,) = sum_all((back_one,), 4)
    by_value = -scale_one * inv_one * back_one[1] / count
    coef_one = jnp.stack(
        [scale_one, by_value, -scale_one * back_one[0] / count - center_one * by_value]
    )
    grad_before, grad_scaled, route_project = project_back(
        grad_normed, before, coef_one, pair_one, each, project_low
    )
    row_scale = jnp.tile(route_one.astype(low_type).T, (1, PIX)).reshape(PAIRS, 2, -1)
    grad_project = project_grad(grad_before, scaled, row_scale)
    grad_project, grad_scaled = lax.optimization_barrier((grad_project, grad_scaled))
    grad_hidden, grad_logit_one, grad_gate, grad_squeeze, grad_depth = expand_back(
        grad_scaled, turned, hidden, img_two, gate, squeeze, excite, depth_full, route_one,
        route_project, balance_grad(means_one, every)[None], expand_low,
    )
    grad_expand = kern_grad(grad_hidden, img_two, pair_in, "expand_grad")
    grad_excite = jnp.stack(
        [
            dot_tn(pooled_act, grad_squeeze, HIGH),
            dot_tn(grad_gate, squeeze * jax.nn.sigmoid(squeeze), HIGH),
        ]
    )
    grad_router_one = dot_tn(pooled_one, grad_logit_one, HIGH)
    grad_depth = grad_depth.transpose(1, 0, 2)
    grad_bias_se = jnp.sum(grad_squeeze, axis=0)
    grad_bias_ex = jnp.sum(grad_gate, axis=0)
    small = lax.psum(
        (
            grad_excite,
            jnp.concatenate([grad_router_one, grad_router_two], axis=0),
            jnp.concatenate([grad_bias_se, grad_bias_ex]),
        ),
        ("dp", "wide"),
    )
    depth_flat = grad_depth.transpose(2, 0, 1).astype(low_type).reshape(C_MID, -1)
    full = (grad_expand, depth_flat, grad_project, grad_head, grad_class.astype(low_type))
    shares = [
        lax.psum_scatter(grad, "wide", scatter_dimension=0, tiled=True) for grad in full
    ]
    reduced = [lax.psum(share, "dp") for share in shares]
    depth_reduced = reduced[1].reshape(-1, EXPERTS, KSIZE * KSIZE).transpose(1, 2, 0)
    loss = cross_total[0, 0] / every + balance_weight * (
        jnp.mean((means_one - jnp.mean(means_one)) ** 2)
        + jnp.mean((means_two - jnp.mean(means_two)) ** 2)
    )
    grad_gains = jnp.concatenate(
        [small[2], back_one[1], back_one[0], back_two[1], back_two[0], grad_bias_cls[0]]
    )
    expand_out = soap(expand_weight, reduced[0], expand_first, expand_second, expand_state, every)
    project_out = soap(
        project_weight, reduced[2], project_first, project_second, project_state, every
    )
    head_out = soap(head_weight, reduced[3], head_first, head_second, head_state, every)
    depth_out = adam(
        depth_weight, depth_reduced.astype(FULL), depth_first, depth_second, rate_matrix
    )
    class_out = adam(
        classifier_weight, reduced[4].astype(FULL), classifier_first, classifier_second, rate_matrix
    )
    excite_out = adam(excite_weight, small[0], excite_first, excite_second, rate_matrix)
    router_out = adam(router_weight, small[1], router_first, router_second, rate_matrix)
    gains_out = adam(gains_weight, grad_gains, gains_first, gains_second, rate_gains)
    return (
        loss,
        expand_out[0],
        expand_out[1],
        expand_out[2],
        expand_out[3],
        project_out[0],
        project_out[1],
        project_out[2],
        project_out[3],
        head_out[0],
        head_out[1],
        head_out[2],
        head_out[3],
        depth_out[0],
        depth_out[1],
        depth_out[2],
        class_out[0],
        class_out[1],
        class_out[2],
        excite_out[0],
        excite_out[1],
        excite_out[2],
        router_out[0],
        router_out[1],
        router_out[2],
        gains_out[0],
        gains_out[1],
        gains_out[2],
    )


def solution(mesh):
    return jax.shard_map(
        local,
        mesh=mesh,
        in_specs=(
            P(("dp", "wide"), None, None),
            P(("dp", "wide")),
            P(("dp", "wide")),
            P("wide", None),
            P("wide", None),
            P("wide", None),
            P(None, None, "wide", None),
            P("wide", None),
            P("wide", None),
            P("wide", None),
            P(None, None, "wide", None),
            P("wide", None),
            P("wide", None),
            P("wide", None),
            P(None, None, "wide", None),
            P(None, None, "wide"),
            P(None, None, "wide"),
            P(None, None, "wide"),
            P("wide", None),
            P("wide", None),
            P("wide", None),
            P(),
            P(),
            P(),
            P(),
            P(),
            P(),
            P(),
            P(),
            P(),
        ),
        out_specs=(
            P(),
            P("wide", None),
            P("wide", None),
            P(None, None, "wide", None),
            P("wide", None),
            P("wide", None),
            P("wide", None),
            P(None, None, "wide", None),
            P("wide", None),
            P("wide", None),
            P("wide", None),
            P(None, None, "wide", None),
            P("wide", None),
            P(None, None, "wide"),
            P(None, None, "wide"),
            P(None, None, "wide"),
            P("wide", None),
            P("wide", None),
            P("wide", None),
            P(),
            P(),
            P(),
            P(),
            P(),
            P(),
            P(),
            P(),
            P(),
        ),
        check_vma=False,
    )
```

time: 1410 us -> 1070 us (0.76)
  Pallas kernels: 44.5 us -> 516 us
  local copies, waits for them, and re-layouts: 422 us -> 20.3 us
  other arithmetic: 365 us -> 30.5 us
  matrix products: 320 us -> 3.68 us
  waiting for transfers between devices: 153 us -> 398 us
    pallas_call x0 -> x13, Pallas kernels: none -> 473 us  [the longest x1 71 us: expand_back(): device_kernel(expand_back_kernel, 'expand_back', images // GROUP, [images...]
    dot_general x41 -> x5, matrix products: 320 us -> 3.68 us  [dot_tn(): lax.dot_general(left, right, (((0,), (0,)), ((), ())), precision=precisio...]
    mul x35 -> x0, local copies, waits for them, and re-layouts: 252 us -> none  [the longest x12 184 us: scaled_by(): cube = act[:, :, None, :] * route[None, :, :, None]]
    reduce_sum x42 -> x1, other arithmetic: 235 us -> 0.03 us  [local(): grad_bias_se = jnp.sum(grad_squeeze, axis=0)]
    reduce_scatter x4, waiting for transfers between devices: 0.02 us -> 178 us  [local(): lax.psum_scatter(grad, 'wide', scatter_dimension=0, tiled=True)]
    convert_element_type x6 -> x2, other arithmetic: 49.3 us -> 0.71 us  [the longest x1 0.69 us: local(): (dom_label[:, None] == jnp.arange(EXPERTS)[None, :]).astype(jnp.float32)]
    convert_element_type x6 -> x5, local copies, waits for them, and re-layouts: 42.8 us -> 0.97 us  [the longest x2 0.89 us: local(): depth_low.reshape(C_MID, EXPERTS, KSIZE * KSIZE).transpose(2, 1, 0)]
    dot_general x3 -> x0, local copies, waits for them, and re-layouts: 37.4 us -> none  [the longest x1 21.9 us: rows_tn(): lax.dot_general(left, right, (((0,), (0,)), ((), ())), preferred_element_...]
  transfers between devices with their start and end apart: 11 -> 11, of which waited for: 3 -> 9; matrix products, arithmetic and copies ran while one was open for 49% -> 3% of each run, Pallas kernels for 2% -> 30%
where the time goes in v2:
time: 1070 us; the launch traced here: 1060 us
  Pallas kernels  516 us (48%)
  waiting for transfers between devices  398 us (37%)
  blocking collectives  72.1 us (7%)
  other arithmetic  30.5 us (3%)
  local copies, waits for them, and re-layouts  20.3 us (2%)
  between operations  19.3 us (2%)
    reduce_scatter x4, waiting for transfers between devices, local(): lax.psum_scatter(grad, 'wide', scatter_dimension=0, tiled=True)  178 us
    psum x1, waiting for transfers between devices, local(): lax.psum((grad_excite, jnp.concatenate([grad_router_one, grad_router_two]...  82.2 us
    pallas_call x1, Pallas kernels, expand_back(): device_kernel(expand_back_kernel, 'expand_back', images // GROUP, [images...  71 us
    pallas_call x1, Pallas kernels, head_back(): device_kernel(head_back_kernel, 'head_back', images // GROUP, [images_blo...  62.9 us
    pallas_call x2, Pallas kernels, kern_grad(): device_kernel(kern_grad_kernel, name, PAIRS, [whole(PIX, images, out_widt...  59.3 us
    pallas_call x3, Pallas kernels, soap(): device_kernel(functools.partial(soap_kernel, gained), 'soap', PAIRS, [col...  58.5 us
    psum x1, waiting for transfers between devices, local(): reduced = [lax.psum(share, 'dp') for share in shares]  57.4 us
    pallas_call x1, Pallas kernels, project_back(): device_kernel(project_back_kernel, 'project_back', images // GROUP, [imag...  54.8 us
  transfers between devices with their start and end apart: 11, of which 9 were waited for; matrix products, arithmetic and copies ran while one was open for 3% of the time, Pallas kernels for 30%

profile of v2, /device:TPU:0, one launch (start us, length us, event | category | flops | bytes accessed | tf_op | source)
XLA Modules:
  0.0 1060.6 jit_solution(2143326260227542777)
XLA Ops:
  15.0 2.4 pad_maximum_fusion.img_ref.twice_ref
  18.3 16.8 %all_gather.16 = bf16[1152,72]{1,0:T(8,128)(2,1)S(1)} all-gather(bf16[144,72]{1,0:T(8,128)(2,1)S(1)} %copy.108), channel_id=1, replica_groups=mesh['dp'=4,'wide'=8] {'wide'}, dimensions={0}, use_global_device_ids=true | all-gather | bytes 186624 | tf_op jit(solution)/shard_map/all_gather | solution.py:1031
  37.4 19.8 %all-gather.5.cloned.1.call-done.expand_ref.weight_ref = bf16[1152,1536]{1,0:T(8,128)(2,1)} async-done(((bf16[144,1536]{1,0:T(8,128)(2,1)}), bf16[1152,1536]{1,0:T(8,128)(2,1)}) %all-gather.5.cloned.1.call-update) | async-done | bytes 3538960 | tf_op jit(solution)/shard_map/all_gather | solution.py:1026
  57.2 41.6 %expand_forward.1 = (bf16[49,64,1152]{2,1,0:T(8,128)(2,1)}, bf16[49,64,1152]{2,1,0:T(8,128)(2,1)}, bf16[49,64,1152]{2,1,0:T(8,128)(2,1)}, f32[64,8]{1,0:T(8,128)...) custom-call(bf16[49,64,384]{2,1,0:T(8,128)(2,1)} %pad_maximum_fusion, ...), custom_call_target="tpu_custom_call" | custom-call | flops 11098128384 | bytes 28901376 | tf_op jit(solution)/shard_map/expand_forward/pallas_call | solution.py:301
  100.5 19.4 %all-gather.7.cloned.1.call-done.source = bf16[320,9216]{1,0:T(8,128)(2,1)} async-done(((bf16[40,9216]{1,0:T(8,128)(2,1)}), bf16[320,9216]{1,0:T(8,128)(2,1)}) %all-gather.7.cloned.1.call-update) | async-done | bytes 5898256 | tf_op jit(solution)/shard_map/all_gather | solution.py:1027
  119.9 46.7 %project_forward.1 = (bf16[49,64,2560]{2,1,0:T(8,128)(2,1)}, f32[49,64,320]{2,1,0:T(8,128)}, f32[2,320]{1,0:T(2,128)}) custom-call(bf16[49,64,1152]{2,1,0:T(8,128)(2,1)} %get-tuple-element.84.scaled_ref, bf16[320,9216]{1,0:T(8,128)(2,1)} %all-gather.7.cloned.1.call-done.source, bf16[4,64,640]{2,1,0:T(8,128)(2,1)} %get-tuple-element.85.pair_ref), custom_call_target="tpu_custom_call" | custom-call | flops 18496880640 | bytes 23281664 | tf_op jit(solution)/shard_map/project_forward/pallas_call | solution.py:383
  168.0 11.0 %shard_map.501 = f32[8,128]{1,0:T(8,128)} custom-call(f32[8,128]{1,0:T(8,128)} %fusion.20.x_ref), custom_call_target="tpu_custom_call" | custom-call | tf_op jit(solution)/shard_map/pallas_call | solution.py:97
  181.0 7.4 all-gather.9.cloned.1.call-done.weight_ref
  188.5 29.8 %head_forward.1 = (bf16[49,64,1280]{2,1,0:T(8,128)(2,1)}, bf16[49,64,640]{2,1,0:T(8,128)(2,1)}, f32[64,8]{1,0:T(8,128)}, bf16[4,64,640]{2,1,0:T(8,128)(2,1)}, f3...) custom-call(f32[49,64,320]{2,1,0:T(8,128)} %get-tuple-element.86.before_ref, ...), custom_call_target="tpu_custom_call" | custom-call | flops 20552089600 | bytes 10035200 | tf_op jit(solution)/shard_map/head_forward/pallas_call | solution.py:439
  220.2 11.2 %shard_map.502 = f32[24,128]{1,0:T(8,128)} custom-call(f32[24,128]{1,0:T(8,128)} %fusion.14.x_ref), custom_call_target="tpu_custom_call" | custom-call | tf_op jit(solution)/shard_map/pallas_call | solution.py:97
  233.8 19.8 %loss_part.1 = (bf16[64,1280]{1,0:T(8,128)(2,1)}, bf16[64,1000]{1,0:T(8,128)(2,1)}, f32[64,1280]{1,0:T(8,128)}, f32[2,1280]{1,0:T(2,128)}, f32[1,1]{1,0:T(1,128)}, /*index=5*/f32[1,1000]{1,0:T(1,128)}) custom-call(bf16[49,64,1280]{2,1,0:T(8,128)(2,1)} %get-tuple-element.89.widened_ref, f32[8,1280]{1,0:T(8,128)} %stack.64.norm_ref, s32[64,1]{1,0:T(8,128)} %copy.111.label_ref, ...), custom_call_target="tpu_custom_call" | custom-call | flops 327680000 | bytes 8028160 | tf_op jit(solution)/shard_map/loss_part/pallas_call | solution.py:513
  256.4 10.5 shard_map.503
  272.1 62.9 %head_back.1 = (bf16[49,64,1280]{2,1,0:T(8,128)(2,1)}, f32[49,64,320]{2,1,0:T(8,128)}, f32[64,8]{1,0:T(8,128)}, f32[2,320]{1,0:T(2,128)}) custom-call(bf16[49,64,1280]{2,1,0:T(8,128)(2,1)} %get-tuple-element.89.widened_ref, f32[64,1280]{1,0:T(8,128)} %get-tuple-element.95.grad_feats_ref, f32[4,1280]{1,0:T(4,128)} %pad_maximum_fusion.2.coef_ref, ...), custom_call_target="tpu_custom_call" | custom-call | flops 20552089600 | bytes 18063360 | tf_op jit(solution)/shard_map/head_back/pallas_call | solution.py:606
  335.0 35.9 %head_grad.1 = bf16[1280,2560]{1,0:T(8,128)(2,1)} custom-call(bf16[49,64,1280]{2,1,0:T(8,128)(2,1)} %get-tuple-element.100.grad_ref, bf16[49,64,640]{2,1,0:T(8,128)(2,1)} %get-tuple-element.97.twice_ref, bf16[4,64,640]{2,1,0:T(8,128)(2,1)} %get-tuple-element.96.pair_ref), custom_call_target="tpu_custom_call" | custom-call | flops 20552089600 | bytes 8028160 | tf_op jit(solution)/shard_map/head_grad/pallas_call | solution.py:644
  372.4 10.7 %shard_map.504 = f32[8,128]{1,0:T(8,128)} custom-call(f32[8,128]{1,0:T(8,128)} %pad_bitcast_fusion.1.x_ref), custom_call_target="tpu_custom_call" | custom-call | tf_op jit(solution)/shard_map/pallas_call | solution.py:97
  383.9 3.7 copy.118
  388.3 54.8 %project_back.1 = (bf16[49,64,320]{2,1,0:T(8,128)(2,1)}, bf16[49,64,1152]{2,1,0:T(8,128)(2,1)}, f32[64,8]{1,0:T(8,128)}) custom-call(f32[49,64,320]{2,1,0:T(8,128)} %get-tuple-element.99.grad_ref, f32[49,64,320]{2,1,0:T(8,128)} %get-tuple-element.86.before_ref, f32[3,320]{1,0:T(4,128)} %pad_maximum_fusion.5.coef_ref, ...), custom_call_target="tpu_custom_call" | custom-call | flops 18496880640 | bytes 23281664 | tf_op jit(solution)/shard_map/project_back/pallas_call | solution.py:731
  443.2 28.3 %project_grad.1 = bf16[320,9216]{1,0:T(8,128)(2,1)} custom-call(bf16[49,64,320]{2,1,0:T(8,128)(2,1)} %get-tuple-element.106.grad_ref, bf16[49,64,1152]{2,1,0:T(8,128)(2,1)} %get-tuple-element.84.scaled_ref, bf16[4,2,3136]{2,1,0:T(2,128)(2,1)} %tile.9.scale_ref), custom_call_target="tpu_custom_call" | custom-call | flops 18496880640 | bytes 9232384 | tf_op jit(solution)/shard_map/project_grad/pallas_call | solution.py:677
  473.3 71.0 %expand_back.1 = (bf16[49,64,1152]{2,1,0:T(8,128)(2,1)}, f32[64,8]{1,0:T(8,128)}, f32[64,1152]{1,0:T(8,128)}, f32[64,48]{1,0:T(8,128)}, f32[9,8,1152]{2,1,0:T(8,128)}) custom-call(bf16[49,64,1152]{2,1,0:T(8,128)(2,1)} %get-tuple-element.109.grad_scaled_ref, bf16[49,64,1152]{2,1,0:T(8,128)(2,1)} %get-tuple-element.110.turned_ref, ...), custom_call_target="tpu_custom_call" | custom-call | flops 11098128384 | bytes 28901376 | tf_op jit(solution)/shard_map/expand_back/pallas_call | solution.py:845
  544.3 23.4 %expand_grad.1 = bf16[1152,1536]{1,0:T(8,128)(2,1)} custom-call(bf16[49,64,1152]{2,1,0:T(8,128)(2,1)} %get-tuple-element.115.grad_ref, bf16[49,64,384]{2,1,0:T(8,128)(2,1)} %pad_maximum_fusion.img_ref.twice_ref, bf16[4,64,384]{2,1,0:T(8,128)(2,1)} %get-tuple-element.116.pair_ref), custom_call_target="tpu_custom_call" | custom-call | flops 11098128384 | bytes 7225344 | tf_op jit(solution)/shard_map/expand_grad/pallas_call | solution.py:644
  572.6 38.1 %reduce-scatter.10.cloned.1.call-done = bf16[144,1536]{1,0:T(8,128)(2,1)} async-done(((bf16[1152,1536]{1,0:T(8,128)(2,1)}), bf16[144,1536]{1,0:T(8,128)(2,1)}) %reduce-scatter.10.cloned.1.call-update) | async-done | bytes 442384 | tf_op jit(solution)/shard_map/reduce_scatter | solution.py:1119
  610.7 67.1 %reduce-scatter.12.cloned.1.call-done = bf16[40,9216]{1,0:T(8,128)(2,1)} async-done(((bf16[320,9216]{1,0:T(8,128)(2,1)}), bf16[40,9216]{1,0:T(8,128)(2,1)}) %reduce-scatter.12.cloned.1.call-update) | async-done | bytes 737296 | tf_op jit(solution)/shard_map/reduce_scatter | solution.py:1119
  677.7 73.0 %reduce-scatter.14.cloned.1.call-done = bf16[160,2560]{1,0:T(8,128)(2,1)} async-done(((bf16[1280,2560]{1,0:T(8,128)(2,1)}), bf16[160,2560]{1,0:T(8,128)(2,1)}) %reduce-scatter.14.cloned.1.call-update) | async-done | bytes 819216 | tf_op jit(solution)/shard_map/reduce_scatter | solution.py:1119
  756.9 38.1 %all-reduce.4 = (f32[512,8]{0,1:T(8,128)S(1)}, f32[1200]{0:T(1024)S(1)}) all-reduce(f32[512,8]{0,1:T(8,128)S(1)} %pad_maximum_fusion.3, f32[1200]{0:T(1024)S(1)} %pad_maximum_fusion.4), channel_id=1, replica_groups=mesh['dp'=4,'wide'=8] {'dp','wide'}, use_global_device_ids=true, to_apply=%region_15.16 | all-reduce | flops 5296 | bytes 42368 | tf_op jit(solution)/shard_map/psum | solution.py:1108
  798.6 82.2 %all-reduce.9.cloned.1.call-done = f32[2,1152,48]{1,2,0:T(8,128)} async-done(((f32[2,1152,48]{1,2,0:T(8,128)}), f32[2,1152,48]{1,2,0:T(8,128)}) %all-reduce.9.cloned.1.call-update) | async-done | bytes 442384 | tf_op jit(solution)/shard_map/psum | solution.py:1108
  883.2 31.9 %reduce-scatter.16.cloned.1.call-done = bf16[144,72]{1,0:T(8,128)(2,1)} async-done(((bf16[1152,72]{1,0:T(8,128)(2,1)}), bf16[144,72]{1,0:T(8,128)(2,1)}) %reduce-scatter.16.cloned.1.call-update) | async-done | bytes 20752
  916.0 17.2 %psum.59 = bf16[8,9,144]{2,0,1:T(8,128)(2,1)S(1)} all-reduce(bf16[8,9,144]{2,0,1:T(8,128)(2,1)S(1)} %bitcast.127), channel_id=1, replica_groups=mesh['dp'=4,'wide'=8] {'dp'}, use_global_device_ids=true, to_apply=%region_11.12 | all-reduce | flops 10368 | bytes 41472 | tf_op jit(solution)/shard_map/psum | solution.py:1121
  934.0 57.4 %all-reduce.11.cloned.1.call-done = (bf16[144,1536]{1,0:T(8,128)(2,1)}, bf16[40,9216]{1,0:T(8,128)(2,1)}, bf16[160,2560]{1,0:T(8,128)(2,1)}, bf16[160,1000]{1,0:T(8,128)(2,1)}) async-done(((bf16[144,1536]{1,0:T(8,128)(2,1)}, bf16[40,9216]{1,0:T(8,128)(2,1)}, bf16[160,2560]{1,0:T(8,128)(2,1)}, bf16[160,1000]{1,0:T(8,128)(2,1)}), (bf16[144,1536]{1,0:T(8,128)(2,1)}, bf16[40,9216]{1,0:T(8,128)(2,1)}, ...) | async-done | bytes 2318864 | tf_op jit(solution)/shard_map/psum | solution.py:1121
  991.4 2.6 multiply_subtract_fusion
  994.0 19.2 %soap.3 = (f32[144,1536]{1,0:T(8,128)}, f32[144,1536]{1,0:T(8,128)}, f32[2,8,4,144]{3,2,1,0:T(4,128)}, f32[144,1536]{1,0:T(8,128)}) custom-call(f32[144,1536]{1,0:T(8,128)} %weight_ref.3, bf16[144,1536]{1,0:T(8,128)(2,1)} %get-tuple-element.230.grad_ref, f32[144,1536]{1,0:T(8,128)} %first_ref.3, f32[144,1536]{1,0:T(8,128)} %second_ref.3, ...), custom_call_target="tpu_custom_call" | custom-call | flops 63700992 | bytes 5750784 | tf_op jit(solution)/shard_map/soap/pallas_call | solution.py:960
  1013.2 16.6 %soap.4 = (f32[40,9216]{1,0:T(8,128)}, f32[40,9216]{1,0:T(8,128)}, f32[2,8,4,40]{3,2,1,0:T(4,128)}, f32[40,9216]{1,0:T(8,128)}) custom-call(f32[40,9216]{1,0:T(8,128)} %weight_ref.4, bf16[40,9216]{1,0:T(8,128)(2,1)} %get-tuple-element.231.grad_ref, f32[40,9216]{1,0:T(8,128)} %first_ref.4, f32[40,9216]{1,0:T(8,128)} %second_ref.4, f32[2,8,4,40]{3,2,1,0:T(4,128)} %bitcast.132), custom_call_target="tpu_custom_call" | custom-call | flops 29491200 | bytes 9584640 | tf_op jit(solution)/shard_map/soap/pallas_call | solution.py:960
  1029.8 22.8 %soap.5 = (f32[160,2560]{1,0:T(8,128)}, f32[160,2560]{1,0:T(8,128)}, f32[2,8,4,160]{3,2,1,0:T(4,128)}, f32[160,2560]{1,0:T(8,128)}) custom-call(f32[160,2560]{1,0:T(8,128)} %weight_ref.5, bf16[160,2560]{1,0:T(8,128)(2,1)} %get-tuple-element.232.grad_ref, f32[160,2560]{1,0:T(8,128)} %first_ref.5, f32[160,2560]{1,0:T(8,128)} %second_ref.5, ...), custom_call_target="tpu_custom_call" | custom-call | flops 131072000 | bytes 10649600 | tf_op jit(solution)/shard_map/soap/pallas_call | solution.py:960
  (172 shorter events, 48.0 us)
Async XLA Ops:
  7.2 50.0 %all-gather.5.cloned.1.call-start = ((), (), s32[]{:S(2)}) async-start(), calls=%async_computation.5 | async-start | bytes 3981312 | tf_op jit(solution)/shard_map/all_gather | solution.py:1026
  9.4 110.5 %all-gather.7.cloned.1.call-start = ((), (), s32[]{:S(2)}) async-start(), calls=%async_computation.6 | async-start | bytes 6635520 | tf_op jit(solution)/shard_map/all_gather | solution.py:1027
  10.5 178.0 %all-gather.9.cloned.1.call-start = ((), (), s32[]{:S(2)}) async-start(), calls=%async_computation.7 | async-start | bytes 7372800 | tf_op jit(solution)/shard_map/all_gather | solution.py:1028
  11.5 3.5 copy-start.4
  11.5 5.9 copy-start.29
  11.5 6.6 copy-start.13
  11.5 222.3 %all-gather.11.cloned.1.call-start = ((), (), s32[]{:S(2)}) async-start(), calls=%async_computation.8 | async-start | bytes 2949120 | tf_op jit(solution)/shard_map/all_gather | solution.py:1029
  12.4 560.2 %reduce-scatter.18.cloned.1.call-start = ((), (), s32[]{:S(2)}) async-start(), calls=%async_computation.14 | async-start | bytes 2949120 | tf_op jit(solution)/shard_map/reduce_scatter | solution.py:1119
  15.0 21.7 %copy-start.30 = (s32[64]{0:T(128)S(1)}, s32[64]{0:T(128)}, u32[]{:S(2)}) copy-start(s32[64]{0:T(128)} %param.32) | copy-start | bytes 772
  119.9 47.5 %copy-start.31 = (f32[1,8]{1,0:T(1,128)S(1)}, f32[1,8]{1,0:T(1,128)}, u32[]{:S(2)}) copy-start(f32[1,8]{1,0:T(1,128)} %get-tuple-element.88) | copy-start | bytes 100
  233.8 33.1 %copy-start.11 = (f32[24,128]{1,0:T(8,128)S(1)}, f32[24,128]{1,0:T(8,128)}, u32[]{:S(2)}) copy-start(f32[24,128]{1,0:T(8,128)} %shard_map.502) | copy-start | bytes 36868
  334.9 35.9 %copy-start.16 = (bf16[64,1280]{1,0:T(8,128)(2,1)S(1)}, bf16[64,1280]{1,0:T(8,128)(2,1)}, u32[]{:S(2)}) copy-start(bf16[64,1280]{1,0:T(8,128)(2,1)} %get-tuple-element.101) | copy-start | bytes 491524
  335.0 35.9 %copy-start.18 = (bf16[64,1000]{1,0:T(8,128)(2,1)S(1)}, bf16[64,1000]{1,0:T(8,128)(2,1)}, u32[]{:S(2)}) copy-start(bf16[64,1000]{1,0:T(8,128)(2,1)} %get-tuple-element.102) | copy-start | bytes 384004
  383.9 3.8 copy-start.26
  383.9 3.8 copy-start.27
  387.7 223.0 %reduce-scatter.10.cloned.1.call-start = ((), (), s32[]{:S(2)}) async-start(), calls=%async_computation.9 | async-start | bytes 3981312 | tf_op jit(solution)/shard_map/reduce_scatter | solution.py:1119
  567.7 110.0 %reduce-scatter.12.cloned.1.call-start = ((), (), s32[]{:S(2)}) async-start(), calls=%async_computation.10 | async-start | bytes 6635520 | tf_op jit(solution)/shard_map/reduce_scatter | solution.py:1119
  568.5 182.2 %reduce-scatter.14.cloned.1.call-start = ((), (), s32[]{:S(2)}) async-start(), calls=%async_computation.11 | async-start | bytes 7372800 | tf_op jit(solution)/shard_map/reduce_scatter | solution.py:1119
  569.3 311.5 %all-reduce.9.cloned.1.call-start = ((), (), s32[]{:S(2)}) async-start(), calls=%async_computation.12 | async-start | bytes 884736 | tf_op jit(solution)/shard_map/psum | solution.py:1108
  571.1 180.4 %copy-start.15 = (f32[32,128]{1,0:T(8,128)S(1)}, f32[32,128]{1,0:T(8,128)}, u32[]{:S(2)}) copy-start(f32[32,128]{1,0:T(8,128)} %shard_map.503) | copy-start | bytes 49156
  571.1 184.8 %copy-start.20 = (f32[64,320]{1,0:T(8,128)S(1)}, f32[64,320]{1,0:T(8,128)}, u32[]{:S(2)}) copy-start(f32[64,320]{1,0:T(8,128)} %get-tuple-element.138) | copy-start | bytes 245764
  571.1 344.0 %reduce-scatter.16.cloned.1.call-start = ((), (), s32[]{:S(2)}) async-start(), calls=%async_computation.13 | async-start | bytes 331776
  571.1 224.6 %copy-start.22 = (f32[512,8]{0,1:T(8,128)S(1)}, f32[512,8]{0,1:T(8,128)}, u32[]{:S(2)}) copy-start(f32[512,8]{0,1:T(8,128)} %param.54) | copy-start | bytes 49156
  571.2 309.6 %copy-start.8 = (f32[2,1152,48]{1,2,0:T(8,128)S(1)}, f32[2,1152,48]{1,2,0:T(8,128)}, u32[]{:S(2)}) copy-start(f32[2,1152,48]{1,2,0:T(8,128)} %param.51) | copy-start | bytes 1327108
  571.2 309.6 %copy-start.9 = (f32[2,1152,48]{1,2,0:T(8,128)S(1)}, f32[2,1152,48]{1,2,0:T(8,128)}, u32[]{:S(2)}) copy-start(f32[2,1152,48]{1,2,0:T(8,128)} %param.53) | copy-start | bytes 1327108
  572.3 419.1 %all-reduce.11.cloned.1.call-start = ((), (), s32[]{:S(2)}) async-start(), calls=%async_computation.15 | async-start | bytes 4653056 | tf_op jit(solution)/shard_map/psum | solution.py:1121
  750.8 182.5 %copy-start.14 = (f32[8,9,144]{2,0,1:T(8,128)S(1)}, f32[8,9,144]{2,0,1:T(8,128)}, u32[]{:S(2)}) copy-start(f32[8,9,144]{2,0,1:T(8,128)} %param.45) | copy-start | bytes 124420
  750.8 182.5 %copy-start.23 = (f32[8,9,144]{2,0,1:T(8,128)S(1)}, f32[8,9,144]{2,0,1:T(8,128)}, u32[]{:S(2)}) copy-start(f32[8,9,144]{2,0,1:T(8,128)} %param.47) | copy-start | bytes 124420
  750.8 182.5 %copy-start.24 = (f32[8,9,144]{2,0,1:T(8,128)S(1)}, f32[8,9,144]{2,0,1:T(8,128)}, u32[]{:S(2)}) copy-start(f32[8,9,144]{2,0,1:T(8,128)} %param.46) | copy-start | bytes 124420
  750.8 240.6 %copy-start.3 = (f32[160,1000]{1,0:T(8,128)S(1)}, f32[160,1000]{1,0:T(8,128)}, u32[]{:S(2)}) copy-start(f32[160,1000]{1,0:T(8,128)} %param.48) | copy-start | bytes 1920004
  750.8 240.6 %copy-start.6 = (f32[160,1000]{1,0:T(8,128)S(1)}, f32[160,1000]{1,0:T(8,128)}, u32[]{:S(2)}) copy-start(f32[160,1000]{1,0:T(8,128)} %param.50) | copy-start | bytes 1920004
  750.8 240.6 %copy-start.7 = (f32[160,1000]{1,0:T(8,128)S(1)}, f32[160,1000]{1,0:T(8,128)}, u32[]{:S(2)}) copy-start(f32[160,1000]{1,0:T(8,128)} %param.49) | copy-start | bytes 1920004
  (11 other events, 18.7 us)
Sparse Core Ops, SparseCore 0:
  10.3 46.8 all-gather.4
  59.4 60.4 all-gather.6
  122.1 66.2 all-gather.8
  190.5 32.3 all-gather.10
  387.8 36.6 reduce-scatter.17
  567.8 42.7 reduce-scatter.9
  613.1 64.6 reduce-scatter.11
  680.1 70.6 reduce-scatter.13
  756.6 124.0 all-reduce.8
  883.6 31.4 reduce-scatter.15
  918.6 72.7 all-reduce.10

commit v3 on v2

--- a/solution.py
+++ b/solution.py
@@ -126,6 +126,7 @@
 GROUP = 16
 PAIRS = EXPERTS // 2
 ROWS = PIX * GROUP
+CLASS_PAD = 1024
 LOW = jnp.bfloat16
 FULL = jnp.float32
 VMEM_CAP = 60 * 1024 * 1024
@@ -500,7 +501,8 @@
         cross_ref[...] = jnp.sum(cross, axis=0, keepdims=True)
         grad = (powers / totals - jnp.where(picked, 1.0, 0.0)) * norm_ref[4:5, 0:1]
         grad = grad.astype(LOW)
-        logits_ref[...] = grad
+        logits_ref[...] = jnp.zeros_like(logits_ref)
+        logits_ref[:, :CLASSES] = grad
         bias_grad_ref[...] = jnp.sum(grad.astype(FULL), axis=0, keepdims=True)
         grad_feats = dot_nt(grad, class_ref[...]) * (1.0 / PIX)
         grad_feats_ref[...] = grad_feats
@@ -519,11 +521,11 @@
             whole(1, CLASSES),
         ],
         [
-            ((images, C_HEAD), LOW), ((images, CLASSES), LOW), ((images, C_HEAD), FULL),
+            ((images, C_HEAD), LOW), ((images, CLASS_PAD), LOW), ((images, C_HEAD), FULL),
             ((2, C_HEAD), FULL), ((1, 1), FULL), ((1, CLASSES), FULL),
         ],
         [
-            total_block(images, C_HEAD), total_block(images, CLASSES), total_block(images, C_HEAD),
+            total_block(images, C_HEAD), total_block(images, CLASS_PAD), total_block(images, C_HEAD),
             total_block(2, C_HEAD), total_block(1, 1), total_block(1, CLASSES),
         ],
         [pltpu.VMEM((images, C_HEAD), FULL)] * 3,
@@ -635,7 +637,7 @@
     scale = pair_ref[0]
     for pixel in range(PIX):
         routed[pixel * images : (pixel + 1) * images] = twice_ref[pixel] * scale
-    out_ref[...] = dot_nn(turned[...], routed[...]).astype(LOW)
+    out_ref[0] = dot_nn(turned[...], routed[...]).astype(LOW)
 
 
 def kern_grad(grad, twice, pair_scales, name):
@@ -649,8 +651,8 @@
             whole(PIX, images, out_width), whole(PIX, images, width),
             pl.BlockSpec((1, images, width), lambda i: (i, 0, 0)),
         ],
-        [((out_width, PAIRS * width), LOW)],
-        [pl.BlockSpec((out_width, width), lambda i: (0, i))],
+        [((PAIRS, out_width, width), LOW)],
+        [pl.BlockSpec((1, out_width, width), lambda i: (i, 0, 0))],
         [pltpu.VMEM((out_width, rows), LOW), pltpu.VMEM((rows, width), LOW)],
         2 * rows * out_width * PAIRS * width,
         rows * out_width * 2,
@@ -668,7 +670,9 @@
         routed[side * C_OUT : (side + 1) * C_OUT] = turned[...] * scale_ref[0, side : side + 1]
     product = dot_nn(routed[...], scaled_ref[...].reshape(rows, C_MID)).astype(LOW)
     for side in range(2):
-        out_ref[:, side * C_MID : (side + 1) * C_MID] = product[side * C_OUT : (side + 1) * C_OUT]
+        out_ref[0, :, side * C_MID : (side + 1) * C_MID] = product[
+            side * C_OUT : (side + 1) * C_OUT
+        ]
 
 
 def project_grad(grad, scaled, scale):
@@ -682,8 +686,8 @@
             whole(PIX, images, C_OUT), whole(PIX, images, C_MID),
             pl.BlockSpec((1, 2, rows), lambda i: (i, 0, 0)),
         ],
-        [((C_OUT, EXPERTS * C_MID), LOW)],
-        [pl.BlockSpec((C_OUT, 2 * C_MID), lambda i: (0, i))],
+        [((PAIRS, C_OUT, 2 * C_MID), LOW)],
+        [pl.BlockSpec((1, C_OUT, 2 * C_MID), lambda i: (i, 0, 0))],
         [pltpu.VMEM((C_OUT, rows), LOW), pltpu.VMEM((2 * C_OUT, rows), LOW)],
         2 * rows * EXPERTS * C_OUT * C_MID,
         rows * (C_OUT + C_MID) * 2,
@@ -873,6 +877,169 @@
     )
 
 
+def reduce_kernel(n_wide, n_dp, n_full, n_share, *refs):
+    n_in = n_full + n_share
+    fulls, shares = refs[:n_full], refs[n_full:n_in]
+    full_outs, share_outs, spread_out = refs[n_in : n_in + n_full], refs[n_in + n_full : 2 * n_in], refs[2 * n_in]
+    scratch = list(refs[2 * n_in + 1 :])
+    firsts, seconds, thirds, halves, lineds = (
+        [scratch.pop(0) for _ in range(n_full)] for _ in range(5)
+    )
+    slots = [scratch.pop(0) for _ in range(n_share)]
+    send, recv = scratch
+    lines = n_wide // 2
+    me_wide, me_dp = lax.axis_index("wide"), lax.axis_index("dp")
+    core, line = lax.rem(me_wide, 2), lax.div(me_wide, 2)
+    sibling = line * 2 + 1 - core
+    used = [0]
+
+    barrier = pltpu.get_barrier_semaphore()
+    for k in range(1, n_wide):
+        pl.semaphore_signal(
+            barrier, inc=1, device_id={"wide": lax.rem(me_wide + k, n_wide)}, device_id_type=MESH
+        )
+    for k in range(1, n_dp):
+        pl.semaphore_signal(
+            barrier, inc=1, device_id={"dp": lax.rem(me_dp + k, n_dp)}, device_id_type=MESH
+        )
+    pl.semaphore_wait(barrier, n_wide + n_dp - 2)
+
+    def launch(src, dst, device):
+        copy = pltpu.make_async_remote_copy(
+            src_ref=src, dst_ref=dst, send_sem=send.at[used[0]], recv_sem=recv.at[used[0]],
+            device_id=device, device_id_type=MESH,
+        )
+        used[0] += 1
+        copy.start()
+        return copy
+
+    def finish(copies):
+        for copy in copies:
+            copy.wait()
+
+    def dp_peer(k):
+        return lax.rem(me_dp + k, n_dp)
+
+    to_sibling = [
+        launch(full.at[:, :, 1 - core], first, {"wide": sibling})
+        for full, first in zip(fulls, firsts)
+    ]
+    scattered = [
+        launch(share.at[dp_peer(k)], slot.at[k - 1], {"dp": dp_peer(k)})
+        for k in range(1, n_dp)
+        for share, slot in zip(shares, slots)
+    ]
+    finish(to_sibling)
+    for full, first, half in zip(fulls, firsts, halves):
+        def pair_sum(index, carry, full=full, first=first, half=half):
+            at_dp, at_line = lax.div(index, lines), lax.rem(index, lines)
+            total = full[at_dp, at_line, core].astype(FULL) + first[at_dp, at_line].astype(FULL)
+            half[at_dp, at_line] = total.astype(LOW)
+            return carry
+
+        lax.fori_loop(0, n_dp * lines, pair_sum, 0)
+    across = [
+        launch(half.at[dp_peer(k)], second.at[k - 1], {"dp": dp_peer(k)})
+        for k in range(1, n_dp)
+        for half, second in zip(halves, seconds)
+    ]
+    finish(scattered)
+    for share, slot, out in zip(shares, slots, share_outs):
+        total = share[me_dp].astype(FULL)
+        for k in range(1, n_dp):
+            total = total + slot[k - 1].astype(FULL)
+        out[me_dp] = total.astype(LOW)
+    finish(across)
+    for half, second, lined in zip(halves, seconds, lineds):
+        def dp_sum(at_line, carry, half=half, second=second, lined=lined):
+            total = half[me_dp, at_line].astype(FULL)
+            for k in range(1, n_dp):
+                total = total + second[k - 1, at_line].astype(FULL)
+            lined[at_line] = total.astype(LOW)
+            return carry
+
+        lax.fori_loop(0, lines, dp_sum, 0)
+    along = []
+    for k in range(1, lines):
+        other = lax.rem(line + k, lines)
+        for lined, third in zip(lineds, thirds):
+            along.append(launch(lined.at[other], third.at[k - 1], {"wide": other * 2 + core}))
+    gathered = [
+        launch(out.at[me_dp], out.at[me_dp], {"dp": dp_peer(k)})
+        for k in range(1, n_dp)
+        for out in share_outs
+    ]
+    finish(along)
+    for lined, third, out in zip(lineds, thirds, full_outs):
+        total = lined[line].astype(FULL)
+        for k in range(1, lines):
+            total = total + third[k - 1].astype(FULL)
+        out[me_dp] = total.astype(LOW)
+    last = [
+        launch(out.at[me_dp], out.at[me_dp], {"dp": dp_peer(k)})
+        for out in reversed(full_outs)
+        for k in range(1, n_dp)
+    ]
+    own = full_outs[-1]
+    finish(last[: n_dp - 1])
+    spread_out[me_wide] = own[...]
+    everywhere = [
+        launch(own, spread_out.at[me_wide], {"wide": lax.rem(me_wide + k, n_wide)})
+        for k in range(1, n_wide)
+    ]
+    finish(last[n_dp - 1 :] + gathered + everywhere)
+
+
+def reduce_grads(fulls, shares, ident):
+    n_wide, n_dp = lax.axis_size("wide"), lax.axis_size("dp")
+    lines = n_wide // 2
+    views = [full.reshape((n_dp, lines, 2) + full.shape[2:]) for full in fulls]
+    tails = [full.shape[2:] for full in fulls]
+    copies = (
+        len(fulls) * (1 + (n_dp - 1) * 2 + lines - 1) + len(shares) * 2 * (n_dp - 1) + n_wide - 1
+    )
+    vmem = pl.BlockSpec(memory_space=pltpu.VMEM)
+    outs = [jax.ShapeDtypeStruct((n_dp,) + tail, LOW) for tail in tails]
+    outs += [jax.ShapeDtypeStruct(share.shape, LOW) for share in shares]
+    outs += [jax.ShapeDtypeStruct((n_wide, n_dp) + tails[-1], LOW)]
+    found = pl.pallas_call(
+        functools.partial(reduce_kernel, n_wide, n_dp, len(fulls), len(shares)),
+        name="reduce_grads",
+        out_shape=outs,
+        in_specs=[vmem] * (len(fulls) + len(shares)),
+        out_specs=[vmem] * len(outs),
+        scratch_shapes=[pltpu.VMEM((n_dp, lines) + tail, LOW) for tail in tails]
+        + [pltpu.VMEM((n_dp - 1, lines) + tail, LOW) for tail in tails]
+        + [pltpu.VMEM((lines - 1,) + tail, LOW) for tail in tails]
+        + [pltpu.VMEM((n_dp, lines) + tail, LOW) for tail in tails]
+        + [pltpu.VMEM((lines,) + tail, LOW) for tail in tails]
+        + [pltpu.VMEM((n_dp - 1,) + share.shape[1:], LOW) for share in shares]
+        + [pltpu.SemaphoreType.DMA((copies,)), pltpu.SemaphoreType.DMA((copies,))],
+        compiler_params=pltpu.CompilerParams(
+            collective_id=ident, has_side_effects=True, vmem_limit_bytes=VMEM_CAP
+        ),
+    )(*views, *shares)
+    return found[: len(fulls)], found[len(fulls) : len(fulls) + len(shares)], found[-1]
+
+
+def to_pieces(cube, count):
+    pairs, rows, width = cube.shape
+    if pairs == count:
+        return cube
+    more = count // pairs
+    cube = cube.reshape(pairs, rows, more, width // more).transpose(0, 2, 1, 3)
+    return cube.reshape(count, rows, width // more)
+
+
+def from_pieces(pieces, pairs):
+    count, rows, width = pieces.shape
+    if pairs == count:
+        return pieces
+    more = count // pairs
+    cube = pieces.reshape(pairs, more, rows, width).transpose(0, 2, 1, 3)
+    return cube.reshape(pairs, rows, width * more)
+
+
 def soap_kernel(
     gained, weight_ref, grad_ref, first_ref, second_ref, state_ref,
     first_out, second_out, state_out, weight_out, raised,
@@ -907,7 +1074,7 @@
 
     old = [state_ref[1, 2 * step + side] for side in range(2)]
     turns = [spread_out(rows) for rows in old]
-    grad = grad_ref[...].astype(FULL)
+    grad = grad_ref[0].astype(FULL)
     turned = by_half(lambda side, value: dot_nn(turns[side], value, HIGH), grad)
     first_new = beta_one * first_ref[...] + (1.0 - beta_one) * grad
     second_new = beta_two * second_ref[...] + (1.0 - beta_two) * (turned * turned)
@@ -956,12 +1123,14 @@
     turned_state = state.transpose(0, 1, 3, 2)
     gained = stat_gain * every / (total // EXPERTS)
     column = pl.BlockSpec((height, width), lambda i: (0, i))
-    sheet = jax.ShapeDtypeStruct(weight.shape, FULL)
     first_new, second_new, state_new, weight_new = device_kernel(
         functools.partial(soap_kernel, gained),
         "soap",
         PAIRS,
-        [column, column, column, column, whole(2, EXPERTS, BLK, height)],
+        [
+            column, pl.BlockSpec((1, height, width), lambda i: (i, 0, 0)), column, column,
+            whole(2, EXPERTS, BLK, height),
+        ],
         [(weight.shape, FULL), (weight.shape, FULL), (turned_state.shape, FULL),
          (weight.shape, FULL)],
         [column, column, total_block(2, EXPERTS, BLK, height), column],
@@ -1060,7 +1229,11 @@
     feats, grad_logits, grad_feats, back_two, cross_part, grad_bias_cls = loss_part(
         widened, norm_two, class_label[:, None], class_low, bias_cls[None]
     )
-    grad_class = dot_tn(feats, grad_logits)
+    grad_class = jnp.stack(
+        [dot_tn(feats, part).astype(low_type) for part in jnp.split(grad_logits, PAIRS, axis=1)]
+    )
+    grad_class, grad_feats = lax.optimization_barrier((grad_class, grad_feats))
+    share_class = lax.psum_scatter(grad_class, "wide", scatter_dimension=1, tiled=True)
     back_two, cross_total, grad_bias_cls = sum_all((back_two, cross_part, grad_bias_cls), 3)
     means_one = route_one_sum[0] / every
     means_two = route_two_sum[0] / every
@@ -1076,8 +1249,10 @@
         widened, grad_feats, coef_two, head_low, pair_two, twice, before, hat_one, route_two,
         balance_grad(means_two, every)[None], router_two,
     )
+    share_class, twice = lax.optimization_barrier((share_class, twice))
     grad_head = kern_grad(grad_widened, twice, pair_two, "head_grad")
-    grad_head, grad_class, back_one = lax.optimization_barrier((grad_head, grad_class, back_one))
+    grad_head, back_one = lax.optimization_barrier((grad_head, back_one))
+    share_head = lax.psum_scatter(grad_head, "wide", scatter_dimension=1, tiled=True)
     grad_router_two = dot_tn(pooled_two, grad_logit_two, HIGH)
     (back_one,) = sum_all((back_one,), 4)
     by_value = -scale_one * inv_one * back_one[1] / count
@@ -1089,57 +1264,84 @@
     )
     row_scale = jnp.tile(route_one.astype(low_type).T, (1, PIX)).reshape(PAIRS, 2, -1)
     grad_project = project_grad(grad_before, scaled, row_scale)
-    grad_project, grad_scaled = lax.optimization_barrier((grad_project, grad_scaled))
+    grad_project, grad_scaled, share_head = lax.optimization_barrier(
+        (grad_project, grad_scaled, share_head)
+    )
+    share_project = lax.psum_scatter(grad_project, "wide", scatter_dimension=1, tiled=True)
     grad_hidden, grad_logit_one, grad_gate, grad_squeeze, grad_depth = expand_back(
         grad_scaled, turned, hidden, img_two, gate, squeeze, excite, depth_full, route_one,
         route_project, balance_grad(means_one, every)[None], expand_low,
     )
+    share_project, grad_hidden = lax.optimization_barrier((share_project, grad_hidden))
     grad_expand = kern_grad(grad_hidden, img_two, pair_in, "expand_grad")
     grad_excite = jnp.stack(
         [
-            dot_tn(pooled_act, grad_squeeze, HIGH),
-            dot_tn(grad_gate, squeeze * jax.nn.sigmoid(squeeze), HIGH),
+            dot_tn(grad_squeeze, pooled_act, HIGH),
+            dot_tn(squeeze * jax.nn.sigmoid(squeeze), grad_gate, HIGH),
         ]
     )
     grad_router_one = dot_tn(pooled_one, grad_logit_one, HIGH)
     grad_depth = grad_depth.transpose(1, 0, 2)
     grad_bias_se = jnp.sum(grad_squeeze, axis=0)
     grad_bias_ex = jnp.sum(grad_gate, axis=0)
-    small = lax.psum(
-        (
-            grad_excite,
-            jnp.concatenate([grad_router_one, grad_router_two], axis=0),
-            jnp.concatenate([grad_bias_se, grad_bias_ex]),
+    n_wide, n_dp = lax.axis_size("wide"), lax.axis_size("dp")
+    parts = n_wide * n_dp
+    depth_piece = grad_depth.size // parts
+    extras = [
+        grad_depth.reshape(-1, n_wide, depth_weight.shape[2]).transpose(1, 0, 2),
+        jnp.concatenate(
+            [
+                grad_excite.reshape(-1), grad_router_one.reshape(-1), grad_router_two.reshape(-1),
+                grad_bias_se, grad_bias_ex,
+            ]
         ),
-        ("dp", "wide"),
-    )
-    depth_flat = grad_depth.transpose(2, 0, 1).astype(low_type).reshape(C_MID, -1)
-    full = (grad_expand, depth_flat, grad_project, grad_head, grad_class.astype(low_type))
-    shares = [
-        lax.psum_scatter(grad, "wide", scatter_dimension=0, tiled=True) for grad in full
     ]
-    reduced = [lax.psum(share, "dp") for share in shares]
-    depth_reduced = reduced[1].reshape(-1, EXPERTS, KSIZE * KSIZE).transpose(1, 2, 0)
+    depth_part = extras[0].reshape(n_wide, n_dp, depth_piece).transpose(1, 0, 2)
+    rest_size = extras[1].size
+    rest_piece = -(-rest_size // parts)
+    rest_part = jnp.pad(extras[1], (0, rest_piece * parts - rest_size))
+    rest_part = rest_part.reshape(n_dp, n_wide, rest_piece)
+    extra_rows = -(-(depth_piece + rest_piece) // (16 * 384)) * 16
+    extra = jnp.concatenate([depth_part, rest_part], axis=2).astype(low_type)
+    extra = jnp.pad(extra, ((0, 0), (0, 0), (0, extra_rows * 384 - extra.shape[2])))
+    extra = extra.reshape(n_dp, n_wide, extra_rows, 384)
+    pieces = to_pieces(grad_expand, n_dp)
+    pieces = pieces.reshape(n_dp, n_wide, -1, pieces.shape[2])
+    (own_expand, own_extra), own_shares, every_extra = reduce_grads(
+        [pieces, extra],
+        [to_pieces(share, n_dp) for share in (share_project, share_head, share_class)],
+        5,
+    )
+    sum_project, sum_head, sum_class = (from_pieces(share, PAIRS) for share in own_shares)
+    sum_expand = from_pieces(own_expand, PAIRS)
+    sum_class = sum_class.transpose(1, 0, 2).reshape(-1, CLASS_PAD)[:, :CLASSES].astype(FULL)
+    own_extra = own_extra.reshape(n_dp, -1)[:, :depth_piece].reshape(EXPERTS, KSIZE * KSIZE, -1)
+    rest = every_extra.reshape(n_wide, n_dp, -1)[:, :, depth_piece : depth_piece + rest_piece]
+    rest = rest.transpose(1, 0, 2).reshape(-1)[:rest_size].astype(FULL)
+    split = grad_excite.size
+    sum_excite = rest[:split].reshape(2, C_SE, C_MID).transpose(0, 2, 1)
+    sum_router = rest[split : split + router_weight.size].reshape(router_weight.shape)
+    sum_bias = rest[split + router_weight.size :]
     loss = cross_total[0, 0] / every + balance_weight * (
         jnp.mean((means_one - jnp.mean(means_one)) ** 2)
         + jnp.mean((means_two - jnp.mean(means_two)) ** 2)
     )
     grad_gains = jnp.concatenate(
-        [small[2], back_one[1], back_one[0], back_two[1], back_two[0], grad_bias_cls[0]]
-    )
-    expand_out = soap(expand_weight, reduced[0], expand_first, expand_second, expand_state, every)
+        [sum_bias, back_one[1], back_one[0], back_two[1], back_two[0], grad_bias_cls[0]]
+    )
+    expand_out = soap(expand_weight, sum_expand, expand_first, expand_second, expand_state, every)
     project_out = soap(
-        project_weight, reduced[2], project_first, project_second, project_state, every
-    )
-    head_out = soap(head_weight, reduced[3], head_first, head_second, head_state, every)
+        project_weight, sum_project, project_first, project_second, project_state, every
+    )
+    head_out = soap(head_weight, sum_head, head_first, head_second, head_state, every)
     depth_out = adam(
-        depth_weight, depth_reduced.astype(FULL), depth_first, depth_second, rate_matrix
+        depth_weight, own_extra.astype(FULL), depth_first, depth_second, rate_matrix
     )
     class_out = adam(
-        classifier_weight, reduced[4].astype(FULL), classifier_first, classifier_second, rate_matrix
-    )
-    excite_out = adam(excite_weight, small[0], excite_first, excite_second, rate_matrix)
-    router_out = adam(router_weight, small[1], router_first, router_second, rate_matrix)
+        classifier_weight, sum_class, classifier_first, classifier_second, rate_matrix
+    )
+    excite_out = adam(excite_weight, sum_excite, excite_first, excite_second, rate_matrix)
+    router_out = adam(router_weight, sum_router, router_first, router_second, rate_matrix)
     gains_out = adam(gains_weight, grad_gains, gains_first, gains_second, rate_gains)
     return (
         loss,

time: 1070 us -> 788 us (0.74)
  waiting for transfers between devices: 398 us -> 49 us
  Pallas kernels: 516 us -> 608 us
  blocking collectives: 72.1 us -> 16.8 us
  local copies, waits for them, and re-layouts: 20.3 us -> 44.6 us
    reduce_scatter x4 -> x2, waiting for transfers between devices: 178 us -> 0.04 us  [the longest x1 0.02 us: local(): lax.psum_scatter(grad_class, 'wide', scatter_dimension=1, tiled=True)]
    psum x2 -> x0, waiting for transfers between devices: 140 us -> none  [the longest x1 82.2 us: local(): lax.psum((grad_excite, jnp.concatenate([grad_router_one, grad_router_two]...]
    pallas_call x0 -> x1, Pallas kernels: none -> 89.2 us  [reduce_grads(): pl.pallas_call(functools.partial(reduce_kernel, n_wide, n_dp, len(fulls),...]
    psum x2 -> x0, blocking collectives: 55.3 us -> none  [the longest x1 38.1 us: local(): lax.psum((grad_excite, jnp.concatenate([grad_router_one, grad_router_two]...]
    unnamed x12 -> x8, waiting for transfers between devices: 33.4 us -> 0.12 us
    unnamed x67 -> x93, local copies, waits for them, and re-layouts: 5.72 us -> 16.8 us
  transfers between devices with their start and end apart: 11 -> 7, of which waited for: 9 -> 3; matrix products, arithmetic and copies ran while one was open for 3% -> 5% of each run, Pallas kernels for 30% -> 49%
where the time goes in v3:
time: 788 us; the launch traced here: 776 us
  Pallas kernels  608 us (77%)
  waiting for transfers between devices  49 us (6%)
  local copies, waits for them, and re-layouts  44.6 us (6%)
  other arithmetic  28.7 us (4%)
  between operations  19.6 us (2%)
  blocking collectives  16.8 us (2%)
  matrix products  8.71 us (1%)
    pallas_call x1, Pallas kernels, reduce_grads(): pl.pallas_call(functools.partial(reduce_kernel, n_wide, n_dp, len(fulls),...  89.2 us
    pallas_call x1, Pallas kernels, expand_back(): device_kernel(expand_back_kernel, 'expand_back', images // GROUP, [images...  71.6 us
    pallas_call x1, Pallas kernels, head_back(): device_kernel(head_back_kernel, 'head_back', images // GROUP, [images_blo...  63.3 us
    pallas_call x3, Pallas kernels, soap(): device_kernel(functools.partial(soap_kernel, gained), 'soap', PAIRS, [col...  59 us
    pallas_call x2, Pallas kernels, kern_grad(): device_kernel(kern_grad_kernel, name, PAIRS, [whole(PIX, images, out_widt...  58.7 us
    pallas_call x1, Pallas kernels, project_back(): device_kernel(project_back_kernel, 'project_back', images // GROUP, [imag...  54.8 us
    pallas_call x1, Pallas kernels, project_forward(): device_kernel(project_kernel, 'project_forward', images // GROUP, [images...  46.7 us
    pallas_call x4, Pallas kernels, sum_all(): pl.pallas_call(functools.partial(sum_kernel, n_wide, n_dp), out_shape=jax...  45.3 us
  transfers between devices with their start and end apart: 7, of which 3 were waited for; matrix products, arithmetic and copies ran while one was open for 5% of the time, Pallas kernels for 49%

profile of v3, /device:TPU:0, one launch (start us, length us, event | category | flops | bytes accessed | tf_op | source)
XLA Modules:
  0.0 775.9 jit_solution(9930877808452806778)
XLA Ops:
  7.3 2.1 convert_element_type.67
  15.0 2.4 pad_maximum_fusion.1.img_ref.twice_ref
  18.3 16.8 %all_gather.16 = bf16[1152,72]{1,0:T(8,128)(2,1)S(1)} all-gather(bf16[144,72]{1,0:T(8,128)(2,1)S(1)} %copy.125), channel_id=1, replica_groups=mesh['dp'=4,'wide'=8] {'wide'}, dimensions={0}, use_global_device_ids=true | all-gather | bytes 186624 | tf_op jit(solution)/shard_map/all_gather | solution.py:1200
  37.4 19.8 %all-gather.5.cloned.1.call-done.expand_ref.weight_ref = bf16[1152,1536]{1,0:T(8,128)(2,1)} async-done(((bf16[144,1536]{1,0:T(8,128)(2,1)}), bf16[1152,1536]{1,0:T(8,128)(2,1)}) %all-gather.5.cloned.1.call-update) | async-done | bytes 3538960 | tf_op jit(solution)/shard_map/all_gather | solution.py:1195
  57.2 41.6 %expand_forward.1 = (bf16[49,64,1152]{2,1,0:T(8,128)(2,1)}, bf16[49,64,1152]{2,1,0:T(8,128)(2,1)}, bf16[49,64,1152]{2,1,0:T(8,128)(2,1)}, f32[64,8]{1,0:T(8,128)...) custom-call(bf16[49,64,384]{2,1,0:T(8,128)(2,1)} %pad_maximum_fusion, ...), custom_call_target="tpu_custom_call" | custom-call | flops 11098128384 | bytes 28901376 | tf_op jit(solution)/shard_map/expand_forward/pallas_call | solution.py:302
  98.9 21.0 %all-gather.7.cloned.1.call-done.source = bf16[320,9216]{1,0:T(8,128)(2,1)} async-done(((bf16[40,9216]{1,0:T(8,128)(2,1)}), bf16[320,9216]{1,0:T(8,128)(2,1)}) %all-gather.7.cloned.1.call-update) | async-done | bytes 5898256 | tf_op jit(solution)/shard_map/all_gather | solution.py:1196
  119.9 46.7 %project_forward.1 = (bf16[49,64,2560]{2,1,0:T(8,128)(2,1)}, f32[49,64,320]{2,1,0:T(8,128)}, f32[2,320]{1,0:T(2,128)}) custom-call(bf16[49,64,1152]{2,1,0:T(8,128)(2,1)} %get-tuple-element.96.scaled_ref, bf16[320,9216]{1,0:T(8,128)(2,1)} %all-gather.7.cloned.1.call-done.source, bf16[4,64,640]{2,1,0:T(8,128)(2,1)} %get-tuple-element.97.pair_ref), custom_call_target="tpu_custom_call" | custom-call | flops 18496880640 | bytes 23281664 | tf_op jit(solution)/shard_map/project_forward/pallas_call | solution.py:384
  167.9 11.0 %shard_map.501 = f32[8,128]{1,0:T(8,128)} custom-call(f32[8,128]{1,0:T(8,128)} %fusion.34.x_ref), custom_call_target="tpu_custom_call" | custom-call | tf_op jit(solution)/shard_map/pallas_call | solution.py:97
  180.4 8.0 %all-gather.9.cloned.1.call-done.weight_ref = bf16[1280,2560]{1,0:T(8,128)(2,1)} async-done(((bf16[160,2560]{1,0:T(8,128)(2,1)}), bf16[1280,2560]{1,0:T(8,128)(2,1)}) %all-gather.9.cloned.1.call-update) | async-done | bytes 6553616 | tf_op jit(solution)/shard_map/all_gather | solution.py:1197
  188.4 29.7 %head_forward.1 = (bf16[49,64,1280]{2,1,0:T(8,128)(2,1)}, bf16[49,64,640]{2,1,0:T(8,128)(2,1)}, f32[64,8]{1,0:T(8,128)}, bf16[4,64,640]{2,1,0:T(8,128)(2,1)}, f3...) custom-call(f32[49,64,320]{2,1,0:T(8,128)} %get-tuple-element.98.before_ref, ...), custom_call_target="tpu_custom_call" | custom-call | flops 20552089600 | bytes 10035200 | tf_op jit(solution)/shard_map/head_forward/pallas_call | solution.py:440
  220.2 11.2 %shard_map.502 = f32[24,128]{1,0:T(8,128)} custom-call(f32[24,128]{1,0:T(8,128)} %fusion.28.x_ref), custom_call_target="tpu_custom_call" | custom-call | tf_op jit(solution)/shard_map/pallas_call | solution.py:97
  233.8 19.8 %loss_part.1 = (bf16[64,1280]{1,0:T(8,128)(2,1)}, bf16[64,1024]{1,0:T(8,128)(2,1)}, f32[64,1280]{1,0:T(8,128)}, f32[2,1280]{1,0:T(2,128)}, f32[1,1]{1,0:T(1,128)}, /*index=5*/f32[1,1000]{1,0:T(1,128)}) custom-call(bf16[49,64,1280]{2,1,0:T(8,128)(2,1)} %get-tuple-element.101.widened_ref, f32[8,1280]{1,0:T(8,128)} %stack.82.norm_ref, ...), custom_call_target="tpu_custom_call" | custom-call | flops 327680000 | bytes 8028160 | tf_op jit(solution)/shard_map/loss_part/pallas_call | solution.py:515
  258.6 1.8 pad_maximum_fusion
  262.5 11.6 %shard_map.503 = f32[32,128]{1,0:T(8,128)} custom-call(f32[32,128]{1,0:T(8,128)} %pad_bitcast_fusion.x_ref), custom_call_target="tpu_custom_call" | custom-call | tf_op jit(solution)/shard_map/pallas_call | solution.py:97
  278.6 63.3 %head_back.1 = (bf16[49,64,1280]{2,1,0:T(8,128)(2,1)}, f32[49,64,320]{2,1,0:T(8,128)}, f32[64,8]{1,0:T(8,128)}, f32[2,320]{1,0:T(2,128)}) custom-call(bf16[49,64,1280]{2,1,0:T(8,128)(2,1)} %get-tuple-element.101.widened_ref, f32[64,1280]{1,0:T(8,128)} %get-tuple-element.110.grad_feats_ref, f32[4,1280]{1,0:T(4,128)} %pad_maximum_fusion.3.coef_ref, ...), custom_call_target="tpu_custom_call" | custom-call | flops 20552089600 | bytes 18063360 | tf_op jit(solution)/shard_map/head_back/pallas_call | solution.py:608
  342.0 35.4 %head_grad.1 = bf16[4,1280,640]{2,1,0:T(8,128)(2,1)} custom-call(bf16[49,64,1280]{2,1,0:T(8,128)(2,1)} %get-tuple-element.115.grad_ref, bf16[49,64,640]{2,1,0:T(8,128)(2,1)} %get-tuple-element.117.twice_ref, bf16[4,64,640]{2,1,0:T(8,128)(2,1)} %get-tuple-element.111.pair_ref), custom_call_target="tpu_custom_call" | custom-call | flops 20552089600 | bytes 8028160 | tf_op jit(solution)/shard_map/head_grad/pallas_call | solution.py:646
  379.6 11.5 %shard_map.504 = f32[8,128]{1,0:T(8,128)} custom-call(f32[8,128]{1,0:T(8,128)} %pad_bitcast_fusion.1.x_ref), custom_call_target="tpu_custom_call" | custom-call | tf_op jit(solution)/shard_map/pallas_call | solution.py:97
  393.1 54.8 %project_back.1 = (bf16[49,64,320]{2,1,0:T(8,128)(2,1)}, bf16[49,64,1152]{2,1,0:T(8,128)(2,1)}, f32[64,8]{1,0:T(8,128)}) custom-call(f32[49,64,320]{2,1,0:T(8,128)} %get-tuple-element.114.grad_ref, f32[49,64,320]{2,1,0:T(8,128)} %get-tuple-element.98.before_ref, f32[3,320]{1,0:T(4,128)} %pad_maximum_fusion.4.coef_ref, ...), custom_call_target="tpu_custom_call" | custom-call | flops 18496880640 | bytes 23281664 | tf_op jit(solution)/shard_map/project_back/pallas_call | solution.py:735
  447.9 28.5 %project_grad.1 = bf16[4,320,2304]{2,1,0:T(8,128)(2,1)} custom-call(bf16[49,64,320]{2,1,0:T(8,128)(2,1)} %get-tuple-element.121.grad_ref, bf16[49,64,1152]{2,1,0:T(8,128)(2,1)} %get-tuple-element.96.scaled_ref, bf16[4,2,3136]{2,1,0:T(2,128)(2,1)} %tile.9.scale_ref), custom_call_target="tpu_custom_call" | custom-call | flops 18496880640 | bytes 9232384 | tf_op jit(solution)/shard_map/project_grad/pallas_call | solution.py:681
  476.4 7.2 copy.141
  483.6 3.7 copy.148
  491.1 1.8 multiply_bitcast_fusion
  494.8 71.6 %expand_back.1 = (bf16[49,64,1152]{2,1,0:T(8,128)(2,1)}, f32[64,8]{1,0:T(8,128)}, f32[64,1152]{1,0:T(8,128)}, f32[64,48]{1,0:T(8,128)}, f32[9,8,1152]{2,1,0:T(8,128)}) custom-call(bf16[49,64,1152]{2,1,0:T(8,128)(2,1)} %get-tuple-element.126.grad_scaled_ref, bf16[49,64,1152]{2,1,0:T(8,128)(2,1)} %get-tuple-element.127.turned_ref, ...), custom_call_target="tpu_custom_call" | custom-call | flops 11098128384 | bytes 28901376 | tf_op jit(solution)/shard_map/expand_back/pallas_call | solution.py:849
  575.9 2.0 reshape.281
  578.8 23.3 %expand_grad.1 = bf16[4,1152,384]{2,1,0:T(8,128)(2,1)} custom-call(bf16[49,64,1152]{2,1,0:T(8,128)(2,1)} %get-tuple-element.133.grad_ref, bf16[49,64,384]{2,1,0:T(8,128)(2,1)} %pad_maximum_fusion.1.img_ref.twice_ref, bf16[4,64,384]{2,1,0:T(8,128)(2,1)} %get-tuple-element.134.pair_ref), custom_call_target="tpu_custom_call" | custom-call | flops 11098128384 | bytes 7225344 | tf_op jit(solution)/shard_map/expand_grad/pallas_call | solution.py:646
  602.2 89.2 %reduce_grads.1 = (bf16[4,144,384]{2,1,0:T(8,128)(2,1)}, bf16[4,32,384]{2,1,0:T(8,128)(2,1)}, bf16[4,40,2304]{2,1,0:T(8,128)(2,1)}, bf16[4,160,640]{2,1,0:T(8,12...) custom-call(bf16[4,4,2,144,384]{4,3,2,1,0:T(8,128)(2,1)} %bitcast.149, ...), custom_call_target="tpu_custom_call" | custom-call | tf_op jit(solution)/shard_map/reduce_grads/pallas_call | solution.py:1005
  691.4 2.0 reshape.274
  694.0 6.3 slice.143
  702.5 1.7 multiply_subtract_fusion.2
  708.7 19.3 %soap.3 = (f32[144,1536]{1,0:T(8,128)}, f32[144,1536]{1,0:T(8,128)}, f32[2,8,4,144]{3,2,1,0:T(4,128)}, f32[144,1536]{1,0:T(8,128)}) custom-call(f32[144,1536]{1,0:T(8,128)} %weight_ref.3, bf16[4,144,384]{2,1,0:T(8,128)(2,1)} %get-tuple-element.146.grad_ref, f32[144,1536]{1,0:T(8,128)} %first_ref.3, f32[144,1536]{1,0:T(8,128)} %second_ref.3, ...), custom_call_target="tpu_custom_call" | custom-call | flops 63700992 | bytes 5750784 | tf_op jit(solution)/shard_map/soap/pallas_call | solution.py:1126
  728.0 16.8 %soap.4 = (f32[40,9216]{1,0:T(8,128)}, f32[40,9216]{1,0:T(8,128)}, f32[2,8,4,40]{3,2,1,0:T(4,128)}, f32[40,9216]{1,0:T(8,128)}) custom-call(f32[40,9216]{1,0:T(8,128)} %weight_ref.4, bf16[4,40,2304]{2,1,0:T(8,128)(2,1)} %get-tuple-element.151.grad_ref, f32[40,9216]{1,0:T(8,128)} %first_ref.4, f32[40,9216]{1,0:T(8,128)} %second_ref.4, f32[2,8,4,40]{3,2,1,0:T(4,128)} %bitcast.174), custom_call_target="tpu_custom_call" | custom-call | flops 29491200 | bytes 9584640 | tf_op jit(solution)/shard_map/soap/pallas_call | solution.py:1126
  744.8 22.9 %soap.5 = (f32[160,2560]{1,0:T(8,128)}, f32[160,2560]{1,0:T(8,128)}, f32[2,8,4,160]{3,2,1,0:T(4,128)}, f32[160,2560]{1,0:T(8,128)}) custom-call(f32[160,2560]{1,0:T(8,128)} %weight_ref.5, bf16[4,160,640]{2,1,0:T(8,128)(2,1)} %get-tuple-element.156.grad_ref, f32[160,2560]{1,0:T(8,128)} %first_ref.5, f32[160,2560]{1,0:T(8,128)} %second_ref.5, ...), custom_call_target="tpu_custom_call" | custom-call | flops 131072000 | bytes 10649600 | tf_op jit(solution)/shard_map/soap/pallas_call | solution.py:1126
  (211 shorter events, 51.5 us)
Async XLA Ops:
  7.2 3.3 copy-start
  7.2 50.0 %all-gather.5.cloned.1.call-start = ((), (), s32[]{:S(2)}) async-start(), calls=%async_computation.3 | async-start | bytes 3981312 | tf_op jit(solution)/shard_map/all_gather | solution.py:1195
  9.4 110.5 %all-gather.7.cloned.1.call-start = ((), (), s32[]{:S(2)}) async-start(), calls=%async_computation.4 | async-start | bytes 6635520 | tf_op jit(solution)/shard_map/all_gather | solution.py:1196
  10.4 2.6 copy-start.20
  10.5 178.0 %all-gather.9.cloned.1.call-start = ((), (), s32[]{:S(2)}) async-start(), calls=%async_computation.5 | async-start | bytes 7372800 | tf_op jit(solution)/shard_map/all_gather | solution.py:1197
  11.5 3.5 copy-start.5
  11.5 5.9 copy-start.40
  11.5 6.6 copy-start.13
  11.5 222.2 %all-gather.11.cloned.1.call-start = ((), (), s32[]{:S(2)}) async-start(), calls=%async_computation.6 | async-start | bytes 2949120 | tf_op jit(solution)/shard_map/all_gather | solution.py:1198
  12.4 329.6 %reduce-scatter.6.cloned.1.call-start = ((), (), s32[]{:S(2)}) async-start(), calls=%async_computation.7 | async-start | bytes 2949120 | tf_op jit(solution)/shard_map/reduce_scatter | solution.py:1236
  15.0 21.8 %copy-start.41 = (s32[64]{0:T(128)S(1)}, s32[64]{0:T(128)}, u32[]{:S(2)}) copy-start(s32[64]{0:T(128)} %param.32) | copy-start | bytes 772
  119.9 47.4 %copy-start.42 = (f32[1,8]{1,0:T(1,128)S(1)}, f32[1,8]{1,0:T(1,128)}, u32[]{:S(2)}) copy-start(f32[1,8]{1,0:T(1,128)} %get-tuple-element.100) | copy-start | bytes 100
  253.5 3.9 copy-start.2
  260.5 13.6 %copy-start.12 = (f32[24,128]{1,0:T(8,128)S(1)}, f32[24,128]{1,0:T(8,128)}, u32[]{:S(2)}) copy-start(f32[24,128]{1,0:T(8,128)} %shard_map.502) | copy-start | bytes 36868
  260.5 215.9 %reduce-scatter.8.cloned.1.call-start = ((), (), s32[]{:S(2)}) async-start(), calls=%async_computation.8 | async-start | bytes 7372800 | tf_op jit(solution)/shard_map/reduce_scatter | solution.py:1255
  377.3 198.6 %reduce-scatter.10.cloned.1.call-start = ((), (), s32[]{:S(2)}) async-start(), calls=%async_computation.9 | async-start | bytes 6635520
  487.3 2.6 copy-start.25
  494.8 73.4 %copy-start.27 = (f32[64,48]{1,0:T(8,128)S(1)}, f32[64,48]{1,0:T(8,128)}, u32[]{:S(2)}) copy-start(f32[64,48]{1,0:T(8,128)} %get-tuple-element.130.squeeze_ref) | copy-start | bytes 36868
  494.8 74.8 %copy-start.15 = (f32[64,1152]{1,0:T(8,128)S(1)}, f32[64,1152]{1,0:T(8,128)}, u32[]{:S(2)}) copy-start(f32[64,1152]{1,0:T(8,128)} %get-tuple-element.137) | copy-start | bytes 884740
  494.8 76.3 %copy-start.22 = (f32[64,192]{1,0:T(8,128)S(1)}, f32[64,192]{1,0:T(8,128)}, u32[]{:S(2)}) copy-start(f32[64,192]{1,0:T(8,128)} %get-tuple-element.139) | copy-start | bytes 147460
  566.4 7.5 copy-start.11
  693.9 6.4 copy-start.18
  700.2 4.1 copy-start.4
  700.2 4.1 copy-start.6
  700.2 4.1 copy-start.7
  701.8 4.1 copy-start.8
  702.5 3.4 copy-start.9
  702.5 3.4 copy-start.10
  704.3 3.0 copy-start.21
  704.3 3.0 copy-start.26
  704.3 3.0 copy-start.35
  704.3 3.0 copy-start.36
  (19 other events, 29.7 us)
Sparse Core Ops, SparseCore 0:
  10.3 46.9 all-gather.4
  59.4 60.4 all-gather.6
  122.1 66.2 all-gather.8
  190.5 32.3 all-gather.10
  260.6 37.3 reduce-scatter.5
  377.5 72.5 reduce-scatter.7
  487.5 65.5 reduce-scatter.9

commit v4 on v3

--- a/solution.py
+++ b/solution.py
@@ -221,11 +221,16 @@
 
 
 def expand_kernel(
-    img_ref, hot_ref, router_ref, expand_ref, depth_ref, excite_ref, bias_se_ref, bias_ex_ref,
+    img_ref, hot_ref, router_ref, source, depth_ref, excite_ref, bias_se_ref, bias_ex_ref,
     hidden_ref, turned_ref, scaled_ref, route_ref, pair_in_ref, pair_out_ref, gate_ref,
     squeeze_ref, pooled_one_ref, pooled_act_ref, route_sum_ref,
-    routed, hidden_full, act_full, kern,
+    routed, hidden_full, act_full, kern, expand_ref, sem,
 ):
+    @pl.when(pl.program_id(0) == 0)
+    def _():
+        for copy in pair_copies(source, expand_ref, sem):
+            copy.start()
+
     pooled = img_ref[0].astype(FULL)
     for pixel in range(1, PIX):
         pooled = pooled + img_ref[pixel].astype(FULL)
@@ -253,11 +258,20 @@
         for expert in range(1, EXPERTS):
             total = total + columns[expert] * depth_ref[tap, expert : expert + 1, :]
         kern[tap] = total
-    product = dot_nt(routed[...].reshape(ROWS, EXPERTS * C_IN), expand_ref[...])
-    hidden_full[...] = product.reshape(PIX, GROUP, C_MID)
-
-    def chunk(index, carry):
-        lanes = pl.ds(pl.multiple_of(index * 128, 128), 128)
+    flat = routed[...].reshape(ROWS, EXPERTS * C_IN)
+    third = C_MID // 3
+
+    @pl.when(pl.program_id(0) == 0)
+    def _():
+        for copy in pair_copies(source, expand_ref, sem):
+            copy.wait()
+
+    def multiply(part):
+        place = slice(part * third, (part + 1) * third)
+        hidden_full[:, :, place] = dot_nt(flat, expand_ref[place]).reshape(PIX, GROUP, third)
+
+    def chunk(index):
+        lanes = slice(index * 128, index * 128 + 128)
         taps = [kern[tap, :, lanes] for tap in range(KSIZE * KSIZE)]
         start = [None] * PIX
 
@@ -282,9 +296,13 @@
                 pooled_act = pooled_act + act
                 act_full[pixel, :, lanes] = act
         pooled_act_ref[:, lanes] = pooled_act * (1.0 / PIX)
-        return carry
-
-    lax.fori_loop(0, C_MID // 128, chunk, 0)
+
+    multiply(0)
+    for part in range(3):
+        if part < 2:
+            multiply(part + 1)
+        for index in range(3 * part, 3 * part + 3):
+            chunk(index)
     squeeze = dot_nt(pooled_act_ref[...], excite_ref[0], HIGH) + bias_se_ref[...]
     squeeze_ref[...] = squeeze
     gate = sig(dot_nn(squeeze * sig(squeeze), excite_ref[1], HIGH) + bias_ex_ref[...])
@@ -294,7 +312,7 @@
         scaled_ref[pixel] = (act_full[pixel] * gate).astype(LOW)
         return carry
 
-    lax.fori_loop(0, PIX, finish, 0)
+    lax.fori_loop(0, PIX, finish, 0, unroll=7)
 
 
 def expand_forward(img_two, hot, router, expand_low, depth_full, excite, bias_se, bias_ex):
@@ -305,7 +323,7 @@
         images // GROUP,
         [
             images_block(2 * C_IN), group_block(EXPERTS), whole(EXPERTS, C_IN),
-            whole(C_MID, EXPERTS * C_IN), whole(KSIZE * KSIZE, EXPERTS, C_MID),
+            pl.BlockSpec(memory_space=pl.ANY), whole(KSIZE * KSIZE, EXPERTS, C_MID),
             whole(2, C_SE, C_MID), whole(1, C_SE), whole(1, C_MID),
         ],
         [
@@ -322,6 +340,7 @@
         [
             pltpu.VMEM((PIX, GROUP, EXPERTS * C_IN), LOW), pltpu.VMEM((PIX, GROUP, C_MID), FULL),
             pltpu.VMEM((PIX, GROUP, C_MID), FULL), pltpu.VMEM((KSIZE * KSIZE, GROUP, C_MID), FULL),
+            pltpu.VMEM((C_MID, EXPERTS * C_IN), LOW), pltpu.SemaphoreType.DMA((PAIRS,)),
         ],
         2 * PIX * images * EXPERTS * C_IN * C_MID,
         PIX * images * 4 * C_MID * 2,
@@ -343,6 +362,16 @@
         copy.wait()
 
 
+def pair_copies(source, stacked, sem):
+    width = source.shape[2]
+    return [
+        pltpu.make_async_copy(
+            source.at[pair], stacked.at[:, pair * width : (pair + 1) * width], sem.at[pair]
+        )
+        for pair in range(PAIRS)
+    ]
+
+
 def project_kernel(
     scaled_ref, source, pair_ref, each_ref, before_ref, sums_ref, product, weight_ref, sem
 ):
@@ -354,28 +383,20 @@
         stack_experts(source, weight_ref, sem)
         sums_ref[...] = jnp.zeros_like(sums_ref)
 
+    total = None
     for part in range(2):
-        product[part] = dot_nt(flat, weight_ref[part * half : (part + 1) * half]).reshape(
-            PIX, GROUP, half
-        )
-    scales = [pair_ref[pair].astype(FULL) for pair in range(PAIRS)]
-
-    def mix(pixel, carry):
-        plain, square = carry
-        total = jnp.zeros((GROUP, 2 * C_OUT), FULL)
-        for pair in range(PAIRS):
-            part, place = pair // 2, pair % 2 * 2 * C_OUT
-            value = product[part, pixel, :, place : place + 2 * C_OUT]
-            each_ref[pixel, :, pair * 2 * C_OUT : (pair + 1) * 2 * C_OUT] = value.astype(LOW)
-            total = total + value * scales[pair]
-        before = (total + pltpu.roll(total, C_OUT, 1))[:, :C_OUT]
-        before_ref[pixel] = before
-        return plain + before, square + before * before
-
-    zero = jnp.zeros((GROUP, C_OUT), FULL)
-    plain, square = lax.fori_loop(0, PIX, mix, (zero, zero))
-    sums_ref[0:1] += jnp.sum(plain, axis=0, keepdims=True)
-    sums_ref[1:2] += jnp.sum(square, axis=0, keepdims=True)
+        value = dot_nt(flat, weight_ref[part * half : (part + 1) * half])
+        value = value.reshape(PIX, GROUP, half)
+        each_ref[:, :, part * half : (part + 1) * half] = value.astype(LOW)
+        for side in range(2):
+            term = value[:, :, side * 2 * C_OUT : (side + 1) * 2 * C_OUT]
+            term = term * pair_ref[2 * part + side].astype(FULL)[None]
+            total = term if total is None else total + term
+    total = total.reshape(ROWS, 2 * C_OUT)
+    before = (total + pltpu.roll(total, C_OUT, 1))[:, :C_OUT]
+    before_ref[...] = before.reshape(PIX, GROUP, C_OUT)
+    sums_ref[0:1] += jnp.sum(before, axis=0, keepdims=True)
+    sums_ref[1:2] += jnp.sum(before * before, axis=0, keepdims=True)
 
 
 def project_forward(scaled, project_low, pair_out):
@@ -468,22 +489,26 @@
 ):
     step = pl.program_id(0)
     rows = pl.ds(pl.multiple_of(step * GROUP, GROUP), GROUP)
-    gain, shift, inv, offset = (norm_ref[k : k + 1] for k in range(4))
-
-    def pixel_sums(pixel, carry):
-        total, slope, moved = carry
-        value = widened_ref[pixel].astype(FULL)
-        lifted = value * gain + shift
-        part = sig(lifted)
-        grown = lifted * part
-        bent = part + grown * (1.0 - part)
-        return total + grown, slope + bent, moved + bent * (value * inv + offset)
-
-    zero = jnp.zeros((GROUP, C_HEAD), FULL)
-    total, slope, moved = lax.fori_loop(0, PIX, pixel_sums, (zero, zero, zero))
-    silu_sum[rows] = total
-    slope_sum[rows] = slope
-    cross_sum[rows] = moved
+
+    def chunk(index, carry):
+        lanes = pl.ds(pl.multiple_of(index * 128, 128), 128)
+        gain, shift, inv, offset = (norm_ref[k : k + 1, lanes] for k in range(4))
+        total = slope = moved = jnp.zeros((GROUP, 128), FULL)
+        for pixel in range(PIX):
+            value = widened_ref[pixel, :, lanes].astype(FULL)
+            lifted = value * gain + shift
+            part = sig(lifted)
+            grown = lifted * part
+            bent = part + grown * (1.0 - part)
+            total = total + grown
+            slope = slope + bent
+            moved = moved + bent * (value * inv + offset)
+        silu_sum[rows, lanes] = total
+        slope_sum[rows, lanes] = slope
+        cross_sum[rows, lanes] = moved
+        return carry
+
+    lax.fori_loop(0, C_HEAD // 128, chunk, 0)
 
     @pl.when(step == pl.num_programs(0) - 1)
     def _():
@@ -558,29 +583,21 @@
         grad_wide_ref[pixel] = grad.astype(LOW)
         return carry
 
-    lax.fori_loop(0, PIX, widen, 0)
+    lax.fori_loop(0, PIX, widen, 0, unroll=7)
     flat = grad_wide_ref[...].reshape(ROWS, C_HEAD)
+    twice = twice_ref[...].astype(FULL)
     route_sums = []
+    total = None
     for part in range(2):
-        product[part] = dot_nn(flat, weight_ref[:, part * half : (part + 1) * half]).reshape(
-            PIX, GROUP, half
-        )
-    scales = [pair_ref[pair].astype(FULL) for pair in range(PAIRS)]
-
-    def mix(pixel, carry):
-        twice = twice_ref[pixel].astype(FULL)
-        total = jnp.zeros((GROUP, 2 * C_OUT), FULL)
-        found = []
-        for pair in range(PAIRS):
-            part, place = pair // 2, pair % 2 * 2 * C_OUT
-            value = product[part, pixel, :, place : place + 2 * C_OUT]
-            total = total + value * scales[pair]
-            found.append(carry[pair] + value * twice)
-        mixed[pixel] = (total + pltpu.roll(total, C_OUT, 1))[:, :C_OUT]
-        return tuple(found)
-
-    zero = jnp.zeros((GROUP, 2 * C_OUT), FULL)
-    route_sums = lax.fori_loop(0, PIX, mix, (zero,) * PAIRS)
+        value = dot_nn(flat, weight_ref[:, part * half : (part + 1) * half])
+        value = value.reshape(PIX, GROUP, half)
+        for side in range(2):
+            piece = value[:, :, side * 2 * C_OUT : (side + 1) * 2 * C_OUT]
+            route_sums.append(jnp.sum(piece * twice, axis=0))
+            term = piece * pair_ref[2 * part + side].astype(FULL)[None]
+            total = term if total is None else total + term
+    total = total.reshape(ROWS, 2 * C_OUT)
+    mixed[...] = (total + pltpu.roll(total, C_OUT, 1))[:, :C_OUT].reshape(PIX, GROUP, C_OUT)
     route = route_ref[...]
     grad_route = pair_columns(route_sums, C_OUT) + balance_ref[...]
     logit = grad_route * route * (1.0 - route)
@@ -595,7 +612,7 @@
         return plain + grad, cross + grad * hat
 
     zero = jnp.zeros((GROUP, C_OUT), FULL)
-    plain, cross = lax.fori_loop(0, PIX, close, (zero, zero))
+    plain, cross = lax.fori_loop(0, PIX, close, (zero, zero), unroll=7)
     sums_ref[0:1] += jnp.sum(plain, axis=0, keepdims=True)
     sums_ref[1:2] += jnp.sum(cross, axis=0, keepdims=True)
 
@@ -628,16 +645,21 @@
 
 
 def kern_grad_kernel(grad_ref, twice_ref, pair_ref, out_ref, turned, routed):
-    images = twice_ref.shape[1]
+    images, width = twice_ref.shape[1:]
 
     @pl.when(pl.program_id(0) == 0)
     def _():
         turned[...] = grad_ref[...].reshape(turned.shape[1], turned.shape[0]).T
 
-    scale = pair_ref[0]
-    for pixel in range(PIX):
-        routed[pixel * images : (pixel + 1) * images] = twice_ref[pixel] * scale
-    out_ref[0] = dot_nn(turned[...], routed[...]).astype(LOW)
+    for side in range(2):
+        scale = pair_ref[side]
+        for pixel in range(PIX):
+            routed[pixel * images : (pixel + 1) * images, side * width : (side + 1) * width] = (
+                twice_ref[pixel] * scale
+            )
+    product = dot_nn(turned[...], routed[...])
+    for side in range(2):
+        out_ref[side] = product[:, side * width : (side + 1) * width].astype(LOW)
 
 
 def kern_grad(grad, twice, pair_scales, name):
@@ -646,14 +668,14 @@
     return device_kernel(
         kern_grad_kernel,
         name,
-        PAIRS,
+        PAIRS // 2,
         [
             whole(PIX, images, out_width), whole(PIX, images, width),
-            pl.BlockSpec((1, images, width), lambda i: (i, 0, 0)),
+            pl.BlockSpec((2, images, width), lambda i: (i, 0, 0)),
         ],
         [((PAIRS, out_width, width), LOW)],
-        [pl.BlockSpec((1, out_width, width), lambda i: (i, 0, 0))],
-        [pltpu.VMEM((out_width, rows), LOW), pltpu.VMEM((rows, width), LOW)],
+        [pl.BlockSpec((2, out_width, width), lambda i: (i, 0, 0))],
+        [pltpu.VMEM((out_width, rows), LOW), pltpu.VMEM((rows, 2 * width), LOW)],
         2 * rows * out_width * PAIRS * width,
         rows * out_width * 2,
     )(grad, twice, pair_scales)[0]
@@ -668,14 +690,17 @@
 
     for side in range(2):
         routed[side * C_OUT : (side + 1) * C_OUT] = turned[...] * scale_ref[0, side : side + 1]
-    product = dot_nn(routed[...], scaled_ref[...].reshape(rows, C_MID)).astype(LOW)
+    product = dot_nn(routed[...], scaled_ref[...].reshape(rows, C_MID))
+    owners, _, height, _ = out_ref.shape
     for side in range(2):
-        out_ref[0, :, side * C_MID : (side + 1) * C_MID] = product[
-            side * C_OUT : (side + 1) * C_OUT
-        ]
-
-
-def project_grad(grad, scaled, scale):
+        for owner in range(owners):
+            place = side * C_OUT + owner * height
+            out_ref[owner, 0, :, side * C_MID : (side + 1) * C_MID] = product[
+                place : place + height
+            ].astype(LOW)
+
+
+def project_grad(grad, scaled, scale, owners):
     images = grad.shape[1]
     rows = PIX * images
     return device_kernel(
@@ -686,8 +711,8 @@
             whole(PIX, images, C_OUT), whole(PIX, images, C_MID),
             pl.BlockSpec((1, 2, rows), lambda i: (i, 0, 0)),
         ],
-        [((PAIRS, C_OUT, 2 * C_MID), LOW)],
-        [pl.BlockSpec((1, C_OUT, 2 * C_MID), lambda i: (i, 0, 0))],
+        [((owners, PAIRS, C_OUT // owners, 2 * C_MID), LOW)],
+        [pl.BlockSpec((owners, 1, C_OUT // owners, 2 * C_MID), lambda i: (0, i, 0, 0))],
         [pltpu.VMEM((C_OUT, rows), LOW), pltpu.VMEM((2 * C_OUT, rows), LOW)],
         2 * rows * EXPERTS * C_OUT * C_MID,
         rows * (C_OUT + C_MID) * 2,
@@ -723,7 +748,7 @@
         return tuple(found)
 
     zero = jnp.zeros((GROUP, 2 * C_OUT), FULL)
-    route_sums = lax.fori_loop(0, PIX, turn, (zero,) * PAIRS)
+    route_sums = lax.fori_loop(0, PIX, turn, (zero,) * PAIRS, unroll=7)
     route_ref[...] = pair_columns(route_sums, C_OUT)
     product = dot_nn(routed[...].reshape(ROWS, EXPERTS * C_OUT), weight_ref[...])
     grad_scaled_ref[...] = product.reshape(PIX, GROUP, C_MID).astype(LOW)
@@ -755,12 +780,14 @@
 
 def expand_back_kernel(
     grad_scaled_ref, turned_ref, hidden_ref, img_ref, gate_ref, squeeze_ref, excite_ref, depth_ref,
-    route_ref, route_part_ref, balance_ref, weight_ref,
+    route_ref, route_part_ref, balance_ref, source,
     grad_hidden_ref, logit_ref, grad_gate_ref, grad_squeeze_ref, grad_depth_ref,
-    kern, start, grad_turned, grad_kern, pooled, product,
+    kern, start, grad_turned, grad_kern, pooled, product, weight_ref, sem,
 ):
     @pl.when(pl.program_id(0) == 0)
     def _():
+        for copy in pair_copies(source, weight_ref, sem):
+            copy.start()
         grad_depth_ref[...] = jnp.zeros_like(grad_depth_ref)
 
     route = route_ref[...]
@@ -777,7 +804,7 @@
         return carry + grad_scaled_ref[pixel].astype(FULL) * (value * sig(value))
 
     gate = gate_ref[...]
-    grad_gate = lax.fori_loop(0, PIX, gate_sum, jnp.zeros((GROUP, C_MID), FULL))
+    grad_gate = lax.fori_loop(0, PIX, gate_sum, jnp.zeros((GROUP, C_MID), FULL), unroll=7)
     grad_gate = grad_gate * gate * (1.0 - gate)
     grad_gate_ref[...] = grad_gate
     squeeze = squeeze_ref[...]
@@ -786,26 +813,33 @@
     grad_squeeze_ref[...] = grad_squeeze
     pooled[...] = dot_nn(grad_squeeze, excite_ref[0], HIGH) * (1.0 / PIX)
 
-    def chunk(index, carry):
-        lanes = pl.ds(pl.multiple_of(index * 128, 128), 128)
+    third = C_MID // 3
+
+    @pl.when(pl.program_id(0) == 0)
+    def _():
+        for copy in pair_copies(source, weight_ref, sem):
+            copy.wait()
+
+    def chunk(index):
+        lanes = slice(index * 128, index * 128 + 128)
         gate_part = gate_ref[:, lanes]
         pooled_part = pooled[:, lanes]
         for pixel in range(PIX):
             value = turned_ref[pixel, :, lanes].astype(FULL)
             part = sig(value)
             grad = grad_scaled_ref[pixel, :, lanes].astype(FULL) * gate_part + pooled_part
-            grad_turned[pixel] = grad * (part + value * part * (1.0 - part))
+            grad_turned[index % 2, pixel] = grad * (part + value * part * (1.0 - part))
             value = hidden_ref[pixel, :, lanes].astype(FULL)
-            start[pixel] = value * sig(value)
+            start[index % 2, pixel] = value * sig(value)
         taps = [kern[tap, :, lanes] for tap in range(KSIZE * KSIZE)]
         sums = [None] * (KSIZE * KSIZE)
         for pixel in range(PIX):
             total = None
-            here = grad_turned[pixel]
+            here = grad_turned[index % 2, pixel]
             for tap, source in taps_of(pixel):
-                term = start[source] * here
+                term = start[index % 2, source] * here
                 sums[tap] = term if sums[tap] is None else sums[tap] + term
-                term = grad_turned[source] * taps[KSIZE * KSIZE - 1 - tap]
+                term = grad_turned[index % 2, source] * taps[KSIZE * KSIZE - 1 - tap]
                 total = term if total is None else total + term
             value = hidden_ref[pixel, :, lanes].astype(FULL)
             part = sig(value)
@@ -813,18 +847,25 @@
             grad_hidden_ref[pixel, :, lanes] = grad.astype(LOW)
         for tap in range(KSIZE * KSIZE):
             grad_kern[tap, :, lanes] = sums[tap]
-        return carry
-
-    lax.fori_loop(0, C_MID // 128, chunk, 0)
+
+    for part in range(3):
+        for index in range(3 * part, 3 * part + 3):
+            chunk(index)
+        inner = slice(part * third, (part + 1) * third)
+        term = dot_nn(grad_hidden_ref[:, :, inner].reshape(ROWS, third), weight_ref[inner])
+        term = term.reshape(PIX, GROUP, EXPERTS * C_IN)
+        product[...] = term if part == 0 else product[...] + term
+    place = lax.broadcasted_iota(jnp.int32, (GROUP, EXPERTS), 1)
     depth_term = jnp.zeros((GROUP, EXPERTS), FULL)
-    for tap in range(KSIZE * KSIZE):
-        value = grad_kern[tap]
-        grad_depth_ref[tap] += dot_tn(low, value, HIGH)
-        depth_term = depth_term + dot_nt(value, depth_ref[tap], HIGH)
-    product[...] = dot_nn(grad_hidden_ref[...].reshape(ROWS, C_MID), weight_ref[...]).reshape(
-        PIX, GROUP, EXPERTS * C_IN
-    )
-
+    for expert in range(EXPERTS):
+        total = jnp.zeros((GROUP, C_MID), FULL)
+        for tap in range(KSIZE * KSIZE):
+            value = grad_kern[tap]
+            total = total + value * depth_ref[tap, expert : expert + 1, :]
+            weighed = value * columns[expert]
+            grad_depth_ref[tap, expert : expert + 1, :] += jnp.sum(weighed, axis=0, keepdims=True)
+        total = jnp.sum(total, axis=1, keepdims=True)
+        depth_term = depth_term + jnp.where(place == expert, total, 0.0)
     def route_part(pixel, carry):
         value = img_ref[pixel].astype(FULL)
         return tuple(
@@ -833,7 +874,7 @@
         )
 
     zero = jnp.zeros((GROUP, 2 * C_IN), FULL)
-    route_sums = lax.fori_loop(0, PIX, route_part, (zero,) * PAIRS)
+    route_sums = lax.fori_loop(0, PIX, route_part, (zero,) * PAIRS, unroll=7)
     grad_route = (
         pair_columns(route_sums, C_IN) + route_part_ref[...] + depth_term + balance_ref[...]
     )
@@ -854,7 +895,7 @@
             images_block(C_MID), images_block(C_MID), images_block(C_MID), images_block(2 * C_IN),
             group_block(C_MID), group_block(C_SE), whole(2, C_SE, C_MID),
             whole(taps, EXPERTS, C_MID), group_block(EXPERTS), group_block(EXPERTS),
-            whole(1, EXPERTS), whole(C_MID, EXPERTS * C_IN),
+            whole(1, EXPERTS), pl.BlockSpec(memory_space=pl.ANY),
         ],
         [
             ((PIX, images, C_MID), LOW), ((images, EXPERTS), FULL), ((images, C_MID), FULL),
@@ -865,9 +906,10 @@
             total_block(taps, EXPERTS, C_MID),
         ],
         [
-            pltpu.VMEM((taps, GROUP, C_MID), FULL), pltpu.VMEM((PIX, GROUP, 128), FULL),
-            pltpu.VMEM((PIX, GROUP, 128), FULL), pltpu.VMEM((taps, GROUP, C_MID), FULL),
+            pltpu.VMEM((taps, GROUP, C_MID), FULL), pltpu.VMEM((2, PIX, GROUP, 128), FULL),
+            pltpu.VMEM((2, PIX, GROUP, 128), FULL), pltpu.VMEM((taps, GROUP, C_MID), FULL),
             pltpu.VMEM((GROUP, C_MID), FULL), pltpu.VMEM((PIX, GROUP, EXPERTS * C_IN), FULL),
+            pltpu.VMEM((C_MID, EXPERTS * C_IN), LOW), pltpu.SemaphoreType.DMA((PAIRS,)),
         ],
         2 * PIX * images * EXPERTS * C_IN * C_MID,
         PIX * images * 4 * C_MID * 2,
@@ -1038,6 +1080,121 @@
     more = count // pairs
     cube = pieces.reshape(pairs, more, rows, width).transpose(0, 2, 1, 3)
     return cube.reshape(pairs, rows, width * more)
+
+
+def send_around(value, hop):
+    count = lax.axis_size("dp")
+    return lax.ppermute(value, "dp", [(at, (at + hop) % count) for at in range(count)])
+
+
+def scatter_sum(pieces):
+    count, me = lax.axis_size("dp"), lax.axis_index("dp")
+    total = lax.dynamic_index_in_dim(pieces, me, 0, keepdims=False).astype(FULL)
+    arrived = [
+        send_around(lax.dynamic_index_in_dim(pieces, (me + hop) % count, 0, keepdims=False), hop)
+        for hop in range(1, count)
+    ]
+    return total, arrived
+
+
+def add_arrived(total, arrived):
+    for part in arrived:
+        total = total + part.astype(FULL)
+    return total.astype(LOW)
+
+
+def spread_sum(piece):
+    count, me = lax.axis_size("dp"), lax.axis_index("dp")
+    found = jnp.zeros((count,) + piece.shape, piece.dtype)
+    for hop in range(count):
+        part = piece if hop == 0 else send_around(piece, hop)
+        found = lax.dynamic_update_index_in_dim(found, part, (me - hop) % count, 0)
+    return found
+
+
+def gather_kernel(n_wide, n_dp, weight_ref, depth_ref, out_ref, depth_out, send, recv):
+    lines = n_wide // 2
+    me_wide, me_dp = lax.axis_index("wide"), lax.axis_index("dp")
+    core, line = lax.rem(me_wide, 2), lax.div(me_wide, 2)
+    sibling = {"wide": line * 2 + 1 - core}
+    width = out_ref.shape[4]
+    used = [0]
+
+    barrier = pltpu.get_barrier_semaphore()
+    for k in range(1, n_wide):
+        pl.semaphore_signal(
+            barrier, inc=1, device_id={"wide": lax.rem(me_wide + k, n_wide)}, device_id_type=MESH
+        )
+    for k in range(1, n_dp):
+        pl.semaphore_signal(
+            barrier, inc=1, device_id={"dp": lax.rem(me_dp + k, n_dp)}, device_id_type=MESH
+        )
+    for piece in range(n_dp):
+        out_ref[piece, line, core] = weight_ref[:, piece * width : (piece + 1) * width].astype(LOW)
+    depth_out[me_wide] = depth_ref[...]
+    pl.semaphore_wait(barrier, n_wide + n_dp - 2)
+
+    def launch(part, device, ref=out_ref):
+        copy = pltpu.make_async_remote_copy(
+            src_ref=ref.at[part], dst_ref=ref.at[part], send_sem=send.at[used[0]],
+            recv_sem=recv.at[used[0]], device_id=device, device_id_type=MESH,
+        )
+        used[0] += 1
+        copy.start()
+        return copy
+
+    def dp_from(hop):
+        return lax.rem(me_dp + n_dp - hop, n_dp)
+
+    along = [
+        launch((me_dp, line, core), {"wide": lax.rem(line + k, lines) * 2 + core})
+        for k in range(1, lines)
+    ]
+    started = [launch((piece, line, core), sibling) for piece in range(n_dp)]
+    started += [
+        launch((me_wide,), {"wide": lax.rem(me_wide + k, n_wide)}, depth_out)
+        for k in range(1, n_wide)
+    ]
+    across = []
+    for k in range(1, lines):
+        source = lax.rem(line + lines - k, lines)
+        along[k - 1].wait_recv()
+        for hop in range(1, n_dp):
+            copy = launch((me_dp, source, core), {"dp": lax.rem(me_dp + hop, n_dp)})
+            across.append((copy, hop, source))
+        started.append(launch((me_dp, source, core), sibling))
+    for copy, hop, source in across:
+        copy.wait_recv()
+        started.append(launch((dp_from(hop), source, core), sibling))
+    for copy in started:
+        copy.wait()
+    for copy in along:
+        copy.wait_send()
+    for copy, _, _ in across:
+        copy.wait_send()
+
+
+def gather_expand(weight, depth, ident):
+    n_wide, n_dp = lax.axis_size("wide"), lax.axis_size("dp")
+    lines = n_wide // 2
+    height, width = weight.shape
+    copies = (lines - 1) * (1 + n_dp) + (lines - 1) * (n_dp - 1) + n_dp + n_wide - 1
+    vmem = pl.BlockSpec(memory_space=pltpu.VMEM)
+    found, depths = pl.pallas_call(
+        functools.partial(gather_kernel, n_wide, n_dp),
+        name="gather_expand",
+        out_shape=[
+            jax.ShapeDtypeStruct((n_dp, lines, 2, height, width // n_dp), LOW),
+            jax.ShapeDtypeStruct((n_wide,) + depth.shape, LOW),
+        ],
+        in_specs=[vmem] * 2,
+        out_specs=[vmem] * 2,
+        scratch_shapes=[pltpu.SemaphoreType.DMA((copies,)), pltpu.SemaphoreType.DMA((copies,))],
+        compiler_params=pltpu.CompilerParams(
+            collective_id=ident, has_side_effects=True, vmem_limit_bytes=VMEM_CAP
+        ),
+    )(weight, depth)
+    return found.reshape(n_dp, n_wide * height, width // n_dp), depths
 
 
 def soap_kernel(
@@ -1188,17 +1345,21 @@
     images_here = images.shape[0]
     every = images.shape[0] * lax.axis_size("dp") * lax.axis_size("wide")
     count = every * PIX
+    n_wide, n_dp = lax.axis_size("wide"), lax.axis_size("dp")
     bias_se, bias_ex, gain_one, shift_one, gain_two, shift_two, bias_cls = split_gains(gains_weight)
     hot = boost * (dom_label[:, None] == jnp.arange(EXPERTS)[None, :]).astype(jnp.float32)
     img = images.transpose(1, 0, 2)
     img_two = jnp.concatenate([img, img], axis=2)
-    expand_low = lax.all_gather(expand_weight.astype(low_type), "wide", axis=0, tiled=True)
     project_low = lax.all_gather(project_weight.astype(low_type), "wide", axis=0, tiled=True)
     head_low = lax.all_gather(head_weight.astype(low_type), "wide", axis=0, tiled=True)
     class_low = lax.all_gather(classifier_weight.astype(low_type), "wide", axis=0, tiled=True)
-    depth_own = depth_weight.astype(low_type).transpose(2, 0, 1).reshape(depth_weight.shape[2], -1)
-    depth_low = lax.all_gather(depth_own, "wide", axis=0, tiled=True)
-    depth_full = depth_low.reshape(C_MID, EXPERTS, KSIZE * KSIZE).transpose(2, 1, 0).astype(FULL)
+    taps = KSIZE * KSIZE
+    depth_own = depth_weight.transpose(1, 0, 2).reshape(taps * EXPERTS, -1).astype(low_type)
+    depth_own = jnp.pad(depth_own, ((0, -taps * EXPERTS % 16), (0, 0)))
+    expand_low, depth_low = gather_expand(expand_weight, depth_own, 6)
+    expand_low = from_pieces(expand_low, PAIRS)
+    depth_full = depth_low[:, : taps * EXPERTS].reshape(n_wide, taps, EXPERTS, -1)
+    depth_full = depth_full.transpose(1, 2, 0, 3).reshape(taps, EXPERTS, C_MID).astype(FULL)
     excite = excite_weight.transpose(0, 2, 1)
     router = router_weight.T
     router_one, router_two = router[:, :C_IN], router[:, C_IN:]
@@ -1249,9 +1410,8 @@
         widened, grad_feats, coef_two, head_low, pair_two, twice, before, hat_one, route_two,
         balance_grad(means_two, every)[None], router_two,
     )
-    share_class, twice = lax.optimization_barrier((share_class, twice))
     grad_head = kern_grad(grad_widened, twice, pair_two, "head_grad")
-    grad_head, back_one = lax.optimization_barrier((grad_head, back_one))
+    grad_head, back_one, share_class = lax.optimization_barrier((grad_head, back_one, share_class))
     share_head = lax.psum_scatter(grad_head, "wide", scatter_dimension=1, tiled=True)
     grad_router_two = dot_tn(pooled_two, grad_logit_two, HIGH)
     (back_one,) = sum_all((back_one,), 4)
@@ -1263,16 +1423,24 @@
         grad_normed, before, coef_one, pair_one, each, project_low
     )
     row_scale = jnp.tile(route_one.astype(low_type).T, (1, PIX)).reshape(PAIRS, 2, -1)
-    grad_project = project_grad(grad_before, scaled, row_scale)
+    grad_project = project_grad(grad_before, scaled, row_scale, n_wide)
     grad_project, grad_scaled, share_head = lax.optimization_barrier(
         (grad_project, grad_scaled, share_head)
     )
-    share_project = lax.psum_scatter(grad_project, "wide", scatter_dimension=1, tiled=True)
+    wide_head = share_head.shape[2]
+    own_late, arrived = scatter_sum(
+        to_pieces(jnp.concatenate([share_head, share_class], axis=2), n_dp)
+    )
+    share_project = lax.psum_scatter(grad_project, "wide", scatter_dimension=0, tiled=True)[0]
     grad_hidden, grad_logit_one, grad_gate, grad_squeeze, grad_depth = expand_back(
         grad_scaled, turned, hidden, img_two, gate, squeeze, excite, depth_full, route_one,
         route_project, balance_grad(means_one, every)[None], expand_low,
     )
-    share_project, grad_hidden = lax.optimization_barrier((share_project, grad_hidden))
+    arrived, share_project, grad_hidden = lax.optimization_barrier(
+        (arrived, share_project, grad_hidden)
+    )
+    sum_late = spread_sum(add_arrived(own_late, arrived))
+    own_project, arrived = scatter_sum(to_pieces(share_project, n_dp))
     grad_expand = kern_grad(grad_hidden, img_two, pair_in, "expand_grad")
     grad_excite = jnp.stack(
         [
@@ -1284,7 +1452,11 @@
     grad_depth = grad_depth.transpose(1, 0, 2)
     grad_bias_se = jnp.sum(grad_squeeze, axis=0)
     grad_bias_ex = jnp.sum(grad_gate, axis=0)
-    n_wide, n_dp = lax.axis_size("wide"), lax.axis_size("dp")
+    sum_late, arrived, grad_expand = lax.optimization_barrier((sum_late, arrived, grad_expand))
+    sum_late = from_pieces(sum_late, PAIRS)
+    sum_head, sum_class = sum_late[:, :, :wide_head], sum_late[:, :, wide_head:]
+    sum_project = from_pieces(spread_sum(add_arrived(own_project, arrived)), PAIRS)
+    share_expand = lax.psum_scatter(grad_expand, "wide", scatter_dimension=1, tiled=True)
     parts = n_wide * n_dp
     depth_piece = grad_depth.size // parts
     extras = [
@@ -1301,20 +1473,25 @@
     rest_piece = -(-rest_size // parts)
     rest_part = jnp.pad(extras[1], (0, rest_piece * parts - rest_size))
     rest_part = rest_part.reshape(n_dp, n_wide, rest_piece)
-    extra_rows = -(-(depth_piece + rest_piece) // (16 * 384)) * 16
+    extra_rows = -(-(depth_piece + rest_piece) // (16 * 128)) * 16
     extra = jnp.concatenate([depth_part, rest_part], axis=2).astype(low_type)
-    extra = jnp.pad(extra, ((0, 0), (0, 0), (0, extra_rows * 384 - extra.shape[2])))
-    extra = extra.reshape(n_dp, n_wide, extra_rows, 384)
-    pieces = to_pieces(grad_expand, n_dp)
-    pieces = pieces.reshape(n_dp, n_wide, -1, pieces.shape[2])
-    (own_expand, own_extra), own_shares, every_extra = reduce_grads(
-        [pieces, extra],
-        [to_pieces(share, n_dp) for share in (share_project, share_head, share_class)],
-        5,
-    )
-    sum_project, sum_head, sum_class = (from_pieces(share, PAIRS) for share in own_shares)
+    extra = jnp.pad(extra, ((0, 0), (0, 0), (0, extra_rows * 128 - extra.shape[2])))
+    extra = extra.reshape(n_dp, n_wide, extra_rows, 128)
+    head_out = soap(head_weight, sum_head, head_first, head_second, head_state, every)
+    project_out = soap(
+        project_weight, sum_project, project_first, project_second, project_state, every
+    )
+    sum_class = sum_class.transpose(1, 0, 2).reshape(-1, CLASS_PAD)[:, :CLASSES].astype(FULL)
+    class_out = adam(
+        classifier_weight, sum_class, classifier_first, classifier_second, rate_matrix
+    )
+    share_expand, head_out, project_out, class_out = lax.optimization_barrier(
+        (share_expand, head_out, project_out, class_out)
+    )
+    (own_extra,), (own_expand,), every_extra = reduce_grads(
+        [extra], [to_pieces(share_expand, n_dp)], 5
+    )
     sum_expand = from_pieces(own_expand, PAIRS)
-    sum_class = sum_class.transpose(1, 0, 2).reshape(-1, CLASS_PAD)[:, :CLASSES].astype(FULL)
     own_extra = own_extra.reshape(n_dp, -1)[:, :depth_piece].reshape(EXPERTS, KSIZE * KSIZE, -1)
     rest = every_extra.reshape(n_wide, n_dp, -1)[:, :, depth_piece : depth_piece + rest_piece]
     rest = rest.transpose(1, 0, 2).reshape(-1)[:rest_size].astype(FULL)
@@ -1330,15 +1507,8 @@
         [sum_bias, back_one[1], back_one[0], back_two[1], back_two[0], grad_bias_cls[0]]
     )
     expand_out = soap(expand_weight, sum_expand, expand_first, expand_second, expand_state, every)
-    project_out = soap(
-        project_weight, sum_project, project_first, project_second, project_state, every
-    )
-    head_out = soap(head_weight, sum_head, head_first, head_second, head_state, every)
     depth_out = adam(
         depth_weight, own_extra.astype(FULL), depth_first, depth_second, rate_matrix
-    )
-    class_out = adam(
-        classifier_weight, sum_class, classifier_first, classifier_second, rate_matrix
     )
     excite_out = adam(excite_weight, sum_excite, excite_first, excite_second, rate_matrix)
     router_out = adam(router_weight, sum_router, router_first, router_second, rate_matrix)

time: 788 us -> 638 us (0.81)
  Pallas kernels: 608 us -> 519 us
  waiting for transfers between devices: 49 us -> 9.95 us
  blocking collectives: 16.8 us -> 0 us
  starting transfers between devices: 0.29 us -> 16.2 us
  local copies, waits for them, and re-layouts: 44.6 us -> 32.8 us
    pallas_call x1, Pallas kernels: 89.2 us -> 31 us  [reduce_grads(): pl.pallas_call(functools.partial(reduce_kernel, n_wide, n_dp, len(fulls),...]
    pallas_call x2 -> x3, Pallas kernels: 58.7 us -> 89.1 us  [the longest x2 51.8 us: kern_grad(): device_kernel(kern_grad_kernel, name, PAIRS // 2, [whole(PIX, images, out...]
    pallas_call x1, Pallas kernels: 63.3 us -> 40.2 us  [head_back(): device_kernel(head_back_kernel, 'head_back', images // GROUP, [images_blo...]
    all_gather x1, waiting for transfers between devices: 21 us -> 0.02 us  [local(): lax.all_gather(project_weight.astype(low_type), 'wide', axis=0, tiled=True)]
    all_gather x1 -> x0, waiting for transfers between devices: 19.8 us -> none  [local(): lax.all_gather(expand_weight.astype(low_type), 'wide', axis=0, tiled=True)]
    all_gather x1 -> x0, blocking collectives: 16.8 us -> none  [local(): depth_low = lax.all_gather(depth_own, 'wide', axis=0, tiled=True)]
    pallas_call x1, Pallas kernels: 46.7 us -> 30.2 us  [project_forward(): device_kernel(project_kernel, 'project_forward', images // GROUP, [images...]
    pallas_call x1, Pallas kernels: 54.8 us -> 38.4 us  [project_back(): device_kernel(project_back_kernel, 'project_back', images // GROUP, [imag...]
  transfers between devices with their start and end apart: 7 -> 19, of which waited for: 3 -> 2; matrix products, arithmetic and copies ran while one was open for 5% -> 7% of each run, Pallas kernels for 49% -> 72%
where the time goes in v4:
time: 638 us; the launch traced here: 633 us
  Pallas kernels  519 us (81%)
  local copies, waits for them, and re-layouts  32.8 us (5%)
  other arithmetic  29.3 us (5%)
  between operations  20.1 us (3%)
  starting transfers between devices  16.2 us (3%)
  waiting for transfers between devices  9.95 us (2%)
    pallas_call x1, Pallas kernels, expand_back(): device_kernel(expand_back_kernel, 'expand_back', images // GROUP, [images...  62.5 us
    pallas_call x3, Pallas kernels, soap(): device_kernel(functools.partial(soap_kernel, gained), 'soap', PAIRS, [col...  59.3 us
    pallas_call x4, Pallas kernels, sum_all(): pl.pallas_call(functools.partial(sum_kernel, n_wide, n_dp), out_shape=jax...  55 us
    pallas_call x2, Pallas kernels, kern_grad(): device_kernel(kern_grad_kernel, name, PAIRS // 2, [whole(PIX, images, out...  51.8 us
    pallas_call x1, Pallas kernels, head_back(): device_kernel(head_back_kernel, 'head_back', images // GROUP, [images_blo...  40.2 us
    pallas_call x1, Pallas kernels, expand_forward(): device_kernel(expand_kernel, 'expand_forward', images // GROUP, [images_b...  40.1 us
    pallas_call x1, Pallas kernels, project_back(): device_kernel(project_back_kernel, 'project_back', images // GROUP, [imag...  38.4 us
    pallas_call x1, Pallas kernels, gather_expand(): pl.pallas_call(functools.partial(gather_kernel, n_wide, n_dp), name='gath...  37.3 us
  transfers between devices with their start and end apart: 19, of which 2 were waited for; matrix products, arithmetic and copies ran while one was open for 7% of the time, Pallas kernels for 72%

profile of v4, /device:TPU:0, one launch (start us, length us, event | category | flops | bytes accessed | tf_op | source)
XLA Modules:
  0.0 632.9 jit_solution(3000206266334216037)
XLA Ops:
  7.3 2.4 convert_element_type.117
  14.3 2.4 pad_maximum_fusion.1.img_ref.twice_ref
  18.0 37.3 %gather_expand.1 = (bf16[4,4,2,144,384]{4,3,2,1,0:T(8,128)(2,1)}, bf16[8,80,144]{2,1,0:T(8,128)(2,1)}) custom-call(f32[144,1536]{1,0:T(8,128)} %weight_ref.7, bf16[80,144]{1,0:T(8,128)(2,1)} %pad.29.depth_ref), custom_call_target="tpu_custom_call" | custom-call | tf_op jit(solution)/shard_map/gather_expand/pallas_call | solution.py:1183
  58.8 40.1 %expand_forward.1 = (bf16[49,64,1152]{2,1,0:T(8,128)(2,1)}, bf16[49,64,1152]{2,1,0:T(8,128)(2,1)}, bf16[49,64,1152]{2,1,0:T(8,128)(2,1)}, f32[64,8]{1,0:T(8,128)...) custom-call(bf16[49,64,384]{2,1,0:T(8,128)(2,1)} %pad_maximum_fusion, ...), custom_call_target="tpu_custom_call" | custom-call | flops 11098128384 | bytes 28901376 | tf_op jit(solution)/shard_map/expand_forward/pallas_call | solution.py:320
  98.9 30.2 %project_forward.1 = (bf16[49,64,2560]{2,1,0:T(8,128)(2,1)}, f32[49,64,320]{2,1,0:T(8,128)}, f32[2,320]{1,0:T(2,128)}) custom-call(bf16[49,64,1152]{2,1,0:T(8,128)(2,1)} %get-tuple-element.116.scaled_ref, bf16[320,9216]{1,0:T(8,128)(2,1)} %all-gather.4.cloned.1.call-done.source, bf16[4,64,640]{2,1,0:T(8,128)(2,1)} %get-tuple-element.117.pair_ref), custom_call_target="tpu_custom_call" | custom-call | flops 18496880640 | bytes 23281664 | tf_op jit(solution)/shard_map/project_forward/pallas_call | solution.py:405
  130.5 20.8 %shard_map.501 = f32[8,128]{1,0:T(8,128)} custom-call(f32[8,128]{1,0:T(8,128)} %fusion.41.x_ref), custom_call_target="tpu_custom_call" | custom-call | tf_op jit(solution)/shard_map/pallas_call | solution.py:97
  152.8 6.3 all-gather.6.cloned.1.call-done.weight_ref
  159.1 29.7 %head_forward.1 = (bf16[49,64,1280]{2,1,0:T(8,128)(2,1)}, bf16[49,64,640]{2,1,0:T(8,128)(2,1)}, f32[64,8]{1,0:T(8,128)}, bf16[4,64,640]{2,1,0:T(8,128)(2,1)}, f3...) custom-call(f32[49,64,320]{2,1,0:T(8,128)} %get-tuple-element.118.before_ref, ...), custom_call_target="tpu_custom_call" | custom-call | flops 20552089600 | bytes 10035200 | tf_op jit(solution)/shard_map/head_forward/pallas_call | solution.py:461
  190.8 11.2 %shard_map.502 = f32[24,128]{1,0:T(8,128)} custom-call(f32[24,128]{1,0:T(8,128)} %fusion.35.x_ref), custom_call_target="tpu_custom_call" | custom-call | tf_op jit(solution)/shard_map/pallas_call | solution.py:97
  204.3 15.2 %loss_part.1 = (bf16[64,1280]{1,0:T(8,128)(2,1)}, bf16[64,1024]{1,0:T(8,128)(2,1)}, f32[64,1280]{1,0:T(8,128)}, f32[2,1280]{1,0:T(2,128)}, f32[1,1]{1,0:T(1,128)}, /*index=5*/f32[1,1000]{1,0:T(1,128)}) custom-call(bf16[49,64,1280]{2,1,0:T(8,128)(2,1)} %get-tuple-element.121.widened_ref, f32[8,1280]{1,0:T(8,128)} %stack.82.norm_ref, s32[64,1]{1,0:T(8,128)} %copy.92.label_ref, ...), custom_call_target="tpu_custom_call" | custom-call | flops 327680000 | bytes 8028160 | tf_op jit(solution)/shard_map/loss_part/pallas_call | solution.py:540
  222.9 1.9 pad_maximum_fusion
  226.9 11.5 %shard_map.503 = f32[32,128]{1,0:T(8,128)} custom-call(f32[32,128]{1,0:T(8,128)} %pad_bitcast_fusion.x_ref), custom_call_target="tpu_custom_call" | custom-call | tf_op jit(solution)/shard_map/pallas_call | solution.py:97
  242.9 40.2 %head_back.1 = (bf16[49,64,1280]{2,1,0:T(8,128)(2,1)}, f32[49,64,320]{2,1,0:T(8,128)}, f32[64,8]{1,0:T(8,128)}, f32[2,320]{1,0:T(2,128)}) custom-call(bf16[49,64,1280]{2,1,0:T(8,128)(2,1)} %get-tuple-element.121.widened_ref, f32[64,1280]{1,0:T(8,128)} %get-tuple-element.130.grad_feats_ref, f32[4,1280]{1,0:T(4,128)} %pad_maximum_fusion.3.coef_ref, ...), custom_call_target="tpu_custom_call" | custom-call | flops 20552089600 | bytes 18063360 | tf_op jit(solution)/shard_map/head_back/pallas_call | solution.py:625
  283.1 32.0 %head_grad.1 = bf16[4,1280,640]{2,1,0:T(8,128)(2,1)} custom-call(bf16[49,64,1280]{2,1,0:T(8,128)(2,1)} %get-tuple-element.135.grad_ref, bf16[49,64,640]{2,1,0:T(8,128)(2,1)} %get-tuple-element.132.twice_ref, bf16[4,64,640]{2,1,0:T(8,128)(2,1)} %get-tuple-element.131.pair_ref), custom_call_target="tpu_custom_call" | custom-call | flops 20552089600 | bytes 8028160 | tf_op jit(solution)/shard_map/head_grad/pallas_call | solution.py:668
  317.4 11.5 %shard_map.504 = f32[8,128]{1,0:T(8,128)} custom-call(f32[8,128]{1,0:T(8,128)} %pad_bitcast_fusion.1.x_ref), custom_call_target="tpu_custom_call" | custom-call | tf_op jit(solution)/shard_map/pallas_call | solution.py:97
  330.9 38.4 %project_back.1 = (bf16[49,64,320]{2,1,0:T(8,128)(2,1)}, bf16[49,64,1152]{2,1,0:T(8,128)(2,1)}, f32[64,8]{1,0:T(8,128)}) custom-call(f32[49,64,320]{2,1,0:T(8,128)} %get-tuple-element.134.grad_ref, f32[49,64,320]{2,1,0:T(8,128)} %get-tuple-element.118.before_ref, f32[3,320]{1,0:T(4,128)} %pad_maximum_fusion.4.coef_ref, ...), custom_call_target="tpu_custom_call" | custom-call | flops 18496880640 | bytes 23281664 | tf_op jit(solution)/shard_map/project_back/pallas_call | solution.py:760
  369.3 28.4 %project_grad.1 = bf16[8,4,40,2304]{3,2,1,0:T(8,128)(2,1)} custom-call(bf16[49,64,320]{2,1,0:T(8,128)(2,1)} %get-tuple-element.140.grad_ref, bf16[49,64,1152]{2,1,0:T(8,128)(2,1)} %get-tuple-element.116.scaled_ref, bf16[4,2,3136]{2,1,0:T(2,128)(2,1)} %tile.9.scale_ref), custom_call_target="tpu_custom_call" | custom-call | flops 18496880640 | bytes 9232384 | tf_op jit(solution)/shard_map/project_grad/pallas_call | solution.py:706
  398.7 1.8 multiply_bitcast_fusion
  402.6 1.7 collective-permute-start.2
  404.3 62.5 %expand_back.1 = (bf16[49,64,1152]{2,1,0:T(8,128)(2,1)}, f32[64,8]{1,0:T(8,128)}, f32[64,1152]{1,0:T(8,128)}, f32[64,48]{1,0:T(8,128)}, f32[9,8,1152]{2,1,0:T(8,128)}) custom-call(bf16[49,64,1152]{2,1,0:T(8,128)(2,1)} %get-tuple-element.144.grad_scaled_ref, bf16[49,64,1152]{2,1,0:T(8,128)(2,1)} %get-tuple-element.145.turned_ref, ...), custom_call_target="tpu_custom_call" | custom-call | flops 11098128384 | bytes 28901376 | tf_op jit(solution)/shard_map/expand_back/pallas_call | solution.py:890
  470.8 2.6 collective-permute-start.5
  474.9 19.8 %expand_grad.1 = bf16[4,1152,384]{2,1,0:T(8,128)(2,1)} custom-call(bf16[49,64,1152]{2,1,0:T(8,128)(2,1)} %get-tuple-element.166.grad_ref, bf16[49,64,384]{2,1,0:T(8,128)(2,1)} %pad_maximum_fusion.1.img_ref.twice_ref, bf16[4,64,384]{2,1,0:T(8,128)(2,1)} %get-tuple-element.167.pair_ref), custom_call_target="tpu_custom_call" | custom-call | flops 11098128384 | bytes 7225344 | tf_op jit(solution)/shard_map/expand_grad/pallas_call | solution.py:668
  494.7 2.9 collective-permute-start.8
  497.9 3.5 collective-permute-done.8
  511.8 1.7 bitcast_dynamic-update-slice_fusion.7
  513.5 2.9 collective-permute-start.9
  518.9 23.5 %soap.3 = (f32[160,2560]{1,0:T(8,128)}, f32[160,2560]{1,0:T(8,128)}, f32[2,8,4,160]{3,2,1,0:T(4,128)}, f32[160,2560]{1,0:T(8,128)}) custom-call(f32[160,2560]{1,0:T(8,128)} %weight_ref.5, bf16[4,160,640]{2,1,0:T(8,128)(2,1)} %slice.148.grad_ref, f32[160,2560]{1,0:T(8,128)} %first_ref.3, f32[160,2560]{1,0:T(8,128)} %second_ref.3, f32[2,8,4,160]{3,2,1,0:T(4,128)} %bitcast.206), custom_call_target="tpu_custom_call" | custom-call | flops 131072000 | bytes 10649600 | tf_op jit(solution)/shard_map/soap/pallas_call | solution.py:1283
  542.4 1.6 multiply_subtract_fusion
  545.0 16.6 %soap.4 = (f32[40,9216]{1,0:T(8,128)}, f32[40,9216]{1,0:T(8,128)}, f32[2,8,4,40]{3,2,1,0:T(4,128)}, f32[40,9216]{1,0:T(8,128)}) custom-call(f32[40,9216]{1,0:T(8,128)} %weight_ref.6, bf16[4,40,2304]{2,1,0:T(8,128)(2,1)} %copy-done.1, f32[40,9216]{1,0:T(8,128)} %first_ref.4, f32[40,9216]{1,0:T(8,128)} %second_ref.4, f32[2,8,4,40]{3,2,1,0:T(4,128)} %bitcast.209), custom_call_target="tpu_custom_call" | custom-call | flops 29491200 | bytes 9584640 | tf_op jit(solution)/shard_map/soap/pallas_call | solution.py:1283
  561.7 31.0 %reduce_grads.1 = (bf16[4,64,128]{2,1,0:T(8,128)(2,1)}, bf16[4,144,384]{2,1,0:T(8,128)(2,1)}, bf16[8,4,64,128]{3,2,1,0:T(8,128)(2,1)}) custom-call(bf16[4,4,2,64,128]{4,3,2,1,0:T(8,128)(2,1)} %bitcast.190, bf16[4,144,384]{2,1,0:T(8,128)(2,1)} %reduce-scatter.11.cloned.1.call-done.refs_1_), custom_call_target="tpu_custom_call" | custom-call | tf_op jit(solution)/shard_map/reduce_grads/pallas_call | solution.py:1047
  594.4 6.3 slice.155
  605.5 19.2 %soap.5 = (f32[144,1536]{1,0:T(8,128)}, f32[144,1536]{1,0:T(8,128)}, f32[2,8,4,144]{3,2,1,0:T(4,128)}, f32[144,1536]{1,0:T(8,128)}) custom-call(f32[144,1536]{1,0:T(8,128)} %weight_ref.7, bf16[4,144,384]{2,1,0:T(8,128)(2,1)} %get-tuple-element.182.grad_ref, f32[144,1536]{1,0:T(8,128)} %first_ref.5, f32[144,1536]{1,0:T(8,128)} %second_ref.5, ...), custom_call_target="tpu_custom_call" | custom-call | flops 63700992 | bytes 5750784 | tf_op jit(solution)/shard_map/soap/pallas_call | solution.py:1283
  (270 shorter events, 55.7 us)
Async XLA Ops:
  7.2 91.7 %all-gather.4.cloned.1.call-start = ((), (), s32[]{:S(2)}) async-start(), calls=%async_computation.4 | async-start | bytes 6635520 | tf_op jit(solution)/shard_map/all_gather | solution.py:1353
  9.7 149.4 %all-gather.6.cloned.1.call-start = ((), (), s32[]{:S(2)}) async-start(), calls=%async_computation.5 | async-start | bytes 7372800 | tf_op jit(solution)/shard_map/all_gather | solution.py:1354
  10.8 193.5 %all-gather.8.cloned.1.call-start = ((), (), s32[]{:S(2)}) async-start(), calls=%async_computation.6 | async-start | bytes 2949120 | tf_op jit(solution)/shard_map/all_gather | solution.py:1355
  11.7 303.4 %reduce-scatter.5.cloned.1.call-start = ((), (), s32[]{:S(2)}) async-start(), calls=%async_computation.7 | async-start | bytes 2949120 | tf_op jit(solution)/shard_map/reduce_scatter | solution.py:1397
  98.9 31.0 %copy-start.55 = (f32[1,8]{1,0:T(1,128)S(1)}, f32[1,8]{1,0:T(1,128)}, u32[]{:S(2)}) copy-start(f32[1,8]{1,0:T(1,128)} %get-tuple-element.120) | copy-start | bytes 100
  224.8 13.6 %copy-start.16 = (f32[24,128]{1,0:T(8,128)S(1)}, f32[24,128]{1,0:T(8,128)}, u32[]{:S(2)}) copy-start(f32[24,128]{1,0:T(8,128)} %shard_map.502) | copy-start | bytes 36868
  224.8 172.9 %reduce-scatter.7.cloned.1.call-start = ((), (), s32[]{:S(2)}) async-start(), calls=%async_computation.8 | async-start | bytes 7372800 | tf_op jit(solution)/shard_map/reduce_scatter | solution.py:1415
  315.1 151.8 %reduce-scatter.9.cloned.1.call-start = ((), (), s32[]{:S(2)}) async-start(), calls=%async_computation.9 | async-start | bytes 6635520 | tf_op jit(solution)/shard_map/reduce_scatter | solution.py:1434
  397.8 163.9 %reduce-scatter.11.cloned.1.call-start = ((), (), s32[]{:S(2)}) async-start(), calls=%async_computation.10 | async-start | bytes 3981312 | tf_op jit(solution)/shard_map/reduce_scatter | solution.py:1459
  400.7 66.1 %collective-permute-start = (bf16[160,896]{1,0:T(8,128)(2,1)S(1)}, bf16[160,896]{1,0:T(8,128)(2,1)S(1)}, u32[]{:S(2)}, u32[]{:S(2)}) collective-permute-start(bf16[160,896]{1,0:T(8,128)(2,1)S(1)} %get-tuple-element.265), channel_id=1, source_target_pairs={{0,8},{8,16},{16,24},{24,0},{1,9},{9,17},{17,25},{25,1},{2,10},{10... | collective-permute-start | bytes 860168 | tf_op jit(solution)/shard_map/ppermute | solution.py:1087
  401.4 65.4 %collective-permute-start.1 = (bf16[160,896]{1,0:T(8,128)(2,1)S(1)}, bf16[160,896]{1,0:T(8,128)(2,1)S(1)}, u32[]{:S(2)}, u32[]{:S(2)}) collective-permute-start(bf16[160,896]{1,0:T(8,128)(2,1)S(1)} %get-tuple-element.264), channel_id=1, source_target_pairs={{0,16},{8,24},{16,0},{24,8},{1,17},{9,25},{17,1},{25,9},{2,18},{10... | collective-permute-start | bytes 860168 | tf_op jit(solution)/shard_map/ppermute | solution.py:1087
  402.6 64.3 %collective-permute-start.2 = (bf16[160,896]{1,0:T(8,128)(2,1)S(1)}, bf16[160,896]{1,0:T(8,128)(2,1)S(1)}, u32[]{:S(2)}, u32[]{:S(2)}) collective-permute-start(bf16[160,896]{1,0:T(8,128)(2,1)S(1)} %get-tuple-element.263), channel_id=1, source_target_pairs={{0,24},{8,0},{16,8},{24,16},{1,25},{9,1},{17,9},{25,17},{2,26},{10... | collective-permute-start | bytes 860168 | tf_op jit(solution)/shard_map/ppermute | solution.py:1087
  466.9 6.6 %copy-start.8 = (bf16[1,4,40,2304]{3,2,1,0:T(8,128)(2,1)S(1)}, bf16[1,4,40,2304]{3,2,1,0:T(8,128)(2,1)}, u32[]{:S(2)}) copy-start(bf16[1,4,40,2304]{3,2,1,0:T(8,128)(2,1)} %reduce-scatter.9.cloned.1.call-done) | copy-start | bytes 2211844
  469.1 25.6 %collective-permute-start.3 = (bf16[160,896]{1,0:T(8,128)(2,1)S(1)}, bf16[160,896]{1,0:T(8,128)(2,1)S(1)}, u32[]{:S(2)}, u32[]{:S(2)}) collective-permute-start(bf16[160,896]{1,0:T(8,128)(2,1)S(1)} %get-tuple-element.250), channel_id=1, source_target_pairs={{0,8},{8,16},{16,24},{24,0},{1,9},{9,17},{17,25},{25,1},{2,10},{10... | collective-permute-start | bytes 860168 | tf_op jit(solution)/shard_map/ppermute | solution.py:1087
  469.7 28.0 %collective-permute-start.4 = (bf16[160,896]{1,0:T(8,128)(2,1)S(1)}, bf16[160,896]{1,0:T(8,128)(2,1)S(1)}, u32[]{:S(2)}, u32[]{:S(2)}) collective-permute-start(bf16[160,896]{1,0:T(8,128)(2,1)S(1)} %get-tuple-element.250), channel_id=1, source_target_pairs={{0,16},{8,24},{16,0},{24,8},{1,17},{9,25},{17,1},{25,9},{2,18},{10... | collective-permute-start | bytes 860168 | tf_op jit(solution)/shard_map/ppermute | solution.py:1087
  470.8 26.9 %collective-permute-start.5 = (bf16[160,896]{1,0:T(8,128)(2,1)S(1)}, bf16[160,896]{1,0:T(8,128)(2,1)S(1)}, u32[]{:S(2)}, u32[]{:S(2)}) collective-permute-start(bf16[160,896]{1,0:T(8,128)(2,1)S(1)} %get-tuple-element.250), channel_id=1, source_target_pairs={{0,24},{8,0},{16,8},{24,16},{1,25},{9,1},{17,9},{25,17},{2,26},{10... | collective-permute-start | bytes 860168 | tf_op jit(solution)/shard_map/ppermute | solution.py:1087
  474.3 23.6 %collective-permute-start.6 = (bf16[40,2304]{1,0:T(8,128)(2,1)}, bf16[40,2304]{1,0:T(8,128)(2,1)S(1)}, u32[]{:S(2)}, u32[]{:S(2)}) collective-permute-start(bf16[40,2304]{1,0:T(8,128)(2,1)} %get-tuple-element.268), channel_id=1, source_target_pairs={{0,8},{8,16},{16,24},{24,0},{1,9},{9,17},{17,25},{25,1},{2,10},{10... | collective-permute-start | bytes 552968 | tf_op jit(solution)/shard_map/ppermute | solution.py:1087
  474.3 23.6 %collective-permute-start.7 = (bf16[40,2304]{1,0:T(8,128)(2,1)}, bf16[40,2304]{1,0:T(8,128)(2,1)S(1)}, u32[]{:S(2)}, u32[]{:S(2)}) collective-permute-start(bf16[40,2304]{1,0:T(8,128)(2,1)} %get-tuple-element.267), channel_id=1, source_target_pairs={{0,16},{8,24},{16,0},{24,8},{1,17},{9,25},{17,1},{25,9},{2,18},{10... | collective-permute-start | bytes 552968 | tf_op jit(solution)/shard_map/ppermute | solution.py:1087
  494.7 6.7 %collective-permute-start.8 = (bf16[40,2304]{1,0:T(8,128)(2,1)}, bf16[40,2304]{1,0:T(8,128)(2,1)}, u32[]{:S(2)}, u32[]{:S(2)}) collective-permute-start(bf16[40,2304]{1,0:T(8,128)(2,1)} %get-tuple-element.266), channel_id=1, source_target_pairs={{0,24},{8,0},{16,8},{24,16},{1,25},{9,1},{17,9},{25,17},{2,26},{10... | collective-permute-start | bytes 552968 | tf_op jit(solution)/shard_map/ppermute | solution.py:1087
  497.8 4.8 copy-start.30
  497.8 4.8 copy-start.40
  497.8 7.9 %copy-start.28 = (f32[64,48]{1,0:T(8,128)S(1)}, f32[64,48]{1,0:T(8,128)}, u32[]{:S(2)}) copy-start(f32[64,48]{1,0:T(8,128)} %get-tuple-element.151) | copy-start | bytes 36868
  497.8 7.9 %copy-start.6 = (f32[64,1152]{1,0:T(8,128)S(1)}, f32[64,1152]{1,0:T(8,128)}, u32[]{:S(2)}) copy-start(f32[64,1152]{1,0:T(8,128)} %get-tuple-element.153) | copy-start | bytes 884740
  497.8 9.1 %copy-start.19 = (f32[64,1152]{1,0:T(8,128)S(1)}, f32[64,1152]{1,0:T(8,128)}, u32[]{:S(2)}) copy-start(f32[64,1152]{1,0:T(8,128)} %get-tuple-element.152) | copy-start | bytes 884740
  501.4 6.3 copy-start.35
  501.4 6.3 copy-start.37
  513.5 30.5 %collective-permute-start.9 = (bf16[40,2304]{1,0:T(8,128)(2,1)}, bf16[40,2304]{1,0:T(8,128)(2,1)S(1)}, u32[]{:S(2)}, u32[]{:S(2)}) collective-permute-start(bf16[40,2304]{1,0:T(8,128)(2,1)} %get-tuple-element.248), channel_id=1, source_target_pairs={{0,8},{8,16},{16,24},{24,0},{1,9},{9,17},{17,25},{25,1},{2,10},{10... | collective-permute-start | bytes 552968 | tf_op jit(solution)/shard_map/ppermute | solution.py:1087
  516.4 27.6 %collective-permute-start.10 = (bf16[40,2304]{1,0:T(8,128)(2,1)}, bf16[40,2304]{1,0:T(8,128)(2,1)S(1)}, u32[]{:S(2)}, u32[]{:S(2)}) collective-permute-start(bf16[40,2304]{1,0:T(8,128)(2,1)} %get-tuple-element.248), channel_id=1, source_target_pairs={{0,16},{8,24},{16,0},{24,8},{1,17},{9,25},{17,1},{25,9},{2,18},{10... | collective-permute-start | bytes 552968 | tf_op jit(solution)/shard_map/ppermute | solution.py:1087
  517.1 27.0 %collective-permute-start.11 = (bf16[40,2304]{1,0:T(8,128)(2,1)}, bf16[40,2304]{1,0:T(8,128)(2,1)S(1)}, u32[]{:S(2)}, u32[]{:S(2)}) collective-permute-start(bf16[40,2304]{1,0:T(8,128)(2,1)} %get-tuple-element.248), channel_id=1, source_target_pairs={{0,24},{8,0},{16,8},{24,16},{1,25},{9,1},{17,9},{25,17},{2,26},{10... | collective-permute-start | bytes 552968 | tf_op jit(solution)/shard_map/ppermute | solution.py:1087
  518.9 23.5 %copy-start.4 = (f32[160,1000]{1,0:T(8,128)S(1)}, f32[160,1000]{1,0:T(8,128)}, u32[]{:S(2)}) copy-start(f32[160,1000]{1,0:T(8,128)} %param.48) | copy-start | bytes 1920004
  518.9 23.5 %copy-start.9 = (f32[160,1000]{1,0:T(8,128)S(1)}, f32[160,1000]{1,0:T(8,128)}, u32[]{:S(2)}) copy-start(f32[160,1000]{1,0:T(8,128)} %param.50) | copy-start | bytes 1920004
  518.9 23.5 %copy-start.10 = (f32[160,1000]{1,0:T(8,128)S(1)}, f32[160,1000]{1,0:T(8,128)}, u32[]{:S(2)}) copy-start(f32[160,1000]{1,0:T(8,128)} %param.49) | copy-start | bytes 1920004
  (44 other events, 78.8 us)
Sparse Core Ops, SparseCore 0:
  10.3 80.3 all-gather.3
  92.9 66.1 all-gather.5
  161.3 32.3 all-gather.7
  224.9 37.2 reduce-scatter.4
  315.2 72.5 reduce-scatter.6
  397.9 65.5 reduce-scatter.8
  501.5 44.7 reduce-scatter.10

commit v5 on v4

--- a/solution.py
+++ b/solution.py
@@ -47,7 +47,12 @@
 MESH = pl.DeviceIdType.MESH
 
 
-def sum_kernel(n_wide, n_dp, x_ref, o_ref, wide_slots, dp_slots, part, s_wide, r_wide, s_dp, r_dp):
+def sum_kernel(n_wide, n_dp, count, extra, finish, *refs):
+    parts, extras = refs[:count], refs[count : count + extra]
+    scratch = list(refs[-(3 * count + 4) :])
+    outs = refs[count + extra : len(refs) - len(scratch)]
+    wide_slots, dp_slots, halves = (scratch[k * count : (k + 1) * count] for k in range(3))
+    s_wide, r_wide, s_dp, r_dp = scratch[3 * count :]
     me_wide = lax.axis_index("wide")
     me_dp = lax.axis_index("dp")
     barrier = pltpu.get_barrier_semaphore()
@@ -61,62 +66,80 @@
         )
     pl.semaphore_wait(barrier, n_wide + n_dp - 2)
 
-    def exchange(src, slots, me, axis, size, send, recv):
+    def exchange(sources, slots, me, axis, size, send, recv):
         copies = []
         for k in range(1, size):
-            copy = pltpu.make_async_remote_copy(
-                src_ref=src,
-                dst_ref=slots.at[me],
-                send_sem=send.at[k],
-                recv_sem=recv.at[k],
-                device_id={axis: lax.rem(me + k, size)},
-                device_id_type=MESH,
-            )
-            copy.start()
-            copies.append(copy)
-        slots[me] = src[...]
+            for index in range(count):
+                copy = pltpu.make_async_remote_copy(
+                    src_ref=sources[index],
+                    dst_ref=slots[index].at[me],
+                    send_sem=send.at[k * count + index],
+                    recv_sem=recv.at[k * count + index],
+                    device_id={axis: lax.rem(me + k, size)},
+                    device_id_type=MESH,
+                )
+                copy.start()
+                copies.append(copy)
+        for source, slot in zip(sources, slots):
+            slot[me] = source[...]
         for copy in copies:
             copy.wait()
-        total = slots[0]
-        for k in range(1, size):
-            total = total + slots[k]
-        return total
-
-    part[...] = exchange(x_ref, wide_slots, me_wide, "wide", n_wide, s_wide, r_wide)
-    o_ref[...] = exchange(part, dp_slots, me_dp, "dp", n_dp, s_dp, r_dp)
-
-
-def sum_all(parts, ident):
-    shapes = [part.shape for part in parts]
-    sizes = [part.size for part in parts]
-    flat = jnp.concatenate([part.reshape(-1) for part in parts])
-    rows = -(-flat.size // 1024) * 8
-    flat = jnp.pad(flat, (0, rows * 128 - flat.size)).reshape(rows, 128)
+        found = []
+        for slot in slots:
+            total = slot[0]
+            for k in range(1, size):
+                total = total + slot[k]
+            found.append(total)
+        return found
+
+    for half, total in zip(halves, exchange(parts, wide_slots, me_wide, "wide", n_wide, s_wide, r_wide)):
+        half[...] = total
+    totals = exchange(halves, dp_slots, me_dp, "dp", n_dp, s_dp, r_dp)
+    finish(totals, extras, outs)
+
+
+def sum_all(parts, extras, finish, outs, ident):
     n_wide = lax.axis_size("wide")
     n_dp = lax.axis_size("dp")
-    out = pl.pallas_call(
-        functools.partial(sum_kernel, n_wide, n_dp),
-        out_shape=jax.ShapeDtypeStruct((rows, 128), jnp.float32),
-        in_specs=[pl.BlockSpec(memory_space=pltpu.VMEM)],
-        out_specs=pl.BlockSpec(memory_space=pltpu.VMEM),
-        scratch_shapes=[
-            pltpu.VMEM((n_wide, rows, 128), jnp.float32),
-            pltpu.VMEM((n_dp, rows, 128), jnp.float32),
-            pltpu.VMEM((rows, 128), jnp.float32),
-            pltpu.SemaphoreType.DMA((n_wide,)),
-            pltpu.SemaphoreType.DMA((n_wide,)),
-            pltpu.SemaphoreType.DMA((n_dp,)),
-            pltpu.SemaphoreType.DMA((n_dp,)),
-        ],
+    count = len(parts)
+    vmem = pl.BlockSpec(memory_space=pltpu.VMEM)
+    scratch = [pltpu.VMEM((n_wide,) + part.shape, jnp.float32) for part in parts]
+    scratch += [pltpu.VMEM((n_dp,) + part.shape, jnp.float32) for part in parts]
+    scratch += [pltpu.VMEM(part.shape, jnp.float32) for part in parts]
+    sems = [pltpu.SemaphoreType.DMA((size * count,)) for size in (n_wide, n_wide, n_dp, n_dp)]
+    return pl.pallas_call(
+        functools.partial(sum_kernel, n_wide, n_dp, count, len(extras), finish),
+        name="sum_all",
+        out_shape=[jax.ShapeDtypeStruct(shape, jnp.float32) for shape in outs],
+        in_specs=[vmem] * (count + len(extras)),
+        out_specs=[vmem] * len(outs),
+        scratch_shapes=scratch + sems,
         compiler_params=pltpu.CompilerParams(collective_id=ident, has_side_effects=True),
-    )(flat)
-    out = out.reshape(-1)
-    found = []
-    start = 0
-    for shape, size in zip(shapes, sizes):
-        found.append(out[start : start + size].reshape(shape))
-        start = start + size
-    return found
+    )(*parts, *extras)
+
+
+def norm_finish(count, every, totals, extras, outs):
+    sums, route = totals
+    center = sums[0:1] / count
+    inv = lax.rsqrt(sums[1:2] / count - center * center + eps_norm)
+    scale = inv * extras[0][...]
+    outs[0][0:1] = scale
+    outs[0][1:2] = extras[1][...] - center * scale
+    outs[0][2:3] = inv
+    outs[0][3:4] = -center * inv
+    outs[0][4:8] = jnp.full((4, scale.shape[1]), 1.0 / every, jnp.float32)
+    outs[1][...] = route
+
+
+def back_finish(count, totals, extras, outs):
+    sums = totals[0]
+    norm = extras[0]
+    scale, part = norm[0:1], norm[0:1] * sums[1:2] / count
+    outs[0][0:2] = norm[0:2]
+    outs[0][2:3] = -part * norm[2:3]
+    outs[0][3:4] = -scale * sums[0:1] / count - part * norm[3:4]
+    for out, total in zip(outs[1:], totals):
+        out[...] = total
 
 
 def balance_grad(means, every):
@@ -136,6 +159,27 @@
     return 0.5 + 0.5 * jnp.tanh(0.5 * value)
 
 
+def silu_of(value):
+    half = 0.5 * value
+    return half * (1.0 + jnp.tanh(half))
+
+
+def silu_pair(value):
+    half = 0.5 * value
+    bent = jnp.tanh(half)
+    upper = 1.0 + bent
+    return half * upper, upper * (1.0 + half * (1.0 - bent))
+
+
+def sum_of(terms):
+    while len(terms) > 1:
+        terms = [
+            terms[k] + terms[k + 1] if k + 1 < len(terms) else terms[k]
+            for k in range(0, len(terms), 2)
+        ]
+    return terms[0]
+
+
 def dot_nn(left, right, precision=None):
     return lax.dot_general(
         left, right, (((1,), (0,)), ((), ())), precision=precision, preferred_element_type=FULL
@@ -174,7 +218,7 @@
     return pl.BlockSpec(shape, lambda i: (0,) * len(shape))
 
 
-def device_kernel(kernel, name, grid, in_specs, outs, out_specs, scratch, flops, moved):
+def device_kernel(kernel, name, grid, in_specs, outs, out_specs, scratch, flops, moved, cap=None):
     return pl.pallas_call(
         kernel,
         name=name,
@@ -184,7 +228,7 @@
         out_specs=out_specs,
         scratch_shapes=scratch,
         compiler_params=pltpu.CompilerParams(
-            vmem_limit_bytes=VMEM_CAP, dimension_semantics=("arbitrary",)
+            vmem_limit_bytes=cap or VMEM_CAP, dimension_semantics=("arbitrary",)
         ),
         cost_estimate=pl.CostEstimate(flops=flops, bytes_accessed=moved, transcendentals=0),
     )
@@ -463,7 +507,7 @@
         "head_forward",
         images // GROUP,
         [
-            images_block(C_OUT), whole(2, C_OUT), group_block(EXPERTS), whole(EXPERTS, C_OUT),
+            images_block(C_OUT), whole(8, C_OUT), group_block(EXPERTS), whole(EXPERTS, C_OUT),
             whole(C_HEAD, wide),
         ],
         [
@@ -572,14 +616,12 @@
         sums_ref[...] = jnp.zeros_like(sums_ref)
 
     gain, shift, by_value, constant = (coef_ref[k : k + 1] for k in range(4))
-    grad_feats = grad_feats_ref[...]
+    grad_feats = grad_feats_ref[...] * (0.5 * gain)
 
     def widen(pixel, carry):
         value = widened_ref[pixel].astype(FULL)
-        lifted = value * gain + shift
-        part = sig(lifted)
-        bent = part + lifted * part * (1.0 - part)
-        grad = grad_feats * bent * gain + value * by_value + constant
+        _, bent = silu_pair(value * gain + shift)
+        grad = grad_feats * bent + value * by_value + constant
         grad_wide_ref[pixel] = grad.astype(LOW)
         return carry
 
@@ -608,7 +650,7 @@
         plain, cross = carry
         grad = mixed[pixel] + added
         grad_normed_ref[pixel] = grad
-        hat = before_ref[pixel] * norm_ref[0:1] + norm_ref[1:2]
+        hat = before_ref[pixel] * norm_ref[2:3] + norm_ref[3:4]
         return plain + grad, cross + grad * hat
 
     zero = jnp.zeros((GROUP, C_OUT), FULL)
@@ -628,7 +670,7 @@
         images // GROUP,
         [
             images_block(C_HEAD), group_block(C_HEAD), whole(4, C_HEAD), whole(C_HEAD, wide),
-            pair_block(2 * C_OUT), images_block(2 * C_OUT), images_block(C_OUT), whole(2, C_OUT),
+            pair_block(2 * C_OUT), images_block(2 * C_OUT), images_block(C_OUT), whole(8, C_OUT),
             group_block(EXPERTS), whole(1, EXPERTS), whole(EXPERTS, C_OUT),
         ],
         [
@@ -722,14 +764,14 @@
 def project_back_kernel(
     grad_ref, before_ref, coef_ref, pair_ref, each_ref, source,
     grad_before_ref, grad_scaled_ref, route_ref,
-    routed, padded, weight_ref, sem,
+    routed, padded, twice, weight_ref, sem,
 ):
     @pl.when(pl.program_id(0) == 0)
     def _():
         stack_experts(source, weight_ref, sem)
         padded[...] = jnp.zeros_like(padded)
 
-    gain, by_value, constant = (coef_ref[k : k + 1] for k in range(3))
+    gain, _, by_value, constant = (coef_ref[k : k + 1] for k in range(4))
     scales = [pair_ref[pair] for pair in range(PAIRS)]
 
     def turn(pixel, carry):
@@ -738,20 +780,22 @@
         grad_before_ref[pixel] = grad
         padded[:, :C_OUT] = grad.astype(FULL)
         value = padded[...]
-        value = value + pltpu.roll(value, C_OUT, 1)
-        low = value.astype(LOW)
-        found = []
+        value = (value + pltpu.roll(value, C_OUT, 1)).astype(LOW)
+        twice[pixel] = value
         for pair in range(PAIRS):
             place = slice(2 * pair * C_OUT, 2 * (pair + 1) * C_OUT)
-            routed[pixel, :, place] = low * scales[pair]
-            found.append(carry[pair] + each_ref[pixel, :, place].astype(FULL) * value)
-        return tuple(found)
-
-    zero = jnp.zeros((GROUP, 2 * C_OUT), FULL)
-    route_sums = lax.fori_loop(0, PIX, turn, (zero,) * PAIRS, unroll=7)
-    route_ref[...] = pair_columns(route_sums, C_OUT)
+            routed[pixel, :, place] = value * scales[pair]
+        return carry
+
+    lax.fori_loop(0, PIX, turn, 0, unroll=7)
     product = dot_nn(routed[...].reshape(ROWS, EXPERTS * C_OUT), weight_ref[...])
     grad_scaled_ref[...] = product.reshape(PIX, GROUP, C_MID).astype(LOW)
+    route_sums = []
+    for pair in range(PAIRS):
+        place = slice(2 * pair * C_OUT, 2 * (pair + 1) * C_OUT)
+        term = each_ref[:, :, place].astype(FULL) * twice[...].astype(FULL)
+        route_sums.append(jnp.sum(term, axis=0))
+    route_ref[...] = pair_columns(route_sums, C_OUT)
 
 
 def project_back(grad_normed, before, coef, pair_out, each, project_low):
@@ -762,7 +806,7 @@
         "project_back",
         images // GROUP,
         [
-            images_block(C_OUT), images_block(C_OUT), whole(3, C_OUT), pair_block(2 * C_OUT),
+            images_block(C_OUT), images_block(C_OUT), whole(4, C_OUT), pair_block(2 * C_OUT),
             images_block(wide), pl.BlockSpec(memory_space=pl.ANY),
         ],
         [
@@ -771,10 +815,12 @@
         [images_block(C_OUT), images_block(C_MID), group_block(EXPERTS)],
         [
             pltpu.VMEM((PIX, GROUP, wide), LOW), pltpu.VMEM((GROUP, 2 * C_OUT), FULL),
+            pltpu.VMEM((PIX, GROUP, 2 * C_OUT), LOW),
             pltpu.VMEM((wide, C_MID), LOW), pltpu.SemaphoreType.DMA((EXPERTS,)),
         ],
         2 * PIX * images * wide * C_MID,
         PIX * images * (C_MID + wide) * 2,
+
     )(grad_normed, before, coef, pair_out, each, project_low)
 
 
@@ -782,7 +828,7 @@
     grad_scaled_ref, turned_ref, hidden_ref, img_ref, gate_ref, squeeze_ref, excite_ref, depth_ref,
     route_ref, route_part_ref, balance_ref, source,
     grad_hidden_ref, logit_ref, grad_gate_ref, grad_squeeze_ref, grad_depth_ref,
-    kern, start, grad_turned, grad_kern, pooled, product, weight_ref, sem,
+    kern, start, slope, grad_turned, grad_kern, pooled, product, weight_ref, sem,
 ):
     @pl.when(pl.program_id(0) == 0)
     def _():
@@ -801,7 +847,7 @@
 
     def gate_sum(pixel, carry):
         value = turned_ref[pixel].astype(FULL)
-        return carry + grad_scaled_ref[pixel].astype(FULL) * (value * sig(value))
+        return carry + grad_scaled_ref[pixel].astype(FULL) * silu_of(value)
 
     gate = gate_ref[...]
     grad_gate = lax.fori_loop(0, PIX, gate_sum, jnp.zeros((GROUP, C_MID), FULL), unroll=7)
@@ -822,29 +868,26 @@
 
     def chunk(index):
         lanes = slice(index * 128, index * 128 + 128)
-        gate_part = gate_ref[:, lanes]
-        pooled_part = pooled[:, lanes]
+        side = index % 2
+        gate_part = 0.5 * gate_ref[:, lanes]
+        pooled_part = 0.5 * pooled[:, lanes]
         for pixel in range(PIX):
-            value = turned_ref[pixel, :, lanes].astype(FULL)
-            part = sig(value)
+            _, bent = silu_pair(turned_ref[pixel, :, lanes].astype(FULL))
             grad = grad_scaled_ref[pixel, :, lanes].astype(FULL) * gate_part + pooled_part
-            grad_turned[index % 2, pixel] = grad * (part + value * part * (1.0 - part))
-            value = hidden_ref[pixel, :, lanes].astype(FULL)
-            start[index % 2, pixel] = value * sig(value)
-        taps = [kern[tap, :, lanes] for tap in range(KSIZE * KSIZE)]
+            grad_turned[side, pixel] = grad * bent
+            value, bent = silu_pair(hidden_ref[pixel, :, lanes].astype(FULL))
+            start[side, pixel] = value
+            slope[side, pixel] = bent
+        taps = [0.5 * kern[tap, :, lanes] for tap in range(KSIZE * KSIZE)]
         sums = [None] * (KSIZE * KSIZE)
         for pixel in range(PIX):
-            total = None
-            here = grad_turned[index % 2, pixel]
+            here = grad_turned[side, pixel]
+            terms = []
             for tap, source in taps_of(pixel):
-                term = start[index % 2, source] * here
+                term = start[side, source] * here
                 sums[tap] = term if sums[tap] is None else sums[tap] + term
-                term = grad_turned[index % 2, source] * taps[KSIZE * KSIZE - 1 - tap]
-                total = term if total is None else total + term
-            value = hidden_ref[pixel, :, lanes].astype(FULL)
-            part = sig(value)
-            grad = total * (part + value * part * (1.0 - part))
-            grad_hidden_ref[pixel, :, lanes] = grad.astype(LOW)
+                terms.append(grad_turned[side, source] * taps[KSIZE * KSIZE - 1 - tap])
+            grad_hidden_ref[pixel, :, lanes] = (sum_of(terms) * slope[side, pixel]).astype(LOW)
         for tap in range(KSIZE * KSIZE):
             grad_kern[tap, :, lanes] = sums[tap]
 
@@ -907,7 +950,7 @@
         ],
         [
             pltpu.VMEM((taps, GROUP, C_MID), FULL), pltpu.VMEM((2, PIX, GROUP, 128), FULL),
-            pltpu.VMEM((2, PIX, GROUP, 128), FULL), pltpu.VMEM((taps, GROUP, C_MID), FULL),
+            pltpu.VMEM((2, PIX, GROUP, 128), FULL), pltpu.VMEM((2, PIX, GROUP, 128), FULL), pltpu.VMEM((taps, GROUP, C_MID), FULL),
             pltpu.VMEM((GROUP, C_MID), FULL), pltpu.VMEM((PIX, GROUP, EXPERTS * C_IN), FULL),
             pltpu.VMEM((C_MID, EXPERTS * C_IN), LOW), pltpu.SemaphoreType.DMA((PAIRS,)),
         ],
@@ -1212,17 +1255,26 @@
     def iota(shape, axis):
         return lax.broadcasted_iota(jnp.int32, shape, axis)
 
-    pick = (iota((height, BLK), 0) % BLK == iota((height, BLK), 1)).astype(FULL)
-    pick_t = (iota((BLK, height), 1) % BLK == iota((BLK, height), 0)).astype(FULL)
+    pick = (iota((height, BLK), 0) % BLK == iota((height, BLK), 1)).astype(LOW)
+    pick_t = (iota((BLK, height), 1) % BLK == iota((BLK, height), 0)).astype(LOW)
     same = iota((height, height), 0) // BLK == iota((height, height), 1) // BLK
-    ones = same.astype(FULL)
+    ones = same.astype(LOW)
+
+    def parts(value):
+        high = value.astype(LOW)
+        return high, (value - high.astype(FULL)).astype(LOW)
+
+    def by_ones(value):
+        high, rest = parts(value)
+        return dot_nn(high, ones) + dot_nn(rest, ones)
 
     def spread_out(rows):
-        return jnp.where(same, dot_nn(pick, rows, HIGH), 0.0)
-
-    def by_half(product, value):
-        first = product(0, value[:, :upper])
-        second = product(1, value[:, lower:])
+        high, rest = parts(rows)
+        return jnp.where(same, dot_nn(pick, high) + dot_nn(pick, rest), 0.0)
+
+    def by_half(product, *values):
+        first = product(0, *(value[:, :upper] for value in values))
+        second = product(1, *(value[:, lower:] for value in values))
         if upper == lower:
             return jnp.concatenate([first, second], axis=1)
         lane = iota((height, upper - lower), 1)
@@ -1230,16 +1282,26 @@
         return jnp.concatenate([first[:, :lower], middle, second[:, upper - lower :]], axis=1)
 
     old = [state_ref[1, 2 * step + side] for side in range(2)]
-    turns = [spread_out(rows) for rows in old]
-    grad = grad_ref[0].astype(FULL)
-    turned = by_half(lambda side, value: dot_nn(turns[side], value, HIGH), grad)
+    turns = [parts(spread_out(rows)) for rows in old]
+
+    def turn(side, high, rest):
+        return dot_nn(turns[side][0], high) + dot_nn(turns[side][0], rest) + dot_nn(turns[side][1], high)
+
+    def turn_back(side, high, rest):
+        return dot_tn(turns[side][0], high) + dot_tn(turns[side][0], rest) + dot_tn(turns[side][1], high)
+
+    raw = grad_ref[0]
+    grad = raw.astype(FULL)
+    turned = by_half(
+        lambda side, value: dot_nn(turns[side][0], value) + dot_nn(turns[side][1], value), raw
+    )
     first_new = beta_one * first_ref[...] + (1.0 - beta_one) * grad
     second_new = beta_two * second_ref[...] + (1.0 - beta_two) * (turned * turned)
     first_out[...] = first_new
     second_out[...] = second_new
-    moment = by_half(lambda side, value: dot_nn(turns[side], value, HIGH), first_new)
+    moment = by_half(turn, *parts(first_new))
     ratio = moment / corr_one / (jnp.sqrt(second_new / corr_two) + eps_adam)
-    back = by_half(lambda side, value: dot_tn(turns[side], value, HIGH), ratio)
+    back = by_half(turn_back, *parts(ratio))
     weight = weight_ref[...]
     weight_out[...] = weight - rate_matrix * (back + decay * weight)
 
@@ -1250,14 +1312,18 @@
         else:
             piece = grad[:, lower:]
             piece = jnp.where(iota(piece.shape, 1) >= half - lower, piece, 0.0)
-        gram = jnp.where(same, dot_nt(piece, piece, HIGH), 0.0)
+        piece = piece.astype(LOW)
+        gram = parts(jnp.where(same, dot_nt(piece, piece), 0.0))
         summed = beta_two * state_ref[0, 2 * step + side]
-        summed = summed + (1.0 - beta_two) * gained * dot_nn(pick_t, gram, HIGH)
-        diagonal = jnp.sum(summed * pick_t, axis=0, keepdims=True)
-        trace = dot_nn(diagonal, ones, HIGH)
-        stats = summed / trace
+        summed = summed + (1.0 - beta_two) * gained * (
+            dot_nn(pick_t, gram[0]) + dot_nn(pick_t, gram[1])
+        )
+        diagonal = jnp.sum(summed * pick_t.astype(FULL), axis=0, keepdims=True)
+        stats = summed / by_ones(diagonal)
         state_out[0, 2 * step + side] = stats
-        lifted = dot_nn(old[side], spread_out(stats), HIGH)
+        high, rest = parts(old[side])
+        wide_high, wide_rest = parts(spread_out(stats))
+        lifted = dot_nn(high, wide_high) + dot_nn(high, wide_rest) + dot_nn(rest, wide_high)
         for column in range(BLK):
             raised[column, pl.ds(2 * step + side, 1), :] = lifted[column : column + 1]
 
@@ -1267,8 +1333,8 @@
         for index in range(BLK):
             column = raised[index]
             for previous in columns:
-                column = column - dot_nn(previous * column, ones, HIGH) * previous
-            column = column * lax.rsqrt(dot_nn(column * column, ones, HIGH))
+                column = column - by_ones(previous * column) * previous
+            column = column * lax.rsqrt(by_ones(column * column))
             columns.append(column)
             for expert in range(EXPERTS):
                 state_out[1, expert, index : index + 1, :] = column[expert : expert + 1]
@@ -1371,21 +1437,16 @@
         img_two, hot, router_one, expand_low, depth_full, excite, bias_se[None], bias_ex[None]
     )
     each, before, sums_one = project_forward(scaled, project_low, pair_one)
-    sums_one, route_one_sum = sum_all((sums_one, route_one_sum), 1)
-    center_one = sums_one[0] / count
-    inv_one = lax.rsqrt(sums_one[1] / count - center_one * center_one + eps_norm)
-    scale_one = inv_one * gain_one
-    norm_one = jnp.stack([scale_one, shift_one - center_one * scale_one])
+    norm_one, route_one_sum = sum_all(
+        (sums_one, route_one_sum), (gain_one[None], shift_one[None]),
+        functools.partial(norm_finish, count, every), ((8, C_OUT), (1, EXPERTS)), 1,
+    )
     widened, twice, route_two, pair_two, pooled_two, sums_two, route_two_sum = head_forward(
         before, norm_one, hot, router_two, head_low
     )
-    sums_two, route_two_sum = sum_all((sums_two, route_two_sum), 2)
-    center_two = sums_two[0] / count
-    inv_two = lax.rsqrt(sums_two[1] / count - center_two * center_two + eps_norm)
-    scale_two = inv_two * gain_two
-    norm_two = jnp.stack(
-        [scale_two, shift_two - center_two * scale_two, inv_two, -center_two * inv_two]
-        + [jnp.full_like(inv_two, 1.0 / every)] * 4
+    norm_two, route_two_sum = sum_all(
+        (sums_two, route_two_sum), (gain_two[None], shift_two[None]),
+        functools.partial(norm_finish, count, every), ((8, C_HEAD), (1, EXPERTS)), 2,
     )
     feats, grad_logits, grad_feats, back_two, cross_part, grad_bias_cls = loss_part(
         widened, norm_two, class_label[:, None], class_low, bias_cls[None]
@@ -1395,29 +1456,23 @@
     )
     grad_class, grad_feats = lax.optimization_barrier((grad_class, grad_feats))
     share_class = lax.psum_scatter(grad_class, "wide", scatter_dimension=1, tiled=True)
-    back_two, cross_total, grad_bias_cls = sum_all((back_two, cross_part, grad_bias_cls), 3)
+    coef_two, back_two, cross_total, grad_bias_cls = sum_all(
+        (back_two, cross_part, grad_bias_cls), (norm_two,), functools.partial(back_finish, count),
+        ((4, C_HEAD), (2, C_HEAD), (1, 1), (1, CLASSES)), 3,
+    )
     means_one = route_one_sum[0] / every
     means_two = route_two_sum[0] / every
-    by_value = -scale_two * inv_two * back_two[1] / count
-    coef_two = jnp.stack(
-        [
-            scale_two, shift_two - center_two * scale_two, by_value,
-            -scale_two * back_two[0] / count - center_two * by_value,
-        ]
-    )
-    hat_one = jnp.stack([inv_one, -center_one * inv_one])
     grad_widened, grad_normed, grad_logit_two, back_one = head_back(
-        widened, grad_feats, coef_two, head_low, pair_two, twice, before, hat_one, route_two,
+        widened, grad_feats, coef_two, head_low, pair_two, twice, before, norm_one, route_two,
         balance_grad(means_two, every)[None], router_two,
     )
     grad_head = kern_grad(grad_widened, twice, pair_two, "head_grad")
     grad_head, back_one, share_class = lax.optimization_barrier((grad_head, back_one, share_class))
     share_head = lax.psum_scatter(grad_head, "wide", scatter_dimension=1, tiled=True)
     grad_router_two = dot_tn(pooled_two, grad_logit_two, HIGH)
-    (back_one,) = sum_all((back_one,), 4)
-    by_value = -scale_one * inv_one * back_one[1] / count
-    coef_one = jnp.stack(
-        [scale_one, by_value, -scale_one * back_one[0] / count - center_one * by_value]
+    coef_one, back_one = sum_all(
+        (back_one,), (norm_one,), functools.partial(back_finish, count),
+        ((4, C_OUT), (2, C_OUT)), 4,
     )
     grad_before, grad_scaled, route_project = project_back(
         grad_normed, before, coef_one, pair_one, each, project_low
@@ -1458,25 +1513,18 @@
     sum_project = from_pieces(spread_sum(add_arrived(own_project, arrived)), PAIRS)
     share_expand = lax.psum_scatter(grad_expand, "wide", scatter_dimension=1, tiled=True)
     parts = n_wide * n_dp
-    depth_piece = grad_depth.size // parts
-    extras = [
-        grad_depth.reshape(-1, n_wide, depth_weight.shape[2]).transpose(1, 0, 2),
-        jnp.concatenate(
-            [
-                grad_excite.reshape(-1), grad_router_one.reshape(-1), grad_router_two.reshape(-1),
-                grad_bias_se, grad_bias_ex,
-            ]
-        ),
-    ]
-    depth_part = extras[0].reshape(n_wide, n_dp, depth_piece).transpose(1, 0, 2)
-    rest_size = extras[1].size
-    rest_piece = -(-rest_size // parts)
-    rest_part = jnp.pad(extras[1], (0, rest_piece * parts - rest_size))
-    rest_part = rest_part.reshape(n_dp, n_wide, rest_piece)
-    extra_rows = -(-(depth_piece + rest_piece) // (16 * 128)) * 16
-    extra = jnp.concatenate([depth_part, rest_part], axis=2).astype(low_type)
-    extra = jnp.pad(extra, ((0, 0), (0, 0), (0, extra_rows * 128 - extra.shape[2])))
-    extra = extra.reshape(n_dp, n_wide, extra_rows, 128)
+    depth_part = grad_depth.reshape(taps * EXPERTS, n_wide, -1).transpose(1, 0, 2)
+    depth_part = depth_part.reshape(n_wide, n_dp, taps * EXPERTS // n_dp, -1).transpose(1, 0, 2, 3)
+    rest = jnp.concatenate(
+        [
+            grad_excite.reshape(-1), grad_router_one.reshape(-1), grad_router_two.reshape(-1),
+            grad_bias_se, grad_bias_ex,
+        ]
+    )
+    rest_size = rest.size
+    rest_rows = -(-rest_size // (parts * 16 * 128)) * 16
+    rest = jnp.pad(rest.astype(low_type), (0, parts * rest_rows * 128 - rest_size))
+    rest = rest.reshape(n_dp, n_wide, rest_rows, 128)
     head_out = soap(head_weight, sum_head, head_first, head_second, head_state, every)
     project_out = soap(
         project_weight, sum_project, project_first, project_second, project_state, every
@@ -1488,17 +1536,17 @@
     share_expand, head_out, project_out, class_out = lax.optimization_barrier(
         (share_expand, head_out, project_out, class_out)
     )
-    (own_extra,), (own_expand,), every_extra = reduce_grads(
-        [extra], [to_pieces(share_expand, n_dp)], 5
+    (own_depth, _), (own_expand,), rest = reduce_grads(
+        [depth_part.astype(low_type), rest], [to_pieces(share_expand, n_dp)], 5
     )
     sum_expand = from_pieces(own_expand, PAIRS)
-    own_extra = own_extra.reshape(n_dp, -1)[:, :depth_piece].reshape(EXPERTS, KSIZE * KSIZE, -1)
-    rest = every_extra.reshape(n_wide, n_dp, -1)[:, :, depth_piece : depth_piece + rest_piece]
-    rest = rest.transpose(1, 0, 2).reshape(-1)[:rest_size].astype(FULL)
-    split = grad_excite.size
-    sum_excite = rest[:split].reshape(2, C_SE, C_MID).transpose(0, 2, 1)
-    sum_router = rest[split : split + router_weight.size].reshape(router_weight.shape)
-    sum_bias = rest[split + router_weight.size :]
+    sum_depth = own_depth.reshape(EXPERTS, taps, -1).astype(FULL)
+    rest = rest.transpose(1, 0, 2, 3).reshape(-1, 128)
+    split = grad_excite.size // 128
+    sum_excite = rest[:split].reshape(2, C_SE, C_MID).transpose(0, 2, 1).astype(FULL)
+    rest = rest[split:].reshape(-1)[: rest_size - grad_excite.size].astype(FULL)
+    sum_router = rest[: router_weight.size].reshape(router_weight.shape)
+    sum_bias = rest[router_weight.size :]
     loss = cross_total[0, 0] / every + balance_weight * (
         jnp.mean((means_one - jnp.mean(means_one)) ** 2)
         + jnp.mean((means_two - jnp.mean(means_two)) ** 2)
@@ -1508,7 +1556,7 @@
     )
     expand_out = soap(expand_weight, sum_expand, expand_first, expand_second, expand_state, every)
     depth_out = adam(
-        depth_weight, own_extra.astype(FULL), depth_first, depth_second, rate_matrix
+        depth_weight, sum_depth, depth_first, depth_second, rate_matrix
     )
     excite_out = adam(excite_weight, sum_excite, excite_first, excite_second, rate_matrix)
     router_out = adam(router_weight, sum_router, router_first, router_second, rate_matrix)

time: 638 us -> 589 us (0.923)
  Pallas kernels: 519 us -> 489 us
  local copies, waits for them, and re-layouts: 32.8 us -> 21.2 us
  other arithmetic: 29.3 us -> 21 us
    pallas_call x3, Pallas kernels: 59.3 us -> 36.3 us  [soap(): device_kernel(functools.partial(soap_kernel, gained), 'soap', PAIRS, [col...]
    slice x8 -> x3, local copies, waits for them, and re-layouts: 7.7 us -> 0.28 us  [the longest x2 0.25 us: local(): sum_router = rest[:router_weight.size].reshape(router_weight.shape)]
    reshape x14 -> x1, local copies, waits for them, and re-layouts: 6.93 us -> 0.01 us  [local(): rest = rest[split:].reshape(-1)[:rest_size - grad_excite.size].astype(FULL)]
  transfers between devices with their start and end apart: 19 -> 19, of which waited for: 2 -> 3; matrix products, arithmetic and copies ran while one was open for 7% -> 5% of each run, Pallas kernels for 72% -> 74%
where the time goes in v5:
time: 589 us; the launch traced here: 586 us
  Pallas kernels  489 us (83%)
  local copies, waits for them, and re-layouts  21.2 us (4%)
  other arithmetic  21 us (4%)
  between operations  19.9 us (3%)
  starting transfers between devices  16.6 us (3%)
  waiting for transfers between devices  13.3 us (2%)
    pallas_call x1, Pallas kernels, expand_back(): device_kernel(expand_back_kernel, 'expand_back', images // GROUP, [images...  59 us
    pallas_call x4, Pallas kernels, sum_all(): pl.pallas_call(functools.partial(sum_kernel, n_wide, n_dp, count, len(ext...  56.1 us
    pallas_call x2, Pallas kernels, kern_grad(): device_kernel(kern_grad_kernel, name, PAIRS // 2, [whole(PIX, images, out...  52.3 us
    pallas_call x1, Pallas kernels, expand_forward(): device_kernel(expand_kernel, 'expand_forward', images // GROUP, [images_b...  40 us
    pallas_call x1, Pallas kernels, head_back(): device_kernel(head_back_kernel, 'head_back', images // GROUP, [images_blo...  39.7 us
    pallas_call x1, Pallas kernels, gather_expand(): pl.pallas_call(functools.partial(gather_kernel, n_wide, n_dp), name='gath...  37.2 us
    pallas_call x3, Pallas kernels, soap(): device_kernel(functools.partial(soap_kernel, gained), 'soap', PAIRS, [col...  36.3 us
    pallas_call x1, Pallas kernels, project_back(): device_kernel(project_back_kernel, 'project_back', images // GROUP, [imag...  36.3 us
  transfers between devices with their start and end apart: 19, of which 3 were waited for; matrix products, arithmetic and copies ran while one was open for 5% of the time, Pallas kernels for 74%

profile of v5, /device:TPU:0, one launch (start us, length us, event | category | flops | bytes accessed | tf_op | source)
XLA Modules:
  0.0 585.5 jit_solution(17836645016237591805)
XLA Ops:
  7.3 2.4 convert_element_type.127
  14.4 2.4 pad_maximum_fusion.1.img_ref.twice_ref
  18.2 37.2 %gather_expand.1 = (bf16[4,4,2,144,384]{4,3,2,1,0:T(8,128)(2,1)}, bf16[8,80,144]{2,1,0:T(8,128)(2,1)}) custom-call(f32[144,1536]{1,0:T(8,128)} %weight_ref.7, bf16[80,144]{1,0:T(8,128)(2,1)} %pad.8.depth_ref), custom_call_target="tpu_custom_call" | custom-call | tf_op jit(solution)/shard_map/gather_expand/pallas_call | solution.py:1226
  61.2 40.0 %expand_forward.1 = (bf16[49,64,1152]{2,1,0:T(8,128)(2,1)}, bf16[49,64,1152]{2,1,0:T(8,128)(2,1)}, bf16[49,64,1152]{2,1,0:T(8,128)(2,1)}, f32[64,8]{1,0:T(8,128)...) custom-call(bf16[49,64,384]{2,1,0:T(8,128)(2,1)} %pad_maximum_fusion, ...), custom_call_target="tpu_custom_call" | custom-call | flops 11098128384 | bytes 28901376 | tf_op jit(solution)/shard_map/expand_forward/pallas_call | solution.py:364
  101.2 30.0 %project_forward.1 = (bf16[49,64,2560]{2,1,0:T(8,128)(2,1)}, f32[49,64,320]{2,1,0:T(8,128)}, f32[2,320]{1,0:T(2,128)}) custom-call(bf16[49,64,1152]{2,1,0:T(8,128)(2,1)} %get-tuple-element.126.scaled_ref, bf16[320,9216]{1,0:T(8,128)(2,1)} %all-gather.4.cloned.1.call-done.source, bf16[4,64,640]{2,1,0:T(8,128)(2,1)} %get-tuple-element.127.pair_ref), custom_call_target="tpu_custom_call" | custom-call | flops 18496880640 | bytes 23281664 | tf_op jit(solution)/shard_map/project_forward/pallas_call | solution.py:449
  131.2 21.1 %sum_all.4 = (f32[8,320]{1,0:T(8,128)}, f32[1,8]{1,0:T(1,128)}) custom-call(f32[2,320]{1,0:T(2,128)} %get-tuple-element.129.refs_0_, f32[1,8]{1,0:T(1,128)} %get-tuple-element.130.refs_1_, f32[1,320]{1,0:T(1,128)} %broadcast_in_dim.62.refs_2_, f32[1,320]{1,0:T(1,128)} %broadcast_in_dim.63.refs_3_), custom_call_target="tpu_custom_call" | custom-call | tf_op jit(solution)/shard_map/sum_all/pallas_call | solution.py:110
  152.3 6.8 %all-gather.6.cloned.1.call-done.weight_ref = bf16[1280,2560]{1,0:T(8,128)(2,1)} async-done(((bf16[160,2560]{1,0:T(8,128)(2,1)}), bf16[1280,2560]{1,0:T(8,128)(2,1)}) %all-gather.6.cloned.1.call-update) | async-done | bytes 6553616 | tf_op jit(solution)/shard_map/all_gather | solution.py:1420
  159.1 29.7 %head_forward.1 = (bf16[49,64,1280]{2,1,0:T(8,128)(2,1)}, bf16[49,64,640]{2,1,0:T(8,128)(2,1)}, f32[64,8]{1,0:T(8,128)}, bf16[4,64,640]{2,1,0:T(8,128)(2,1)}, f3...) custom-call(f32[49,64,320]{2,1,0:T(8,128)} %get-tuple-element.128.before_ref, ...), custom_call_target="tpu_custom_call" | custom-call | flops 20552089600 | bytes 10035200 | tf_op jit(solution)/shard_map/head_forward/pallas_call | solution.py:505
  188.8 11.5 %sum_all.5 = (f32[8,1280]{1,0:T(8,128)}, f32[1,8]{1,0:T(1,128)}) custom-call(f32[2,1280]{1,0:T(2,128)} %get-tuple-element.133.refs_0_, f32[1,8]{1,0:T(1,128)} %get-tuple-element.134.refs_1_, f32[1,1280]{1,0:T(1,128)} %broadcast_in_dim.64.refs_2_, f32[1,1280]{1,0:T(1,128)} %broadcast_in_dim.65.refs_3_), custom_call_target="tpu_custom_call" | custom-call | tf_op jit(solution)/shard_map/sum_all/pallas_call | solution.py:110
  200.3 15.2 %loss_part.1 = (bf16[64,1280]{1,0:T(8,128)(2,1)}, bf16[64,1024]{1,0:T(8,128)(2,1)}, f32[64,1280]{1,0:T(8,128)}, f32[2,1280]{1,0:T(2,128)}, f32[1,1]{1,0:T(1,128)}, /*index=5*/f32[1,1000]{1,0:T(1,128)}) custom-call(bf16[49,64,1280]{2,1,0:T(8,128)(2,1)} %get-tuple-element.132.widened_ref, f32[8,1280]{1,0:T(8,128)} %get-tuple-element.135.norm_ref.refs_3_, ...), custom_call_target="tpu_custom_call" | custom-call | flops 327680000 | bytes 8028160 | tf_op jit(solution)/shard_map/loss_part/pallas_call | solution.py:584
  215.6 1.3 fusion.3
  219.0 1.8 pad_maximum_fusion
  222.8 12.2 %sum_all.6 = (f32[4,1280]{1,0:T(4,128)}, f32[2,1280]{1,0:T(2,128)}, f32[1,1]{1,0:T(1,128)}, f32[1,1000]{1,0:T(1,128)}) custom-call(f32[2,1280]{1,0:T(2,128)} %get-tuple-element.136.refs_0_, f32[1,1]{1,0:T(1,128)} %get-tuple-element.137.refs_1_, f32[1,1000]{1,0:T(1,128)} %get-tuple-element.138.refs_2_, f32[8,1280]{1,0:T(8,128)} %get-tuple-element.135.norm_ref.refs_3_), custom_call_target="tpu_custom_call" | custom-call | tf_op jit(solution)/shard_map/sum_all/pallas_call | solution.py:110
  236.1 39.7 %head_back.1 = (bf16[49,64,1280]{2,1,0:T(8,128)(2,1)}, f32[49,64,320]{2,1,0:T(8,128)}, f32[64,8]{1,0:T(8,128)}, f32[2,320]{1,0:T(2,128)}) custom-call(bf16[49,64,1280]{2,1,0:T(8,128)(2,1)} %get-tuple-element.132.widened_ref, f32[64,1280]{1,0:T(8,128)} %get-tuple-element.145.grad_feats_ref, f32[4,1280]{1,0:T(4,128)} %get-tuple-element.146.coef_ref, ...), custom_call_target="tpu_custom_call" | custom-call | flops 20552089600 | bytes 18063360 | tf_op jit(solution)/shard_map/head_back/pallas_call | solution.py:667
  275.8 32.2 %head_grad.1 = bf16[4,1280,640]{2,1,0:T(8,128)(2,1)} custom-call(bf16[49,64,1280]{2,1,0:T(8,128)(2,1)} %get-tuple-element.151.grad_ref, bf16[49,64,640]{2,1,0:T(8,128)(2,1)} %get-tuple-element.148.twice_ref, bf16[4,64,640]{2,1,0:T(8,128)(2,1)} %get-tuple-element.147.pair_ref), custom_call_target="tpu_custom_call" | custom-call | flops 20552089600 | bytes 8028160 | tf_op jit(solution)/shard_map/head_grad/pallas_call | solution.py:710
  309.6 11.4 %sum_all.7 = (f32[4,320]{1,0:T(4,128)}, f32[2,320]{1,0:T(2,128)}) custom-call(f32[2,320]{1,0:T(2,128)} %get-tuple-element.154.refs_0_, f32[8,320]{1,0:T(8,128)} %get-tuple-element.131.norm_ref.refs_1_), custom_call_target="tpu_custom_call" | custom-call | tf_op jit(solution)/shard_map/sum_all/pallas_call | solution.py:110
  320.9 36.3 %project_back.1 = (bf16[49,64,320]{2,1,0:T(8,128)(2,1)}, bf16[49,64,1152]{2,1,0:T(8,128)(2,1)}, f32[64,8]{1,0:T(8,128)}) custom-call(f32[49,64,320]{2,1,0:T(8,128)} %get-tuple-element.150.grad_ref, f32[49,64,320]{2,1,0:T(8,128)} %get-tuple-element.128.before_ref, f32[4,320]{1,0:T(4,128)} %get-tuple-element.155.coef_ref, ...), custom_call_target="tpu_custom_call" | custom-call | flops 18496880640 | bytes 23281664 | tf_op jit(solution)/shard_map/project_back/pallas_call | solution.py:804
  357.2 28.4 %project_grad.1 = bf16[8,4,40,2304]{3,2,1,0:T(8,128)(2,1)} custom-call(bf16[49,64,320]{2,1,0:T(8,128)(2,1)} %get-tuple-element.157.grad_ref, bf16[49,64,1152]{2,1,0:T(8,128)(2,1)} %get-tuple-element.126.scaled_ref, bf16[4,2,3136]{2,1,0:T(2,128)(2,1)} %tile.9.scale_ref), custom_call_target="tpu_custom_call" | custom-call | flops 18496880640 | bytes 9232384 | tf_op jit(solution)/shard_map/project_grad/pallas_call | solution.py:748
  389.7 1.5 collective-permute-start.1
  391.2 1.4 collective-permute-start.2
  392.6 59.0 %expand_back.1 = (bf16[49,64,1152]{2,1,0:T(8,128)(2,1)}, f32[64,8]{1,0:T(8,128)}, f32[64,1152]{1,0:T(8,128)}, f32[64,48]{1,0:T(8,128)}, f32[9,8,1152]{2,1,0:T(8,128)}) custom-call(bf16[49,64,1152]{2,1,0:T(8,128)(2,1)} %get-tuple-element.161.grad_scaled_ref, bf16[49,64,1152]{2,1,0:T(8,128)(2,1)} %get-tuple-element.162.turned_ref, ...), custom_call_target="tpu_custom_call" | custom-call | flops 11098128384 | bytes 28901376 | tf_op jit(solution)/shard_map/expand_back/pallas_call | solution.py:933
  455.5 2.6 collective-permute-start.5
  459.8 20.2 %expand_grad.1 = bf16[4,1152,384]{2,1,0:T(8,128)(2,1)} custom-call(bf16[49,64,1152]{2,1,0:T(8,128)(2,1)} %get-tuple-element.183.grad_ref, bf16[49,64,384]{2,1,0:T(8,128)(2,1)} %pad_maximum_fusion.1.img_ref.twice_ref, bf16[4,64,384]{2,1,0:T(8,128)(2,1)} %get-tuple-element.184.pair_ref), custom_call_target="tpu_custom_call" | custom-call | flops 11098128384 | bytes 7225344 | tf_op jit(solution)/shard_map/expand_grad/pallas_call | solution.py:710
  480.0 2.9 collective-permute-start.8
  483.2 3.3 collective-permute-done.8
  495.1 3.0 collective-permute-start.9
  500.7 13.8 %soap.3 = (f32[160,2560]{1,0:T(8,128)}, f32[160,2560]{1,0:T(8,128)}, f32[2,8,4,160]{3,2,1,0:T(4,128)}, f32[160,2560]{1,0:T(8,128)}) custom-call(f32[160,2560]{1,0:T(8,128)} %weight_ref.5, bf16[4,160,640]{2,1,0:T(8,128)(2,1)} %slice.88.grad_ref, f32[160,2560]{1,0:T(8,128)} %first_ref.3, f32[160,2560]{1,0:T(8,128)} %second_ref.3, f32[2,8,4,160]{3,2,1,0:T(4,128)} %bitcast.130), custom_call_target="tpu_custom_call" | custom-call | flops 131072000 | bytes 10649600 | tf_op jit(solution)/shard_map/soap/pallas_call | solution.py:1349
  514.5 1.6 multiply_subtract_fusion
  517.1 11.1 %soap.4 = (f32[40,9216]{1,0:T(8,128)}, f32[40,9216]{1,0:T(8,128)}, f32[2,8,4,40]{3,2,1,0:T(4,128)}, f32[40,9216]{1,0:T(8,128)}) custom-call(f32[40,9216]{1,0:T(8,128)} %weight_ref.6, bf16[4,40,2304]{2,1,0:T(8,128)(2,1)} %copy-done.1, f32[40,9216]{1,0:T(8,128)} %first_ref.4, f32[40,9216]{1,0:T(8,128)} %second_ref.4, f32[2,8,4,40]{3,2,1,0:T(4,128)} %bitcast.132), custom_call_target="tpu_custom_call" | custom-call | flops 29491200 | bytes 9584640 | tf_op jit(solution)/shard_map/soap/pallas_call | solution.py:1349
  528.2 3.1 reduce-scatter.11.cloned.1.call-done.refs_2_
  531.3 28.7 %reduce_grads.1 = (bf16[4,18,144]{2,1,0:T(8,128)(2,1)}, bf16[4,32,128]{2,1,0:T(8,128)(2,1)}, bf16[4,144,384]{2,1,0:T(8,128)(2,1)}, bf16[8,4,32,128]{3,2,1,0:T(8,128)(2,1)}) custom-call(bf16[4,4,2,18,144]{4,3,2,1,0:T(8,128)(2,1)} %bitcast.116, bf16[4,4,2,32,128]{4,3,2,1,0:T(8,128)(2,1)} %bitcast.122, ...), custom_call_target="tpu_custom_call" | custom-call | tf_op jit(solution)/shard_map/reduce_grads/pallas_call | solution.py:1090
  565.9 11.4 %soap.5 = (f32[144,1536]{1,0:T(8,128)}, f32[144,1536]{1,0:T(8,128)}, f32[2,8,4,144]{3,2,1,0:T(4,128)}, f32[144,1536]{1,0:T(8,128)}) custom-call(f32[144,1536]{1,0:T(8,128)} %weight_ref.7, bf16[4,144,384]{2,1,0:T(8,128)(2,1)} %get-tuple-element.199.grad_ref, f32[144,1536]{1,0:T(8,128)} %first_ref.5, f32[144,1536]{1,0:T(8,128)} %second_ref.5, ...), custom_call_target="tpu_custom_call" | custom-call | flops 63700992 | bytes 5750784 | tf_op jit(solution)/shard_map/soap/pallas_call | solution.py:1349
  (218 shorter events, 42.4 us)
Async XLA Ops:
  7.2 94.0 %all-gather.4.cloned.1.call-start = ((), (), s32[]{:S(2)}) async-start(), calls=%async_computation.4 | async-start | bytes 6635520 | tf_op jit(solution)/shard_map/all_gather | solution.py:1419
  9.7 149.4 %all-gather.6.cloned.1.call-start = ((), (), s32[]{:S(2)}) async-start(), calls=%async_computation.5 | async-start | bytes 7372800 | tf_op jit(solution)/shard_map/all_gather | solution.py:1420
  10.8 3.6 copy-start.5
  10.8 189.6 %all-gather.8.cloned.1.call-start = ((), (), s32[]{:S(2)}) async-start(), calls=%async_computation.6 | async-start | bytes 2949120 | tf_op jit(solution)/shard_map/all_gather | solution.py:1421
  11.7 296.3 %reduce-scatter.5.cloned.1.call-start = ((), (), s32[]{:S(2)}) async-start(), calls=%async_computation.7 | async-start | bytes 2949120 | tf_op jit(solution)/shard_map/reduce_scatter | solution.py:1458
  55.4 5.1 copy-start.46
  220.9 164.8 %reduce-scatter.7.cloned.1.call-start = ((), (), s32[]{:S(2)}) async-start(), calls=%async_computation.8 | async-start | bytes 7372800 | tf_op jit(solution)/shard_map/reduce_scatter | solution.py:1471
  308.0 143.8 %reduce-scatter.9.cloned.1.call-start = ((), (), s32[]{:S(2)}) async-start(), calls=%async_computation.9 | async-start | bytes 6635520 | tf_op jit(solution)/shard_map/reduce_scatter | solution.py:1489
  385.7 145.6 %reduce-scatter.11.cloned.1.call-start = ((), (), s32[]{:S(2)}) async-start(), calls=%async_computation.10 | async-start | bytes 3981312 | tf_op jit(solution)/shard_map/reduce_scatter | solution.py:1514
  388.8 62.9 %collective-permute-start = (bf16[160,896]{1,0:T(8,128)(2,1)S(1)}, bf16[160,896]{1,0:T(8,128)(2,1)S(1)}, u32[]{:S(2)}, u32[]{:S(2)}) collective-permute-start(bf16[160,896]{1,0:T(8,128)(2,1)S(1)} %get-tuple-element.273), channel_id=1, source_target_pairs={{0,8},{8,16},{16,24},{24,0},{1,9},{9,17},{17,25},{25,1},{2,10},{10... | collective-permute-start | bytes 860168 | tf_op jit(solution)/shard_map/ppermute | solution.py:1130
  389.7 62.0 %collective-permute-start.1 = (bf16[160,896]{1,0:T(8,128)(2,1)S(1)}, bf16[160,896]{1,0:T(8,128)(2,1)S(1)}, u32[]{:S(2)}, u32[]{:S(2)}) collective-permute-start(bf16[160,896]{1,0:T(8,128)(2,1)S(1)} %get-tuple-element.272), channel_id=1, source_target_pairs={{0,16},{8,24},{16,0},{24,8},{1,17},{9,25},{17,1},{25,9},{2,18},{10... | collective-permute-start | bytes 860168 | tf_op jit(solution)/shard_map/ppermute | solution.py:1130
  391.2 60.5 %collective-permute-start.2 = (bf16[160,896]{1,0:T(8,128)(2,1)S(1)}, bf16[160,896]{1,0:T(8,128)(2,1)S(1)}, u32[]{:S(2)}, u32[]{:S(2)}) collective-permute-start(bf16[160,896]{1,0:T(8,128)(2,1)S(1)} %get-tuple-element.271), channel_id=1, source_target_pairs={{0,24},{8,0},{16,8},{24,16},{1,25},{9,1},{17,9},{25,17},{2,26},{10... | collective-permute-start | bytes 860168 | tf_op jit(solution)/shard_map/ppermute | solution.py:1130
  451.8 6.3 %copy-start.8 = (bf16[1,4,40,2304]{3,2,1,0:T(8,128)(2,1)S(1)}, bf16[1,4,40,2304]{3,2,1,0:T(8,128)(2,1)}, u32[]{:S(2)}) copy-start(bf16[1,4,40,2304]{3,2,1,0:T(8,128)(2,1)} %reduce-scatter.9.cloned.1.call-done) | copy-start | bytes 2211844
  454.0 26.0 %collective-permute-start.3 = (bf16[160,896]{1,0:T(8,128)(2,1)S(1)}, bf16[160,896]{1,0:T(8,128)(2,1)S(1)}, u32[]{:S(2)}, u32[]{:S(2)}) collective-permute-start(bf16[160,896]{1,0:T(8,128)(2,1)S(1)} %get-tuple-element.270), channel_id=1, source_target_pairs={{0,8},{8,16},{16,24},{24,0},{1,9},{9,17},{17,25},{25,1},{2,10},{10... | collective-permute-start | bytes 860168 | tf_op jit(solution)/shard_map/ppermute | solution.py:1130
  454.6 28.4 %collective-permute-start.4 = (bf16[160,896]{1,0:T(8,128)(2,1)S(1)}, bf16[160,896]{1,0:T(8,128)(2,1)S(1)}, u32[]{:S(2)}, u32[]{:S(2)}) collective-permute-start(bf16[160,896]{1,0:T(8,128)(2,1)S(1)} %get-tuple-element.270), channel_id=1, source_target_pairs={{0,16},{8,24},{16,0},{24,8},{1,17},{9,25},{17,1},{25,9},{2,18},{10... | collective-permute-start | bytes 860168 | tf_op jit(solution)/shard_map/ppermute | solution.py:1130
  455.5 27.5 %collective-permute-start.5 = (bf16[160,896]{1,0:T(8,128)(2,1)S(1)}, bf16[160,896]{1,0:T(8,128)(2,1)S(1)}, u32[]{:S(2)}, u32[]{:S(2)}) collective-permute-start(bf16[160,896]{1,0:T(8,128)(2,1)S(1)} %get-tuple-element.270), channel_id=1, source_target_pairs={{0,24},{8,0},{16,8},{24,16},{1,25},{9,1},{17,9},{25,17},{2,26},{10... | collective-permute-start | bytes 860168 | tf_op jit(solution)/shard_map/ppermute | solution.py:1130
  458.9 24.2 %collective-permute-start.6 = (bf16[40,2304]{1,0:T(8,128)(2,1)}, bf16[40,2304]{1,0:T(8,128)(2,1)S(1)}, u32[]{:S(2)}, u32[]{:S(2)}) collective-permute-start(bf16[40,2304]{1,0:T(8,128)(2,1)} %get-tuple-element.276), channel_id=1, source_target_pairs={{0,8},{8,16},{16,24},{24,0},{1,9},{9,17},{17,25},{25,1},{2,10},{10... | collective-permute-start | bytes 552968 | tf_op jit(solution)/shard_map/ppermute | solution.py:1130
  458.9 24.2 %collective-permute-start.7 = (bf16[40,2304]{1,0:T(8,128)(2,1)}, bf16[40,2304]{1,0:T(8,128)(2,1)S(1)}, u32[]{:S(2)}, u32[]{:S(2)}) collective-permute-start(bf16[40,2304]{1,0:T(8,128)(2,1)} %get-tuple-element.275), channel_id=1, source_target_pairs={{0,16},{8,24},{16,0},{24,8},{1,17},{9,25},{17,1},{25,9},{2,18},{10... | collective-permute-start | bytes 552968 | tf_op jit(solution)/shard_map/ppermute | solution.py:1130
  480.0 6.4 %collective-permute-start.8 = (bf16[40,2304]{1,0:T(8,128)(2,1)}, bf16[40,2304]{1,0:T(8,128)(2,1)}, u32[]{:S(2)}, u32[]{:S(2)}) collective-permute-start(bf16[40,2304]{1,0:T(8,128)(2,1)} %get-tuple-element.274), channel_id=1, source_target_pairs={{0,24},{8,0},{16,8},{24,16},{1,25},{9,1},{17,9},{25,17},{2,26},{10... | collective-permute-start | bytes 552968 | tf_op jit(solution)/shard_map/ppermute | solution.py:1130
  483.1 5.9 %copy-start.42 = (f32[2,1280]{1,0:T(2,128)S(1)}, f32[2,1280]{1,0:T(2,128)}, u32[]{:S(2)}) copy-start(f32[2,1280]{1,0:T(2,128)} %get-tuple-element.218) | copy-start | bytes 30724
  483.1 6.0 %copy-start.44 = (f32[2,320]{1,0:T(2,128)S(1)}, f32[2,320]{1,0:T(2,128)}, u32[]{:S(2)}) copy-start(f32[2,320]{1,0:T(2,128)} %get-tuple-element.217) | copy-start | bytes 7684
  483.1 6.0 %copy-start.14 = (f32[9,8,1152]{2,1,0:T(8,128)S(1)}, f32[9,8,1152]{2,1,0:T(8,128)}, u32[]{:S(2)}) copy-start(f32[9,8,1152]{2,1,0:T(8,128)} %get-tuple-element.167) | copy-start | bytes 995332
  486.5 4.0 copy-start.26
  486.5 4.0 copy-start.6
  486.5 4.0 copy-start.37
  486.7 4.2 copy-start.18
  495.1 21.0 %collective-permute-start.9 = (bf16[40,2304]{1,0:T(8,128)(2,1)S(1)}, bf16[40,2304]{1,0:T(8,128)(2,1)S(1)}, u32[]{:S(2)}, u32[]{:S(2)}) collective-permute-start(bf16[40,2304]{1,0:T(8,128)(2,1)S(1)} %get-tuple-element.268), channel_id=1, source_target_pairs={{0,8},{8,16},{16,24},{24,0},{1,9},{9,17},{17,25},{25,1},{2,10},{10... | collective-permute-start | bytes 552968 | tf_op jit(solution)/shard_map/ppermute | solution.py:1130
  498.1 18.1 %collective-permute-start.10 = (bf16[40,2304]{1,0:T(8,128)(2,1)S(1)}, bf16[40,2304]{1,0:T(8,128)(2,1)S(1)}, u32[]{:S(2)}, u32[]{:S(2)}) collective-permute-start(bf16[40,2304]{1,0:T(8,128)(2,1)S(1)} %get-tuple-element.268), channel_id=1, source_target_pairs={{0,16},{8,24},{16,0},{24,8},{1,17},{9,25},{17,1},{25,9},{2,18},{10... | collective-permute-start | bytes 552968 | tf_op jit(solution)/shard_map/ppermute | solution.py:1130
  499.0 17.2 %collective-permute-start.11 = (bf16[40,2304]{1,0:T(8,128)(2,1)S(1)}, bf16[40,2304]{1,0:T(8,128)(2,1)S(1)}, u32[]{:S(2)}, u32[]{:S(2)}) collective-permute-start(bf16[40,2304]{1,0:T(8,128)(2,1)S(1)} %get-tuple-element.268), channel_id=1, source_target_pairs={{0,24},{8,0},{16,8},{24,16},{1,25},{9,1},{17,9},{25,17},{2,26},{10... | collective-permute-start | bytes 552968 | tf_op jit(solution)/shard_map/ppermute | solution.py:1130
  500.7 13.8 %copy-start.4 = (f32[160,1000]{1,0:T(8,128)S(1)}, f32[160,1000]{1,0:T(8,128)}, u32[]{:S(2)}) copy-start(f32[160,1000]{1,0:T(8,128)} %param.48) | copy-start | bytes 1920004
  500.7 13.8 %copy-start.9 = (f32[160,1000]{1,0:T(8,128)S(1)}, f32[160,1000]{1,0:T(8,128)}, u32[]{:S(2)}) copy-start(f32[160,1000]{1,0:T(8,128)} %param.50) | copy-start | bytes 1920004
  500.7 13.8 %copy-start.10 = (f32[160,1000]{1,0:T(8,128)S(1)}, f32[160,1000]{1,0:T(8,128)}, u32[]{:S(2)}) copy-start(f32[160,1000]{1,0:T(8,128)} %param.49) | copy-start | bytes 1920004
  (36 other events, 75.3 us)
Sparse Core Ops, SparseCore 0:
  10.3 80.3 all-gather.3
  92.9 66.1 all-gather.5
  161.3 32.4 all-gather.7
  221.0 37.6 reduce-scatter.4
  308.1 72.8 reduce-scatter.6
  385.8 65.2 reduce-scatter.8
  486.6 44.6 reduce-scatter.10

commit v6 on v5

--- a/solution.py
+++ b/solution.py
@@ -47,14 +47,8 @@
 MESH = pl.DeviceIdType.MESH
 
 
-def sum_kernel(n_wide, n_dp, count, extra, finish, *refs):
-    parts, extras = refs[:count], refs[count : count + extra]
-    scratch = list(refs[-(3 * count + 4) :])
-    outs = refs[count + extra : len(refs) - len(scratch)]
-    wide_slots, dp_slots, halves = (scratch[k * count : (k + 1) * count] for k in range(3))
-    s_wide, r_wide, s_dp, r_dp = scratch[3 * count :]
-    me_wide = lax.axis_index("wide")
-    me_dp = lax.axis_index("dp")
+def greet(n_wide, n_dp):
+    me_wide, me_dp = lax.axis_index("wide"), lax.axis_index("dp")
     barrier = pltpu.get_barrier_semaphore()
     for k in range(1, n_wide):
         pl.semaphore_signal(
@@ -64,58 +58,74 @@
         pl.semaphore_signal(
             barrier, inc=1, device_id={"dp": lax.rem(me_dp + k, n_dp)}, device_id_type=MESH
         )
-    pl.semaphore_wait(barrier, n_wide + n_dp - 2)
-
-    def exchange(sources, slots, me, axis, size, send, recv):
-        copies = []
+
+
+def await_greetings(n_wide, n_dp):
+    pl.semaphore_wait(pltpu.get_barrier_semaphore(), n_wide + n_dp - 2)
+
+
+def sum_scratch(shapes, n_wide, n_dp):
+    count = len(shapes)
+    found = [pltpu.VMEM((n_wide,) + shape, jnp.float32) for shape in shapes]
+    found += [pltpu.VMEM((n_dp,) + shape, jnp.float32) for shape in shapes]
+    found += [pltpu.VMEM(shape, jnp.float32) for shape in shapes] * 2
+    return found + [
+        pltpu.SemaphoreType.DMA((size * count,)) for size in (n_wide, n_wide, n_dp, n_dp)
+    ]
+
+
+def sum_copies(axis, size, sources, slots, send, recv):
+    me, count = lax.axis_index(axis), len(sources)
+    return [
+        pltpu.make_async_remote_copy(
+            src_ref=sources[index],
+            dst_ref=slots[index].at[me],
+            send_sem=send.at[k * count + index],
+            recv_sem=recv.at[k * count + index],
+            device_id={axis: lax.rem(me + k, size)},
+            device_id_type=MESH,
+        )
+        for k in range(1, size)
+        for index in range(count)
+    ]
+
+
+def sum_slots(axis, size, sources, slots):
+    me = lax.axis_index(axis)
+    for source, slot in zip(sources, slots):
+        slot[me] = source[...]
+    found = []
+    for slot in slots:
+        total = slot[0]
         for k in range(1, size):
-            for index in range(count):
-                copy = pltpu.make_async_remote_copy(
-                    src_ref=sources[index],
-                    dst_ref=slots[index].at[me],
-                    send_sem=send.at[k * count + index],
-                    recv_sem=recv.at[k * count + index],
-                    device_id={axis: lax.rem(me + k, size)},
-                    device_id_type=MESH,
-                )
-                copy.start()
-                copies.append(copy)
-        for source, slot in zip(sources, slots):
-            slot[me] = source[...]
-        for copy in copies:
-            copy.wait()
-        found = []
-        for slot in slots:
-            total = slot[0]
-            for k in range(1, size):
-                total = total + slot[k]
-            found.append(total)
-        return found
-
-    for half, total in zip(halves, exchange(parts, wide_slots, me_wide, "wide", n_wide, s_wide, r_wide)):
+            total = total + slot[k]
+        found.append(total)
+    return found
+
+
+def sum_open(n_wide, n_dp, values, scratch):
+    count = len(values)
+    wide_slots, own = scratch[:count], scratch[2 * count : 3 * count]
+    for ref, value in zip(own, values):
+        ref[...] = value
+    for copy in sum_copies("wide", n_wide, own, wide_slots, *scratch[4 * count : 4 * count + 2]):
+        copy.start()
+
+
+def sum_close(n_wide, n_dp, scratch):
+    count = (len(scratch) - 4) // 4
+    wide_slots, dp_slots, own, halves = (scratch[k * count : (k + 1) * count] for k in range(4))
+    s_wide, r_wide, s_dp, r_dp = scratch[4 * count :]
+    for copy in sum_copies("wide", n_wide, own, wide_slots, s_wide, r_wide):
+        copy.wait()
+    for half, total in zip(halves, sum_slots("wide", n_wide, own, wide_slots)):
         half[...] = total
-    totals = exchange(halves, dp_slots, me_dp, "dp", n_dp, s_dp, r_dp)
-    finish(totals, extras, outs)
-
-
-def sum_all(parts, extras, finish, outs, ident):
-    n_wide = lax.axis_size("wide")
-    n_dp = lax.axis_size("dp")
-    count = len(parts)
-    vmem = pl.BlockSpec(memory_space=pltpu.VMEM)
-    scratch = [pltpu.VMEM((n_wide,) + part.shape, jnp.float32) for part in parts]
-    scratch += [pltpu.VMEM((n_dp,) + part.shape, jnp.float32) for part in parts]
-    scratch += [pltpu.VMEM(part.shape, jnp.float32) for part in parts]
-    sems = [pltpu.SemaphoreType.DMA((size * count,)) for size in (n_wide, n_wide, n_dp, n_dp)]
-    return pl.pallas_call(
-        functools.partial(sum_kernel, n_wide, n_dp, count, len(extras), finish),
-        name="sum_all",
-        out_shape=[jax.ShapeDtypeStruct(shape, jnp.float32) for shape in outs],
-        in_specs=[vmem] * (count + len(extras)),
-        out_specs=[vmem] * len(outs),
-        scratch_shapes=scratch + sems,
-        compiler_params=pltpu.CompilerParams(collective_id=ident, has_side_effects=True),
-    )(*parts, *extras)
+    copies = sum_copies("dp", n_dp, halves, dp_slots, s_dp, r_dp)
+    for copy in copies:
+        copy.start()
+    for copy in copies:
+        copy.wait()
+    return sum_slots("dp", n_dp, halves, dp_slots)
 
 
 def norm_finish(count, every, totals, extras, outs):
@@ -218,7 +228,9 @@
     return pl.BlockSpec(shape, lambda i: (0,) * len(shape))
 
 
-def device_kernel(kernel, name, grid, in_specs, outs, out_specs, scratch, flops, moved, cap=None):
+def device_kernel(
+    kernel, name, grid, in_specs, outs, out_specs, scratch, flops, moved, ident=None
+):
     return pl.pallas_call(
         kernel,
         name=name,
@@ -228,7 +240,8 @@
         out_specs=out_specs,
         scratch_shapes=scratch,
         compiler_params=pltpu.CompilerParams(
-            vmem_limit_bytes=cap or VMEM_CAP, dimension_semantics=("arbitrary",)
+            vmem_limit_bytes=VMEM_CAP, dimension_semantics=("arbitrary",), collective_id=ident,
+            has_side_effects=ident is not None,
         ),
         cost_estimate=pl.CostEstimate(flops=flops, bytes_accessed=moved, transcendentals=0),
     )
@@ -417,13 +430,17 @@
 
 
 def project_kernel(
-    scaled_ref, source, pair_ref, each_ref, before_ref, sums_ref, product, weight_ref, sem
+    n_wide, n_dp, count, every,
+    scaled_ref, source, pair_ref, route_ref, gain_ref, shift_ref,
+    each_ref, before_ref, norm_ref, route_total_ref,
+    weight_ref, sem, sums_ref, *small
 ):
     half = 2 * 2 * C_OUT
     flat = scaled_ref[...].reshape(ROWS, C_MID)
 
     @pl.when(pl.program_id(0) == 0)
     def _():
+        greet(n_wide, n_dp)
         stack_experts(source, weight_ref, sem)
         sums_ref[...] = jnp.zeros_like(sums_ref)
 
@@ -442,33 +459,54 @@
     sums_ref[0:1] += jnp.sum(before, axis=0, keepdims=True)
     sums_ref[1:2] += jnp.sum(before * before, axis=0, keepdims=True)
 
-
-def project_forward(scaled, project_low, pair_out):
+    @pl.when(pl.program_id(0) == pl.num_programs(0) - 1)
+    def _():
+        await_greetings(n_wide, n_dp)
+        sum_open(n_wide, n_dp, [sums_ref[...], route_ref[...]], small)
+        totals = sum_close(n_wide, n_dp, small)
+        norm_finish(count, every, totals, (gain_ref, shift_ref), (norm_ref, route_total_ref))
+
+
+def project_forward(scaled, project_low, pair_out, route_sum, gain, shift, every, ident):
     images = scaled.shape[1]
     wide = EXPERTS * C_OUT
+    n_wide, n_dp = lax.axis_size("wide"), lax.axis_size("dp")
     return device_kernel(
-        project_kernel,
+        functools.partial(project_kernel, n_wide, n_dp, every * PIX, every),
         "project_forward",
         images // GROUP,
-        [images_block(C_MID), pl.BlockSpec(memory_space=pl.ANY), pair_block(2 * C_OUT)],
-        [((PIX, images, wide), LOW), ((PIX, images, C_OUT), FULL), ((2, C_OUT), FULL)],
-        [images_block(wide), images_block(C_OUT), total_block(2, C_OUT)],
-        [
-            pltpu.VMEM((2, PIX, GROUP, wide // 2), FULL), pltpu.VMEM((wide, C_MID), LOW),
-            pltpu.SemaphoreType.DMA((EXPERTS,)),
-        ],
+        [
+            images_block(C_MID), pl.BlockSpec(memory_space=pl.ANY), pair_block(2 * C_OUT),
+            whole(1, EXPERTS), whole(1, C_OUT), whole(1, C_OUT),
+        ],
+        [
+            ((PIX, images, wide), LOW), ((PIX, images, C_OUT), FULL), ((8, C_OUT), FULL),
+            ((1, EXPERTS), FULL),
+        ],
+        [
+            images_block(wide), images_block(C_OUT), total_block(8, C_OUT),
+            total_block(1, EXPERTS),
+        ],
+        [
+            pltpu.VMEM((wide, C_MID), LOW), pltpu.SemaphoreType.DMA((EXPERTS,)),
+            pltpu.VMEM((2, C_OUT), FULL),
+        ]
+        + sum_scratch([(2, C_OUT), (1, EXPERTS)], n_wide, n_dp),
         2 * PIX * images * wide * C_MID,
         PIX * images * (wide + C_MID) * 2,
-    )(scaled, project_low, pair_out)
+        ident,
+    )(scaled, project_low, pair_out, route_sum, gain, shift)
 
 
 def head_kernel(
-    before_ref, norm_ref, hot_ref, router_ref, weight_ref,
-    widened_ref, twice_ref, route_ref, pair_ref, pooled_ref, sums_ref, route_sum_ref,
-    routed, padded,
+    n_wide, n_dp, count, every,
+    before_ref, norm_ref, hot_ref, router_ref, weight_ref, gain_ref, shift_ref,
+    widened_ref, twice_ref, route_ref, pair_ref, pooled_ref, new_norm_ref, route_total_ref,
+    routed, padded, sums_ref, route_sum_ref, *small
 ):
     @pl.when(pl.program_id(0) == 0)
     def _():
+        greet(n_wide, n_dp)
         sums_ref[...] = jnp.zeros_like(sums_ref)
         route_sum_ref[...] = jnp.zeros_like(route_sum_ref)
         padded[...] = jnp.zeros_like(padded)
@@ -498,40 +536,59 @@
     sums_ref[0:1] += jnp.sum(product, axis=0, keepdims=True)
     sums_ref[1:2] += jnp.sum(product * product, axis=0, keepdims=True)
 
-
-def head_forward(before, norm, hot, router, head_low):
+    @pl.when(pl.program_id(0) == pl.num_programs(0) - 1)
+    def _():
+        await_greetings(n_wide, n_dp)
+        sum_open(n_wide, n_dp, [sums_ref[...], route_sum_ref[...]], small)
+        totals = sum_close(n_wide, n_dp, small)
+        norm_finish(count, every, totals, (gain_ref, shift_ref), (new_norm_ref, route_total_ref))
+
+
+def head_forward(before, norm, hot, router, head_low, gain, shift, every, ident):
     images = before.shape[1]
     wide = EXPERTS * C_OUT
+    n_wide, n_dp = lax.axis_size("wide"), lax.axis_size("dp")
     return device_kernel(
-        head_kernel,
+        functools.partial(head_kernel, n_wide, n_dp, every * PIX, every),
         "head_forward",
         images // GROUP,
         [
             images_block(C_OUT), whole(8, C_OUT), group_block(EXPERTS), whole(EXPERTS, C_OUT),
-            whole(C_HEAD, wide),
+            whole(C_HEAD, wide), whole(1, C_HEAD), whole(1, C_HEAD),
         ],
         [
             ((PIX, images, C_HEAD), LOW), ((PIX, images, 2 * C_OUT), LOW),
             ((images, EXPERTS), FULL), ((PAIRS, images, 2 * C_OUT), LOW), ((images, C_OUT), FULL),
-            ((2, C_HEAD), FULL), ((1, EXPERTS), FULL),
+            ((8, C_HEAD), FULL), ((1, EXPERTS), FULL),
         ],
         [
             images_block(C_HEAD), images_block(2 * C_OUT), group_block(EXPERTS),
-            pair_block(2 * C_OUT), group_block(C_OUT), total_block(2, C_HEAD),
+            pair_block(2 * C_OUT), group_block(C_OUT), total_block(8, C_HEAD),
             total_block(1, EXPERTS),
         ],
-        [pltpu.VMEM((PIX, GROUP, wide), LOW), pltpu.VMEM((GROUP, 2 * C_OUT), FULL)],
+        [
+            pltpu.VMEM((PIX, GROUP, wide), LOW), pltpu.VMEM((GROUP, 2 * C_OUT), FULL),
+            pltpu.VMEM((2, C_HEAD), FULL), pltpu.VMEM((1, EXPERTS), FULL),
+        ]
+        + sum_scratch([(2, C_HEAD), (1, EXPERTS)], n_wide, n_dp),
         2 * PIX * images * wide * C_HEAD,
         PIX * images * (C_HEAD + C_OUT) * 2,
-    )(before, norm, hot, router, head_low)
+        ident,
+    )(before, norm, hot, router, head_low, gain, shift)
 
 
 def loss_kernel(
+    n_wide, n_dp, count,
     widened_ref, norm_ref, label_ref, class_ref, bias_ref,
-    feats_ref, logits_ref, grad_feats_ref, sums_ref, cross_ref, bias_grad_ref,
-    silu_sum, slope_sum, cross_sum,
+    feats_ref, logits_ref, grad_feats_ref, coef_ref, sums_ref, cross_ref, bias_grad_ref,
+    silu_sum, slope_sum, cross_sum, *small
 ):
     step = pl.program_id(0)
+
+    @pl.when(step == 0)
+    def _():
+        greet(n_wide, n_dp)
+
     rows = pl.ds(pl.multiple_of(step * GROUP, GROUP), GROUP)
 
     def chunk(index, carry):
@@ -567,22 +624,27 @@
         cross = top + jnp.log(totals) - jnp.sum(
             jnp.where(picked, logits, 0.0), axis=1, keepdims=True
         )
-        cross_ref[...] = jnp.sum(cross, axis=0, keepdims=True)
+        cross = jnp.sum(cross, axis=0, keepdims=True)
         grad = (powers / totals - jnp.where(picked, 1.0, 0.0)) * norm_ref[4:5, 0:1]
         grad = grad.astype(LOW)
         logits_ref[...] = jnp.zeros_like(logits_ref)
         logits_ref[:, :CLASSES] = grad
-        bias_grad_ref[...] = jnp.sum(grad.astype(FULL), axis=0, keepdims=True)
+        bias_grad = jnp.sum(grad.astype(FULL), axis=0, keepdims=True)
         grad_feats = dot_nt(grad, class_ref[...]) * (1.0 / PIX)
         grad_feats_ref[...] = grad_feats
         sums_ref[0:1] = jnp.sum(grad_feats * slope_sum[...], axis=0, keepdims=True)
         sums_ref[1:2] = jnp.sum(grad_feats * cross_sum[...], axis=0, keepdims=True)
-
-
-def loss_part(widened, norm, label, class_low, bias):
+        await_greetings(n_wide, n_dp)
+        sum_open(n_wide, n_dp, [sums_ref[...], cross, bias_grad], small)
+        totals = sum_close(n_wide, n_dp, small)
+        back_finish(count, totals, (norm_ref,), (coef_ref, sums_ref, cross_ref, bias_grad_ref))
+
+
+def loss_part(widened, norm, label, class_low, bias, every, ident):
     images = widened.shape[1]
+    n_wide, n_dp = lax.axis_size("wide"), lax.axis_size("dp")
     return device_kernel(
-        loss_kernel,
+        functools.partial(loss_kernel, n_wide, n_dp, every * PIX),
         "loss_part",
         images // GROUP,
         [
@@ -591,15 +653,18 @@
         ],
         [
             ((images, C_HEAD), LOW), ((images, CLASS_PAD), LOW), ((images, C_HEAD), FULL),
-            ((2, C_HEAD), FULL), ((1, 1), FULL), ((1, CLASSES), FULL),
+            ((4, C_HEAD), FULL), ((2, C_HEAD), FULL), ((1, 1), FULL), ((1, CLASSES), FULL),
         ],
         [
             total_block(images, C_HEAD), total_block(images, CLASS_PAD), total_block(images, C_HEAD),
-            total_block(2, C_HEAD), total_block(1, 1), total_block(1, CLASSES),
-        ],
-        [pltpu.VMEM((images, C_HEAD), FULL)] * 3,
+            total_block(4, C_HEAD), total_block(2, C_HEAD), total_block(1, 1),
+            total_block(1, CLASSES),
+        ],
+        [pltpu.VMEM((images, C_HEAD), FULL)] * 3
+        + sum_scratch([(2, C_HEAD), (1, 1), (1, CLASSES)], n_wide, n_dp),
         4 * images * C_HEAD * CLASSES,
         PIX * images * C_HEAD * 2,
+        ident,
     )(widened, norm, label, class_low, bias)
 
 
@@ -721,6 +786,54 @@
         2 * rows * out_width * PAIRS * width,
         rows * out_width * 2,
     )(grad, twice, pair_scales)[0]
+
+
+def head_grad_kernel(
+    n_wide, n_dp, count, sums_ref, norm_ref, grad_ref, twice_ref, pair_ref,
+    coef_ref, total_ref, out_ref, turned, routed, *small
+):
+    step = pl.program_id(0)
+
+    @pl.when(step == 0)
+    def _():
+        greet(n_wide, n_dp)
+
+    kern_grad_kernel(grad_ref, twice_ref, pair_ref, out_ref, turned, routed)
+
+    @pl.when(step == 0)
+    def _():
+        await_greetings(n_wide, n_dp)
+        sum_open(n_wide, n_dp, [sums_ref[...]], small)
+
+    @pl.when(step == pl.num_programs(0) - 1)
+    def _():
+        totals = sum_close(n_wide, n_dp, small)
+        back_finish(count, totals, (norm_ref,), (coef_ref, total_ref))
+
+
+def head_grad(sums, norm, grad, twice, pair_scales, every, ident):
+    images, out_width, width = grad.shape[1], grad.shape[2], twice.shape[2]
+    rows = PIX * images
+    n_wide, n_dp = lax.axis_size("wide"), lax.axis_size("dp")
+    return device_kernel(
+        functools.partial(head_grad_kernel, n_wide, n_dp, every * PIX),
+        "head_grad",
+        PAIRS // 2,
+        [
+            whole(2, C_OUT), whole(8, C_OUT), whole(PIX, images, out_width),
+            whole(PIX, images, width), pl.BlockSpec((2, images, width), lambda i: (i, 0, 0)),
+        ],
+        [((4, C_OUT), FULL), ((2, C_OUT), FULL), ((PAIRS, out_width, width), LOW)],
+        [
+            total_block(4, C_OUT), total_block(2, C_OUT),
+            pl.BlockSpec((2, out_width, width), lambda i: (i, 0, 0)),
+        ],
+        [pltpu.VMEM((out_width, rows), LOW), pltpu.VMEM((rows, 2 * width), LOW)]
+        + sum_scratch([(2, C_OUT)], n_wide, n_dp),
+        2 * rows * out_width * PAIRS * width,
+        rows * out_width * 2,
+        ident,
+    )(sums, norm, grad, twice, pair_scales)
 
 
 def project_grad_kernel(grad_ref, scaled_ref, scale_ref, out_ref, turned, routed):
@@ -1436,44 +1549,32 @@
     ) = expand_forward(
         img_two, hot, router_one, expand_low, depth_full, excite, bias_se[None], bias_ex[None]
     )
-    each, before, sums_one = project_forward(scaled, project_low, pair_one)
-    norm_one, route_one_sum = sum_all(
-        (sums_one, route_one_sum), (gain_one[None], shift_one[None]),
-        functools.partial(norm_finish, count, every), ((8, C_OUT), (1, EXPERTS)), 1,
-    )
-    widened, twice, route_two, pair_two, pooled_two, sums_two, route_two_sum = head_forward(
-        before, norm_one, hot, router_two, head_low
-    )
-    norm_two, route_two_sum = sum_all(
-        (sums_two, route_two_sum), (gain_two[None], shift_two[None]),
-        functools.partial(norm_finish, count, every), ((8, C_HEAD), (1, EXPERTS)), 2,
-    )
-    feats, grad_logits, grad_feats, back_two, cross_part, grad_bias_cls = loss_part(
-        widened, norm_two, class_label[:, None], class_low, bias_cls[None]
+    each, before, norm_one, route_one_sum = project_forward(
+        scaled, project_low, pair_one, route_one_sum, gain_one[None], shift_one[None], every, 1
+    )
+    widened, twice, route_two, pair_two, pooled_two, norm_two, route_two_sum = head_forward(
+        before, norm_one, hot, router_two, head_low, gain_two[None], shift_two[None], every, 2
+    )
+    feats, grad_logits, grad_feats, coef_two, back_two, cross_total, grad_bias_cls = loss_part(
+        widened, norm_two, class_label[:, None], class_low, bias_cls[None], every, 3
     )
     grad_class = jnp.stack(
         [dot_tn(feats, part).astype(low_type) for part in jnp.split(grad_logits, PAIRS, axis=1)]
     )
     grad_class, grad_feats = lax.optimization_barrier((grad_class, grad_feats))
     share_class = lax.psum_scatter(grad_class, "wide", scatter_dimension=1, tiled=True)
-    coef_two, back_two, cross_total, grad_bias_cls = sum_all(
-        (back_two, cross_part, grad_bias_cls), (norm_two,), functools.partial(back_finish, count),
-        ((4, C_HEAD), (2, C_HEAD), (1, 1), (1, CLASSES)), 3,
-    )
     means_one = route_one_sum[0] / every
     means_two = route_two_sum[0] / every
     grad_widened, grad_normed, grad_logit_two, back_one = head_back(
         widened, grad_feats, coef_two, head_low, pair_two, twice, before, norm_one, route_two,
         balance_grad(means_two, every)[None], router_two,
     )
-    grad_head = kern_grad(grad_widened, twice, pair_two, "head_grad")
-    grad_head, back_one, share_class = lax.optimization_barrier((grad_head, back_one, share_class))
+    coef_one, back_one, grad_head = head_grad(
+        back_one, norm_one, grad_widened, twice, pair_two, every, 4
+    )
+    coef_one, share_class = lax.optimization_barrier((coef_one, share_class))
     share_head = lax.psum_scatter(grad_head, "wide", scatter_dimension=1, tiled=True)
     grad_router_two = dot_tn(pooled_two, grad_logit_two, HIGH)
-    coef_one, back_one = sum_all(
-        (back_one,), (norm_one,), functools.partial(back_finish, count),
-        ((4, C_OUT), (2, C_OUT)), 4,
-    )
     grad_before, grad_scaled, route_project = project_back(
         grad_normed, before, coef_one, pair_one, each, project_low
     )

time: 589 us -> 580 us (0.985)
  Pallas kernels: 489 us -> 473 us
  waiting for transfers between devices: 13.3 us -> 19.5 us
    pallas_call x2 -> x1, Pallas kernels: 52.3 us -> 20.2 us  [kern_grad(): device_kernel(kern_grad_kernel, name, PAIRS // 2, [whole(PIX, images, out...]
    pallas_call x7 -> x4, Pallas kernels: 131 us -> 147 us  [the longest x1 48.4 us: project_forward(): device_kernel(functools.partial(project_kernel, n_wide, n_dp, every * PIX...]
  transfers between devices with their start and end apart: 19 -> 19, of which waited for: 3 -> 4; matrix products, arithmetic and copies ran while one was open for 5% -> 5% of each run, Pallas kernels for 74% -> 71%
where the time goes in v6:
time: 580 us; the launch traced here: 576 us
  Pallas kernels  473 us (82%)
  local copies, waits for them, and re-layouts  21.2 us (4%)
  other arithmetic  21 us (4%)
  between operations  19.8 us (3%)
  waiting for transfers between devices  19.5 us (3%)
  starting transfers between devices  16.8 us (3%)
    pallas_call x1, Pallas kernels, expand_back(): device_kernel(expand_back_kernel, 'expand_back', images // GROUP, [images...  59 us
    pallas_call x1, Pallas kernels, project_forward(): device_kernel(functools.partial(project_kernel, n_wide, n_dp, every * PIX...  48.4 us
    pallas_call x1, Pallas kernels, expand_forward(): device_kernel(expand_kernel, 'expand_forward', images // GROUP, [images_b...  40 us
    pallas_call x1, Pallas kernels, head_back(): device_kernel(head_back_kernel, 'head_back', images // GROUP, [images_blo...  39.9 us
    pallas_call x1, Pallas kernels, head_forward(): device_kernel(functools.partial(head_kernel, n_wide, n_dp, every * PIX, e...  39.1 us
    pallas_call x1, Pallas kernels, gather_expand(): pl.pallas_call(functools.partial(gather_kernel, n_wide, n_dp), name='gath...  37.2 us
    pallas_call x1, Pallas kernels, project_back(): device_kernel(project_back_kernel, 'project_back', images // GROUP, [imag...  36.7 us
    pallas_call x1, Pallas kernels, head_grad(): device_kernel(functools.partial(head_grad_kernel, n_wide, n_dp, every * P...  36.4 us
  transfers between devices with their start and end apart: 19, of which 4 were waited for; matrix products, arithmetic and copies ran while one was open for 5% of the time, Pallas kernels for 71%

profile of v6, /device:TPU:0, one launch (start us, length us, event | category | flops | bytes accessed | tf_op | source)
XLA Modules:
  0.0 576.3 jit_solution(15085284619000545961)
XLA Ops:
  7.3 2.4 convert_element_type.127
  14.4 2.4 pad_maximum_fusion.1.img_ref.twice_ref
  18.2 37.2 %gather_expand.1 = (bf16[4,4,2,144,384]{4,3,2,1,0:T(8,128)(2,1)}, bf16[8,80,144]{2,1,0:T(8,128)(2,1)}) custom-call(f32[144,1536]{1,0:T(8,128)} %weight_ref.7, bf16[80,144]{1,0:T(8,128)(2,1)} %pad.8.depth_ref), custom_call_target="tpu_custom_call" | custom-call | tf_op jit(solution)/shard_map/gather_expand/pallas_call | solution.py:1339
  61.2 40.0 %expand_forward.1 = (bf16[49,64,1152]{2,1,0:T(8,128)(2,1)}, bf16[49,64,1152]{2,1,0:T(8,128)(2,1)}, bf16[49,64,1152]{2,1,0:T(8,128)(2,1)}, f32[64,8]{1,0:T(8,128)...) custom-call(bf16[49,64,384]{2,1,0:T(8,128)(2,1)} %pad_maximum_fusion, ...), custom_call_target="tpu_custom_call" | custom-call | flops 11098128384 | bytes 28901376 | tf_op jit(solution)/shard_map/expand_forward/pallas_call | solution.py:377
  101.2 48.4 %project_forward.1 = (bf16[49,64,2560]{2,1,0:T(8,128)(2,1)}, f32[49,64,320]{2,1,0:T(8,128)}, f32[8,320]{1,0:T(8,128)}, f32[1,8]{1,0:T(1,128)}) custom-call(bf16[49,64,1152]{2,1,0:T(8,128)(2,1)} %get-tuple-element.120.scaled_ref, bf16[320,9216]{1,0:T(8,128)(2,1)} %all-gather.4.cloned.1.call-done.source, bf16[4,64,640]{2,1,0:T(8,128)(2,1)} %get-tuple-element.121.pair_ref, ...), custom_call_target="tpu_custom_call" | custom-call | flops 18496880640 | bytes 23281664 | tf_op jit(solution)/shard_map/project_forward/pallas_call | solution.py:474
  149.6 9.4 %all-gather.6.cloned.1.call-done.weight_ref = bf16[1280,2560]{1,0:T(8,128)(2,1)} async-done(((bf16[160,2560]{1,0:T(8,128)(2,1)}), bf16[1280,2560]{1,0:T(8,128)(2,1)}) %all-gather.6.cloned.1.call-update) | async-done | bytes 6553616 | tf_op jit(solution)/shard_map/all_gather | solution.py:1533
  159.1 39.1 %head_forward.1 = (bf16[49,64,1280]{2,1,0:T(8,128)(2,1)}, bf16[49,64,640]{2,1,0:T(8,128)(2,1)}, f32[64,8]{1,0:T(8,128)}, bf16[4,64,640]{2,1,0:T(8,128)(2,1)}, f3...) custom-call(f32[49,64,320]{2,1,0:T(8,128)} %get-tuple-element.123.before_ref, ...), custom_call_target="tpu_custom_call" | custom-call | flops 20552089600 | bytes 10035200 | tf_op jit(solution)/shard_map/head_forward/pallas_call | solution.py:551
  198.2 23.3 %loss_part.1 = (bf16[64,1280]{1,0:T(8,128)(2,1)}, bf16[64,1024]{1,0:T(8,128)(2,1)}, f32[64,1280]{1,0:T(8,128)}, f32[4,1280]{1,0:T(4,128)}, f32[2,1280]{1,0:T(2,128)}, /*index=5*/f32[1,1]{1,0:T(1,128)}, f32[1,1000]{1,0:T(1,128)}) custom-call(bf16[49,64,1280]{2,1,0:T(8,128)(2,1)} %get-tuple-element.125.widened_ref, f32[8,1280]{1,0:T(8,128)} %get-tuple-element.126.norm_ref, ...), custom_call_target="tpu_custom_call" | custom-call | flops 327680000 | bytes 8028160 | tf_op jit(solution)/shard_map/loss_part/pallas_call | solution.py:646
  221.5 1.3 fusion.3
  224.9 1.8 pad_maximum_fusion
  229.8 39.9 %head_back.1 = (bf16[49,64,1280]{2,1,0:T(8,128)(2,1)}, f32[49,64,320]{2,1,0:T(8,128)}, f32[64,8]{1,0:T(8,128)}, f32[2,320]{1,0:T(2,128)}) custom-call(bf16[49,64,1280]{2,1,0:T(8,128)(2,1)} %get-tuple-element.125.widened_ref, f32[64,1280]{1,0:T(8,128)} %get-tuple-element.133.grad_feats_ref, f32[4,1280]{1,0:T(4,128)} %get-tuple-element.134.coef_ref, ...), custom_call_target="tpu_custom_call" | custom-call | flops 20552089600 | bytes 18063360 | tf_op jit(solution)/shard_map/head_back/pallas_call | solution.py:732
  269.6 36.4 %head_grad.1 = (f32[4,320]{1,0:T(4,128)}, f32[2,320]{1,0:T(2,128)}, bf16[4,1280,640]{2,1,0:T(8,128)(2,1)}) custom-call(f32[2,320]{1,0:T(2,128)} %get-tuple-element.139.sums_ref, f32[8,320]{1,0:T(8,128)} %get-tuple-element.124.norm_ref, bf16[49,64,1280]{2,1,0:T(8,128)(2,1)} %get-tuple-element.140.grad_ref, bf16[49,64,640]{2,1,0:T(8,128)(2,1)} %get-tuple-element.136.twice_ref, ...), custom_call_target="tpu_custom_call" | custom-call | flops 20552089600 | bytes 8028160 | tf_op jit(solution)/shard_map/head_grad/pallas_call | solution.py:818
  307.7 36.7 %project_back.1 = (bf16[49,64,320]{2,1,0:T(8,128)(2,1)}, bf16[49,64,1152]{2,1,0:T(8,128)(2,1)}, f32[64,8]{1,0:T(8,128)}) custom-call(f32[49,64,320]{2,1,0:T(8,128)} %get-tuple-element.138.grad_ref, f32[49,64,320]{2,1,0:T(8,128)} %get-tuple-element.123.before_ref, f32[4,320]{1,0:T(4,128)} %get-tuple-element.143.coef_ref, ...), custom_call_target="tpu_custom_call" | custom-call | flops 18496880640 | bytes 23281664 | tf_op jit(solution)/shard_map/project_back/pallas_call | solution.py:917
  344.3 28.4 %project_grad.1 = bf16[8,4,40,2304]{3,2,1,0:T(8,128)(2,1)} custom-call(bf16[49,64,320]{2,1,0:T(8,128)(2,1)} %get-tuple-element.145.grad_ref, bf16[49,64,1152]{2,1,0:T(8,128)(2,1)} %get-tuple-element.120.scaled_ref, bf16[4,2,3136]{2,1,0:T(2,128)(2,1)} %tile.9.scale_ref), custom_call_target="tpu_custom_call" | custom-call | flops 18496880640 | bytes 9232384 | tf_op jit(solution)/shard_map/project_grad/pallas_call | solution.py:861
  372.7 4.1 reduce-scatter.7.cloned.1.call-done
  380.1 1.5 collective-permute-start
  381.6 1.5 collective-permute-start.1
  383.1 1.4 collective-permute-start.2
  384.5 59.0 %expand_back.1 = (bf16[49,64,1152]{2,1,0:T(8,128)(2,1)}, f32[64,8]{1,0:T(8,128)}, f32[64,1152]{1,0:T(8,128)}, f32[64,48]{1,0:T(8,128)}, f32[9,8,1152]{2,1,0:T(8,128)}) custom-call(bf16[49,64,1152]{2,1,0:T(8,128)(2,1)} %get-tuple-element.149.grad_scaled_ref, bf16[49,64,1152]{2,1,0:T(8,128)(2,1)} %get-tuple-element.150.turned_ref, ...), custom_call_target="tpu_custom_call" | custom-call | flops 11098128384 | bytes 28901376 | tf_op jit(solution)/shard_map/expand_back/pallas_call | solution.py:1046
  446.5 1.4 collective-permute-start.4
  448.0 1.5 collective-permute-start.5
  451.6 20.2 %expand_grad.1 = bf16[4,1152,384]{2,1,0:T(8,128)(2,1)} custom-call(bf16[49,64,1152]{2,1,0:T(8,128)(2,1)} %get-tuple-element.171.grad_ref, bf16[49,64,384]{2,1,0:T(8,128)(2,1)} %pad_maximum_fusion.1.img_ref.twice_ref, bf16[4,64,384]{2,1,0:T(8,128)(2,1)} %get-tuple-element.172.pair_ref), custom_call_target="tpu_custom_call" | custom-call | flops 11098128384 | bytes 7225344 | tf_op jit(solution)/shard_map/expand_grad/pallas_call | solution.py:775
  471.8 2.9 collective-permute-start.8
  475.0 3.1 collective-permute-done.8
  486.7 2.6 collective-permute-start.9
  489.4 1.4 collective-permute-start.10
  492.0 13.8 %soap.3 = (f32[160,2560]{1,0:T(8,128)}, f32[160,2560]{1,0:T(8,128)}, f32[2,8,4,160]{3,2,1,0:T(4,128)}, f32[160,2560]{1,0:T(8,128)}) custom-call(f32[160,2560]{1,0:T(8,128)} %weight_ref.5, bf16[4,160,640]{2,1,0:T(8,128)(2,1)} %slice.88.grad_ref, f32[160,2560]{1,0:T(8,128)} %first_ref.3, f32[160,2560]{1,0:T(8,128)} %second_ref.3, f32[2,8,4,160]{3,2,1,0:T(4,128)} %bitcast.130), custom_call_target="tpu_custom_call" | custom-call | flops 131072000 | bytes 10649600 | tf_op jit(solution)/shard_map/soap/pallas_call | solution.py:1462
  505.8 1.6 multiply_subtract_fusion
  508.3 11.1 %soap.4 = (f32[40,9216]{1,0:T(8,128)}, f32[40,9216]{1,0:T(8,128)}, f32[2,8,4,40]{3,2,1,0:T(4,128)}, f32[40,9216]{1,0:T(8,128)}) custom-call(f32[40,9216]{1,0:T(8,128)} %weight_ref.6, bf16[4,40,2304]{2,1,0:T(8,128)(2,1)} %copy-done.1, f32[40,9216]{1,0:T(8,128)} %first_ref.4, f32[40,9216]{1,0:T(8,128)} %second_ref.4, f32[2,8,4,40]{3,2,1,0:T(4,128)} %bitcast.132), custom_call_target="tpu_custom_call" | custom-call | flops 29491200 | bytes 9584640 | tf_op jit(solution)/shard_map/soap/pallas_call | solution.py:1462
  519.5 2.6 reduce-scatter.11.cloned.1.call-done.refs_2_
  522.0 28.7 %reduce_grads.1 = (bf16[4,18,144]{2,1,0:T(8,128)(2,1)}, bf16[4,32,128]{2,1,0:T(8,128)(2,1)}, bf16[4,144,384]{2,1,0:T(8,128)(2,1)}, bf16[8,4,32,128]{3,2,1,0:T(8,128)(2,1)}) custom-call(bf16[4,4,2,18,144]{4,3,2,1,0:T(8,128)(2,1)} %bitcast.116, bf16[4,4,2,32,128]{4,3,2,1,0:T(8,128)(2,1)} %bitcast.122, ...), custom_call_target="tpu_custom_call" | custom-call | tf_op jit(solution)/shard_map/reduce_grads/pallas_call | solution.py:1203
  556.7 11.4 %soap.5 = (f32[144,1536]{1,0:T(8,128)}, f32[144,1536]{1,0:T(8,128)}, f32[2,8,4,144]{3,2,1,0:T(4,128)}, f32[144,1536]{1,0:T(8,128)}) custom-call(f32[144,1536]{1,0:T(8,128)} %weight_ref.7, bf16[4,144,384]{2,1,0:T(8,128)(2,1)} %get-tuple-element.187.grad_ref, f32[144,1536]{1,0:T(8,128)} %first_ref.5, f32[144,1536]{1,0:T(8,128)} %second_ref.5, ...), custom_call_target="tpu_custom_call" | custom-call | flops 63700992 | bytes 5750784 | tf_op jit(solution)/shard_map/soap/pallas_call | solution.py:1462
  (214 shorter events, 39.9 us)
Async XLA Ops:
  7.2 94.0 %all-gather.4.cloned.1.call-start = ((), (), s32[]{:S(2)}) async-start(), calls=%async_computation.4 | async-start | bytes 6635520 | tf_op jit(solution)/shard_map/all_gather | solution.py:1532
  9.7 149.3 %all-gather.6.cloned.1.call-start = ((), (), s32[]{:S(2)}) async-start(), calls=%async_computation.5 | async-start | bytes 7372800 | tf_op jit(solution)/shard_map/all_gather | solution.py:1533
  10.8 3.6 copy-start.5
  10.8 187.4 %all-gather.8.cloned.1.call-start = ((), (), s32[]{:S(2)}) async-start(), calls=%async_computation.6 | async-start | bytes 2949120 | tf_op jit(solution)/shard_map/all_gather | solution.py:1534
  11.7 296.0 %reduce-scatter.5.cloned.1.call-start = ((), (), s32[]{:S(2)}) async-start(), calls=%async_computation.7 | async-start | bytes 2949120 | tf_op jit(solution)/shard_map/reduce_scatter | solution.py:1565
  55.4 5.1 copy-start.46
  226.8 150.0 %reduce-scatter.7.cloned.1.call-start = ((), (), s32[]{:S(2)}) async-start(), calls=%async_computation.8 | async-start | bytes 7372800 | tf_op jit(solution)/shard_map/reduce_scatter | solution.py:1576
  306.1 137.5 %reduce-scatter.9.cloned.1.call-start = ((), (), s32[]{:S(2)}) async-start(), calls=%async_computation.9 | async-start | bytes 6635520 | tf_op jit(solution)/shard_map/reduce_scatter | solution.py:1590
  376.9 145.2 %reduce-scatter.11.cloned.1.call-start = ((), (), s32[]{:S(2)}) async-start(), calls=%async_computation.10 | async-start | bytes 3981312 | tf_op jit(solution)/shard_map/reduce_scatter | solution.py:1615
  380.1 63.5 %collective-permute-start = (bf16[160,896]{1,0:T(8,128)(2,1)S(1)}, bf16[160,896]{1,0:T(8,128)(2,1)S(1)}, u32[]{:S(2)}, u32[]{:S(2)}) collective-permute-start(bf16[160,896]{1,0:T(8,128)(2,1)S(1)} %get-tuple-element.261), channel_id=1, source_target_pairs={{0,8},{8,16},{16,24},{24,0},{1,9},{9,17},{17,25},{25,1},{2,10},{10... | collective-permute-start | bytes 860168 | tf_op jit(solution)/shard_map/ppermute | solution.py:1243
  381.6 62.0 %collective-permute-start.1 = (bf16[160,896]{1,0:T(8,128)(2,1)S(1)}, bf16[160,896]{1,0:T(8,128)(2,1)S(1)}, u32[]{:S(2)}, u32[]{:S(2)}) collective-permute-start(bf16[160,896]{1,0:T(8,128)(2,1)S(1)} %get-tuple-element.260), channel_id=1, source_target_pairs={{0,16},{8,24},{16,0},{24,8},{1,17},{9,25},{17,1},{25,9},{2,18},{10... | collective-permute-start | bytes 860168 | tf_op jit(solution)/shard_map/ppermute | solution.py:1243
  383.1 60.5 %collective-permute-start.2 = (bf16[160,896]{1,0:T(8,128)(2,1)S(1)}, bf16[160,896]{1,0:T(8,128)(2,1)S(1)}, u32[]{:S(2)}, u32[]{:S(2)}) collective-permute-start(bf16[160,896]{1,0:T(8,128)(2,1)S(1)} %get-tuple-element.259), channel_id=1, source_target_pairs={{0,24},{8,0},{16,8},{24,16},{1,25},{9,1},{17,9},{25,17},{2,26},{10... | collective-permute-start | bytes 860168 | tf_op jit(solution)/shard_map/ppermute | solution.py:1243
  443.6 5.8 %copy-start.8 = (bf16[1,4,40,2304]{3,2,1,0:T(8,128)(2,1)S(1)}, bf16[1,4,40,2304]{3,2,1,0:T(8,128)(2,1)}, u32[]{:S(2)}) copy-start(bf16[1,4,40,2304]{3,2,1,0:T(8,128)(2,1)} %reduce-scatter.9.cloned.1.call-done) | copy-start | bytes 2211844
  445.8 26.0 %collective-permute-start.3 = (bf16[160,896]{1,0:T(8,128)(2,1)S(1)}, bf16[160,896]{1,0:T(8,128)(2,1)S(1)}, u32[]{:S(2)}, u32[]{:S(2)}) collective-permute-start(bf16[160,896]{1,0:T(8,128)(2,1)S(1)} %get-tuple-element.258), channel_id=1, source_target_pairs={{0,8},{8,16},{16,24},{24,0},{1,9},{9,17},{17,25},{25,1},{2,10},{10... | collective-permute-start | bytes 860168 | tf_op jit(solution)/shard_map/ppermute | solution.py:1243
  446.5 28.2 %collective-permute-start.4 = (bf16[160,896]{1,0:T(8,128)(2,1)S(1)}, bf16[160,896]{1,0:T(8,128)(2,1)S(1)}, u32[]{:S(2)}, u32[]{:S(2)}) collective-permute-start(bf16[160,896]{1,0:T(8,128)(2,1)S(1)} %get-tuple-element.258), channel_id=1, source_target_pairs={{0,16},{8,24},{16,0},{24,8},{1,17},{9,25},{17,1},{25,9},{2,18},{10... | collective-permute-start | bytes 860168 | tf_op jit(solution)/shard_map/ppermute | solution.py:1243
  448.0 26.9 %collective-permute-start.5 = (bf16[160,896]{1,0:T(8,128)(2,1)S(1)}, bf16[160,896]{1,0:T(8,128)(2,1)S(1)}, u32[]{:S(2)}, u32[]{:S(2)}) collective-permute-start(bf16[160,896]{1,0:T(8,128)(2,1)S(1)} %get-tuple-element.258), channel_id=1, source_target_pairs={{0,24},{8,0},{16,8},{24,16},{1,25},{9,1},{17,9},{25,17},{2,26},{10... | collective-permute-start | bytes 860168 | tf_op jit(solution)/shard_map/ppermute | solution.py:1243
  450.3 24.7 %collective-permute-start.6 = (bf16[40,2304]{1,0:T(8,128)(2,1)}, bf16[40,2304]{1,0:T(8,128)(2,1)S(1)}, u32[]{:S(2)}, u32[]{:S(2)}) collective-permute-start(bf16[40,2304]{1,0:T(8,128)(2,1)} %get-tuple-element.264), channel_id=1, source_target_pairs={{0,8},{8,16},{16,24},{24,0},{1,9},{9,17},{17,25},{25,1},{2,10},{10... | collective-permute-start | bytes 552968 | tf_op jit(solution)/shard_map/ppermute | solution.py:1243
  450.8 24.1 %collective-permute-start.7 = (bf16[40,2304]{1,0:T(8,128)(2,1)}, bf16[40,2304]{1,0:T(8,128)(2,1)S(1)}, u32[]{:S(2)}, u32[]{:S(2)}) collective-permute-start(bf16[40,2304]{1,0:T(8,128)(2,1)} %get-tuple-element.263), channel_id=1, source_target_pairs={{0,16},{8,24},{16,0},{24,8},{1,17},{9,25},{17,1},{25,9},{2,18},{10... | collective-permute-start | bytes 552968 | tf_op jit(solution)/shard_map/ppermute | solution.py:1243
  471.8 6.3 %collective-permute-start.8 = (bf16[40,2304]{1,0:T(8,128)(2,1)}, bf16[40,2304]{1,0:T(8,128)(2,1)}, u32[]{:S(2)}, u32[]{:S(2)}) collective-permute-start(bf16[40,2304]{1,0:T(8,128)(2,1)} %get-tuple-element.262), channel_id=1, source_target_pairs={{0,24},{8,0},{16,8},{24,16},{1,25},{9,1},{17,9},{25,17},{2,26},{10... | collective-permute-start | bytes 552968 | tf_op jit(solution)/shard_map/ppermute | solution.py:1243
  474.9 5.7 copy-start.44
  474.9 5.8 copy-start.42
  474.9 5.8 %copy-start.14 = (f32[9,8,1152]{2,1,0:T(8,128)S(1)}, f32[9,8,1152]{2,1,0:T(8,128)}, u32[]{:S(2)}) copy-start(f32[9,8,1152]{2,1,0:T(8,128)} %get-tuple-element.155) | copy-start | bytes 995332
  478.1 3.9 copy-start.26
  478.1 3.9 copy-start.6
  478.2 3.9 copy-start.37
  478.4 4.1 copy-start.18
  486.7 20.6 %collective-permute-start.9 = (bf16[40,2304]{1,0:T(8,128)(2,1)S(1)}, bf16[40,2304]{1,0:T(8,128)(2,1)S(1)}, u32[]{:S(2)}, u32[]{:S(2)}) collective-permute-start(bf16[40,2304]{1,0:T(8,128)(2,1)S(1)} %get-tuple-element.256), channel_id=1, source_target_pairs={{0,8},{8,16},{16,24},{24,0},{1,9},{9,17},{17,25},{25,1},{2,10},{10... | collective-permute-start | bytes 552968 | tf_op jit(solution)/shard_map/ppermute | solution.py:1243
  489.4 18.1 %collective-permute-start.10 = (bf16[40,2304]{1,0:T(8,128)(2,1)S(1)}, bf16[40,2304]{1,0:T(8,128)(2,1)S(1)}, u32[]{:S(2)}, u32[]{:S(2)}) collective-permute-start(bf16[40,2304]{1,0:T(8,128)(2,1)S(1)} %get-tuple-element.256), channel_id=1, source_target_pairs={{0,16},{8,24},{16,0},{24,8},{1,17},{9,25},{17,1},{25,9},{2,18},{10... | collective-permute-start | bytes 552968 | tf_op jit(solution)/shard_map/ppermute | solution.py:1243
  490.7 16.7 %collective-permute-start.11 = (bf16[40,2304]{1,0:T(8,128)(2,1)S(1)}, bf16[40,2304]{1,0:T(8,128)(2,1)S(1)}, u32[]{:S(2)}, u32[]{:S(2)}) collective-permute-start(bf16[40,2304]{1,0:T(8,128)(2,1)S(1)} %get-tuple-element.256), channel_id=1, source_target_pairs={{0,24},{8,0},{16,8},{24,16},{1,25},{9,1},{17,9},{25,17},{2,26},{10... | collective-permute-start | bytes 552968 | tf_op jit(solution)/shard_map/ppermute | solution.py:1243
  491.9 13.8 %copy-start.4 = (f32[160,1000]{1,0:T(8,128)S(1)}, f32[160,1000]{1,0:T(8,128)}, u32[]{:S(2)}) copy-start(f32[160,1000]{1,0:T(8,128)} %param.48) | copy-start | bytes 1920004
  491.9 13.8 %copy-start.9 = (f32[160,1000]{1,0:T(8,128)S(1)}, f32[160,1000]{1,0:T(8,128)}, u32[]{:S(2)}) copy-start(f32[160,1000]{1,0:T(8,128)} %param.50) | copy-start | bytes 1920004
  491.9 13.8 %copy-start.10 = (f32[160,1000]{1,0:T(8,128)S(1)}, f32[160,1000]{1,0:T(8,128)}, u32[]{:S(2)}) copy-start(f32[160,1000]{1,0:T(8,128)} %param.49) | copy-start | bytes 1920004
  (36 other events, 75.1 us)
Sparse Core Ops, SparseCore 0:
  10.3 80.3 all-gather.3
  92.9 66.1 all-gather.5
  161.3 34.3 all-gather.7
  226.9 37.4 reduce-scatter.4
  306.2 70.5 reduce-scatter.6
  379.0 64.4 reduce-scatter.8
  478.2 43.7 reduce-scatter.10

commit v7 on v6

--- a/solution.py
+++ b/solution.py
@@ -112,7 +112,7 @@
         copy.start()
 
 
-def sum_close(n_wide, n_dp, scratch):
+def sum_middle(n_wide, n_dp, scratch):
     count = (len(scratch) - 4) // 4
     wide_slots, dp_slots, own, halves = (scratch[k * count : (k + 1) * count] for k in range(4))
     s_wide, r_wide, s_dp, r_dp = scratch[4 * count :]
@@ -120,12 +120,21 @@
         copy.wait()
     for half, total in zip(halves, sum_slots("wide", n_wide, own, wide_slots)):
         half[...] = total
-    copies = sum_copies("dp", n_dp, halves, dp_slots, s_dp, r_dp)
-    for copy in copies:
+    for copy in sum_copies("dp", n_dp, halves, dp_slots, s_dp, r_dp):
         copy.start()
-    for copy in copies:
+
+
+def sum_end(n_wide, n_dp, scratch):
+    count = (len(scratch) - 4) // 4
+    dp_slots, halves = scratch[count : 2 * count], scratch[3 * count : 4 * count]
+    for copy in sum_copies("dp", n_dp, halves, dp_slots, *scratch[4 * count + 2 :]):
         copy.wait()
     return sum_slots("dp", n_dp, halves, dp_slots)
+
+
+def sum_close(n_wide, n_dp, scratch):
+    sum_middle(n_wide, n_dp, scratch)
+    return sum_end(n_wide, n_dp, scratch)
 
 
 def norm_finish(count, every, totals, extras, outs):
@@ -329,14 +338,14 @@
 
     def chunk(index):
         lanes = slice(index * 128, index * 128 + 128)
-        taps = [kern[tap, :, lanes] for tap in range(KSIZE * KSIZE)]
+        taps = [kern[tap, :, lanes].astype(LOW) for tap in range(KSIZE * KSIZE)]
         start = [None] * PIX
 
         def fill(row):
             for pixel in range(row * SIDE, row * SIDE + SIDE):
                 value = hidden_full[pixel, :, lanes]
                 hidden_ref[pixel, :, lanes] = value.astype(LOW)
-                start[pixel] = value * sig(value)
+                start[pixel] = silu_of(value).astype(LOW)
 
         fill(0)
         pooled_act = jnp.zeros((GROUP, 128), FULL)
@@ -344,12 +353,9 @@
             if row + 1 < SIDE:
                 fill(row + 1)
             for pixel in range(row * SIDE, row * SIDE + SIDE):
-                total = None
-                for tap, source in taps_of(pixel):
-                    term = start[source] * taps[tap]
-                    total = term if total is None else total + term
-                turned_ref[pixel, :, lanes] = total.astype(LOW)
-                act = total * sig(total)
+                total = sum_of([start[source] * taps[tap] for tap, source in taps_of(pixel)])
+                turned_ref[pixel, :, lanes] = total
+                act = silu_of(total.astype(FULL))
                 pooled_act = pooled_act + act
                 act_full[pixel, :, lanes] = act
         pooled_act_ref[:, lanes] = pooled_act * (1.0 / PIX)
@@ -751,7 +757,7 @@
     )(widened, grad_feats, coef, head_low, pair_two, twice, before, norm, route, balance, router_t)
 
 
-def kern_grad_kernel(grad_ref, twice_ref, pair_ref, out_ref, turned, routed):
+def kern_grad_kernel(grad_ref, twice_ref, pair_ref, out_ref, turned, routed, between=None):
     images, width = twice_ref.shape[1:]
 
     @pl.when(pl.program_id(0) == 0)
@@ -764,6 +770,8 @@
             routed[pixel * images : (pixel + 1) * images, side * width : (side + 1) * width] = (
                 twice_ref[pixel] * scale
             )
+    if between is not None:
+        between()
     product = dot_nn(turned[...], routed[...])
     for side in range(2):
         out_ref[side] = product[:, side * width : (side + 1) * width].astype(LOW)
@@ -798,16 +806,21 @@
     def _():
         greet(n_wide, n_dp)
 
-    kern_grad_kernel(grad_ref, twice_ref, pair_ref, out_ref, turned, routed)
+    def between():
+        @pl.when(step == 0)
+        def _():
+            await_greetings(n_wide, n_dp)
+            sum_open(n_wide, n_dp, [sums_ref[...]], small)
+
+    kern_grad_kernel(grad_ref, twice_ref, pair_ref, out_ref, turned, routed, between)
 
     @pl.when(step == 0)
     def _():
-        await_greetings(n_wide, n_dp)
-        sum_open(n_wide, n_dp, [sums_ref[...]], small)
+        sum_middle(n_wide, n_dp, small)
 
     @pl.when(step == pl.num_programs(0) - 1)
     def _():
-        totals = sum_close(n_wide, n_dp, small)
+        totals = sum_end(n_wide, n_dp, small)
         back_finish(count, totals, (norm_ref,), (coef_ref, total_ref))
 
 

time: 580 us -> 578 us (level)
  Pallas kernels: 473 us -> 467 us
  transfers between devices with their start and end apart: 19 -> 19, of which waited for: 4 -> 4; matrix products, arithmetic and copies ran while one was open for 5% -> 5% of each run, Pallas kernels for 71% -> 70%
where the time goes in v7:
time: 578 us; the launch traced here: 574 us
  Pallas kernels  467 us (81%)
  waiting for transfers between devices  23.5 us (4%)
  local copies, waits for them, and re-layouts  21.2 us (4%)
  other arithmetic  21 us (4%)
  between operations  19.8 us (3%)
  starting transfers between devices  16.8 us (3%)
    pallas_call x1, Pallas kernels, expand_back(): device_kernel(expand_back_kernel, 'expand_back', images // GROUP, [images...  59 us
    pallas_call x1, Pallas kernels, project_forward(): device_kernel(functools.partial(project_kernel, n_wide, n_dp, every * PIX...  48.9 us
    pallas_call x1, Pallas kernels, head_back(): device_kernel(head_back_kernel, 'head_back', images // GROUP, [images_blo...  39.9 us
    pallas_call x1, Pallas kernels, head_forward(): device_kernel(functools.partial(head_kernel, n_wide, n_dp, every * PIX, e...  39 us
    pallas_call x1, Pallas kernels, gather_expand(): pl.pallas_call(functools.partial(gather_kernel, n_wide, n_dp), name='gath...  37.2 us
    pallas_call x1, Pallas kernels, project_back(): device_kernel(project_back_kernel, 'project_back', images // GROUP, [imag...  36.7 us
    pallas_call x1, Pallas kernels, expand_forward(): device_kernel(expand_kernel, 'expand_forward', images // GROUP, [images_b...  36.6 us
    pallas_call x3, Pallas kernels, soap(): device_kernel(functools.partial(soap_kernel, gained), 'soap', PAIRS, [col...  36.4 us
  transfers between devices with their start and end apart: 19, of which 4 were waited for; matrix products, arithmetic and copies ran while one was open for 5% of the time, Pallas kernels for 70%

profile of v7, /device:TPU:0, one launch (start us, length us, event | category | flops | bytes accessed | tf_op | source)
XLA Modules:
  0.0 574.3 jit_solution(8863402146228159052)
XLA Ops:
  7.3 2.4 convert_element_type.127
  14.4 2.4 pad_maximum_fusion.1.img_ref.twice_ref
  18.2 37.2 %gather_expand.1 = (bf16[4,4,2,144,384]{4,3,2,1,0:T(8,128)(2,1)}, bf16[8,80,144]{2,1,0:T(8,128)(2,1)}) custom-call(f32[144,1536]{1,0:T(8,128)} %weight_ref.7, bf16[80,144]{1,0:T(8,128)(2,1)} %pad.8.depth_ref), custom_call_target="tpu_custom_call" | custom-call | tf_op jit(solution)/shard_map/gather_expand/pallas_call | solution.py:1352
  61.2 36.6 %expand_forward.1 = (bf16[49,64,1152]{2,1,0:T(8,128)(2,1)}, bf16[49,64,1152]{2,1,0:T(8,128)(2,1)}, bf16[49,64,1152]{2,1,0:T(8,128)(2,1)}, f32[64,8]{1,0:T(8,128)...) custom-call(bf16[49,64,384]{2,1,0:T(8,128)(2,1)} %pad_maximum_fusion, ...), custom_call_target="tpu_custom_call" | custom-call | flops 11098128384 | bytes 28901376 | tf_op jit(solution)/shard_map/expand_forward/pallas_call | solution.py:383
  97.9 48.9 %project_forward.1 = (bf16[49,64,2560]{2,1,0:T(8,128)(2,1)}, f32[49,64,320]{2,1,0:T(8,128)}, f32[8,320]{1,0:T(8,128)}, f32[1,8]{1,0:T(1,128)}) custom-call(bf16[49,64,1152]{2,1,0:T(8,128)(2,1)} %get-tuple-element.120.scaled_ref, bf16[320,9216]{1,0:T(8,128)(2,1)} %all-gather.4.cloned.1.call-done.source, bf16[4,64,640]{2,1,0:T(8,128)(2,1)} %get-tuple-element.121.pair_ref, ...), custom_call_target="tpu_custom_call" | custom-call | flops 18496880640 | bytes 23281664 | tf_op jit(solution)/shard_map/project_forward/pallas_call | solution.py:480
  146.9 12.1 %all-gather.6.cloned.1.call-done.weight_ref = bf16[1280,2560]{1,0:T(8,128)(2,1)} async-done(((bf16[160,2560]{1,0:T(8,128)(2,1)}), bf16[1280,2560]{1,0:T(8,128)(2,1)}) %all-gather.6.cloned.1.call-update) | async-done | bytes 6553616 | tf_op jit(solution)/shard_map/all_gather | solution.py:1546
  159.0 39.0 %head_forward.1 = (bf16[49,64,1280]{2,1,0:T(8,128)(2,1)}, bf16[49,64,640]{2,1,0:T(8,128)(2,1)}, f32[64,8]{1,0:T(8,128)}, bf16[4,64,640]{2,1,0:T(8,128)(2,1)}, f3...) custom-call(f32[49,64,320]{2,1,0:T(8,128)} %get-tuple-element.123.before_ref, ...), custom_call_target="tpu_custom_call" | custom-call | flops 20552089600 | bytes 10035200 | tf_op jit(solution)/shard_map/head_forward/pallas_call | solution.py:557
  198.1 23.3 %loss_part.1 = (bf16[64,1280]{1,0:T(8,128)(2,1)}, bf16[64,1024]{1,0:T(8,128)(2,1)}, f32[64,1280]{1,0:T(8,128)}, f32[4,1280]{1,0:T(4,128)}, f32[2,1280]{1,0:T(2,128)}, /*index=5*/f32[1,1]{1,0:T(1,128)}, f32[1,1000]{1,0:T(1,128)}) custom-call(bf16[49,64,1280]{2,1,0:T(8,128)(2,1)} %get-tuple-element.125.widened_ref, f32[8,1280]{1,0:T(8,128)} %get-tuple-element.126.norm_ref, ...), custom_call_target="tpu_custom_call" | custom-call | flops 327680000 | bytes 8028160 | tf_op jit(solution)/shard_map/loss_part/pallas_call | solution.py:652
  221.5 1.3 fusion.3
  224.8 1.8 pad_maximum_fusion
  229.7 39.9 %head_back.1 = (bf16[49,64,1280]{2,1,0:T(8,128)(2,1)}, f32[49,64,320]{2,1,0:T(8,128)}, f32[64,8]{1,0:T(8,128)}, f32[2,320]{1,0:T(2,128)}) custom-call(bf16[49,64,1280]{2,1,0:T(8,128)(2,1)} %get-tuple-element.125.widened_ref, f32[64,1280]{1,0:T(8,128)} %get-tuple-element.133.grad_feats_ref, f32[4,1280]{1,0:T(4,128)} %get-tuple-element.134.coef_ref, ...), custom_call_target="tpu_custom_call" | custom-call | flops 20552089600 | bytes 18063360 | tf_op jit(solution)/shard_map/head_back/pallas_call | solution.py:738
  269.6 33.1 %head_grad.1 = (f32[4,320]{1,0:T(4,128)}, f32[2,320]{1,0:T(2,128)}, bf16[4,1280,640]{2,1,0:T(8,128)(2,1)}) custom-call(f32[2,320]{1,0:T(2,128)} %get-tuple-element.139.sums_ref, f32[8,320]{1,0:T(8,128)} %get-tuple-element.124.norm_ref, bf16[49,64,1280]{2,1,0:T(8,128)(2,1)} %get-tuple-element.140.grad_ref, bf16[49,64,640]{2,1,0:T(8,128)(2,1)} %get-tuple-element.136.twice_ref, ...), custom_call_target="tpu_custom_call" | custom-call | flops 20552089600 | bytes 8028160 | tf_op jit(solution)/shard_map/head_grad/pallas_call | solution.py:831
  304.3 36.7 %project_back.1 = (bf16[49,64,320]{2,1,0:T(8,128)(2,1)}, bf16[49,64,1152]{2,1,0:T(8,128)(2,1)}, f32[64,8]{1,0:T(8,128)}) custom-call(f32[49,64,320]{2,1,0:T(8,128)} %get-tuple-element.138.grad_ref, f32[49,64,320]{2,1,0:T(8,128)} %get-tuple-element.123.before_ref, f32[4,320]{1,0:T(4,128)} %get-tuple-element.143.coef_ref, ...), custom_call_target="tpu_custom_call" | custom-call | flops 18496880640 | bytes 23281664 | tf_op jit(solution)/shard_map/project_back/pallas_call | solution.py:930
  341.0 28.4 %project_grad.1 = bf16[8,4,40,2304]{3,2,1,0:T(8,128)(2,1)} custom-call(bf16[49,64,320]{2,1,0:T(8,128)(2,1)} %get-tuple-element.145.grad_ref, bf16[49,64,1152]{2,1,0:T(8,128)(2,1)} %get-tuple-element.120.scaled_ref, bf16[4,2,3136]{2,1,0:T(2,128)(2,1)} %tile.9.scale_ref), custom_call_target="tpu_custom_call" | custom-call | flops 18496880640 | bytes 9232384 | tf_op jit(solution)/shard_map/project_grad/pallas_call | solution.py:874
  369.4 5.5 reduce-scatter.7.cloned.1.call-done
  378.1 1.5 collective-permute-start
  379.6 1.5 collective-permute-start.1
  381.1 1.5 collective-permute-start.2
  382.5 59.0 %expand_back.1 = (bf16[49,64,1152]{2,1,0:T(8,128)(2,1)}, f32[64,8]{1,0:T(8,128)}, f32[64,1152]{1,0:T(8,128)}, f32[64,48]{1,0:T(8,128)}, f32[9,8,1152]{2,1,0:T(8,128)}) custom-call(bf16[49,64,1152]{2,1,0:T(8,128)(2,1)} %get-tuple-element.149.grad_scaled_ref, bf16[49,64,1152]{2,1,0:T(8,128)(2,1)} %get-tuple-element.150.turned_ref, ...), custom_call_target="tpu_custom_call" | custom-call | flops 11098128384 | bytes 28901376 | tf_op jit(solution)/shard_map/expand_back/pallas_call | solution.py:1059
  444.5 1.4 collective-permute-start.4
  446.0 1.5 collective-permute-start.5
  449.7 20.2 %expand_grad.1 = bf16[4,1152,384]{2,1,0:T(8,128)(2,1)} custom-call(bf16[49,64,1152]{2,1,0:T(8,128)(2,1)} %get-tuple-element.171.grad_ref, bf16[49,64,384]{2,1,0:T(8,128)(2,1)} %pad_maximum_fusion.1.img_ref.twice_ref, bf16[4,64,384]{2,1,0:T(8,128)(2,1)} %get-tuple-element.172.pair_ref), custom_call_target="tpu_custom_call" | custom-call | flops 11098128384 | bytes 7225344 | tf_op jit(solution)/shard_map/expand_grad/pallas_call | solution.py:783
  469.8 2.9 collective-permute-start.8
  473.0 3.1 collective-permute-done.8
  484.8 2.6 collective-permute-start.9
  487.4 1.4 collective-permute-start.10
  490.0 13.8 %soap.3 = (f32[160,2560]{1,0:T(8,128)}, f32[160,2560]{1,0:T(8,128)}, f32[2,8,4,160]{3,2,1,0:T(4,128)}, f32[160,2560]{1,0:T(8,128)}) custom-call(f32[160,2560]{1,0:T(8,128)} %weight_ref.5, bf16[4,160,640]{2,1,0:T(8,128)(2,1)} %slice.88.grad_ref, f32[160,2560]{1,0:T(8,128)} %first_ref.3, f32[160,2560]{1,0:T(8,128)} %second_ref.3, f32[2,8,4,160]{3,2,1,0:T(4,128)} %bitcast.130), custom_call_target="tpu_custom_call" | custom-call | flops 131072000 | bytes 10649600 | tf_op jit(solution)/shard_map/soap/pallas_call | solution.py:1475
  503.8 1.6 multiply_subtract_fusion
  506.4 11.1 %soap.4 = (f32[40,9216]{1,0:T(8,128)}, f32[40,9216]{1,0:T(8,128)}, f32[2,8,4,40]{3,2,1,0:T(4,128)}, f32[40,9216]{1,0:T(8,128)}) custom-call(f32[40,9216]{1,0:T(8,128)} %weight_ref.6, bf16[4,40,2304]{2,1,0:T(8,128)(2,1)} %copy-done.1, f32[40,9216]{1,0:T(8,128)} %first_ref.4, f32[40,9216]{1,0:T(8,128)} %second_ref.4, f32[2,8,4,40]{3,2,1,0:T(4,128)} %bitcast.132), custom_call_target="tpu_custom_call" | custom-call | flops 29491200 | bytes 9584640 | tf_op jit(solution)/shard_map/soap/pallas_call | solution.py:1475
  517.5 2.6 reduce-scatter.11.cloned.1.call-done.refs_2_
  520.1 28.7 %reduce_grads.1 = (bf16[4,18,144]{2,1,0:T(8,128)(2,1)}, bf16[4,32,128]{2,1,0:T(8,128)(2,1)}, bf16[4,144,384]{2,1,0:T(8,128)(2,1)}, bf16[8,4,32,128]{3,2,1,0:T(8,128)(2,1)}) custom-call(bf16[4,4,2,18,144]{4,3,2,1,0:T(8,128)(2,1)} %bitcast.116, bf16[4,4,2,32,128]{4,3,2,1,0:T(8,128)(2,1)} %bitcast.122, ...), custom_call_target="tpu_custom_call" | custom-call | tf_op jit(solution)/shard_map/reduce_grads/pallas_call | solution.py:1216
  554.7 11.5 %soap.5 = (f32[144,1536]{1,0:T(8,128)}, f32[144,1536]{1,0:T(8,128)}, f32[2,8,4,144]{3,2,1,0:T(4,128)}, f32[144,1536]{1,0:T(8,128)}) custom-call(f32[144,1536]{1,0:T(8,128)} %weight_ref.7, bf16[4,144,384]{2,1,0:T(8,128)(2,1)} %get-tuple-element.187.grad_ref, f32[144,1536]{1,0:T(8,128)} %first_ref.5, f32[144,1536]{1,0:T(8,128)} %second_ref.5, ...), custom_call_target="tpu_custom_call" | custom-call | flops 63700992 | bytes 5750784 | tf_op jit(solution)/shard_map/soap/pallas_call | solution.py:1475
  (214 shorter events, 39.8 us)
Async XLA Ops:
  7.2 90.7 %all-gather.4.cloned.1.call-start = ((), (), s32[]{:S(2)}) async-start(), calls=%async_computation.4 | async-start | bytes 6635520 | tf_op jit(solution)/shard_map/all_gather | solution.py:1545
  9.7 149.3 %all-gather.6.cloned.1.call-start = ((), (), s32[]{:S(2)}) async-start(), calls=%async_computation.5 | async-start | bytes 7372800 | tf_op jit(solution)/shard_map/all_gather | solution.py:1546
  10.8 3.6 copy-start.5
  10.8 187.3 %all-gather.8.cloned.1.call-start = ((), (), s32[]{:S(2)}) async-start(), calls=%async_computation.6 | async-start | bytes 2949120 | tf_op jit(solution)/shard_map/all_gather | solution.py:1547
  11.7 292.6 %reduce-scatter.5.cloned.1.call-start = ((), (), s32[]{:S(2)}) async-start(), calls=%async_computation.7 | async-start | bytes 2949120 | tf_op jit(solution)/shard_map/reduce_scatter | solution.py:1578
  55.4 5.1 copy-start.46
  226.7 148.1 %reduce-scatter.7.cloned.1.call-start = ((), (), s32[]{:S(2)}) async-start(), calls=%async_computation.8 | async-start | bytes 7372800 | tf_op jit(solution)/shard_map/reduce_scatter | solution.py:1589
  302.7 139.0 %reduce-scatter.9.cloned.1.call-start = ((), (), s32[]{:S(2)}) async-start(), calls=%async_computation.9 | async-start | bytes 6635520 | tf_op jit(solution)/shard_map/reduce_scatter | solution.py:1603
  374.9 145.2 %reduce-scatter.11.cloned.1.call-start = ((), (), s32[]{:S(2)}) async-start(), calls=%async_computation.10 | async-start | bytes 3981312 | tf_op jit(solution)/shard_map/reduce_scatter | solution.py:1628
  378.1 63.5 %collective-permute-start = (bf16[160,896]{1,0:T(8,128)(2,1)S(1)}, bf16[160,896]{1,0:T(8,128)(2,1)S(1)}, u32[]{:S(2)}, u32[]{:S(2)}) collective-permute-start(bf16[160,896]{1,0:T(8,128)(2,1)S(1)} %get-tuple-element.261), channel_id=1, source_target_pairs={{0,8},{8,16},{16,24},{24,0},{1,9},{9,17},{17,25},{25,1},{2,10},{10... | collective-permute-start | bytes 860168 | tf_op jit(solution)/shard_map/ppermute | solution.py:1256
  379.6 62.0 %collective-permute-start.1 = (bf16[160,896]{1,0:T(8,128)(2,1)S(1)}, bf16[160,896]{1,0:T(8,128)(2,1)S(1)}, u32[]{:S(2)}, u32[]{:S(2)}) collective-permute-start(bf16[160,896]{1,0:T(8,128)(2,1)S(1)} %get-tuple-element.260), channel_id=1, source_target_pairs={{0,16},{8,24},{16,0},{24,8},{1,17},{9,25},{17,1},{25,9},{2,18},{10... | collective-permute-start | bytes 860168 | tf_op jit(solution)/shard_map/ppermute | solution.py:1256
  381.1 60.5 %collective-permute-start.2 = (bf16[160,896]{1,0:T(8,128)(2,1)S(1)}, bf16[160,896]{1,0:T(8,128)(2,1)S(1)}, u32[]{:S(2)}, u32[]{:S(2)}) collective-permute-start(bf16[160,896]{1,0:T(8,128)(2,1)S(1)} %get-tuple-element.259), channel_id=1, source_target_pairs={{0,24},{8,0},{16,8},{24,16},{1,25},{9,1},{17,9},{25,17},{2,26},{10... | collective-permute-start | bytes 860168 | tf_op jit(solution)/shard_map/ppermute | solution.py:1256
  441.6 5.8 %copy-start.8 = (bf16[1,4,40,2304]{3,2,1,0:T(8,128)(2,1)S(1)}, bf16[1,4,40,2304]{3,2,1,0:T(8,128)(2,1)}, u32[]{:S(2)}) copy-start(bf16[1,4,40,2304]{3,2,1,0:T(8,128)(2,1)} %reduce-scatter.9.cloned.1.call-done) | copy-start | bytes 2211844
  443.9 26.0 %collective-permute-start.3 = (bf16[160,896]{1,0:T(8,128)(2,1)S(1)}, bf16[160,896]{1,0:T(8,128)(2,1)S(1)}, u32[]{:S(2)}, u32[]{:S(2)}) collective-permute-start(bf16[160,896]{1,0:T(8,128)(2,1)S(1)} %get-tuple-element.258), channel_id=1, source_target_pairs={{0,8},{8,16},{16,24},{24,0},{1,9},{9,17},{17,25},{25,1},{2,10},{10... | collective-permute-start | bytes 860168 | tf_op jit(solution)/shard_map/ppermute | solution.py:1256
  444.5 28.3 %collective-permute-start.4 = (bf16[160,896]{1,0:T(8,128)(2,1)S(1)}, bf16[160,896]{1,0:T(8,128)(2,1)S(1)}, u32[]{:S(2)}, u32[]{:S(2)}) collective-permute-start(bf16[160,896]{1,0:T(8,128)(2,1)S(1)} %get-tuple-element.258), channel_id=1, source_target_pairs={{0,16},{8,24},{16,0},{24,8},{1,17},{9,25},{17,1},{25,9},{2,18},{10... | collective-permute-start | bytes 860168 | tf_op jit(solution)/shard_map/ppermute | solution.py:1256
  446.0 26.9 %collective-permute-start.5 = (bf16[160,896]{1,0:T(8,128)(2,1)S(1)}, bf16[160,896]{1,0:T(8,128)(2,1)S(1)}, u32[]{:S(2)}, u32[]{:S(2)}) collective-permute-start(bf16[160,896]{1,0:T(8,128)(2,1)S(1)} %get-tuple-element.258), channel_id=1, source_target_pairs={{0,24},{8,0},{16,8},{24,16},{1,25},{9,1},{17,9},{25,17},{2,26},{10... | collective-permute-start | bytes 860168 | tf_op jit(solution)/shard_map/ppermute | solution.py:1256
  448.3 24.7 %collective-permute-start.6 = (bf16[40,2304]{1,0:T(8,128)(2,1)}, bf16[40,2304]{1,0:T(8,128)(2,1)S(1)}, u32[]{:S(2)}, u32[]{:S(2)}) collective-permute-start(bf16[40,2304]{1,0:T(8,128)(2,1)} %get-tuple-element.264), channel_id=1, source_target_pairs={{0,8},{8,16},{16,24},{24,0},{1,9},{9,17},{17,25},{25,1},{2,10},{10... | collective-permute-start | bytes 552968 | tf_op jit(solution)/shard_map/ppermute | solution.py:1256
  448.8 24.2 %collective-permute-start.7 = (bf16[40,2304]{1,0:T(8,128)(2,1)}, bf16[40,2304]{1,0:T(8,128)(2,1)S(1)}, u32[]{:S(2)}, u32[]{:S(2)}) collective-permute-start(bf16[40,2304]{1,0:T(8,128)(2,1)} %get-tuple-element.263), channel_id=1, source_target_pairs={{0,16},{8,24},{16,0},{24,8},{1,17},{9,25},{17,1},{25,9},{2,18},{10... | collective-permute-start | bytes 552968 | tf_op jit(solution)/shard_map/ppermute | solution.py:1256
  469.8 6.3 %collective-permute-start.8 = (bf16[40,2304]{1,0:T(8,128)(2,1)}, bf16[40,2304]{1,0:T(8,128)(2,1)}, u32[]{:S(2)}, u32[]{:S(2)}) collective-permute-start(bf16[40,2304]{1,0:T(8,128)(2,1)} %get-tuple-element.262), channel_id=1, source_target_pairs={{0,24},{8,0},{16,8},{24,16},{1,25},{9,1},{17,9},{25,17},{2,26},{10... | collective-permute-start | bytes 552968 | tf_op jit(solution)/shard_map/ppermute | solution.py:1256
  472.9 5.7 copy-start.44
  472.9 5.8 %copy-start.42 = (f32[2,1280]{1,0:T(2,128)S(1)}, f32[2,1280]{1,0:T(2,128)}, u32[]{:S(2)}) copy-start(f32[2,1280]{1,0:T(2,128)} %get-tuple-element.206) | copy-start | bytes 30724
  472.9 5.8 %copy-start.14 = (f32[9,8,1152]{2,1,0:T(8,128)S(1)}, f32[9,8,1152]{2,1,0:T(8,128)}, u32[]{:S(2)}) copy-start(f32[9,8,1152]{2,1,0:T(8,128)} %get-tuple-element.155) | copy-start | bytes 995332
  476.2 3.9 copy-start.26
  476.2 3.9 copy-start.6
  476.2 3.9 copy-start.37
  476.4 4.1 copy-start.18
  484.8 20.6 %collective-permute-start.9 = (bf16[40,2304]{1,0:T(8,128)(2,1)S(1)}, bf16[40,2304]{1,0:T(8,128)(2,1)S(1)}, u32[]{:S(2)}, u32[]{:S(2)}) collective-permute-start(bf16[40,2304]{1,0:T(8,128)(2,1)S(1)} %get-tuple-element.256), channel_id=1, source_target_pairs={{0,8},{8,16},{16,24},{24,0},{1,9},{9,17},{17,25},{25,1},{2,10},{10... | collective-permute-start | bytes 552968 | tf_op jit(solution)/shard_map/ppermute | solution.py:1256
  487.4 18.1 %collective-permute-start.10 = (bf16[40,2304]{1,0:T(8,128)(2,1)S(1)}, bf16[40,2304]{1,0:T(8,128)(2,1)S(1)}, u32[]{:S(2)}, u32[]{:S(2)}) collective-permute-start(bf16[40,2304]{1,0:T(8,128)(2,1)S(1)} %get-tuple-element.256), channel_id=1, source_target_pairs={{0,16},{8,24},{16,0},{24,8},{1,17},{9,25},{17,1},{25,9},{2,18},{10... | collective-permute-start | bytes 552968 | tf_op jit(solution)/shard_map/ppermute | solution.py:1256
  488.8 16.7 %collective-permute-start.11 = (bf16[40,2304]{1,0:T(8,128)(2,1)S(1)}, bf16[40,2304]{1,0:T(8,128)(2,1)S(1)}, u32[]{:S(2)}, u32[]{:S(2)}) collective-permute-start(bf16[40,2304]{1,0:T(8,128)(2,1)S(1)} %get-tuple-element.256), channel_id=1, source_target_pairs={{0,24},{8,0},{16,8},{24,16},{1,25},{9,1},{17,9},{25,17},{2,26},{10... | collective-permute-start | bytes 552968 | tf_op jit(solution)/shard_map/ppermute | solution.py:1256
  489.9 13.8 %copy-start.4 = (f32[160,1000]{1,0:T(8,128)S(1)}, f32[160,1000]{1,0:T(8,128)}, u32[]{:S(2)}) copy-start(f32[160,1000]{1,0:T(8,128)} %param.48) | copy-start | bytes 1920004
  489.9 13.8 %copy-start.9 = (f32[160,1000]{1,0:T(8,128)S(1)}, f32[160,1000]{1,0:T(8,128)}, u32[]{:S(2)}) copy-start(f32[160,1000]{1,0:T(8,128)} %param.50) | copy-start | bytes 1920004
  490.0 13.8 %copy-start.10 = (f32[160,1000]{1,0:T(8,128)S(1)}, f32[160,1000]{1,0:T(8,128)}, u32[]{:S(2)}) copy-start(f32[160,1000]{1,0:T(8,128)} %param.49) | copy-start | bytes 1920004
  (36 other events, 75.1 us)
Sparse Core Ops, SparseCore 0:
  10.3 80.3 all-gather.3
  92.9 66.0 all-gather.5
  161.2 34.2 all-gather.7
  226.8 37.3 reduce-scatter.4
  302.8 71.9 reduce-scatter.6
  377.0 64.4 reduce-scatter.8
  476.3 43.7 reduce-scatter.10
